TPU v7x, 512 devices: a whole 4x8x8 slice. The times are simulated.
512 devices in a mesh: row: 64 (over y, x, core), col: 8 (over z).
Axes of the slice: x: 4, y: 8, z: 8, core: 2. Of those that a mesh axis runs over, the one named last changes fastest.
Arguments:
- tokens: bfloat16 [8192, 16384], P('row', 'col'), may hold values from -6 to 6
- queries: bfloat16 [8192, 16384], P('row', 'col'), may hold values from -6 to 6
- probes: bfloat16 [8192, 16384], P('row', 'col'), may hold values from -6 to 6
- w_key: bfloat16 [16384, 1024], P('row', 'col'), may hold values from -2 to 2
- w_value: bfloat16 [16384, 1024], P('row', 'col'), may hold values from -0.046875 to 0.046875
- down_proj: bfloat16 [16384, 64], P('col'), may hold values from -0.046875 to 0.046875
- up_key: bfloat16 [64, 1024], P(None, 'col'), may hold values from -0.75 to 0.75
- up_value: bfloat16 [64, 1024], P(None, 'col'), may hold values from -0.75 to 0.75
- lengths: int32 [64, 8], P('row'), may hold values from 1 to 42, 128 in all within a row
Outputs:
- grad_down: float32 [16384, 64], P('col')
- grad_up_key: float32 [64, 1024], P(None, 'col')
- grad_up_value: float32 [64, 1024], P(None, 'col')
Inputs may be any that keep to these rules, and one draw needn't show every extreme that they name: Each row holds the lengths of 8 documents that fill one block of 128 tokens exactly; the longest is 42 tokens.
All inputs are finite; a program needn't handle non-finite values.
Results may differ from a plain program's by a relative error of at most 0.019.
Values may be sent and summed in bfloat16 or wider, within the bound.
No kernel may reach another device: no remote copies, remote signals or barrier semaphores. Data moves between devices by JAX's collectives and lax.ppermute only.
A program may use at most 64 MiB of HBM per device.

v0:
```python
import jax
import jax.numpy as jnp
from jax import lax
from jax.sharding import PartitionSpec as P

HD = 128
QPK = 16


npo_beta = 0.5


def attention_probs(query_heads, key_heads, allowed, score_scale):
    scores = (
        jnp.einsum("tgqd,sgd->gqts", query_heads, key_heads, preferred_element_type=jnp.float32)
        * score_scale
    )
    scores = jnp.where(allowed, scores, -1e30)
    row_peak = jnp.max(scores, axis=-1, keepdims=True)
    row_exp = jnp.exp(scores - row_peak)
    return row_exp / jnp.sum(row_exp, axis=-1, keepdims=True)


def on_device(tokens, queries, probes, w_key, w_value, down_proj, up_key, up_value, lengths):
    row_count = tokens.shape[0]
    width = w_key.shape[1]
    groups = width // HD
    whole = lax.all_gather(tokens, "col", axis=1, tiled=True)
    key_full = jnp.dot(
        whole, lax.all_gather(w_key, "row", axis=0, tiled=True), preferred_element_type=jnp.float32
    )
    value_full = jnp.dot(
        whole,
        lax.all_gather(w_value, "row", axis=0, tiled=True),
        preferred_element_type=jnp.float32,
    )
    low_rank = lax.psum(jnp.dot(tokens, down_proj, preferred_element_type=jnp.float32), "col")
    low_half = low_rank.astype(jnp.bfloat16)
    key_ref = key_full.astype(jnp.bfloat16).reshape(row_count, groups, HD)
    value_ref = value_full.astype(jnp.bfloat16).reshape(row_count, groups, HD)
    key_pol = (
        (key_full + jnp.dot(low_half, up_key, preferred_element_type=jnp.float32))
        .astype(jnp.bfloat16)
        .reshape(row_count, groups, HD)
    )
    value_pol = (
        (value_full + jnp.dot(low_half, up_value, preferred_element_type=jnp.float32))
        .astype(jnp.bfloat16)
        .reshape(row_count, groups, HD)
    )
    query_heads = queries.reshape(row_count, groups, QPK, HD)
    probe_heads = probes.reshape(row_count, groups, QPK, HD)
    doc_ends = jnp.cumsum(lengths[0])
    places = jnp.arange(row_count, dtype=jnp.int32)
    doc_of = jnp.sum((places[:, None] >= doc_ends[None, :]).astype(jnp.int32), axis=1)
    allowed = (doc_of[:, None] == doc_of[None, :]) & (places[:, None] >= places[None, :])
    score_scale = HD ** (-0.5)
    probe_scale = (queries.shape[1] * lax.axis_size("col")) ** (-0.5)
    probs_ref = attention_probs(query_heads, key_ref, allowed, score_scale)
    probs_pol = attention_probs(query_heads, key_pol, allowed, score_scale)
    half_pol = probs_pol.astype(jnp.bfloat16)
    out_ref = jnp.einsum(
        "gqts,sgd->tgqd",
        probs_ref.astype(jnp.bfloat16),
        value_ref,
        preferred_element_type=jnp.float32,
    )
    out_pol = jnp.einsum("gqts,sgd->tgqd", half_pol, value_pol, preferred_element_type=jnp.float32)
    gap_local = (
        jnp.sum((out_pol - out_ref) * probe_heads.astype(jnp.float32), axis=(1, 2, 3)) * probe_scale
    )
    gap_part = lax.psum(gap_local, "col")
    member = (doc_of[:, None] == jnp.arange(lengths.shape[1], dtype=jnp.int32)[None, :]).astype(
        jnp.float32
    )
    doc_gap = jnp.sum(member * gap_part[:, None], axis=0)
    token_gap = jnp.sum(member * doc_gap[None, :], axis=1)
    weight = 2.0 * jax.nn.sigmoid(npo_beta * token_gap)
    grad_out = (weight[:, None, None, None] * probe_scale * probe_heads.astype(jnp.float32)).astype(
        jnp.bfloat16
    )
    grad_value = jnp.einsum(
        "gqts,tgqd->sgd", half_pol, grad_out, preferred_element_type=jnp.float32
    ).astype(jnp.bfloat16)
    grad_probs = jnp.einsum(
        "tgqd,sgd->gqts", grad_out, value_pol, preferred_element_type=jnp.float32
    )
    grad_scores = (
        probs_pol
        * (grad_probs - jnp.sum(probs_pol * grad_probs, axis=-1, keepdims=True))
        * score_scale
    ).astype(jnp.bfloat16)
    grad_key = jnp.einsum(
        "gqts,tgqd->sgd", grad_scores, query_heads, preferred_element_type=jnp.float32
    ).astype(jnp.bfloat16)
    grad_key = grad_key.reshape(row_count, width)
    grad_value = grad_value.reshape(row_count, width)
    key_term = jnp.dot(low_half.T, grad_key, preferred_element_type=jnp.float32)
    value_term = jnp.dot(low_half.T, grad_value, preferred_element_type=jnp.float32)
    back_local = jnp.dot(grad_key, up_key.T, preferred_element_type=jnp.float32) + jnp.dot(
        grad_value, up_value.T, preferred_element_type=jnp.float32
    )
    back_half = lax.psum(back_local.astype(jnp.bfloat16), "col")
    down_term = jnp.dot(tokens.T, back_half, preferred_element_type=jnp.float32)
    grad_down, grad_up_key, grad_up_value = lax.psum((down_term, key_term, value_term), "row")
    return (grad_down, grad_up_key, grad_up_value)


def solution(mesh):
    in_specs = (
        P("row", "col"),
        P("row", "col"),
        P("row", "col"),
        P("row", "col"),
        P("row", "col"),
        P("col", None),
        P(None, "col"),
        P(None, "col"),
        P("row", None),
    )
    out_specs = (P("col", None), P(None, "col"), P(None, "col"))
    return jax.shard_map(
        on_device, mesh=mesh, in_specs=in_specs, out_specs=out_specs, check_vma=False
    )
```

profile of v0, /device:TPU:1, one launch (start us, length us, event | category | flops | bytes accessed | tf_op | source)
XLA Modules:
  0.0 678.6 jit_solution(13773820153048202256)
XLA Ops:
  7.2 0.0 copy-start
  7.2 0.0 all-gather.4.cloned.1.call-start
  7.2 0.7 all-gather.4.cloned.1.call-update
  7.9 0.0 all-gather.6.cloned.1.call-start
  8.0 0.7 all-gather.6.cloned.1.call-update
  8.7 0.0 all-gather.8.cloned.1.call-start
  8.7 0.7 all-gather.8.cloned.1.call-update
  9.4 0.0 all-reduce.6.cloned.1.call-start
  9.4 2.3 copy.29
  11.7 0.8 reduce-window.8
  12.6 1.4 fusion.51
  14.0 31.3 %psum.42 = bf16[128,64]{0,1:T(8,128)(2,1)S(1)} all-reduce(f32[128,64]{0,1:T(8,128)S(1)} %fusion.51), channel_id=1, replica_groups=mesh['row'=64,'col'=8] {'col'}, use_global_device_ids=true, to_apply=%region_2.3 | all-reduce | flops 8192 | bytes 49152 | tf_op jit(solution)/shard_map/psum | solution.py:37
  45.3 0.1 convert_reduce_fusion
  45.4 0.1 fusion.39
  45.5 28.9 %all-gather.4.cloned.1.call-done = bf16[128,16384]{1,0:T(8,128)(2,1)} async-done(((bf16[128,2048]{1,0:T(8,128)(2,1)}), bf16[128,16384]{1,0:T(8,128)(2,1)}) %all-gather.4.cloned.1.call-update) | async-done | bytes 4194320 | tf_op jit(solution)/shard_map/all_gather | solution.py:28
  74.4 86.0 %all-gather.6.cloned.1.call-done = bf16[16384,128]{1,0:T(8,128)(2,1)} async-done(((bf16[256,128]{1,0:T(8,128)(2,1)}), bf16[16384,128]{1,0:T(8,128)(2,1)}) %all-gather.6.cloned.1.call-update) | async-done | bytes 4194320 | tf_op jit(solution)/shard_map/all_gather | solution.py:30
  160.4 4.7 fusion.50
  165.1 0.5 fusion.48
  165.6 0.2 fusion.16
  165.7 0.3 fusion.49
  166.1 0.0 copy-start.6
  166.1 79.6 %all-gather.8.cloned.1.call-done = bf16[16384,128]{1,0:T(8,128)(2,1)} async-done(((bf16[256,128]{1,0:T(8,128)(2,1)}), bf16[16384,128]{1,0:T(8,128)(2,1)}) %all-gather.8.cloned.1.call-update) | async-done | bytes 4194320 | tf_op jit(solution)/shard_map/all_gather | solution.py:34
  245.7 4.7 fusion.52
  250.4 0.2 fusion.13
  250.6 0.3 fusion.28
  250.9 0.2 fusion.17
  251.1 0.5 copy-done.2
  251.6 0.5 fusion.6
  252.1 14.4 %psum.43 = f32[128]{0:T(128)S(1)} all-reduce(f32[128]{0:T(128)S(1)} %broadcast_multiply_fusion), channel_id=1, replica_groups=mesh['row'=64,'col'=8] {'col'}, use_global_device_ids=true, to_apply=%region_8.9 | all-reduce | flops 128 | bytes 1024 | tf_op jit(solution)/shard_map/psum | solution.py:72
  266.5 0.1 select_reduce_fusion.1
  266.7 0.1 select_reduce_fusion
  266.8 0.4 multiply_reduce_fusion
  267.2 0.4 fusion.9
  267.7 0.7 fusion.54
  268.4 0.1 fusion.53
  268.5 0.4 fusion.12
  269.0 0.8 fusion.55
  269.7 0.2 fusion.11
  269.9 20.8 %psum.44 = bf16[128,64]{1,0:T(8,128)(2,1)S(1)} all-reduce(bf16[128,64]{1,0:T(8,128)(2,1)S(1)} %fusion.11), channel_id=1, replica_groups=mesh['row'=64,'col'=8] {'col'}, use_global_device_ids=true, to_apply=%region_12.13 | all-reduce | flops 8192 | bytes 32768 | tf_op jit(solution)/shard_map/psum | solution.py:103
  290.7 0.0 all-reduce.6.cloned.1.call-update
  290.7 0.0 all-reduce.4.cloned.1.call-start
  290.8 1.0 convolution_bitcast_fusion
  291.8 0.0 all-reduce.4.cloned.1.call-update
  291.8 183.4 %all-reduce.6.cloned.1.call-done = (f32[64,128]{1,0:T(8,128)}, f32[64,128]{1,0:T(8,128)}) async-done(((f32[64,128]{1,0:T(8,128)}, f32[64,128]{1,0:T(8,128)}), (f32[64,128]{1,0:T(8,128)}, f32[64,128]{1,0:T(8,128)})) %all-reduce.6.cloned.1.call-update) | async-done | bytes 65552 | tf_op jit(solution)/shard_map/psum | solution.py:105
  475.2 192.2 %all-reduce.4.cloned.1.call-done = f32[2048,64]{0,1:T(8,128)} async-done(((f32[2048,64]{0,1:T(8,128)}), f32[2048,64]{0,1:T(8,128)}) %all-reduce.4.cloned.1.call-update) | async-done | bytes 524304 | tf_op jit(solution)/shard_map/psum | solution.py:105
  667.5 1.9 copy.69
  669.3 1.4 copy.70
  670.7 1.4 copy.71
  (13 shorter events, 0.0 us)
Async XLA Ops:
  7.2 157.9 %copy-start = (bf16[128,2048]{1,0:T(8,128)(2,1)S(1)}, bf16[128,2048]{1,0:T(8,128)(2,1)}, u32[]{:S(2)}) copy-start(bf16[128,2048]{1,0:T(8,128)(2,1)} %param.10) | copy-start | bytes 1572868
  7.2 67.2 %all-gather.4.cloned.1.call-start = ((), (), s32[]{:S(2)}) async-start(), calls=%async_computation | async-start | bytes 4718592 | tf_op jit(solution)/shard_map/all_gather | solution.py:28
  7.9 152.5 %all-gather.6.cloned.1.call-start = ((), (), s32[]{:S(2)}) async-start(), calls=%async_computation.1 | async-start | bytes 4259840 | tf_op jit(solution)/shard_map/all_gather | solution.py:30
  8.7 237.0 %all-gather.8.cloned.1.call-start = ((), (), s32[]{:S(2)}) async-start(), calls=%async_computation.2 | async-start | bytes 4259840 | tf_op jit(solution)/shard_map/all_gather | solution.py:34
  9.4 465.8 %all-reduce.6.cloned.1.call-start = ((), (), s32[]{:S(2)}) async-start(), calls=%async_computation.4 | async-start | bytes 131072 | tf_op jit(solution)/shard_map/psum | solution.py:105
  45.5 119.6 %copy-start.5 = (bf16[64,128]{1,0:T(8,128)(2,1)S(1)}, bf16[64,128]{1,0:T(8,128)(2,1)}, u32[]{:S(2)}) copy-start(bf16[64,128]{1,0:T(8,128)(2,1)} %param.15) | copy-start | bytes 49156
  166.1 84.3 %copy-start.6 = (bf16[64,128]{1,0:T(8,128)(2,1)S(1)}, bf16[64,128]{1,0:T(8,128)(2,1)}, u32[]{:S(2)}) copy-start(bf16[64,128]{1,0:T(8,128)(2,1)} %param.16) | copy-start | bytes 49156
  250.4 1.2 copy-start.2
  250.6 16.2 %copy-start.4 = (bf16[128,2048]{1,0:T(8,128)(2,1)S(1)}, bf16[128,2048]{1,0:T(8,128)(2,1)}, u32[]{:S(2)}) copy-start(bf16[128,2048]{1,0:T(8,128)(2,1)} %param.11) | copy-start | bytes 1572868
  267.2 1.3 copy-start.3
  267.2 23.5 %copy-start.1 = (bf16[128,2048]{1,0:T(8,128)(2,1)S(1)}, bf16[128,2048]{1,0:T(8,128)(2,1)}, u32[]{:S(2)}) copy-start(bf16[128,2048]{1,0:T(8,128)(2,1)} %param.9) | copy-start | bytes 1572868
  290.7 376.8 %all-reduce.4.cloned.1.call-start = ((), (), s32[]{:S(2)}) async-start(), calls=%async_computation.3 | async-start | bytes 1048576 | tf_op jit(solution)/shard_map/psum | solution.py:105
Sparse Core Ops, SparseCore 0:
  10.1 64.2 all-gather.3
  77.7 82.6 all-gather.5
  163.7 81.8 all-gather.7
  290.8 184.3 all-reduce.5
  479.2 188.2 all-reduce.3
where the time goes:
time: 679 us
  waiting for transfers between devices  572 us (84%)
  blocking collectives  66.5 us (10%)
  matrix products  16.8 us (2%)
  between operations  14 us (2%)
  local copies, waits for them, and re-layouts  7.46 us (1%)
    psum x2, waiting for transfers between devices, on_device(): lax.psum((down_term, key_term, value_term), 'row')  376 us
    all_gather x1, waiting for transfers between devices, on_device(): lax.all_gather(w_key, 'row', axis=0, tiled=True)  86 us
    all_gather x1, waiting for transfers between devices, on_device(): lax.all_gather(w_value, 'row', axis=0, tiled=True)  79.6 us
    psum x1, blocking collectives, on_device(): lax.psum(jnp.dot(tokens, down_proj, preferred_element_type=jnp.float32),...  31.3 us
    all_gather x1, waiting for transfers between devices, on_device(): whole = lax.all_gather(tokens, 'col', axis=1, tiled=True)  28.9 us
    psum x1, blocking collectives, on_device(): back_half = lax.psum(back_local.astype(jnp.bfloat16), 'col')  20.8 us
    psum x1, blocking collectives, on_device(): gap_part = lax.psum(gap_local, 'col')  14.4 us
  transfers between devices with their start and end apart: 5, of which 5 were waited for; matrix products, arithmetic and copies ran while one was open for 2% of the time, Pallas kernels for 0%

commit v1 on v0

v1 whole, which is shorter than its diff:
```python
import functools
import jax
import jax.numpy as jnp
from jax import lax
from jax.experimental import pallas as pl
from jax.experimental.pallas import tpu as pltpu
from jax.sharding import PartitionSpec as P

HD = 128
QPK = 16
BF = jnp.bfloat16
F32 = jnp.float32
npo_beta = 0.5

VMEM = pl.BlockSpec(memory_space=pltpu.VMEM)
SMEM = pl.BlockSpec(memory_space=pltpu.SMEM)
HBM = pl.BlockSpec(memory_space=pl.ANY)
PARAMS = pltpu.CompilerParams(vmem_limit_bytes=48 * 1024 * 1024)

NT = (((1,), (1,)), ((), ()))
TN = (((0,), (0,)), ((), ()))
NN = (((1,), (0,)), ((), ()))


def mm(a, b, dims):
    return lax.dot_general(a, b, dims, preferred_element_type=F32)


def fold(a):
    half = a.shape[0] // 2
    return jnp.concatenate([a[:half], a[half:]], axis=1)


def unfold(a):
    half = a.shape[1] // 2
    return jnp.concatenate([a[:, :half], a[:, half:]], axis=0)


def doc_ids(lengths_ref, axis, count, docs):
    places = lax.broadcasted_iota(jnp.int32, (count, count), axis)
    ids = jnp.zeros((count, count), jnp.int32)
    end = 0
    for j in range(docs):
        end = end + lengths_ref[0, j]
        ids = ids + jnp.where(places >= end, 1, 0)
    return ids


def split_kernel(pos_ref, t_ref, mine_ref, theirs_ref):
    pieces = t_ref.shape[1] // 512
    for core in range(2):

        @pl.when(pos_ref[0] == core)
        def _():
            for i in range(pieces):
                to = pl.ds(i * 256, 256)
                mine_ref[:, to] = t_ref[:, pl.ds(i * 512 + core * 256, 256)]
                theirs_ref[:, to] = t_ref[:, pl.ds(i * 512 + (1 - core) * 256, 256)]


def low_kernel(t_ref, down_ref, out_ref):
    low = fold(mm(t_ref[...], down_ref[...], NN)).astype(BF)
    for i in range(out_ref.shape[0]):
        out_ref[i] = low


def project_kernel(pos_ref, t_ref, *refs):
    w_refs, (own_ref, other_ref, t_scr, w_scr, t_sem, w_sem) = refs[:9], refs[9:]
    y = pos_ref[1]
    n = t_scr.shape[0]
    half = w_scr.shape[1] // 2
    copies = []
    for e in range(n):
        k = lax.rem(y + e, n)
        mine = [pltpu.make_async_copy(t_ref.at[k], t_scr.at[e], t_sem.at[e])]
        if e == 4:
            for i in range(2):
                mine.append(
                    pltpu.make_async_copy(
                        w_refs[4 + 4 * i], w_scr.at[e, pl.ds(i * half, half)], w_sem.at[e + 4 * i]
                    )
                )
        else:
            mine.append(pltpu.make_async_copy(w_refs[e], w_scr.at[e], w_sem.at[e]))
        for c in mine:
            c.start()
        copies.append(mine)
    total = jnp.zeros((t_scr.shape[1], w_scr.shape[2]), F32)
    for e in range(n):
        for c in copies[e]:
            c.wait()
        total = total + mm(t_scr[e], w_scr[e], NN)
    rows = own_ref.shape[0]
    own_ref[...] = total[:rows]
    other_ref[...] = total[rows:]


def attend_kernel(
    lengths_ref, own_ref, got_ref, low_ref, upk_ref, upv_ref, q_ref, p_ref,
    pack_ref, low_half_ref, gk_ref, gv_ref,
):
    rows = own_ref.shape[0]
    heads = q_ref.shape[1] // HD
    score_scale = HD ** (-0.5)
    probe_scale = (q_ref.shape[1] * pack_ref.shape[0]) ** (-0.5)
    low_sum = low_ref[0].astype(F32)
    for i in range(1, low_ref.shape[0]):
        low_sum = low_sum + low_ref[i].astype(F32)
    low_half = unfold(low_sum).astype(BF)
    low_half_ref[...] = low_half
    full = own_ref[...] + got_ref[...]
    key_full, value_full = full[:, :HD], full[:, HD:]
    key_pol = (key_full + mm(low_half, upk_ref[...], NN)).astype(BF)
    value_pol = (value_full + mm(low_half, upv_ref[...], NN)).astype(BF)
    keys = jnp.concatenate([key_pol, key_full.astype(BF)], axis=0)
    values = jnp.concatenate([value_pol, value_full.astype(BF)], axis=0)
    doc_s = doc_ids(lengths_ref, 0, rows, lengths_ref.shape[1])
    doc_t = doc_ids(lengths_ref, 1, rows, lengths_ref.shape[1])
    s_at = lax.broadcasted_iota(jnp.int32, (rows, rows), 0)
    t_at = lax.broadcasted_iota(jnp.int32, (rows, rows), 1)
    allowed = (doc_s == doc_t) & (t_at >= s_at)

    def probs_of(scores):
        scores = jnp.where(allowed, scores * score_scale, -1e30)
        peak = jnp.max(scores, axis=0, keepdims=True)
        e = jnp.exp(scores - peak)
        return e / jnp.sum(e, axis=0, keepdims=True)

    gk = jnp.zeros((rows, HD), F32)
    gv = jnp.zeros((rows, HD), F32)
    gap = jnp.zeros((1, rows), F32)
    for h in range(heads):
        q = q_ref[:, pl.ds(h * HD, HD)]
        probe = p_ref[:, pl.ds(h * HD, HD)]
        scores = mm(keys, q, NT)
        grads = mm(values, probe, NT)
        pol = probs_of(scores[:rows])
        ref = probs_of(scores[rows:])
        grad_pol = grads[:rows]
        mean_pol = jnp.sum(pol * grad_pol, axis=0, keepdims=True)
        mean_ref = jnp.sum(ref * grads[rows:], axis=0, keepdims=True)
        gap = gap + (mean_pol - mean_ref)
        grad_scores = (pol * (grad_pol - mean_pol)).astype(BF)
        gk = gk + mm(grad_scores, q, NN)
        gv = gv + mm(pol.astype(BF), probe, NN)
    gk = gk * (score_scale * probe_scale)
    gv = gv * probe_scale
    gap = gap * probe_scale
    gk_ref[...] = gk
    gv_ref[...] = gv
    back = mm(gk.astype(BF), upk_ref[...], NT) + mm(gv.astype(BF), upv_ref[...], NT)
    back = fold(back).astype(BF)
    first = gap.astype(BF).astype(F32)
    second = (gap - first).astype(BF).astype(F32)
    third = gap - first - second
    line = lax.broadcasted_iota(jnp.int32, (16, rows), 0)
    tail = jnp.where(line == 0, first, jnp.where(line == 1, second, jnp.where(line == 2, third, 0.0)))
    tail = tail.astype(BF)
    for i in range(pack_ref.shape[0]):
        pack_ref[i, pl.ds(0, 64)] = back
        pack_ref[i, pl.ds(64, 16)] = tail


def weigh_kernel(lengths_ref, pack_ref, low_half_ref, gk_ref, gv_ref, t_ref, out_ref):
    rows = gk_ref.shape[0]
    total = pack_ref[0].astype(F32)
    for i in range(1, pack_ref.shape[0]):
        total = total + pack_ref[i].astype(F32)
    gap = total[64:65] + total[65:66] + total[66:67]
    docs = lengths_ref.shape[1]
    same = doc_ids(lengths_ref, 0, rows, docs) == doc_ids(lengths_ref, 1, rows, docs)
    token_gap = jnp.sum(jnp.where(same, gap, 0.0), axis=1, keepdims=True)
    weight = 2.0 * jax.nn.sigmoid(npo_beta * token_gap)
    back_half = (unfold(total[:64]) * weight).astype(BF)
    down = mm(back_half, t_ref[...], TN).astype(BF)
    both = jnp.concatenate([gk_ref[...] * weight, gv_ref[...] * weight], axis=1).astype(BF)
    up = mm(low_half_ref[...], both, TN).astype(BF)
    groups = 4
    for i in range(16):
        for g in range(groups):
            out_ref[i * groups + g, pl.ds(0, 16)] = down[g * 16:(g + 1) * 16, i * 128:(i + 1) * 128]
    for s in range(64):
        tile, at = s // 8, (s % 8) * 2
        i, g = tile // groups, tile % groups
        piece = up[g * 16 + at:g * 16 + at + 2, i * 128:(i + 1) * 128].astype(F32)
        piece = jnp.concatenate([piece, jnp.zeros((6, 128), F32)], axis=0)
        out_ref[s, pl.ds(16, 8)] = piece.astype(BF)


def sum_kernel(in_ref, out_ref):
    total = in_ref[0].astype(F32)
    for i in range(1, in_ref.shape[0]):
        total = total + in_ref[i].astype(F32)
    total = total.astype(BF)
    for i in range(out_ref.shape[0]):
        out_ref[i] = total


def place_kernel(in_ref, down_ref, upk_ref, upv_ref):
    groups = 4
    for i in range(16):
        tile = jnp.concatenate(
            [in_ref[i * groups + g, pl.ds(0, 16)].astype(F32) for g in range(groups)], axis=0
        )
        down_ref[pl.ds(i * 128, 128)] = tile.T
    for s in range(64):
        tile, at = s // 8, (s % 8) * 2
        i, g = tile // groups, tile % groups
        to = upk_ref if i == 0 else upv_ref
        to[pl.ds(g * 16 + at, 2)] = in_ref[s, pl.ds(16, 8)].astype(F32)[:2]


def call(kernel, outs, in_specs, out_specs, *args, scratch=()):
    return pl.pallas_call(
        kernel,
        out_shape=[jax.ShapeDtypeStruct(s, d) for s, d in outs],
        in_specs=in_specs,
        out_specs=out_specs,
        scratch_shapes=list(scratch),
        compiler_params=PARAMS,
    )(*args)


def on_device(tokens, queries, probes, w_key, w_value, down_proj, up_key, up_value, lengths):
    rows, feats = tokens.shape
    row_at = lax.axis_index("row")
    pos = jnp.stack([row_at % 2, row_at // 8]).astype(jnp.int32)

    def place(y, x, core):
        return ((y % 8) * 4 + x % 4) * 2 + core % 2

    sites = [(y, x, core) for y in range(8) for x in range(4) for core in range(2)]
    swap = [(place(y, x, c), place(y, x, 1 - c)) for y, x, c in sites]
    fore = [(place(y, x, c), place(y + 1, x, c)) for y, x, c in sites]
    aft = [(place(y, x, c), place(y - 1, x, c)) for y, x, c in sites]
    x_lines = [[place(y, x, c) for x in range(4)] for y in range(8) for c in range(2)]

    half = (rows, feats // 2)
    mine, theirs = call(
        split_kernel, [(half, BF), (half, BF)], [SMEM, VMEM], [VMEM, VMEM], pos, tokens
    )
    swapped = lax.ppermute(theirs, "row", swap)
    pair = jnp.concatenate([mine, swapped], axis=0)
    all_tokens = lax.all_gather(pair, "col", axis=0)

    w_both = jnp.concatenate([w_key, w_value], axis=1)
    w_line = lax.all_to_all(
        jnp.broadcast_to(w_both, (4,) + w_both.shape), "row", 0, 0, axis_index_groups=x_lines
    )
    w_own = w_line.reshape(4 * w_both.shape[0], w_both.shape[1])
    up_going, down_going = [w_own], [w_own]
    for _ in range(3):
        up_going.append(lax.ppermute(up_going[-1], "row", fore))
        down_going.append(lax.ppermute(down_going[-1], "row", aft))
    middle = w_own.shape[0] // 2
    last_up = lax.ppermute(up_going[3][:middle], "row", fore)
    last_down = lax.ppermute(down_going[3][middle:], "row", aft)
    w_parts = [
        w_own, down_going[1], down_going[2], down_going[3], last_up,
        up_going[3], up_going[2], up_going[1], last_down,
    ]

    (low_pack,) = call(
        low_kernel, [((8, rows // 2, 128), BF)], [VMEM, VMEM], [VMEM], tokens, down_proj
    )
    low_parts = lax.all_to_all(low_pack, "col", 0, 0)

    wide = w_both.shape[1]
    own, other = call(
        project_kernel,
        [((rows, wide), F32)] * 2,
        [SMEM] + [HBM] * 10,
        [VMEM, VMEM],
        pos, all_tokens, *w_parts,
        scratch=[
            pltpu.VMEM((8, 2 * rows, feats // 2), BF),
            pltpu.VMEM((8, feats // 2, wide), BF),
            pltpu.SemaphoreType.DMA((8,)),
            pltpu.SemaphoreType.DMA((9,)),
        ],
    )
    got = lax.ppermute(other, "row", swap)
    pack, low_half, gk, gv = call(
        attend_kernel,
        [((8, 80, 128), BF), ((rows, 64), BF), ((rows, HD), F32), ((rows, HD), F32)],
        [SMEM] + [VMEM] * 7,
        [VMEM] * 4,
        lengths, own, got, low_parts, up_key, up_value, queries, probes,
    )
    packs = lax.all_to_all(pack, "col", 0, 0)
    (terms,) = call(
        weigh_kernel, [((64, 24, 128), BF)], [SMEM] + [VMEM] * 5, [VMEM],
        lengths, packs, low_half, gk, gv, tokens,
    )
    term_parts = lax.all_to_all(terms, "row", 0, 0)
    (summed,) = call(sum_kernel, [((64, 24, 128), BF)], [VMEM], [VMEM], term_parts)
    pieces = lax.all_to_all(summed, "row", 0, 0)
    return tuple(
        call(
            place_kernel,
            [((feats, 64), F32), ((64, HD), F32), ((64, HD), F32)],
            [VMEM], [VMEM] * 3, pieces,
        )
    )


def solution(mesh):
    in_specs = (
        P("row", "col"),
        P("row", "col"),
        P("row", "col"),
        P("row", "col"),
        P("row", "col"),
        P("col", None),
        P(None, "col"),
        P(None, "col"),
        P("row", None),
    )
    out_specs = (P("col", None), P(None, "col"), P(None, "col"))
    return jax.shard_map(
        on_device, mesh=mesh, in_specs=in_specs, out_specs=out_specs, check_vma=False
    )
```

time: 679 us -> 189 us (0.28)
  waiting for transfers between devices: 572 us -> 25.9 us
  starting transfers between devices: 0.19 us -> 46.5 us
  matrix products: 16.8 us -> 0 us
  Pallas kernels: 0 us -> 13.5 us
  local copies, waits for them, and re-layouts: 7.46 us -> 14.4 us
    psum x2 -> x0, waiting for transfers between devices: 376 us -> none  [on_device(): lax.psum((down_term, key_term, value_term), 'row')]
    all_gather x3 -> x1, waiting for transfers between devices: 194 us -> 0.02 us  [on_device(): all_tokens = lax.all_gather(pair, 'col', axis=0)]
    all_to_all x0 -> x4, blocking collectives: none -> 71.5 us  [the longest x1 24.1 us: on_device(): term_parts = lax.all_to_all(terms, 'row', 0, 0)]
    psum x3 -> x0, blocking collectives: 66.5 us -> none  [the longest x1 31.3 us: on_device(): lax.psum(jnp.dot(tokens, down_proj, preferred_element_type=jnp.float32),...]
    ppermute x0 -> x10, starting transfers between devices: none -> 41.6 us  [the longest x3 13.7 us: on_device(): down_going.append(lax.ppermute(down_going[-1], 'row', aft))]
    ppermute x0 -> x10, waiting for transfers between devices: none -> 25.8 us  [the longest x3 23.5 us: on_device(): up_going.append(lax.ppermute(up_going[-1], 'row', fore))]
    dot_general x16 -> x0, matrix products: 16.8 us -> none  [the longest x1 4.71 us: on_device(): jnp.dot(whole, lax.all_gather(w_value, 'row', axis=0, tiled=True), prefer...]
    pallas_call x0 -> x7, Pallas kernels: none -> 13.5 us  [call(): pl.pallas_call(kernel, out_shape=[jax.ShapeDtypeStruct(s, d) for s, d in...]
  transfers between devices with their start and end apart: 5 -> 12, of which waited for: 5 -> 5; matrix products, arithmetic and copies ran while one was open for 2% -> 2% of each run, Pallas kernels for 0% -> 3%
where the time goes in v1:
time: 189 us; the launch traced here: 188 us
  blocking collectives  71.5 us (38%)
  starting transfers between devices  46.5 us (25%)
  waiting for transfers between devices  25.9 us (14%)
  local copies, waits for them, and re-layouts  14.4 us (8%)
  between operations  14.3 us (8%)
  Pallas kernels  13.5 us (7%)
    all_to_all x1, blocking collectives, on_device(): term_parts = lax.all_to_all(terms, 'row', 0, 0)  24.1 us
    ppermute x3, waiting for transfers between devices, on_device(): up_going.append(lax.ppermute(up_going[-1], 'row', fore))  23.5 us
    all_to_all x1, blocking collectives, on_device(): pieces = lax.all_to_all(summed, 'row', 0, 0)  20.5 us
    all_to_all x1, blocking collectives, on_device(): packs = lax.all_to_all(pack, 'col', 0, 0)  15.3 us
    ppermute x3, starting transfers between devices, on_device(): down_going.append(lax.ppermute(down_going[-1], 'row', aft))  13.7 us
    pallas_call x7, Pallas kernels, call(): pl.pallas_call(kernel, out_shape=[jax.ShapeDtypeStruct(s, d) for s, d in...  13.5 us
    unnamed x35, local copies, waits for them, and re-layouts  11.8 us
    all_to_all x1, blocking collectives, on_device(): lax.all_to_all(jnp.broadcast_to(w_both, (4,) + w_both.shape), 'row', 0, 0...  11.6 us
  transfers between devices with their start and end apart: 12, of which 5 were waited for; matrix products, arithmetic and copies ran while one was open for 2% of the time, Pallas kernels for 3%

profile of v1, /device:TPU:1, one launch (start us, length us, event | category | flops | bytes accessed | tf_op | source)
XLA Modules:
  0.0 187.8 jit_solution(12685486128325045817)
XLA Ops:
  7.2 0.0 all-gather.3.cloned.1.call-start
  7.2 0.1 pad_add_fusion.pos_ref
  7.3 1.0 copy-done
  8.4 0.6 shard_map.112
  9.0 8.8 %collective-permute-start = (bf16[128,1024]{1,0:T(8,128)(2,1)S(1)}, bf16[128,1024]{1,0:T(8,128)(2,1)S(1)}, u32[]{:S(2)}, u32[]{:S(2)}) collective-permute-start(bf16[128,1024]{1,0:T(8,128)(2,1)S(1)} %get-tuple-element.12), channel_id=1, source_target_pairs={{0,8},{8,0},{16,24},{24,16},{32,40},{40,32},{48,56},{56,48},{64,72... | collective-permute-start | bytes 786440 | tf_op jit(solution)/shard_map/ppermute | solution.py:242
  17.8 1.1 collective-permute-done
  18.9 0.8 pad_maximum_fusion
  19.8 0.9 pad_maximum_fusion.1
  20.7 11.6 %all_to_all.25 = bf16[4,256,256]{2,1,0:T(8,128)(2,1)S(1)} all-to-all(bf16[4,256,256]{2,1,0:T(8,128)(2,1)S(1)} %broadcast_in_dim.3), channel_id=1, replica_groups={{0,16,32,48},{8,24,40,56},{64,80,96,112},{72,88,104,120},{128,144,160,1..., dimensions={0} | all-to-all | bytes 1048576 | tf_op jit(solution)/shard_map/all_to_all | solution.py:247
  32.3 1.9 %collective-permute-start.4 = (bf16[1024,256]{1,0:T(8,128)(2,1)S(1)}, bf16[1024,256]{1,0:T(8,128)(2,1)S(1)}, u32[]{:S(2)}, u32[]{:S(2)}) collective-permute-start(bf16[1024,256]{1,0:T(8,128)(2,1)S(1)} %bitcast.4), channel_id=1, source_target_pairs={{0,64},{8,72},{16,80},{24,88},{32,96},{40,104},{48,112},{56,120},{... | collective-permute-start | bytes 1572872 | tf_op jit(solution)/shard_map/ppermute | solution.py:253
  34.2 4.6 %collective-permute-start.1 = (bf16[1024,256]{1,0:T(8,128)(2,1)S(1)}, bf16[1024,256]{1,0:T(8,128)(2,1)S(1)}, u32[]{:S(2)}, u32[]{:S(2)}) collective-permute-start(bf16[1024,256]{1,0:T(8,128)(2,1)S(1)} %bitcast.5), channel_id=1, source_target_pairs={{0,448},{8,456},{16,464},{24,472},{32,480},{40,488},{48,496},{56,5... | collective-permute-start | bytes 1572872 | tf_op jit(solution)/shard_map/ppermute | solution.py:254
  38.8 8.9 %collective-permute-done.4.refs_7_ = bf16[1024,256]{1,0:T(8,128)(2,1)S(1)} collective-permute-done((bf16[1024,256]{1,0:T(8,128)(2,1)S(1)}, bf16[1024,256]{1,0:T(8,128)(2,1)S(1)}, u32[]{:S(2)}, u32[]{:S(2)}) %collective-permute-start.4) | collective-permute-done | bytes 524320 | tf_op jit(solution)/shard_map/ppermute | solution.py:253
  47.7 1.9 %collective-permute-start.5 = (bf16[1024,256]{1,0:T(8,128)(2,1)S(1)}, bf16[1024,256]{1,0:T(8,128)(2,1)S(1)}, u32[]{:S(2)}, u32[]{:S(2)}) collective-permute-start(bf16[1024,256]{1,0:T(8,128)(2,1)S(1)} %collective-permute-done.4.refs_7_), channel_id=1, source_target_pairs={{0,64},{8,72},{16,80},{24,88},{32,96},{40,104},{48,112},{56,120},{... | collective-permute-start | bytes 1572872 | tf_op jit(solution)/shard_map/ppermute | solution.py:253
  49.7 4.6 %collective-permute-start.2 = (bf16[1024,256]{1,0:T(8,128)(2,1)S(1)}, bf16[1024,256]{1,0:T(8,128)(2,1)S(1)}, u32[]{:S(2)}, u32[]{:S(2)}) collective-permute-start(bf16[1024,256]{1,0:T(8,128)(2,1)S(1)} %collective-permute-done.1.refs_1_), channel_id=1, source_target_pairs={{0,448},{8,456},{16,464},{24,472},{32,480},{40,488},{48,496},{56,5... | collective-permute-start | bytes 1572872 | tf_op jit(solution)/shard_map/ppermute | solution.py:254
  54.3 8.1 %collective-permute-done.5.refs_6_ = bf16[1024,256]{1,0:T(8,128)(2,1)S(1)} collective-permute-done((bf16[1024,256]{1,0:T(8,128)(2,1)S(1)}, bf16[1024,256]{1,0:T(8,128)(2,1)S(1)}, u32[]{:S(2)}, u32[]{:S(2)}) %collective-permute-start.5) | collective-permute-done | bytes 524320 | tf_op jit(solution)/shard_map/ppermute | solution.py:253
  62.3 1.9 %collective-permute-start.6 = (bf16[1024,256]{1,0:T(8,128)(2,1)S(1)}, bf16[1024,256]{1,0:T(8,128)(2,1)S(1)}, u32[]{:S(2)}, u32[]{:S(2)}) collective-permute-start(bf16[1024,256]{1,0:T(8,128)(2,1)S(1)} %collective-permute-done.5.refs_6_), channel_id=1, source_target_pairs={{0,64},{8,72},{16,80},{24,88},{32,96},{40,104},{48,112},{56,120},{... | collective-permute-start | bytes 1572872 | tf_op jit(solution)/shard_map/ppermute | solution.py:253
  64.3 0.8 copy-done.4
  65.0 4.6 %collective-permute-start.3 = (bf16[1024,256]{1,0:T(8,128)(2,1)S(1)}, bf16[1024,256]{1,0:T(8,128)(2,1)S(1)}, u32[]{:S(2)}, u32[]{:S(2)}) collective-permute-start(bf16[1024,256]{1,0:T(8,128)(2,1)S(1)} %collective-permute-done.2.refs_2_), channel_id=1, source_target_pairs={{0,448},{8,456},{16,464},{24,472},{32,480},{40,488},{48,496},{56,5... | collective-permute-start | bytes 1572872 | tf_op jit(solution)/shard_map/ppermute | solution.py:254
  69.6 6.5 %collective-permute-done.6.refs_5_ = bf16[1024,256]{1,0:T(8,128)(2,1)S(1)} collective-permute-done((bf16[1024,256]{1,0:T(8,128)(2,1)S(1)}, bf16[1024,256]{1,0:T(8,128)(2,1)S(1)}, u32[]{:S(2)}, u32[]{:S(2)}) %collective-permute-start.6) | collective-permute-done | bytes 524320 | tf_op jit(solution)/shard_map/ppermute | solution.py:253
  76.1 0.7 slice.8
  76.8 1.9 %collective-permute-start.7 = (bf16[512,256]{1,0:T(8,128)(2,1)}, bf16[512,256]{1,0:T(8,128)(2,1)S(1)}, u32[]{:S(2)}, u32[]{:S(2)}) collective-permute-start(bf16[512,256]{1,0:T(8,128)(2,1)} %slice.8), channel_id=1, source_target_pairs={{0,64},{8,72},{16,80},{24,88},{32,96},{40,104},{48,112},{56,120},{... | collective-permute-start | bytes 786440 | tf_op jit(solution)/shard_map/ppermute | solution.py:256
  78.8 0.7 slice.9
  79.5 4.6 %collective-permute-start.8 = (bf16[512,256]{1,0:T(8,128)(2,1)}, bf16[512,256]{1,0:T(8,128)(2,1)}, u32[]{:S(2)}, u32[]{:S(2)}) collective-permute-start(bf16[512,256]{1,0:T(8,128)(2,1)} %slice.9), channel_id=1, source_target_pairs={{0,448},{8,456},{16,464},{24,472},{32,480},{40,488},{48,496},{56,5... | collective-permute-start | bytes 786440 | tf_op jit(solution)/shard_map/ppermute | solution.py:257
  84.1 1.2 copy.12.down_ref
  85.3 1.0 shard_map.114
  86.3 4.8 %all-to-all-start.1 = ((bf16[8,64,128]{2,1,0:T(8,128)(2,1)}), bf16[8,64,128]{2,1,0:T(8,128)(2,1)S(1)}, u32[]{:S(2)}, u32[]{:S(2)}) async-start(bf16[8,64,128]{2,1,0:T(8,128)(2,1)} %shard_map.114), calls=%async_computation.1 | async-start | bytes 262144 | tf_op jit(solution)/shard_map/all_to_all | solution.py:266
  91.2 0.0 all-gather.3.cloned.1.call-done
  91.2 1.0 copy-done.3
  92.3 1.0 copy-done.5
  93.3 1.0 copy-done.7
  94.3 0.7 copy-done.16
  95.0 5.2 %shard_map.113 = (f32[128,256]{1,0:T(8,128)S(1)}, f32[128,256]{1,0:T(8,128)}) custom-call(s32[2]{0:T(128)S(1)} %copy-done.16, bf16[8,256,1024]{2,1,0:T(8,128)(2,1)} %bitcast.7, bf16[1024,256]{1,0:T(8,128)(2,1)S(1)} %bitcast.6, bf16[1024,256]{1,0:T(8,128)(2,1)S(1)} %copy-done.3, bf16[1024,256]{1,0:T(8,128)(2,1)S(1)} %copy-done.7, ...), custom_call_target="tpu_custom_call" | custom-call | tf_op jit(solution)/shard_map/pallas_call | solution.py:214
  100.2 0.6 copy-done.10
  100.8 6.9 %collective-permute-start.9 = (f32[128,256]{1,0:T(8,128)}, f32[128,256]{1,0:T(8,128)S(1)}, u32[]{:S(2)}, u32[]{:S(2)}) collective-permute-start(f32[128,256]{1,0:T(8,128)} %get-tuple-element.14), channel_id=1, source_target_pairs={{0,8},{8,0},{16,24},{24,16},{32,40},{40,32},{48,56},{56,48},{64,72... | collective-permute-start | bytes 393224 | tf_op jit(solution)/shard_map/ppermute | solution.py:282
  107.8 1.2 collective-permute-done.9.got_ref
  108.9 1.0 copy-done.8
  110.0 1.0 copy-done.9
  111.0 0.9 copy-done.11
  111.9 0.7 copy-done.13
  112.6 0.7 copy-done.14
  113.3 4.8 %shard_map.115 = (bf16[8,80,128]{2,1,0:T(8,128)(2,1)S(1)}, bf16[128,64]{1,0:T(8,128)(2,1)S(1)}, f32[128,128]{1,0:T(8,128)S(1)}, f32[128,128]{1,0:T(8,128)S(1)}) custom-call(s32[1,8]{1,0:T(1,128)S(1)} %copy-done.14, f32[128,256]{1,0:T(8,128)S(1)} %copy-done.11, f32[128,256]{1,0:T(8,128)S(1)} %collective-permute-done.9.got_ref, ...), custom_call_target="tpu_custom_call" | custom-call | tf_op jit(solution)/shard_map/pallas_call | solution.py:214
  118.1 15.3 %all_to_all.26.pack_ref = bf16[8,80,128]{2,1,0:T(8,128)(2,1)S(1)} all-to-all(bf16[8,80,128]{2,1,0:T(8,128)(2,1)S(1)} %get-tuple-element.15), channel_id=1, replica_groups=mesh['row'=64,'col'=8] {'col'}, dimensions={0} | all-to-all | bytes 327680 | tf_op jit(solution)/shard_map/all_to_all | solution.py:290
  133.5 1.0 shard_map.116
  134.4 24.1 %all_to_all.27.in_ref = bf16[64,24,128]{2,1,0:T(8,128)(2,1)S(1)} all-to-all(bf16[64,24,128]{2,1,0:T(8,128)(2,1)S(1)} %shard_map.116), channel_id=1, replica_groups=mesh['row'=64,'col'=8] {'row'}, dimensions={0} | all-to-all | bytes 786432 | tf_op jit(solution)/shard_map/all_to_all | solution.py:295
  158.5 0.1 shard_map.117
  158.7 20.5 %all_to_all.28.in_ref = bf16[64,24,128]{2,1,0:T(8,128)(2,1)S(1)} all-to-all(bf16[64,24,128]{2,1,0:T(8,128)(2,1)S(1)} %shard_map.117), channel_id=1, replica_groups=mesh['row'=64,'col'=8] {'row'}, dimensions={0} | all-to-all | bytes 786432 | tf_op jit(solution)/shard_map/all_to_all | solution.py:297
  179.1 0.8 shard_map.118
  179.9 1.1 copy.13
  (30 shorter events, 0.1 us)
Async XLA Ops:
  7.2 84.0 %all-gather.3.cloned.1.call-start = ((), (), s32[]{:S(2)}) async-start(), calls=%async_computation.5 | async-start | bytes 4718592 | tf_op jit(solution)/shard_map/all_gather | solution.py:244
  7.3 1.0 copy-start
  8.3 0.6 copy-start.15
  8.4 77.0 %copy-start.1 = (bf16[128,2048]{1,0:T(8,128)(2,1)S(1)}, bf16[128,2048]{1,0:T(8,128)(2,1)}, u32[]{:S(2)}) copy-start(bf16[128,2048]{1,0:T(8,128)(2,1)} %t_ref.5) | copy-start | bytes 1572868
  9.0 9.9 %collective-permute-start = (bf16[128,1024]{1,0:T(8,128)(2,1)S(1)}, bf16[128,1024]{1,0:T(8,128)(2,1)S(1)}, u32[]{:S(2)}, u32[]{:S(2)}) collective-permute-start(bf16[128,1024]{1,0:T(8,128)(2,1)S(1)} %get-tuple-element.12), channel_id=1, source_target_pairs={{0,8},{8,0},{16,24},{24,16},{32,40},{40,32},{48,56},{56,48},{64,72... | collective-permute-start | bytes 786440 | tf_op jit(solution)/shard_map/ppermute | solution.py:242
  32.3 15.4 %collective-permute-start.4 = (bf16[1024,256]{1,0:T(8,128)(2,1)S(1)}, bf16[1024,256]{1,0:T(8,128)(2,1)S(1)}, u32[]{:S(2)}, u32[]{:S(2)}) collective-permute-start(bf16[1024,256]{1,0:T(8,128)(2,1)S(1)} %bitcast.4), channel_id=1, source_target_pairs={{0,64},{8,72},{16,80},{24,88},{32,96},{40,104},{48,112},{56,120},{... | collective-permute-start | bytes 1572872 | tf_op jit(solution)/shard_map/ppermute | solution.py:253
  34.2 15.4 %collective-permute-start.1 = (bf16[1024,256]{1,0:T(8,128)(2,1)S(1)}, bf16[1024,256]{1,0:T(8,128)(2,1)S(1)}, u32[]{:S(2)}, u32[]{:S(2)}) collective-permute-start(bf16[1024,256]{1,0:T(8,128)(2,1)S(1)} %bitcast.5), channel_id=1, source_target_pairs={{0,448},{8,456},{16,464},{24,472},{32,480},{40,488},{48,496},{56,5... | collective-permute-start | bytes 1572872 | tf_op jit(solution)/shard_map/ppermute | solution.py:254
  47.7 14.6 %collective-permute-start.5 = (bf16[1024,256]{1,0:T(8,128)(2,1)S(1)}, bf16[1024,256]{1,0:T(8,128)(2,1)S(1)}, u32[]{:S(2)}, u32[]{:S(2)}) collective-permute-start(bf16[1024,256]{1,0:T(8,128)(2,1)S(1)} %collective-permute-done.4.refs_7_), channel_id=1, source_target_pairs={{0,64},{8,72},{16,80},{24,88},{32,96},{40,104},{48,112},{56,120},{... | collective-permute-start | bytes 1572872 | tf_op jit(solution)/shard_map/ppermute | solution.py:253
  49.7 29.8 %copy-start.2 = (bf16[1024,256]{1,0:T(8,128)(2,1)}, bf16[1024,256]{1,0:T(8,128)(2,1)S(1)}, u32[]{:S(2)}) copy-start(bf16[1024,256]{1,0:T(8,128)(2,1)S(1)} %collective-permute-done.1.refs_1_) | copy-start | bytes 1572868
  49.7 15.4 %collective-permute-start.2 = (bf16[1024,256]{1,0:T(8,128)(2,1)S(1)}, bf16[1024,256]{1,0:T(8,128)(2,1)S(1)}, u32[]{:S(2)}, u32[]{:S(2)}) collective-permute-start(bf16[1024,256]{1,0:T(8,128)(2,1)S(1)} %collective-permute-done.1.refs_1_), channel_id=1, source_target_pairs={{0,448},{8,456},{16,464},{24,472},{32,480},{40,488},{48,496},{56,5... | collective-permute-start | bytes 1572872 | tf_op jit(solution)/shard_map/ppermute | solution.py:254
  62.3 13.8 %collective-permute-start.6 = (bf16[1024,256]{1,0:T(8,128)(2,1)S(1)}, bf16[1024,256]{1,0:T(8,128)(2,1)S(1)}, u32[]{:S(2)}, u32[]{:S(2)}) collective-permute-start(bf16[1024,256]{1,0:T(8,128)(2,1)S(1)} %collective-permute-done.5.refs_6_), channel_id=1, source_target_pairs={{0,64},{8,72},{16,80},{24,88},{32,96},{40,104},{48,112},{56,120},{... | collective-permute-start | bytes 1572872 | tf_op jit(solution)/shard_map/ppermute | solution.py:253
  64.3 0.8 copy-start.4
  65.0 14.5 %copy-start.6 = (bf16[1024,256]{1,0:T(8,128)(2,1)}, bf16[1024,256]{1,0:T(8,128)(2,1)S(1)}, u32[]{:S(2)}) copy-start(bf16[1024,256]{1,0:T(8,128)(2,1)S(1)} %collective-permute-done.2.refs_2_) | copy-start | bytes 1572868
  65.0 13.7 %collective-permute-start.3 = (bf16[1024,256]{1,0:T(8,128)(2,1)S(1)}, bf16[1024,256]{1,0:T(8,128)(2,1)S(1)}, u32[]{:S(2)}, u32[]{:S(2)}) collective-permute-start(bf16[1024,256]{1,0:T(8,128)(2,1)S(1)} %collective-permute-done.2.refs_2_), channel_id=1, source_target_pairs={{0,448},{8,456},{16,464},{24,472},{32,480},{40,488},{48,496},{56,5... | collective-permute-start | bytes 1572872 | tf_op jit(solution)/shard_map/ppermute | solution.py:254
  76.8 14.3 %collective-permute-start.7 = (bf16[512,256]{1,0:T(8,128)(2,1)}, bf16[512,256]{1,0:T(8,128)(2,1)S(1)}, u32[]{:S(2)}, u32[]{:S(2)}) collective-permute-start(bf16[512,256]{1,0:T(8,128)(2,1)} %slice.8), channel_id=1, source_target_pairs={{0,64},{8,72},{16,80},{24,88},{32,96},{40,104},{48,112},{56,120},{... | collective-permute-start | bytes 786440 | tf_op jit(solution)/shard_map/ppermute | solution.py:256
  79.5 11.7 %collective-permute-start.8 = (bf16[512,256]{1,0:T(8,128)(2,1)}, bf16[512,256]{1,0:T(8,128)(2,1)}, u32[]{:S(2)}, u32[]{:S(2)}) collective-permute-start(bf16[512,256]{1,0:T(8,128)(2,1)} %slice.9), channel_id=1, source_target_pairs={{0,448},{8,456},{16,464},{24,472},{32,480},{40,488},{48,496},{56,5... | collective-permute-start | bytes 786440 | tf_op jit(solution)/shard_map/ppermute | solution.py:257
  86.3 21.4 %all-to-all-start.1 = ((bf16[8,64,128]{2,1,0:T(8,128)(2,1)}), bf16[8,64,128]{2,1,0:T(8,128)(2,1)S(1)}, u32[]{:S(2)}, u32[]{:S(2)}) async-start(bf16[8,64,128]{2,1,0:T(8,128)(2,1)} %shard_map.114), calls=%async_computation.1 | async-start | bytes 262144 | tf_op jit(solution)/shard_map/all_to_all | solution.py:266
  91.2 1.0 copy-start.3
  92.3 1.0 copy-start.5
  93.3 1.0 copy-start.7
  94.3 0.7 copy-start.16
  95.0 13.9 %copy-start.12 = (bf16[64,128]{1,0:T(8,128)(2,1)S(1)}, bf16[64,128]{1,0:T(8,128)(2,1)}, u32[]{:S(2)}) copy-start(bf16[64,128]{1,0:T(8,128)(2,1)} %upk_ref.1) | copy-start | bytes 49156
  100.2 0.6 copy-start.10
  100.8 8.1 %collective-permute-start.9 = (f32[128,256]{1,0:T(8,128)}, f32[128,256]{1,0:T(8,128)S(1)}, u32[]{:S(2)}, u32[]{:S(2)}) collective-permute-start(f32[128,256]{1,0:T(8,128)} %get-tuple-element.14), channel_id=1, source_target_pairs={{0,8},{8,0},{16,24},{24,16},{32,40},{40,32},{48,56},{56,48},{64,72... | collective-permute-start | bytes 393224 | tf_op jit(solution)/shard_map/ppermute | solution.py:282
  108.9 1.0 copy-start.8
  110.0 1.0 copy-start.9
  111.0 0.9 copy-start.11
  111.9 0.7 copy-start.13
  112.6 0.7 copy-start.14
Sparse Core Ops, SparseCore 0:
  19.9 57.2 all-gather.2

commit v2 on v1

--- a/solution.py
+++ b/solution.py
@@ -14,8 +14,7 @@
 
 VMEM = pl.BlockSpec(memory_space=pltpu.VMEM)
 SMEM = pl.BlockSpec(memory_space=pltpu.SMEM)
-HBM = pl.BlockSpec(memory_space=pl.ANY)
-PARAMS = pltpu.CompilerParams(vmem_limit_bytes=48 * 1024 * 1024)
+HBM = pl.BlockSpec(memory_space=pltpu.HBM)
 
 NT = (((1,), (1,)), ((), ()))
 TN = (((0,), (0,)), ((), ()))
@@ -46,50 +45,49 @@
     return ids
 
 
-def split_kernel(pos_ref, t_ref, mine_ref, theirs_ref):
-    pieces = t_ref.shape[1] // 512
-    for core in range(2):
-
-        @pl.when(pos_ref[0] == core)
-        def _():
-            for i in range(pieces):
-                to = pl.ds(i * 256, 256)
-                mine_ref[:, to] = t_ref[:, pl.ds(i * 512 + core * 256, 256)]
-                theirs_ref[:, to] = t_ref[:, pl.ds(i * 512 + (1 - core) * 256, 256)]
+def split_kernel(pos_ref, t_ref, mine_ref, theirs_ref, sem):
+    copies = []
+    for i in range(t_ref.shape[1] // 512):
+        to = pl.ds(i * 256, 256)
+        for k, ref in enumerate((mine_ref, theirs_ref)):
+            core = lax.rem(pos_ref[0] + k, 2)
+            at = pl.ds(pl.multiple_of(i * 512 + core * 256, 256), 256)
+            copies.append(pltpu.make_async_copy(t_ref.at[:, at], ref.at[:, to], sem.at[2 * i + k]))
+    for c in copies:
+        c.start()
+    for c in copies:
+        c.wait()
 
 
 def low_kernel(t_ref, down_ref, out_ref):
-    low = fold(mm(t_ref[...], down_ref[...], NN)).astype(BF)
+    low = fold(mm(t_ref[...], down_ref[...], NT)).astype(BF)
     for i in range(out_ref.shape[0]):
         out_ref[i] = low
 
 
 def project_kernel(pos_ref, t_ref, *refs):
-    w_refs, (own_ref, other_ref, t_scr, w_scr, t_sem, w_sem) = refs[:9], refs[9:]
-    y = pos_ref[1]
+    w_refs, (own_ref, other_ref, t_scr, w_scr, sem) = refs[:16], refs[16:]
     n = t_scr.shape[0]
-    half = w_scr.shape[1] // 2
+    half = w_refs[0].shape[0]
     copies = []
-    for e in range(n):
-        k = lax.rem(y + e, n)
-        mine = [pltpu.make_async_copy(t_ref.at[k], t_scr.at[e], t_sem.at[e])]
-        if e == 4:
-            for i in range(2):
-                mine.append(
-                    pltpu.make_async_copy(
-                        w_refs[4 + 4 * i], w_scr.at[e, pl.ds(i * half, half)], w_sem.at[e + 4 * i]
-                    )
+    for j in range(n):
+        k = lax.rem(pos_ref[1] + j * (2 * pos_ref[0] - 1) + n, n)
+        copies.append(
+            [pltpu.make_async_copy(t_ref.at[k], t_scr.at[j], sem.at[3 * j])]
+            + [
+                pltpu.make_async_copy(
+                    w_refs[8 * i + j], w_scr.at[j, pl.ds(i * half, half)], sem.at[3 * j + 1 + i]
                 )
-        else:
-            mine.append(pltpu.make_async_copy(w_refs[e], w_scr.at[e], w_sem.at[e]))
-        for c in mine:
+                for i in range(2)
+            ]
+        )
+        for c in copies[j]:
             c.start()
-        copies.append(mine)
     total = jnp.zeros((t_scr.shape[1], w_scr.shape[2]), F32)
-    for e in range(n):
-        for c in copies[e]:
+    for j in range(n):
+        for c in copies[j]:
             c.wait()
-        total = total + mm(t_scr[e], w_scr[e], NN)
+        total = total + mm(t_scr[j], w_scr[j], NN)
     rows = own_ref.shape[0]
     own_ref[...] = total[:rows]
     other_ref[...] = total[rows:]
@@ -97,10 +95,18 @@
 
 def attend_kernel(
     lengths_ref, own_ref, got_ref, low_ref, upk_ref, upv_ref, q_ref, p_ref,
-    pack_ref, low_half_ref, gk_ref, gv_ref,
+    pack_ref, low_half_ref, gk_ref, gv_ref, q_scr, p_scr, sem,
 ):
     rows = own_ref.shape[0]
     heads = q_ref.shape[1] // HD
+    batch = 4
+    copies = []
+    for i in range(heads // batch):
+        at = pl.ds(i * batch * HD, batch * HD)
+        for k, (ref, scr) in enumerate(((q_ref, q_scr), (p_ref, p_scr))):
+            copies.append(pltpu.make_async_copy(ref.at[:, at], scr.at[:, at], sem.at[2 * i + k]))
+    for c in copies:
+        c.start()
     score_scale = HD ** (-0.5)
     probe_scale = (q_ref.shape[1] * pack_ref.shape[0]) ** (-0.5)
     low_sum = low_ref[0].astype(F32)
@@ -130,8 +136,11 @@
     gv = jnp.zeros((rows, HD), F32)
     gap = jnp.zeros((1, rows), F32)
     for h in range(heads):
-        q = q_ref[:, pl.ds(h * HD, HD)]
-        probe = p_ref[:, pl.ds(h * HD, HD)]
+        if h % batch == 0:
+            for c in copies[2 * h // batch:2 * h // batch + 2]:
+                c.wait()
+        q = q_scr[:, pl.ds(h * HD, HD)]
+        probe = p_scr[:, pl.ds(h * HD, HD)]
         scores = mm(keys, q, NT)
         grads = mm(values, probe, NT)
         pol = probs_of(scores[:rows])
@@ -175,16 +184,11 @@
     down = mm(back_half, t_ref[...], TN).astype(BF)
     both = jnp.concatenate([gk_ref[...] * weight, gv_ref[...] * weight], axis=1).astype(BF)
     up = mm(low_half_ref[...], both, TN).astype(BF)
-    groups = 4
-    for i in range(16):
-        for g in range(groups):
-            out_ref[i * groups + g, pl.ds(0, 16)] = down[g * 16:(g + 1) * 16, i * 128:(i + 1) * 128]
-    for s in range(64):
-        tile, at = s // 8, (s % 8) * 2
-        i, g = tile // groups, tile % groups
-        piece = up[g * 16 + at:g * 16 + at + 2, i * 128:(i + 1) * 128].astype(F32)
-        piece = jnp.concatenate([piece, jnp.zeros((6, 128), F32)], axis=0)
-        out_ref[s, pl.ds(16, 8)] = piece.astype(BF)
+    slots = out_ref.shape[0]
+    wide, deep = t_ref.shape[1] // slots, up.shape[0] // slots
+    for j in range(slots):
+        out_ref[j, pl.ds(0, 64)] = down[:, j * wide:(j + 1) * wide]
+        out_ref[j, pl.ds(64, deep)] = up[j * deep:(j + 1) * deep]
 
 
 def sum_kernel(in_ref, out_ref):
@@ -197,27 +201,23 @@
 
 
 def place_kernel(in_ref, down_ref, upk_ref, upv_ref):
-    groups = 4
-    for i in range(16):
-        tile = jnp.concatenate(
-            [in_ref[i * groups + g, pl.ds(0, 16)].astype(F32) for g in range(groups)], axis=0
-        )
-        down_ref[pl.ds(i * 128, 128)] = tile.T
-    for s in range(64):
-        tile, at = s // 8, (s % 8) * 2
-        i, g = tile // groups, tile % groups
-        to = upk_ref if i == 0 else upv_ref
-        to[pl.ds(g * 16 + at, 2)] = in_ref[s, pl.ds(16, 8)].astype(F32)[:2]
-
-
-def call(kernel, outs, in_specs, out_specs, *args, scratch=()):
+    slots, _, wide = in_ref.shape
+    deep = upk_ref.shape[0] // slots
+    for j in range(slots):
+        down_ref[:, pl.ds(j * wide, wide)] = in_ref[j, pl.ds(0, 64)].astype(F32)
+        up = in_ref[j, pl.ds(64, deep)].astype(F32)
+        upk_ref[pl.ds(j * deep, deep)] = up[:, :HD]
+        upv_ref[pl.ds(j * deep, deep)] = up[:, HD:]
+
+
+def call(kernel, outs, in_specs, out_specs, *args, scratch=(), mib=8):
     return pl.pallas_call(
         kernel,
         out_shape=[jax.ShapeDtypeStruct(s, d) for s, d in outs],
         in_specs=in_specs,
         out_specs=out_specs,
         scratch_shapes=list(scratch),
-        compiler_params=PARAMS,
+        compiler_params=pltpu.CompilerParams(vmem_limit_bytes=mib * 1024 * 1024),
     )(*args)
 
 
@@ -231,77 +231,81 @@
 
     sites = [(y, x, core) for y in range(8) for x in range(4) for core in range(2)]
     swap = [(place(y, x, c), place(y, x, 1 - c)) for y, x, c in sites]
-    fore = [(place(y, x, c), place(y + 1, x, c)) for y, x, c in sites]
-    aft = [(place(y, x, c), place(y - 1, x, c)) for y, x, c in sites]
+    orbit = [(place(y, x, c), place(y + 1 - 2 * c, x, c)) for y, x, c in sites]
+    y_lines = [[place(y, x, c) for y in range(8)] for x in range(4) for c in range(2)]
+    squares = [[place(y, x, c) for x in range(4) for c in range(2)] for y in range(8)]
     x_lines = [[place(y, x, c) for x in range(4)] for y in range(8) for c in range(2)]
 
     half = (rows, feats // 2)
     mine, theirs = call(
-        split_kernel, [(half, BF), (half, BF)], [SMEM, VMEM], [VMEM, VMEM], pos, tokens
+        split_kernel, [(half, BF), (half, BF)], [SMEM, HBM], [VMEM, VMEM], pos, tokens,
+        scratch=[pltpu.SemaphoreType.DMA((feats // 256,))],
     )
     swapped = lax.ppermute(theirs, "row", swap)
     pair = jnp.concatenate([mine, swapped], axis=0)
     all_tokens = lax.all_gather(pair, "col", axis=0)
 
     w_both = jnp.concatenate([w_key, w_value], axis=1)
+    wide = w_both.shape[1]
     w_line = lax.all_to_all(
         jnp.broadcast_to(w_both, (4,) + w_both.shape), "row", 0, 0, axis_index_groups=x_lines
     )
-    w_own = w_line.reshape(4 * w_both.shape[0], w_both.shape[1])
-    up_going, down_going = [w_own], [w_own]
-    for _ in range(3):
-        up_going.append(lax.ppermute(up_going[-1], "row", fore))
-        down_going.append(lax.ppermute(down_going[-1], "row", aft))
-    middle = w_own.shape[0] // 2
-    last_up = lax.ppermute(up_going[3][:middle], "row", fore)
-    last_down = lax.ppermute(down_going[3][middle:], "row", aft)
-    w_parts = [
-        w_own, down_going[1], down_going[2], down_going[3], last_up,
-        up_going[3], up_going[2], up_going[1], last_down,
-    ]
+    w_parts = []
+    for i in range(2):
+        w_chain = w_line[2 * i:2 * i + 2].reshape(feats // 4, wide)
+        w_parts.append(w_chain)
+        for _ in range(7):
+            w_chain = lax.ppermute(w_chain, "row", orbit)
+            w_parts.append(w_chain)
 
     (low_pack,) = call(
-        low_kernel, [((8, rows // 2, 128), BF)], [VMEM, VMEM], [VMEM], tokens, down_proj
+        low_kernel, [((8, rows // 2, 128), BF)], [VMEM, VMEM], [VMEM], tokens, down_proj.T
     )
     low_parts = lax.all_to_all(low_pack, "col", 0, 0)
 
-    wide = w_both.shape[1]
     own, other = call(
         project_kernel,
         [((rows, wide), F32)] * 2,
-        [SMEM] + [HBM] * 10,
+        [SMEM] + [HBM] * 17,
         [VMEM, VMEM],
         pos, all_tokens, *w_parts,
         scratch=[
             pltpu.VMEM((8, 2 * rows, feats // 2), BF),
             pltpu.VMEM((8, feats // 2, wide), BF),
-            pltpu.SemaphoreType.DMA((8,)),
-            pltpu.SemaphoreType.DMA((9,)),
+            pltpu.SemaphoreType.DMA((24,)),
         ],
+        mib=56,
     )
     got = lax.ppermute(other, "row", swap)
     pack, low_half, gk, gv = call(
         attend_kernel,
         [((8, 80, 128), BF), ((rows, 64), BF), ((rows, HD), F32), ((rows, HD), F32)],
-        [SMEM] + [VMEM] * 7,
+        [SMEM] + [VMEM] * 5 + [HBM] * 2,
         [VMEM] * 4,
         lengths, own, got, low_parts, up_key, up_value, queries, probes,
+        scratch=[
+            pltpu.VMEM((rows, feats), BF),
+            pltpu.VMEM((rows, feats), BF),
+            pltpu.SemaphoreType.DMA((8,)),
+        ],
     )
     packs = lax.all_to_all(pack, "col", 0, 0)
+    slot = (8, 64 + 8, 2 * HD)
     (terms,) = call(
-        weigh_kernel, [((64, 24, 128), BF)], [SMEM] + [VMEM] * 5, [VMEM],
+        weigh_kernel, [(slot, BF)], [SMEM] + [VMEM] * 5, [VMEM],
         lengths, packs, low_half, gk, gv, tokens,
     )
-    term_parts = lax.all_to_all(terms, "row", 0, 0)
-    (summed,) = call(sum_kernel, [((64, 24, 128), BF)], [VMEM], [VMEM], term_parts)
-    pieces = lax.all_to_all(summed, "row", 0, 0)
-    return tuple(
-        call(
-            place_kernel,
-            [((feats, 64), F32), ((64, HD), F32), ((64, HD), F32)],
-            [VMEM], [VMEM] * 3, pieces,
-        )
-    )
+    term_parts = lax.all_to_all(terms, "row", 0, 0, axis_index_groups=squares)
+    (square,) = call(sum_kernel, [(slot, BF)], [VMEM], [VMEM], term_parts)
+    square_parts = lax.all_to_all(square, "row", 0, 0, axis_index_groups=y_lines)
+    (summed,) = call(sum_kernel, [(slot, BF)], [VMEM], [VMEM], square_parts)
+    pieces = lax.all_to_all(summed, "row", 0, 0, axis_index_groups=squares)
+    grad_down, grad_up_key, grad_up_value = call(
+        place_kernel,
+        [((64, feats), F32), ((64, HD), F32), ((64, HD), F32)],
+        [VMEM], [VMEM] * 3, pieces,
+    )
+    return grad_down.T, grad_up_key, grad_up_value
 
 
 def solution(mesh):

time: 189 us -> 185 us (0.979)
  starting transfers between devices: 46.5 us -> 73.5 us
  waiting for transfers between devices: 25.9 us -> 9.54 us
  local copies, waits for them, and re-layouts: 14.4 us -> 2.1 us
  blocking collectives: 71.5 us -> 68.2 us
    ppermute x8 -> x14, starting transfers between devices: 25.9 us -> 49.3 us  [on_device(): w_chain = lax.ppermute(w_chain, 'row', orbit)]
    ppermute x8 -> x14, waiting for transfers between devices: 23.5 us -> 7.19 us  [on_device(): w_chain = lax.ppermute(w_chain, 'row', orbit)]
    unnamed x35 -> x44, local copies, waits for them, and re-layouts: 11.8 us -> 2.03 us
    all_to_all x1, starting transfers between devices: 4.85 us -> 8.46 us  [on_device(): low_parts = lax.all_to_all(low_pack, 'col', 0, 0)]
    all_to_all x2 -> x3, blocking collectives: 44.6 us -> 41.3 us  [the longest x1 17.3 us: on_device(): lax.all_to_all(square, 'row', 0, 0, axis_index_groups=y_lines)]
    pallas_call x7 -> x8, Pallas kernels: 13.5 us -> 14.6 us  [call(): pl.pallas_call(kernel, out_shape=[jax.ShapeDtypeStruct(s, d) for s, d in...]
  transfers between devices with their start and end apart: 12 -> 18, of which waited for: 5 -> 8; matrix products, arithmetic and copies ran while one was open for 2% -> 1% of each run, Pallas kernels for 3% -> 4%
where the time goes in v2:
time: 185 us; the launch traced here: 184 us
  starting transfers between devices  73.5 us (40%)
  blocking collectives  68.2 us (37%)
  Pallas kernels  14.6 us (8%)
  between operations  14.5 us (8%)
  waiting for transfers between devices  9.54 us (5%)
  local copies, waits for them, and re-layouts  2.1 us (1%)
    ppermute x14, starting transfers between devices, on_device(): w_chain = lax.ppermute(w_chain, 'row', orbit)  49.3 us
    all_to_all x1, blocking collectives, on_device(): lax.all_to_all(square, 'row', 0, 0, axis_index_groups=y_lines)  17.3 us
    all_to_all x1, blocking collectives, on_device(): packs = lax.all_to_all(pack, 'col', 0, 0)  15.3 us
    pallas_call x8, Pallas kernels, call(): pl.pallas_call(kernel, out_shape=[jax.ShapeDtypeStruct(s, d) for s, d in...  14.6 us
    all_to_all x1, blocking collectives, on_device(): pieces = lax.all_to_all(summed, 'row', 0, 0, axis_index_groups=squares)  12.2 us
    all_to_all x1, blocking collectives, on_device(): term_parts = lax.all_to_all(terms, 'row', 0, 0, axis_index_groups=squares)  11.8 us
    all_to_all x1, blocking collectives, on_device(): lax.all_to_all(jnp.broadcast_to(w_both, (4,) + w_both.shape), 'row', 0, 0...  11.6 us
    ppermute x1, starting transfers between devices, on_device(): swapped = lax.ppermute(theirs, 'row', swap)  8.79 us
  transfers between devices with their start and end apart: 18, of which 8 were waited for; matrix products, arithmetic and copies ran while one was open for 1% of the time, Pallas kernels for 4%

profile of v2, /device:TPU:1, one launch (start us, length us, event | category | flops | bytes accessed | tf_op | source)
XLA Modules:
  0.0 184.3 jit_solution(6268950022096341116)
XLA Ops:
  7.2 0.0 all-gather.3.cloned.1.call-start
  7.2 0.1 pad_add_fusion.pos_ref
  7.3 1.0 copy-done
  8.4 0.7 shard_map.112
  9.1 8.8 %collective-permute-start = (bf16[128,1024]{1,0:T(8,128)(2,1)S(1)}, bf16[128,1024]{1,0:T(8,128)(2,1)S(1)}, u32[]{:S(2)}, u32[]{:S(2)}) collective-permute-start(bf16[128,1024]{1,0:T(8,128)(2,1)S(1)} %get-tuple-element.15), channel_id=1, source_target_pairs={{0,8},{8,0},{16,24},{24,16},{32,40},{40,32},{48,56},{56,48},{64,72... | collective-permute-start | bytes 786440 | tf_op jit(solution)/shard_map/ppermute | solution.py:244
  17.9 1.1 collective-permute-done
  19.0 0.8 pad_maximum_fusion
  19.8 0.0 all-gather.3.cloned.1.call-update
  19.9 0.9 pad_maximum_fusion.1
  20.8 11.6 %all_to_all.30 = bf16[4,256,256]{2,1,0:T(8,128)(2,1)S(1)} all-to-all(bf16[4,256,256]{2,1,0:T(8,128)(2,1)S(1)} %broadcast_in_dim.3), channel_id=1, replica_groups={{0,16,32,48},{8,24,40,56},{64,80,96,112},{72,88,104,120},{128,144,160,1..., dimensions={0} | all-to-all | bytes 1048576 | tf_op jit(solution)/shard_map/all_to_all | solution.py:250
  32.5 1.9 %collective-permute-start.8 = (bf16[512,256]{1,0:T(8,128)(2,1)S(1)}, bf16[512,256]{1,0:T(8,128)(2,1)S(1)}, u32[]{:S(2)}, u32[]{:S(2)}) collective-permute-start(bf16[512,256]{1,0:T(8,128)(2,1)S(1)} %bitcast.9), channel_id=1, source_target_pairs={{0,64},{8,456},{16,80},{24,472},{32,96},{40,488},{48,112},{56,504}... | collective-permute-start | bytes 786440 | tf_op jit(solution)/shard_map/ppermute | solution.py:258
  34.4 1.9 %collective-permute-start.1 = (bf16[512,256]{1,0:T(8,128)(2,1)S(1)}, bf16[512,256]{1,0:T(8,128)(2,1)S(1)}, u32[]{:S(2)}, u32[]{:S(2)}) collective-permute-start(bf16[512,256]{1,0:T(8,128)(2,1)S(1)} %bitcast.11), channel_id=1, source_target_pairs={{0,64},{8,456},{16,80},{24,472},{32,96},{40,488},{48,112},{56,504}... | collective-permute-start | bytes 786440 | tf_op jit(solution)/shard_map/ppermute | solution.py:258
  36.4 3.7 %collective-permute-done.8.refs_9_ = bf16[512,256]{1,0:T(8,128)(2,1)S(1)} collective-permute-done((bf16[512,256]{1,0:T(8,128)(2,1)S(1)}, bf16[512,256]{1,0:T(8,128)(2,1)S(1)}, u32[]{:S(2)}, u32[]{:S(2)}) %collective-permute-start.8) | collective-permute-done | bytes 262176 | tf_op jit(solution)/shard_map/ppermute | solution.py:258
  40.0 3.1 %collective-permute-start.9 = (bf16[512,256]{1,0:T(8,128)(2,1)S(1)}, bf16[512,256]{1,0:T(8,128)(2,1)S(1)}, u32[]{:S(2)}, u32[]{:S(2)}) collective-permute-start(bf16[512,256]{1,0:T(8,128)(2,1)S(1)} %collective-permute-done.8.refs_9_), channel_id=1, source_target_pairs={{0,64},{8,456},{16,80},{24,472},{32,96},{40,488},{48,112},{56,504}... | collective-permute-start | bytes 786440 | tf_op jit(solution)/shard_map/ppermute | solution.py:258
  43.2 2.8 %collective-permute-start.2 = (bf16[512,256]{1,0:T(8,128)(2,1)S(1)}, bf16[512,256]{1,0:T(8,128)(2,1)S(1)}, u32[]{:S(2)}, u32[]{:S(2)}) collective-permute-start(bf16[512,256]{1,0:T(8,128)(2,1)S(1)} %collective-permute-done.1.refs_1_), channel_id=1, source_target_pairs={{0,64},{8,456},{16,80},{24,472},{32,96},{40,488},{48,112},{56,504}... | collective-permute-start | bytes 786440 | tf_op jit(solution)/shard_map/ppermute | solution.py:258
  46.0 1.6 collective-permute-done.9.refs_10_
  47.5 4.3 %collective-permute-start.10 = (bf16[512,256]{1,0:T(8,128)(2,1)S(1)}, bf16[512,256]{1,0:T(8,128)(2,1)S(1)}, u32[]{:S(2)}, u32[]{:S(2)}) collective-permute-start(bf16[512,256]{1,0:T(8,128)(2,1)S(1)} %collective-permute-done.9.refs_10_), channel_id=1, source_target_pairs={{0,64},{8,456},{16,80},{24,472},{32,96},{40,488},{48,112},{56,504}... | collective-permute-start | bytes 786440 | tf_op jit(solution)/shard_map/ppermute | solution.py:258
  51.9 2.8 %collective-permute-start.3 = (bf16[512,256]{1,0:T(8,128)(2,1)S(1)}, bf16[512,256]{1,0:T(8,128)(2,1)S(1)}, u32[]{:S(2)}, u32[]{:S(2)}) collective-permute-start(bf16[512,256]{1,0:T(8,128)(2,1)S(1)} %collective-permute-done.2.refs_2_), channel_id=1, source_target_pairs={{0,64},{8,456},{16,80},{24,472},{32,96},{40,488},{48,112},{56,504}... | collective-permute-start | bytes 786440 | tf_op jit(solution)/shard_map/ppermute | solution.py:258
  54.7 0.5 collective-permute-done.10.refs_11_
  55.2 5.4 %collective-permute-start.11 = (bf16[512,256]{1,0:T(8,128)(2,1)S(1)}, bf16[512,256]{1,0:T(8,128)(2,1)S(1)}, u32[]{:S(2)}, u32[]{:S(2)}) collective-permute-start(bf16[512,256]{1,0:T(8,128)(2,1)S(1)} %collective-permute-done.10.refs_11_), channel_id=1, source_target_pairs={{0,64},{8,456},{16,80},{24,472},{32,96},{40,488},{48,112},{56,504}... | collective-permute-start | bytes 786440 | tf_op jit(solution)/shard_map/ppermute | solution.py:258
  60.6 2.8 %collective-permute-start.4 = (bf16[512,256]{1,0:T(8,128)(2,1)S(1)}, bf16[512,256]{1,0:T(8,128)(2,1)S(1)}, u32[]{:S(2)}, u32[]{:S(2)}) collective-permute-start(bf16[512,256]{1,0:T(8,128)(2,1)S(1)} %collective-permute-done.3.refs_3_), channel_id=1, source_target_pairs={{0,64},{8,456},{16,80},{24,472},{32,96},{40,488},{48,112},{56,504}... | collective-permute-start | bytes 786440 | tf_op jit(solution)/shard_map/ppermute | solution.py:258
  63.4 0.5 collective-permute-done.11.refs_12_
  63.9 5.4 %collective-permute-start.12 = (bf16[512,256]{1,0:T(8,128)(2,1)S(1)}, bf16[512,256]{1,0:T(8,128)(2,1)S(1)}, u32[]{:S(2)}, u32[]{:S(2)}) collective-permute-start(bf16[512,256]{1,0:T(8,128)(2,1)S(1)} %collective-permute-done.11.refs_12_), channel_id=1, source_target_pairs={{0,64},{8,456},{16,80},{24,472},{32,96},{40,488},{48,112},{56,504}... | collective-permute-start | bytes 786440 | tf_op jit(solution)/shard_map/ppermute | solution.py:258
  69.3 2.8 %collective-permute-start.5 = (bf16[512,256]{1,0:T(8,128)(2,1)S(1)}, bf16[512,256]{1,0:T(8,128)(2,1)S(1)}, u32[]{:S(2)}, u32[]{:S(2)}) collective-permute-start(bf16[512,256]{1,0:T(8,128)(2,1)S(1)} %collective-permute-done.4.refs_4_), channel_id=1, source_target_pairs={{0,64},{8,456},{16,80},{24,472},{32,96},{40,488},{48,112},{56,504}... | collective-permute-start | bytes 786440 | tf_op jit(solution)/shard_map/ppermute | solution.py:258
  72.1 0.5 collective-permute-done.12.refs_13_
  72.6 5.4 %collective-permute-start.13 = (bf16[512,256]{1,0:T(8,128)(2,1)S(1)}, bf16[512,256]{1,0:T(8,128)(2,1)}, u32[]{:S(2)}, u32[]{:S(2)}) collective-permute-start(bf16[512,256]{1,0:T(8,128)(2,1)S(1)} %collective-permute-done.12.refs_13_), channel_id=1, source_target_pairs={{0,64},{8,456},{16,80},{24,472},{32,96},{40,488},{48,112},{56,504}... | collective-permute-start | bytes 786440 | tf_op jit(solution)/shard_map/ppermute | solution.py:258
  78.1 2.8 %collective-permute-start.6 = (bf16[512,256]{1,0:T(8,128)(2,1)S(1)}, bf16[512,256]{1,0:T(8,128)(2,1)}, u32[]{:S(2)}, u32[]{:S(2)}) collective-permute-start(bf16[512,256]{1,0:T(8,128)(2,1)S(1)} %collective-permute-done.5.refs_5_), channel_id=1, source_target_pairs={{0,64},{8,456},{16,80},{24,472},{32,96},{40,488},{48,112},{56,504}... | collective-permute-start | bytes 786440 | tf_op jit(solution)/shard_map/ppermute | solution.py:258
  80.8 0.5 collective-permute-done.13.refs_14_
  81.3 5.1 %collective-permute-start.14 = (bf16[512,256]{1,0:T(8,128)(2,1)}, bf16[512,256]{1,0:T(8,128)(2,1)}, u32[]{:S(2)}, u32[]{:S(2)}) collective-permute-start(bf16[512,256]{1,0:T(8,128)(2,1)} %collective-permute-done.13.refs_14_), channel_id=1, source_target_pairs={{0,64},{8,456},{16,80},{24,472},{32,96},{40,488},{48,112},{56,504}... | collective-permute-start | bytes 786440 | tf_op jit(solution)/shard_map/ppermute | solution.py:258
  86.5 2.8 %collective-permute-start.7 = (bf16[512,256]{1,0:T(8,128)(2,1)}, bf16[512,256]{1,0:T(8,128)(2,1)}, u32[]{:S(2)}, u32[]{:S(2)}) collective-permute-start(bf16[512,256]{1,0:T(8,128)(2,1)} %collective-permute-done.6.refs_6_), channel_id=1, source_target_pairs={{0,64},{8,456},{16,80},{24,472},{32,96},{40,488},{48,112},{56,504}... | collective-permute-start | bytes 786440 | tf_op jit(solution)/shard_map/ppermute | solution.py:258
  89.3 1.0 shard_map.114
  90.3 8.5 %all-to-all-start.1 = ((bf16[8,64,128]{2,1,0:T(8,128)(2,1)}), bf16[8,64,128]{2,1,0:T(8,128)(2,1)S(1)}, u32[]{:S(2)}, u32[]{:S(2)}) async-start(bf16[8,64,128]{2,1,0:T(8,128)(2,1)} %shard_map.114), calls=%async_computation.1 | async-start | bytes 262144 | tf_op jit(solution)/shard_map/all_to_all | solution.py:264
  98.8 0.0 all-gather.3.cloned.1.call-done
  98.9 0.0 copy-start.2
  98.9 0.0 copy-start.3
  98.9 0.0 copy-start.6
  98.9 5.8 %shard_map.113 = (f32[128,256]{1,0:T(8,128)}, f32[128,256]{1,0:T(8,128)}) custom-call(s32[2]{0:T(128)} %copy-done.9, bf16[8,256,1024]{2,1,0:T(8,128)(2,1)} %bitcast.8, bf16[512,256]{1,0:T(8,128)(2,1)} %bitcast.12, bf16[512,256]{1,0:T(8,128)(2,1)} %copy-done.13, bf16[512,256]{1,0:T(8,128)(2,1)} %copy-done.15, bf16[512,256]{1,0:T(8,128)(2,1)} %copy-done.17, ...), custom_call_target="tpu_custom_call" | custom-call | tf_op jit(solution)/shard_map/pallas_call | solution.py:214
  104.8 6.8 %collective-permute-start.15 = (f32[128,256]{1,0:T(8,128)}, f32[128,256]{1,0:T(8,128)S(1)}, u32[]{:S(2)}, u32[]{:S(2)}) collective-permute-start(f32[128,256]{1,0:T(8,128)} %get-tuple-element.17), channel_id=1, source_target_pairs={{0,8},{8,0},{16,24},{24,16},{32,40},{40,32},{48,56},{56,48},{64,72... | collective-permute-start | bytes 393224 | tf_op jit(solution)/shard_map/ppermute | solution.py:279
  111.7 1.2 collective-permute-done.15.got_ref
  112.8 0.0 copy-start.5
  112.9 0.9 copy-done.5
  113.8 5.2 %shard_map.115 = (bf16[8,80,128]{2,1,0:T(8,128)(2,1)S(1)}, bf16[128,64]{1,0:T(8,128)(2,1)S(1)}, f32[128,128]{1,0:T(8,128)S(1)}, f32[128,128]{1,0:T(8,128)S(1)}) custom-call(s32[1,8]{1,0:T(1,128)S(1)} %copy-done.8, f32[128,256]{1,0:T(8,128)S(1)} %copy-done.5, f32[128,256]{1,0:T(8,128)S(1)} %collective-permute-done.15.got_ref, ...), custom_call_target="tpu_custom_call" | custom-call | tf_op jit(solution)/shard_map/pallas_call | solution.py:214
  118.9 15.3 %all_to_all.31.pack_ref = bf16[8,80,128]{2,1,0:T(8,128)(2,1)S(1)} all-to-all(bf16[8,80,128]{2,1,0:T(8,128)(2,1)S(1)} %get-tuple-element.18), channel_id=1, replica_groups=mesh['row'=64,'col'=8] {'col'}, dimensions={0} | all-to-all | bytes 327680 | tf_op jit(solution)/shard_map/all_to_all | solution.py:292
  134.3 0.9 shard_map.116
  135.2 11.8 %all_to_all.32.in_ref = bf16[8,72,256]{2,1,0:T(8,128)(2,1)S(1)} all-to-all(bf16[8,72,256]{2,1,0:T(8,128)(2,1)S(1)} %shard_map.116), channel_id=1, replica_groups={{0,8,16,24,32,40,48,56},{64,72,80,88,96,104,112,120},{128,136,144,152,1..., dimensions={0} | all-to-all | bytes 589824 | tf_op jit(solution)/shard_map/all_to_all | solution.py:298
  147.1 17.3 %all_to_all.33.in_ref = bf16[8,72,256]{2,1,0:T(8,128)(2,1)S(1)} all-to-all(bf16[8,72,256]{2,1,0:T(8,128)(2,1)S(1)} %shard_map.117), channel_id=1, replica_groups={{0,64,128,192,256,320,384,448},{8,72,136,200,264,328,392,456},{16,80,14..., dimensions={0} | all-to-all | bytes 589824 | tf_op jit(solution)/shard_map/all_to_all | solution.py:300
  164.4 12.2 %all_to_all.34.in_ref = bf16[8,72,256]{2,1,0:T(8,128)(2,1)S(1)} all-to-all(bf16[8,72,256]{2,1,0:T(8,128)(2,1)S(1)} %shard_map.118), channel_id=1, replica_groups={{0,8,16,24,32,40,48,56},{64,72,80,88,96,104,112,120},{128,136,144,152,1..., dimensions={0} | all-to-all | bytes 589824 | tf_op jit(solution)/shard_map/all_to_all | solution.py:302
  176.6 0.8 shard_map.119
  (51 shorter events, 0.3 us)
Async XLA Ops:
  7.2 91.6 %all-gather.3.cloned.1.call-start = ((), (), s32[]{:S(2)}) async-start(), calls=%async_computation.6 | async-start | bytes 4718592 | tf_op jit(solution)/shard_map/all_gather | solution.py:246
  7.3 1.0 copy-start
  8.4 90.5 %copy-start.9 = (s32[2]{0:T(128)}, s32[2]{0:T(128)S(1)}, u32[]{:S(2)}) copy-start(s32[2]{0:T(128)S(1)} %pad_add_fusion.pos_ref) | copy-start | bytes 28
  8.4 80.9 %copy-start.1 = (bf16[128,2048]{1,0:T(8,128)(2,1)S(1)}, bf16[128,2048]{1,0:T(8,128)(2,1)}, u32[]{:S(2)}) copy-start(bf16[128,2048]{1,0:T(8,128)(2,1)} %t_ref.5) | copy-start | bytes 1572868
  8.4 80.9 %copy-start.4 = (bf16[2048,64]{0,1:T(8,128)(2,1)S(1)}, bf16[2048,64]{0,1:T(8,128)(2,1)}, u32[]{:S(2)}) copy-start(bf16[2048,64]{0,1:T(8,128)(2,1)} %param.14) | copy-start | bytes 786436
  9.1 9.9 %collective-permute-start = (bf16[128,1024]{1,0:T(8,128)(2,1)S(1)}, bf16[128,1024]{1,0:T(8,128)(2,1)S(1)}, u32[]{:S(2)}, u32[]{:S(2)}) collective-permute-start(bf16[128,1024]{1,0:T(8,128)(2,1)S(1)} %get-tuple-element.15), channel_id=1, source_target_pairs={{0,8},{8,0},{16,24},{24,16},{32,40},{40,32},{48,56},{56,48},{64,72... | collective-permute-start | bytes 786440 | tf_op jit(solution)/shard_map/ppermute | solution.py:244
  32.5 66.4 %copy-start.10 = (bf16[2,256,256]{2,1,0:T(8,128)(2,1)}, bf16[2,256,256]{2,1,0:T(8,128)(2,1)S(1)}, u32[]{:S(2)}) copy-start(bf16[2,256,256]{2,1,0:T(8,128)(2,1)S(1)} %get-tuple-element.25) | copy-start | bytes 786436
  32.5 66.4 %copy-start.11 = (bf16[2,256,256]{2,1,0:T(8,128)(2,1)}, bf16[2,256,256]{2,1,0:T(8,128)(2,1)S(1)}, u32[]{:S(2)}) copy-start(bf16[2,256,256]{2,1,0:T(8,128)(2,1)S(1)} %get-tuple-element.26) | copy-start | bytes 786436
  32.5 7.5 %collective-permute-start.8 = (bf16[512,256]{1,0:T(8,128)(2,1)S(1)}, bf16[512,256]{1,0:T(8,128)(2,1)S(1)}, u32[]{:S(2)}, u32[]{:S(2)}) collective-permute-start(bf16[512,256]{1,0:T(8,128)(2,1)S(1)} %bitcast.9), channel_id=1, source_target_pairs={{0,64},{8,456},{16,80},{24,472},{32,96},{40,488},{48,112},{56,504}... | collective-permute-start | bytes 786440 | tf_op jit(solution)/shard_map/ppermute | solution.py:258
  34.4 8.7 %collective-permute-start.1 = (bf16[512,256]{1,0:T(8,128)(2,1)S(1)}, bf16[512,256]{1,0:T(8,128)(2,1)S(1)}, u32[]{:S(2)}, u32[]{:S(2)}) collective-permute-start(bf16[512,256]{1,0:T(8,128)(2,1)S(1)} %bitcast.11), channel_id=1, source_target_pairs={{0,64},{8,456},{16,80},{24,472},{32,96},{40,488},{48,112},{56,504}... | collective-permute-start | bytes 786440 | tf_op jit(solution)/shard_map/ppermute | solution.py:258
  40.0 58.8 %copy-start.12 = (bf16[512,256]{1,0:T(8,128)(2,1)}, bf16[512,256]{1,0:T(8,128)(2,1)S(1)}, u32[]{:S(2)}) copy-start(bf16[512,256]{1,0:T(8,128)(2,1)S(1)} %collective-permute-done.8.refs_9_) | copy-start | bytes 786436
  40.0 7.5 %collective-permute-start.9 = (bf16[512,256]{1,0:T(8,128)(2,1)S(1)}, bf16[512,256]{1,0:T(8,128)(2,1)S(1)}, u32[]{:S(2)}, u32[]{:S(2)}) collective-permute-start(bf16[512,256]{1,0:T(8,128)(2,1)S(1)} %collective-permute-done.8.refs_9_), channel_id=1, source_target_pairs={{0,64},{8,456},{16,80},{24,472},{32,96},{40,488},{48,112},{56,504}... | collective-permute-start | bytes 786440 | tf_op jit(solution)/shard_map/ppermute | solution.py:258
  43.2 55.7 %copy-start.13 = (bf16[512,256]{1,0:T(8,128)(2,1)}, bf16[512,256]{1,0:T(8,128)(2,1)S(1)}, u32[]{:S(2)}) copy-start(bf16[512,256]{1,0:T(8,128)(2,1)S(1)} %collective-permute-done.1.refs_1_) | copy-start | bytes 786436
  43.2 8.7 %collective-permute-start.2 = (bf16[512,256]{1,0:T(8,128)(2,1)S(1)}, bf16[512,256]{1,0:T(8,128)(2,1)S(1)}, u32[]{:S(2)}, u32[]{:S(2)}) collective-permute-start(bf16[512,256]{1,0:T(8,128)(2,1)S(1)} %collective-permute-done.1.refs_1_), channel_id=1, source_target_pairs={{0,64},{8,456},{16,80},{24,472},{32,96},{40,488},{48,112},{56,504}... | collective-permute-start | bytes 786440 | tf_op jit(solution)/shard_map/ppermute | solution.py:258
  47.5 51.3 %copy-start.14 = (bf16[512,256]{1,0:T(8,128)(2,1)}, bf16[512,256]{1,0:T(8,128)(2,1)S(1)}, u32[]{:S(2)}) copy-start(bf16[512,256]{1,0:T(8,128)(2,1)S(1)} %collective-permute-done.9.refs_10_) | copy-start | bytes 786436
  47.5 7.6 %collective-permute-start.10 = (bf16[512,256]{1,0:T(8,128)(2,1)S(1)}, bf16[512,256]{1,0:T(8,128)(2,1)S(1)}, u32[]{:S(2)}, u32[]{:S(2)}) collective-permute-start(bf16[512,256]{1,0:T(8,128)(2,1)S(1)} %collective-permute-done.9.refs_10_), channel_id=1, source_target_pairs={{0,64},{8,456},{16,80},{24,472},{32,96},{40,488},{48,112},{56,504}... | collective-permute-start | bytes 786440 | tf_op jit(solution)/shard_map/ppermute | solution.py:258
  51.9 47.0 %copy-start.15 = (bf16[512,256]{1,0:T(8,128)(2,1)}, bf16[512,256]{1,0:T(8,128)(2,1)S(1)}, u32[]{:S(2)}) copy-start(bf16[512,256]{1,0:T(8,128)(2,1)S(1)} %collective-permute-done.2.refs_2_) | copy-start | bytes 786436
  51.9 8.7 %collective-permute-start.3 = (bf16[512,256]{1,0:T(8,128)(2,1)S(1)}, bf16[512,256]{1,0:T(8,128)(2,1)S(1)}, u32[]{:S(2)}, u32[]{:S(2)}) collective-permute-start(bf16[512,256]{1,0:T(8,128)(2,1)S(1)} %collective-permute-done.2.refs_2_), channel_id=1, source_target_pairs={{0,64},{8,456},{16,80},{24,472},{32,96},{40,488},{48,112},{56,504}... | collective-permute-start | bytes 786440 | tf_op jit(solution)/shard_map/ppermute | solution.py:258
  55.2 43.6 %copy-start.16 = (bf16[512,256]{1,0:T(8,128)(2,1)}, bf16[512,256]{1,0:T(8,128)(2,1)S(1)}, u32[]{:S(2)}) copy-start(bf16[512,256]{1,0:T(8,128)(2,1)S(1)} %collective-permute-done.10.refs_11_) | copy-start | bytes 786436
  55.2 8.7 %collective-permute-start.11 = (bf16[512,256]{1,0:T(8,128)(2,1)S(1)}, bf16[512,256]{1,0:T(8,128)(2,1)S(1)}, u32[]{:S(2)}, u32[]{:S(2)}) collective-permute-start(bf16[512,256]{1,0:T(8,128)(2,1)S(1)} %collective-permute-done.10.refs_11_), channel_id=1, source_target_pairs={{0,64},{8,456},{16,80},{24,472},{32,96},{40,488},{48,112},{56,504}... | collective-permute-start | bytes 786440 | tf_op jit(solution)/shard_map/ppermute | solution.py:258
  60.6 38.2 %copy-start.17 = (bf16[512,256]{1,0:T(8,128)(2,1)}, bf16[512,256]{1,0:T(8,128)(2,1)S(1)}, u32[]{:S(2)}) copy-start(bf16[512,256]{1,0:T(8,128)(2,1)S(1)} %collective-permute-done.3.refs_3_) | copy-start | bytes 786436
  60.6 8.7 %collective-permute-start.4 = (bf16[512,256]{1,0:T(8,128)(2,1)S(1)}, bf16[512,256]{1,0:T(8,128)(2,1)S(1)}, u32[]{:S(2)}, u32[]{:S(2)}) collective-permute-start(bf16[512,256]{1,0:T(8,128)(2,1)S(1)} %collective-permute-done.3.refs_3_), channel_id=1, source_target_pairs={{0,64},{8,456},{16,80},{24,472},{32,96},{40,488},{48,112},{56,504}... | collective-permute-start | bytes 786440 | tf_op jit(solution)/shard_map/ppermute | solution.py:258
  63.9 34.9 %copy-start.18 = (bf16[512,256]{1,0:T(8,128)(2,1)}, bf16[512,256]{1,0:T(8,128)(2,1)S(1)}, u32[]{:S(2)}) copy-start(bf16[512,256]{1,0:T(8,128)(2,1)S(1)} %collective-permute-done.11.refs_12_) | copy-start | bytes 786436
  63.9 8.7 %collective-permute-start.12 = (bf16[512,256]{1,0:T(8,128)(2,1)S(1)}, bf16[512,256]{1,0:T(8,128)(2,1)S(1)}, u32[]{:S(2)}, u32[]{:S(2)}) collective-permute-start(bf16[512,256]{1,0:T(8,128)(2,1)S(1)} %collective-permute-done.11.refs_12_), channel_id=1, source_target_pairs={{0,64},{8,456},{16,80},{24,472},{32,96},{40,488},{48,112},{56,504}... | collective-permute-start | bytes 786440 | tf_op jit(solution)/shard_map/ppermute | solution.py:258
  69.3 3.3 %copy-start.19 = (bf16[512,256]{1,0:T(8,128)(2,1)}, bf16[512,256]{1,0:T(8,128)(2,1)S(1)}, u32[]{:S(2)}) copy-start(bf16[512,256]{1,0:T(8,128)(2,1)S(1)} %collective-permute-done.4.refs_4_) | copy-start | bytes 786436
  69.3 8.7 %collective-permute-start.5 = (bf16[512,256]{1,0:T(8,128)(2,1)S(1)}, bf16[512,256]{1,0:T(8,128)(2,1)S(1)}, u32[]{:S(2)}, u32[]{:S(2)}) collective-permute-start(bf16[512,256]{1,0:T(8,128)(2,1)S(1)} %collective-permute-done.4.refs_4_), channel_id=1, source_target_pairs={{0,64},{8,456},{16,80},{24,472},{32,96},{40,488},{48,112},{56,504}... | collective-permute-start | bytes 786440 | tf_op jit(solution)/shard_map/ppermute | solution.py:258
  72.6 5.4 %copy-start.20 = (bf16[512,256]{1,0:T(8,128)(2,1)}, bf16[512,256]{1,0:T(8,128)(2,1)S(1)}, u32[]{:S(2)}) copy-start(bf16[512,256]{1,0:T(8,128)(2,1)S(1)} %collective-permute-done.12.refs_13_) | copy-start | bytes 786436
  72.6 8.7 %collective-permute-start.13 = (bf16[512,256]{1,0:T(8,128)(2,1)S(1)}, bf16[512,256]{1,0:T(8,128)(2,1)}, u32[]{:S(2)}, u32[]{:S(2)}) collective-permute-start(bf16[512,256]{1,0:T(8,128)(2,1)S(1)} %collective-permute-done.12.refs_13_), channel_id=1, source_target_pairs={{0,64},{8,456},{16,80},{24,472},{32,96},{40,488},{48,112},{56,504}... | collective-permute-start | bytes 786440 | tf_op jit(solution)/shard_map/ppermute | solution.py:258
  78.0 3.3 %copy-start.21 = (bf16[512,256]{1,0:T(8,128)(2,1)}, bf16[512,256]{1,0:T(8,128)(2,1)S(1)}, u32[]{:S(2)}) copy-start(bf16[512,256]{1,0:T(8,128)(2,1)S(1)} %collective-permute-done.5.refs_5_) | copy-start | bytes 786436
  78.1 8.4 %collective-permute-start.6 = (bf16[512,256]{1,0:T(8,128)(2,1)S(1)}, bf16[512,256]{1,0:T(8,128)(2,1)}, u32[]{:S(2)}, u32[]{:S(2)}) collective-permute-start(bf16[512,256]{1,0:T(8,128)(2,1)S(1)} %collective-permute-done.5.refs_5_), channel_id=1, source_target_pairs={{0,64},{8,456},{16,80},{24,472},{32,96},{40,488},{48,112},{56,504}... | collective-permute-start | bytes 786440 | tf_op jit(solution)/shard_map/ppermute | solution.py:258
  81.3 17.4 %collective-permute-start.14 = (bf16[512,256]{1,0:T(8,128)(2,1)}, bf16[512,256]{1,0:T(8,128)(2,1)}, u32[]{:S(2)}, u32[]{:S(2)}) collective-permute-start(bf16[512,256]{1,0:T(8,128)(2,1)} %collective-permute-done.13.refs_14_), channel_id=1, source_target_pairs={{0,64},{8,456},{16,80},{24,472},{32,96},{40,488},{48,112},{56,504}... | collective-permute-start | bytes 786440 | tf_op jit(solution)/shard_map/ppermute | solution.py:258
  86.5 12.3 %collective-permute-start.7 = (bf16[512,256]{1,0:T(8,128)(2,1)}, bf16[512,256]{1,0:T(8,128)(2,1)}, u32[]{:S(2)}, u32[]{:S(2)}) collective-permute-start(bf16[512,256]{1,0:T(8,128)(2,1)} %collective-permute-done.6.refs_6_), channel_id=1, source_target_pairs={{0,64},{8,456},{16,80},{24,472},{32,96},{40,488},{48,112},{56,504}... | collective-permute-start | bytes 786440 | tf_op jit(solution)/shard_map/ppermute | solution.py:258
  90.3 21.4 %all-to-all-start.1 = ((bf16[8,64,128]{2,1,0:T(8,128)(2,1)}), bf16[8,64,128]{2,1,0:T(8,128)(2,1)S(1)}, u32[]{:S(2)}, u32[]{:S(2)}) async-start(bf16[8,64,128]{2,1,0:T(8,128)(2,1)} %shard_map.114), calls=%async_computation.1 | async-start | bytes 262144 | tf_op jit(solution)/shard_map/all_to_all | solution.py:264
  98.9 13.9 %copy-start.2 = (bf16[128,2048]{1,0:T(8,128)(2,1)S(1)}, bf16[128,2048]{1,0:T(8,128)(2,1)}, u32[]{:S(2)}) copy-start(bf16[128,2048]{1,0:T(8,128)(2,1)} %q_ref.1) | copy-start | bytes 1572868
  98.9 13.9 %copy-start.3 = (bf16[128,2048]{1,0:T(8,128)(2,1)S(1)}, bf16[128,2048]{1,0:T(8,128)(2,1)}, u32[]{:S(2)}) copy-start(bf16[128,2048]{1,0:T(8,128)(2,1)} %p_ref.1) | copy-start | bytes 1572868
  98.9 13.9 %copy-start.6 = (bf16[64,128]{1,0:T(8,128)(2,1)S(1)}, bf16[64,128]{1,0:T(8,128)(2,1)}, u32[]{:S(2)}) copy-start(bf16[64,128]{1,0:T(8,128)(2,1)} %upk_ref.1) | copy-start | bytes 49156
  98.9 13.9 %copy-start.7 = (bf16[64,128]{1,0:T(8,128)(2,1)S(1)}, bf16[64,128]{1,0:T(8,128)(2,1)}, u32[]{:S(2)}) copy-start(bf16[64,128]{1,0:T(8,128)(2,1)} %upv_ref.1) | copy-start | bytes 49156
  98.9 13.9 %copy-start.8 = (s32[1,8]{1,0:T(1,128)S(1)}, s32[1,8]{1,0:T(1,128)}, u32[]{:S(2)}) copy-start(s32[1,8]{1,0:T(1,128)} %lengths_ref.3) | copy-start | bytes 100
  104.8 8.0 %collective-permute-start.15 = (f32[128,256]{1,0:T(8,128)}, f32[128,256]{1,0:T(8,128)S(1)}, u32[]{:S(2)}, u32[]{:S(2)}) collective-permute-start(f32[128,256]{1,0:T(8,128)} %get-tuple-element.17), channel_id=1, source_target_pairs={{0,8},{8,0},{16,24},{24,16},{32,40},{40,32},{48,56},{56,48},{64,72... | collective-permute-start | bytes 393224 | tf_op jit(solution)/shard_map/ppermute | solution.py:279
  112.8 0.9 copy-start.5
Sparse Core Ops, SparseCore 0:
  20.0 57.2 all-gather.2

commit v3 on v2

--- a/solution.py
+++ b/solution.py
@@ -25,14 +25,12 @@
     return lax.dot_general(a, b, dims, preferred_element_type=F32)
 
 
-def fold(a):
-    half = a.shape[0] // 2
-    return jnp.concatenate([a[:half], a[half:]], axis=1)
-
-
-def unfold(a):
-    half = a.shape[1] // 2
-    return jnp.concatenate([a[:, :half], a[:, half:]], axis=0)
+def fold(a, rows):
+    return jnp.concatenate([a[i:i + rows] for i in range(0, a.shape[0], rows)], axis=1)
+
+
+def unfold(a, wide):
+    return jnp.concatenate([a[:, i:i + wide] for i in range(0, a.shape[1], wide)], axis=0)
 
 
 def doc_ids(lengths_ref, axis, count, docs):
@@ -60,42 +58,49 @@
 
 
 def low_kernel(t_ref, down_ref, out_ref):
-    low = fold(mm(t_ref[...], down_ref[...], NT)).astype(BF)
-    for i in range(out_ref.shape[0]):
-        out_ref[i] = low
+    low = mm(t_ref[...], down_ref[...], NT)
+    rows, wide = out_ref.shape
+    low = fold(low, rows // 2)
+    high = low.astype(BF).astype(F32)
+    out_ref[...] = jnp.concatenate([high, low - high], axis=0).astype(BF)
 
 
 def project_kernel(pos_ref, t_ref, *refs):
-    w_refs, (own_ref, other_ref, t_scr, w_scr, sem) = refs[:16], refs[16:]
+    w_refs, (own_ref, other_ref, low_ref, t_scr, w_scr, sem) = refs[:9], refs[9:]
     n = t_scr.shape[0]
-    half = w_refs[0].shape[0]
+    half = w_scr.shape[1] // 2
+    way = 2 * pos_ref[0] - 1
     copies = []
-    for j in range(n):
-        k = lax.rem(pos_ref[1] + j * (2 * pos_ref[0] - 1) + n, n)
+    for j, step in enumerate((0, 1, 2, 3, -1, -2, -3, 4)):
+        k = lax.rem(pos_ref[1] + step * way + n, n)
+        parts = [(t_ref.at[k], t_scr.at[j])]
+        if step == 4:
+            parts.append((w_refs[7], w_scr.at[j, pl.ds(0, half)]))
+            parts.append((w_refs[8], w_scr.at[j, pl.ds(half, half)]))
+        else:
+            parts.append((w_refs[j], w_scr.at[j]))
         copies.append(
-            [pltpu.make_async_copy(t_ref.at[k], t_scr.at[j], sem.at[3 * j])]
-            + [
-                pltpu.make_async_copy(
-                    w_refs[8 * i + j], w_scr.at[j, pl.ds(i * half, half)], sem.at[3 * j + 1 + i]
-                )
-                for i in range(2)
-            ]
+            [pltpu.make_async_copy(a, b, sem.at[3 * j + i]) for i, (a, b) in enumerate(parts)]
         )
         for c in copies[j]:
             c.start()
-    total = jnp.zeros((t_scr.shape[1], w_scr.shape[2]), F32)
+    rows = own_ref.shape[0]
+    total = jnp.zeros((2 * rows, w_scr.shape[2]), F32)
+    low = jnp.zeros((t_scr.shape[1] - 2 * rows, t_scr.shape[2]), F32)
     for j in range(n):
         for c in copies[j]:
             c.wait()
-        total = total + mm(t_scr[j], w_scr[j], NN)
-    rows = own_ref.shape[0]
+        total = total + mm(t_scr[j, pl.ds(0, 2 * rows)], w_scr[j], NN)
+        low = low + t_scr[j, pl.ds(2 * rows, low.shape[0])].astype(F32)
     own_ref[...] = total[:rows]
     other_ref[...] = total[rows:]
+    low = low[:low.shape[0] // 2] + low[low.shape[0] // 2:]
+    low_ref[...] = unfold(low, low_ref.shape[1]).astype(BF)
 
 
 def attend_kernel(
     lengths_ref, own_ref, got_ref, low_ref, upk_ref, upv_ref, q_ref, p_ref,
-    pack_ref, low_half_ref, gk_ref, gv_ref, q_scr, p_scr, sem,
+    pack_ref, gk_ref, gv_ref, q_scr, p_scr, sem,
 ):
     rows = own_ref.shape[0]
     heads = q_ref.shape[1] // HD
@@ -109,11 +114,7 @@
         c.start()
     score_scale = HD ** (-0.5)
     probe_scale = (q_ref.shape[1] * pack_ref.shape[0]) ** (-0.5)
-    low_sum = low_ref[0].astype(F32)
-    for i in range(1, low_ref.shape[0]):
-        low_sum = low_sum + low_ref[i].astype(F32)
-    low_half = unfold(low_sum).astype(BF)
-    low_half_ref[...] = low_half
+    low_half = low_ref[...]
     full = own_ref[...] + got_ref[...]
     key_full, value_full = full[:, :HD], full[:, HD:]
     key_pol = (key_full + mm(low_half, upk_ref[...], NN)).astype(BF)
@@ -158,7 +159,7 @@
     gk_ref[...] = gk
     gv_ref[...] = gv
     back = mm(gk.astype(BF), upk_ref[...], NT) + mm(gv.astype(BF), upv_ref[...], NT)
-    back = fold(back).astype(BF)
+    back = fold(back, 64).astype(BF)
     first = gap.astype(BF).astype(F32)
     second = (gap - first).astype(BF).astype(F32)
     third = gap - first - second
@@ -180,7 +181,7 @@
     same = doc_ids(lengths_ref, 0, rows, docs) == doc_ids(lengths_ref, 1, rows, docs)
     token_gap = jnp.sum(jnp.where(same, gap, 0.0), axis=1, keepdims=True)
     weight = 2.0 * jax.nn.sigmoid(npo_beta * token_gap)
-    back_half = (unfold(total[:64]) * weight).astype(BF)
+    back_half = (unfold(total[:64], 64) * weight).astype(BF)
     down = mm(back_half, t_ref[...], TN).astype(BF)
     both = jnp.concatenate([gk_ref[...] * weight, gv_ref[...] * weight], axis=1).astype(BF)
     up = mm(low_half_ref[...], both, TN).astype(BF)
@@ -231,7 +232,8 @@
 
     sites = [(y, x, core) for y in range(8) for x in range(4) for core in range(2)]
     swap = [(place(y, x, c), place(y, x, 1 - c)) for y, x, c in sites]
-    orbit = [(place(y, x, c), place(y + 1 - 2 * c, x, c)) for y, x, c in sites]
+    fore = [(place(y, x, c), place(y + 1 - 2 * c, x, c)) for y, x, c in sites]
+    aft = [(b, a) for a, b in fore]
     y_lines = [[place(y, x, c) for y in range(8)] for x in range(4) for c in range(2)]
     squares = [[place(y, x, c) for x in range(4) for c in range(2)] for y in range(8)]
     x_lines = [[place(y, x, c) for x in range(4)] for y in range(8) for c in range(2)]
@@ -242,7 +244,10 @@
         scratch=[pltpu.SemaphoreType.DMA((feats // 256,))],
     )
     swapped = lax.ppermute(theirs, "row", swap)
-    pair = jnp.concatenate([mine, swapped], axis=0)
+    (low_part,) = call(
+        low_kernel, [((16, feats // 2), BF)], [VMEM, VMEM], [VMEM], tokens, down_proj.T
+    )
+    pair = jnp.concatenate([mine, swapped, low_part], axis=0)
     all_tokens = lax.all_gather(pair, "col", axis=0)
 
     w_both = jnp.concatenate([w_key, w_value], axis=1)
@@ -250,39 +255,37 @@
     w_line = lax.all_to_all(
         jnp.broadcast_to(w_both, (4,) + w_both.shape), "row", 0, 0, axis_index_groups=x_lines
     )
-    w_parts = []
-    for i in range(2):
-        w_chain = w_line[2 * i:2 * i + 2].reshape(feats // 4, wide)
-        w_parts.append(w_chain)
-        for _ in range(7):
-            w_chain = lax.ppermute(w_chain, "row", orbit)
-            w_parts.append(w_chain)
-
-    (low_pack,) = call(
-        low_kernel, [((8, rows // 2, 128), BF)], [VMEM, VMEM], [VMEM], tokens, down_proj.T
-    )
-    low_parts = lax.all_to_all(low_pack, "col", 0, 0)
-
-    own, other = call(
+    w_own = w_line.reshape(feats // 2, wide)
+    fore_going, aft_going = [w_own], [w_own]
+    for _ in range(3):
+        fore_going.append(lax.ppermute(fore_going[-1], "row", fore))
+        aft_going.append(lax.ppermute(aft_going[-1], "row", aft))
+    middle = feats // 4
+    w_parts = fore_going + aft_going[1:] + [
+        lax.ppermute(fore_going[3][:middle], "row", fore),
+        lax.ppermute(aft_going[3][middle:], "row", aft),
+    ]
+
+    own, other, low_half = call(
         project_kernel,
-        [((rows, wide), F32)] * 2,
-        [SMEM] + [HBM] * 17,
-        [VMEM, VMEM],
+        [((rows, wide), F32), ((rows, wide), F32), ((rows, 64), BF)],
+        [SMEM] + [HBM] * 10,
+        [VMEM] * 3,
         pos, all_tokens, *w_parts,
         scratch=[
-            pltpu.VMEM((8, 2 * rows, feats // 2), BF),
+            pltpu.VMEM((8, 2 * rows + 16, feats // 2), BF),
             pltpu.VMEM((8, feats // 2, wide), BF),
             pltpu.SemaphoreType.DMA((24,)),
         ],
         mib=56,
     )
     got = lax.ppermute(other, "row", swap)
-    pack, low_half, gk, gv = call(
+    pack, gk, gv = call(
         attend_kernel,
-        [((8, 80, 128), BF), ((rows, 64), BF), ((rows, HD), F32), ((rows, HD), F32)],
+        [((8, 80, 128), BF), ((rows, HD), F32), ((rows, HD), F32)],
         [SMEM] + [VMEM] * 5 + [HBM] * 2,
-        [VMEM] * 4,
-        lengths, own, got, low_parts, up_key, up_value, queries, probes,
+        [VMEM] * 3,
+        lengths, own, got, low_half, up_key, up_value, queries, probes,
         scratch=[
             pltpu.VMEM((rows, feats), BF),
             pltpu.VMEM((rows, feats), BF),

time: 185 us -> 177 us (0.957)
  starting transfers between devices: 73.5 us -> 40.6 us
  waiting for transfers between devices: 9.54 us -> 35.5 us
    ppermute x14 -> x8, waiting for transfers between devices: 7.19 us -> 34.3 us  [the longest x3 17.3 us: on_device(): fore_going.append(lax.ppermute(fore_going[-1], 'row', fore))]
    ppermute x14 -> x8, starting transfers between devices: 49.3 us -> 24.6 us  [the longest x3 11.1 us: on_device(): fore_going.append(lax.ppermute(fore_going[-1], 'row', fore))]
    all_to_all x1 -> x0, starting transfers between devices: 8.46 us -> none  [on_device(): low_parts = lax.all_to_all(low_pack, 'col', 0, 0)]
    all_to_all x1, blocking collectives: 17.3 us -> 13.5 us  [on_device(): lax.all_to_all(square, 'row', 0, 0, axis_index_groups=y_lines)]
    all_to_all x1, blocking collectives: 15.3 us -> 18.1 us  [on_device(): packs = lax.all_to_all(pack, 'col', 0, 0)]
    unnamed x44 -> x42, local copies, waits for them, and re-layouts: 2.03 us -> 3.72 us
  transfers between devices with their start and end apart: 18 -> 11, of which waited for: 8 -> 8; matrix products, arithmetic and copies ran while one was open for 1% -> 0% of each run, Pallas kernels for 4% -> 0%
where the time goes in v3:
time: 177 us; the launch traced here: 176 us
  blocking collectives  67.1 us (38%)
  starting transfers between devices  40.6 us (23%)
  waiting for transfers between devices  35.5 us (20%)
  between operations  14.4 us (8%)
  Pallas kernels  14 us (8%)
  local copies, waits for them, and re-layouts  3.79 us (2%)
    all_to_all x1, blocking collectives, on_device(): packs = lax.all_to_all(pack, 'col', 0, 0)  18.1 us
    ppermute x3, waiting for transfers between devices, on_device(): fore_going.append(lax.ppermute(fore_going[-1], 'row', fore))  17.3 us
    pallas_call x8, Pallas kernels, call(): pl.pallas_call(kernel, out_shape=[jax.ShapeDtypeStruct(s, d) for s, d in...  14 us
    all_to_all x1, blocking collectives, on_device(): lax.all_to_all(square, 'row', 0, 0, axis_index_groups=y_lines)  13.5 us
    all_to_all x1, blocking collectives, on_device(): pieces = lax.all_to_all(summed, 'row', 0, 0, axis_index_groups=squares)  12.2 us
    ppermute x3, waiting for transfers between devices, on_device(): aft_going.append(lax.ppermute(aft_going[-1], 'row', aft))  11.9 us
    all_to_all x1, blocking collectives, on_device(): term_parts = lax.all_to_all(terms, 'row', 0, 0, axis_index_groups=squares)  11.8 us
    all_to_all x1, blocking collectives, on_device(): lax.all_to_all(jnp.broadcast_to(w_both, (4,) + w_both.shape), 'row', 0, 0...  11.6 us
  transfers between devices with their start and end apart: 11, of which 8 were waited for; matrix products, arithmetic and copies ran while one was open for 0% of the time, Pallas kernels for 0%

profile of v3, /device:TPU:1, one launch (start us, length us, event | category | flops | bytes accessed | tf_op | source)
XLA Modules:
  0.0 176.4 jit_solution(5996033984796988224)
XLA Ops:
  7.2 0.0 all-gather.3.cloned.1.call-start
  7.2 0.1 pad_add_fusion.pos_ref
  7.3 1.0 copy-done
  8.3 0.7 shard_map.112
  9.1 8.8 %collective-permute-start = (bf16[128,1024]{1,0:T(8,128)(2,1)S(1)}, bf16[128,1024]{1,0:T(8,128)(2,1)S(1)}, u32[]{:S(2)}, u32[]{:S(2)}) collective-permute-start(bf16[128,1024]{1,0:T(8,128)(2,1)S(1)} %get-tuple-element.15), channel_id=1, source_target_pairs={{0,8},{8,0},{16,24},{24,16},{32,40},{40,32},{48,56},{56,48},{64,72... | collective-permute-start | bytes 786440 | tf_op jit(solution)/shard_map/ppermute | solution.py:246
  17.9 0.0 copy-start.4
  17.9 0.9 copy-done.4
  18.8 0.4 shard_map.113
  19.2 0.0 collective-permute-done
  19.2 0.8 pad_maximum_fusion
  20.0 0.0 all-gather.3.cloned.1.call-update
  20.1 0.0 copy-done.19
  20.1 0.0 copy-done.20
  20.1 11.6 %all_to_all.25 = bf16[4,256,256]{2,1,0:T(8,128)(2,1)S(1)} all-to-all(bf16[4,256,256]{2,1,0:T(8,128)(2,1)S(1)} %broadcast_in_dim.3), channel_id=1, replica_groups={{0,16,32,48},{8,24,40,56},{64,80,96,112},{72,88,104,120},{128,144,160,1..., dimensions={0} | all-to-all | bytes 1048576 | tf_op jit(solution)/shard_map/all_to_all | solution.py:255
  31.8 1.9 %collective-permute-start.4 = (bf16[1024,256]{1,0:T(8,128)(2,1)S(1)}, bf16[1024,256]{1,0:T(8,128)(2,1)S(1)}, u32[]{:S(2)}, u32[]{:S(2)}) collective-permute-start(bf16[1024,256]{1,0:T(8,128)(2,1)S(1)} %bitcast.8), channel_id=1, source_target_pairs={{64,0},{456,8},{80,16},{472,24},{96,32},{488,40},{112,48},{504,56}... | collective-permute-start | bytes 1572872 | tf_op jit(solution)/shard_map/ppermute | solution.py:262
  33.7 4.6 %collective-permute-start.1 = (bf16[1024,256]{1,0:T(8,128)(2,1)S(1)}, bf16[1024,256]{1,0:T(8,128)(2,1)S(1)}, u32[]{:S(2)}, u32[]{:S(2)}) collective-permute-start(bf16[1024,256]{1,0:T(8,128)(2,1)S(1)} %bitcast.9), channel_id=1, source_target_pairs={{0,64},{8,456},{16,80},{24,472},{32,96},{40,488},{48,112},{56,504}... | collective-permute-start | bytes 1572872 | tf_op jit(solution)/shard_map/ppermute | solution.py:261
  38.3 7.0 %collective-permute-done.4.refs_4_ = bf16[1024,256]{1,0:T(8,128)(2,1)S(1)} collective-permute-done((bf16[1024,256]{1,0:T(8,128)(2,1)S(1)}, bf16[1024,256]{1,0:T(8,128)(2,1)S(1)}, u32[]{:S(2)}, u32[]{:S(2)}) %collective-permute-start.4) | collective-permute-done | bytes 524320 | tf_op jit(solution)/shard_map/ppermute | solution.py:262
  45.3 1.9 %collective-permute-start.5 = (bf16[1024,256]{1,0:T(8,128)(2,1)S(1)}, bf16[1024,256]{1,0:T(8,128)(2,1)S(1)}, u32[]{:S(2)}, u32[]{:S(2)}) collective-permute-start(bf16[1024,256]{1,0:T(8,128)(2,1)S(1)} %collective-permute-done.4.refs_4_), channel_id=1, source_target_pairs={{64,0},{456,8},{80,16},{472,24},{96,32},{488,40},{112,48},{504,56}... | collective-permute-start | bytes 1572872 | tf_op jit(solution)/shard_map/ppermute | solution.py:262
  47.2 2.2 %collective-permute-done.1.refs_1_ = bf16[1024,256]{1,0:T(8,128)(2,1)S(1)} collective-permute-done((bf16[1024,256]{1,0:T(8,128)(2,1)S(1)}, bf16[1024,256]{1,0:T(8,128)(2,1)S(1)}, u32[]{:S(2)}, u32[]{:S(2)}) %collective-permute-start.1) | collective-permute-done | bytes 524320 | tf_op jit(solution)/shard_map/ppermute | solution.py:261
  49.4 2.8 %collective-permute-start.2 = (bf16[1024,256]{1,0:T(8,128)(2,1)S(1)}, bf16[1024,256]{1,0:T(8,128)(2,1)S(1)}, u32[]{:S(2)}, u32[]{:S(2)}) collective-permute-start(bf16[1024,256]{1,0:T(8,128)(2,1)S(1)} %collective-permute-done.1.refs_1_), channel_id=1, source_target_pairs={{0,64},{8,456},{16,80},{24,472},{32,96},{40,488},{48,112},{56,504}... | collective-permute-start | bytes 1572872 | tf_op jit(solution)/shard_map/ppermute | solution.py:261
  52.2 4.6 %collective-permute-done.5.refs_5_ = bf16[1024,256]{1,0:T(8,128)(2,1)S(1)} collective-permute-done((bf16[1024,256]{1,0:T(8,128)(2,1)S(1)}, bf16[1024,256]{1,0:T(8,128)(2,1)S(1)}, u32[]{:S(2)}, u32[]{:S(2)}) %collective-permute-start.5) | collective-permute-done | bytes 524320 | tf_op jit(solution)/shard_map/ppermute | solution.py:262
  56.8 1.9 %collective-permute-start.6 = (bf16[1024,256]{1,0:T(8,128)(2,1)S(1)}, bf16[1024,256]{1,0:T(8,128)(2,1)S(1)}, u32[]{:S(2)}, u32[]{:S(2)}) collective-permute-start(bf16[1024,256]{1,0:T(8,128)(2,1)S(1)} %collective-permute-done.5.refs_5_), channel_id=1, source_target_pairs={{64,0},{456,8},{80,16},{472,24},{96,32},{488,40},{112,48},{504,56}... | collective-permute-start | bytes 1572872 | tf_op jit(solution)/shard_map/ppermute | solution.py:262
  58.7 6.2 %collective-permute-done.2.refs_2_ = bf16[1024,256]{1,0:T(8,128)(2,1)S(1)} collective-permute-done((bf16[1024,256]{1,0:T(8,128)(2,1)S(1)}, bf16[1024,256]{1,0:T(8,128)(2,1)S(1)}, u32[]{:S(2)}, u32[]{:S(2)}) %collective-permute-start.2) | collective-permute-done | bytes 524320 | tf_op jit(solution)/shard_map/ppermute | solution.py:261
  64.9 3.7 %collective-permute-start.3 = (bf16[1024,256]{1,0:T(8,128)(2,1)S(1)}, bf16[1024,256]{1,0:T(8,128)(2,1)S(1)}, u32[]{:S(2)}, u32[]{:S(2)}) collective-permute-start(bf16[1024,256]{1,0:T(8,128)(2,1)S(1)} %collective-permute-done.2.refs_2_), channel_id=1, source_target_pairs={{0,64},{8,456},{16,80},{24,472},{32,96},{40,488},{48,112},{56,504}... | collective-permute-start | bytes 1572872 | tf_op jit(solution)/shard_map/ppermute | solution.py:261
  68.6 0.3 collective-permute-done.6.refs_6_
  69.0 2.4 %collective-permute-start.8 = (bf16[512,256]{1,0:T(8,128)(2,1)S(1)}, bf16[512,256]{1,0:T(8,128)(2,1)S(1)}, u32[]{:S(2)}, u32[]{:S(2)}) collective-permute-start(bf16[512,256]{1,0:T(8,128)(2,1)S(1)} %slice.9), channel_id=1, source_target_pairs={{64,0},{456,8},{80,16},{472,24},{96,32},{488,40},{112,48},{504,56}... | collective-permute-start | bytes 786440 | tf_op jit(solution)/shard_map/ppermute | solution.py:266
  71.4 8.9 %collective-permute-done.3.refs_3_ = bf16[1024,256]{1,0:T(8,128)(2,1)S(1)} collective-permute-done((bf16[1024,256]{1,0:T(8,128)(2,1)S(1)}, bf16[1024,256]{1,0:T(8,128)(2,1)S(1)}, u32[]{:S(2)}, u32[]{:S(2)}) %collective-permute-start.3) | collective-permute-done | bytes 524320 | tf_op jit(solution)/shard_map/ppermute | solution.py:261
  80.3 5.3 %collective-permute-start.7 = (bf16[512,256]{1,0:T(8,128)(2,1)S(1)}, bf16[512,256]{1,0:T(8,128)(2,1)}, u32[]{:S(2)}, u32[]{:S(2)}) collective-permute-start(bf16[512,256]{1,0:T(8,128)(2,1)S(1)} %slice.8), channel_id=1, source_target_pairs={{0,64},{8,456},{16,80},{24,472},{32,96},{40,488},{48,112},{56,504}... | collective-permute-start | bytes 786440 | tf_op jit(solution)/shard_map/ppermute | solution.py:265
  85.7 0.0 collective-permute-done.8.refs_8_
  85.7 5.2 %collective-permute-done.7.refs_7_ = bf16[512,256]{1,0:T(8,128)(2,1)} collective-permute-done((bf16[512,256]{1,0:T(8,128)(2,1)S(1)}, bf16[512,256]{1,0:T(8,128)(2,1)}, u32[]{:S(2)}, u32[]{:S(2)}) %collective-permute-start.7) | collective-permute-done | bytes 262176 | tf_op jit(solution)/shard_map/ppermute | solution.py:265
  90.9 0.0 copy-start.2
  90.9 0.0 copy-start.3
  90.9 0.0 copy-start.7
  91.0 0.0 copy-start.8
  91.0 0.0 copy-start.9
  91.0 5.9 %shard_map.114 = (f32[128,256]{1,0:T(8,128)}, f32[128,256]{1,0:T(8,128)}, bf16[128,64]{1,0:T(8,128)(2,1)}) custom-call(s32[2]{0:T(128)} %copy-done.10, bf16[8,272,1024]{2,1,0:T(8,128)(2,1)} %bitcast.7, bf16[1024,256]{1,0:T(8,128)(2,1)} %bitcast.10, bf16[1024,256]{1,0:T(8,128)(2,1)} %copy-done.15, bf16[1024,256]{1,0:T(8,128)(2,1)} %copy-done.17, ...), custom_call_target="tpu_custom_call" | custom-call | tf_op jit(solution)/shard_map/pallas_call | solution.py:215
  96.9 0.0 copy-start.1
  96.9 7.2 %collective-permute-start.9 = (f32[128,256]{1,0:T(8,128)}, f32[128,256]{1,0:T(8,128)S(1)}, u32[]{:S(2)}, u32[]{:S(2)}) collective-permute-start(f32[128,256]{1,0:T(8,128)} %get-tuple-element.17), channel_id=1, source_target_pairs={{0,8},{8,0},{16,24},{24,16},{32,40},{40,32},{48,56},{56,48},{64,72... | collective-permute-start | bytes 393224 | tf_op jit(solution)/shard_map/ppermute | solution.py:282
  104.1 1.2 collective-permute-done.9.got_ref
  105.3 0.9 copy-done.5
  106.2 0.8 copy-done.6
  106.9 5.2 %shard_map.115 = (bf16[8,80,128]{2,1,0:T(8,128)(2,1)S(1)}, f32[128,128]{1,0:T(8,128)S(1)}, f32[128,128]{1,0:T(8,128)S(1)}) custom-call(s32[1,8]{1,0:T(1,128)S(1)} %copy-done.9, f32[128,256]{1,0:T(8,128)S(1)} %copy-done.5, f32[128,256]{1,0:T(8,128)S(1)} %collective-permute-done.9.got_ref, bf16[128,64]{1,0:T(8,128)(2,1)S(1)} %copy-done.6, ...), custom_call_target="tpu_custom_call" | custom-call | tf_op jit(solution)/shard_map/pallas_call | solution.py:215
  112.1 18.1 %all_to_all.26.pack_ref = bf16[8,80,128]{2,1,0:T(8,128)(2,1)S(1)} all-to-all(bf16[8,80,128]{2,1,0:T(8,128)(2,1)S(1)} %get-tuple-element.19), channel_id=1, replica_groups=mesh['row'=64,'col'=8] {'col'}, dimensions={0} | all-to-all | bytes 327680 | tf_op jit(solution)/shard_map/all_to_all | solution.py:295
  130.2 0.9 shard_map.116
  131.1 11.8 %all_to_all.27.in_ref = bf16[8,72,256]{2,1,0:T(8,128)(2,1)S(1)} all-to-all(bf16[8,72,256]{2,1,0:T(8,128)(2,1)S(1)} %shard_map.116), channel_id=1, replica_groups={{0,8,16,24,32,40,48,56},{64,72,80,88,96,104,112,120},{128,136,144,152,1..., dimensions={0} | all-to-all | bytes 589824 | tf_op jit(solution)/shard_map/all_to_all | solution.py:301
  143.0 13.5 %all_to_all.28.in_ref = bf16[8,72,256]{2,1,0:T(8,128)(2,1)S(1)} all-to-all(bf16[8,72,256]{2,1,0:T(8,128)(2,1)S(1)} %shard_map.117), channel_id=1, replica_groups={{0,64,128,192,256,320,384,448},{8,72,136,200,264,328,392,456},{16,80,14..., dimensions={0} | all-to-all | bytes 589824 | tf_op jit(solution)/shard_map/all_to_all | solution.py:303
  156.5 12.2 %all_to_all.29.in_ref = bf16[8,72,256]{2,1,0:T(8,128)(2,1)S(1)} all-to-all(bf16[8,72,256]{2,1,0:T(8,128)(2,1)S(1)} %shard_map.118), channel_id=1, replica_groups={{0,8,16,24,32,40,48,56},{64,72,80,88,96,104,112,120},{128,136,144,152,1..., dimensions={0} | all-to-all | bytes 589824 | tf_op jit(solution)/shard_map/all_to_all | solution.py:305
  168.7 0.8 shard_map.119
  (36 shorter events, 0.2 us)
Async XLA Ops:
  7.2 83.7 %all-gather.3.cloned.1.call-start = ((), (), s32[]{:S(2)}) async-start(), calls=%async_computation.5 | async-start | bytes 5013504 | tf_op jit(solution)/shard_map/all_gather | solution.py:251
  7.3 1.0 copy-start
  8.3 11.7 %copy-start.10 = (s32[2]{0:T(128)}, s32[2]{0:T(128)S(1)}, u32[]{:S(2)}) copy-start(s32[2]{0:T(128)S(1)} %pad_add_fusion.pos_ref) | copy-start | bytes 28
  9.1 10.1 %collective-permute-start = (bf16[128,1024]{1,0:T(8,128)(2,1)S(1)}, bf16[128,1024]{1,0:T(8,128)(2,1)S(1)}, u32[]{:S(2)}, u32[]{:S(2)}) collective-permute-start(bf16[128,1024]{1,0:T(8,128)(2,1)S(1)} %get-tuple-element.15), channel_id=1, source_target_pairs={{0,8},{8,0},{16,24},{24,16},{32,40},{40,32},{48,56},{56,48},{64,72... | collective-permute-start | bytes 786440 | tf_op jit(solution)/shard_map/ppermute | solution.py:246
  17.9 1.0 copy-start.4
  18.8 1.2 copy-start.19
  18.8 1.2 copy-start.20
  31.8 59.1 %copy-start.11 = (bf16[4,256,256]{2,1,0:T(8,128)(2,1)}, bf16[4,256,256]{2,1,0:T(8,128)(2,1)S(1)}, u32[]{:S(2)}) copy-start(bf16[4,256,256]{2,1,0:T(8,128)(2,1)S(1)} %all_to_all.25) | copy-start | bytes 1572868
  31.8 13.5 %collective-permute-start.4 = (bf16[1024,256]{1,0:T(8,128)(2,1)S(1)}, bf16[1024,256]{1,0:T(8,128)(2,1)S(1)}, u32[]{:S(2)}, u32[]{:S(2)}) collective-permute-start(bf16[1024,256]{1,0:T(8,128)(2,1)S(1)} %bitcast.8), channel_id=1, source_target_pairs={{64,0},{456,8},{80,16},{472,24},{96,32},{488,40},{112,48},{504,56}... | collective-permute-start | bytes 1572872 | tf_op jit(solution)/shard_map/ppermute | solution.py:262
  33.7 15.7 %collective-permute-start.1 = (bf16[1024,256]{1,0:T(8,128)(2,1)S(1)}, bf16[1024,256]{1,0:T(8,128)(2,1)S(1)}, u32[]{:S(2)}, u32[]{:S(2)}) collective-permute-start(bf16[1024,256]{1,0:T(8,128)(2,1)S(1)} %bitcast.9), channel_id=1, source_target_pairs={{0,64},{8,456},{16,80},{24,472},{32,96},{40,488},{48,112},{56,504}... | collective-permute-start | bytes 1572872 | tf_op jit(solution)/shard_map/ppermute | solution.py:261
  45.3 45.6 %copy-start.14 = (bf16[1024,256]{1,0:T(8,128)(2,1)}, bf16[1024,256]{1,0:T(8,128)(2,1)S(1)}, u32[]{:S(2)}) copy-start(bf16[1024,256]{1,0:T(8,128)(2,1)S(1)} %collective-permute-done.4.refs_4_) | copy-start | bytes 1572868
  45.3 11.5 %collective-permute-start.5 = (bf16[1024,256]{1,0:T(8,128)(2,1)S(1)}, bf16[1024,256]{1,0:T(8,128)(2,1)S(1)}, u32[]{:S(2)}, u32[]{:S(2)}) collective-permute-start(bf16[1024,256]{1,0:T(8,128)(2,1)S(1)} %collective-permute-done.4.refs_4_), channel_id=1, source_target_pairs={{64,0},{456,8},{80,16},{472,24},{96,32},{488,40},{112,48},{504,56}... | collective-permute-start | bytes 1572872 | tf_op jit(solution)/shard_map/ppermute | solution.py:262
  49.4 41.5 %copy-start.15 = (bf16[1024,256]{1,0:T(8,128)(2,1)}, bf16[1024,256]{1,0:T(8,128)(2,1)S(1)}, u32[]{:S(2)}) copy-start(bf16[1024,256]{1,0:T(8,128)(2,1)S(1)} %collective-permute-done.1.refs_1_) | copy-start | bytes 1572868
  49.4 15.5 %collective-permute-start.2 = (bf16[1024,256]{1,0:T(8,128)(2,1)S(1)}, bf16[1024,256]{1,0:T(8,128)(2,1)S(1)}, u32[]{:S(2)}, u32[]{:S(2)}) collective-permute-start(bf16[1024,256]{1,0:T(8,128)(2,1)S(1)} %collective-permute-done.1.refs_1_), channel_id=1, source_target_pairs={{0,64},{8,456},{16,80},{24,472},{32,96},{40,488},{48,112},{56,504}... | collective-permute-start | bytes 1572872 | tf_op jit(solution)/shard_map/ppermute | solution.py:261
  56.8 34.1 %copy-start.16 = (bf16[1024,256]{1,0:T(8,128)(2,1)}, bf16[1024,256]{1,0:T(8,128)(2,1)S(1)}, u32[]{:S(2)}) copy-start(bf16[1024,256]{1,0:T(8,128)(2,1)S(1)} %collective-permute-done.5.refs_5_) | copy-start | bytes 1572868
  56.8 12.2 %collective-permute-start.6 = (bf16[1024,256]{1,0:T(8,128)(2,1)S(1)}, bf16[1024,256]{1,0:T(8,128)(2,1)S(1)}, u32[]{:S(2)}, u32[]{:S(2)}) collective-permute-start(bf16[1024,256]{1,0:T(8,128)(2,1)S(1)} %collective-permute-done.5.refs_5_), channel_id=1, source_target_pairs={{64,0},{456,8},{80,16},{472,24},{96,32},{488,40},{112,48},{504,56}... | collective-permute-start | bytes 1572872 | tf_op jit(solution)/shard_map/ppermute | solution.py:262
  64.9 15.4 %copy-start.17 = (bf16[1024,256]{1,0:T(8,128)(2,1)}, bf16[1024,256]{1,0:T(8,128)(2,1)S(1)}, u32[]{:S(2)}) copy-start(bf16[1024,256]{1,0:T(8,128)(2,1)S(1)} %collective-permute-done.2.refs_2_) | copy-start | bytes 1572868
  64.9 15.4 %collective-permute-start.3 = (bf16[1024,256]{1,0:T(8,128)(2,1)S(1)}, bf16[1024,256]{1,0:T(8,128)(2,1)S(1)}, u32[]{:S(2)}, u32[]{:S(2)}) collective-permute-start(bf16[1024,256]{1,0:T(8,128)(2,1)S(1)} %collective-permute-done.2.refs_2_), channel_id=1, source_target_pairs={{0,64},{8,456},{16,80},{24,472},{32,96},{40,488},{48,112},{56,504}... | collective-permute-start | bytes 1572872 | tf_op jit(solution)/shard_map/ppermute | solution.py:261
  68.9 21.9 %copy-start.12 = (bf16[1024,256]{1,0:T(8,128)(2,1)}, bf16[1024,256]{1,0:T(8,128)(2,1)S(1)}, u32[]{:S(2)}) copy-start(bf16[1024,256]{1,0:T(8,128)(2,1)S(1)} %collective-permute-done.6.refs_6_) | copy-start | bytes 1572868
  69.0 16.7 %collective-permute-start.8 = (bf16[512,256]{1,0:T(8,128)(2,1)S(1)}, bf16[512,256]{1,0:T(8,128)(2,1)S(1)}, u32[]{:S(2)}, u32[]{:S(2)}) collective-permute-start(bf16[512,256]{1,0:T(8,128)(2,1)S(1)} %slice.9), channel_id=1, source_target_pairs={{64,0},{456,8},{80,16},{472,24},{96,32},{488,40},{112,48},{504,56}... | collective-permute-start | bytes 786440 | tf_op jit(solution)/shard_map/ppermute | solution.py:266
  80.3 10.6 %copy-start.13 = (bf16[1024,256]{1,0:T(8,128)(2,1)}, bf16[1024,256]{1,0:T(8,128)(2,1)S(1)}, u32[]{:S(2)}) copy-start(bf16[1024,256]{1,0:T(8,128)(2,1)S(1)} %collective-permute-done.3.refs_3_) | copy-start | bytes 1572868
  80.3 10.5 %collective-permute-start.7 = (bf16[512,256]{1,0:T(8,128)(2,1)S(1)}, bf16[512,256]{1,0:T(8,128)(2,1)}, u32[]{:S(2)}, u32[]{:S(2)}) collective-permute-start(bf16[512,256]{1,0:T(8,128)(2,1)S(1)} %slice.8), channel_id=1, source_target_pairs={{0,64},{8,456},{16,80},{24,472},{32,96},{40,488},{48,112},{56,504}... | collective-permute-start | bytes 786440 | tf_op jit(solution)/shard_map/ppermute | solution.py:265
  85.7 5.2 %copy-start.18 = (bf16[512,256]{1,0:T(8,128)(2,1)}, bf16[512,256]{1,0:T(8,128)(2,1)S(1)}, u32[]{:S(2)}) copy-start(bf16[512,256]{1,0:T(8,128)(2,1)S(1)} %collective-permute-done.8.refs_8_) | copy-start | bytes 786436
  90.9 14.3 %copy-start.2 = (bf16[128,2048]{1,0:T(8,128)(2,1)S(1)}, bf16[128,2048]{1,0:T(8,128)(2,1)}, u32[]{:S(2)}) copy-start(bf16[128,2048]{1,0:T(8,128)(2,1)} %q_ref.1) | copy-start | bytes 1572868
  90.9 14.3 %copy-start.3 = (bf16[128,2048]{1,0:T(8,128)(2,1)S(1)}, bf16[128,2048]{1,0:T(8,128)(2,1)}, u32[]{:S(2)}) copy-start(bf16[128,2048]{1,0:T(8,128)(2,1)} %p_ref.1) | copy-start | bytes 1572868
  90.9 14.3 %copy-start.7 = (bf16[64,128]{1,0:T(8,128)(2,1)S(1)}, bf16[64,128]{1,0:T(8,128)(2,1)}, u32[]{:S(2)}) copy-start(bf16[64,128]{1,0:T(8,128)(2,1)} %upk_ref.1) | copy-start | bytes 49156
  91.0 14.3 %copy-start.8 = (bf16[64,128]{1,0:T(8,128)(2,1)S(1)}, bf16[64,128]{1,0:T(8,128)(2,1)}, u32[]{:S(2)}) copy-start(bf16[64,128]{1,0:T(8,128)(2,1)} %upv_ref.1) | copy-start | bytes 49156
  91.0 14.3 %copy-start.9 = (s32[1,8]{1,0:T(1,128)S(1)}, s32[1,8]{1,0:T(1,128)}, u32[]{:S(2)}) copy-start(s32[1,8]{1,0:T(1,128)} %lengths_ref.3) | copy-start | bytes 100
  96.9 33.3 %copy-start.1 = (bf16[128,2048]{1,0:T(8,128)(2,1)S(1)}, bf16[128,2048]{1,0:T(8,128)(2,1)}, u32[]{:S(2)}) copy-start(bf16[128,2048]{1,0:T(8,128)(2,1)} %t_ref.5) | copy-start | bytes 1572868
  96.9 8.4 %collective-permute-start.9 = (f32[128,256]{1,0:T(8,128)}, f32[128,256]{1,0:T(8,128)S(1)}, u32[]{:S(2)}, u32[]{:S(2)}) collective-permute-start(f32[128,256]{1,0:T(8,128)} %get-tuple-element.17), channel_id=1, source_target_pairs={{0,8},{8,0},{16,24},{24,16},{32,40},{40,32},{48,56},{56,48},{64,72... | collective-permute-start | bytes 393224 | tf_op jit(solution)/shard_map/ppermute | solution.py:282
  105.3 0.9 copy-start.5
  106.2 0.8 copy-start.6
Sparse Core Ops, SparseCore 0:
  20.2 59.5 all-gather.2

commit v4 on v3

--- a/solution.py
+++ b/solution.py
@@ -65,33 +65,49 @@
     out_ref[...] = jnp.concatenate([high, low - high], axis=0).astype(BF)
 
 
-def project_kernel(pos_ref, t_ref, *refs):
-    w_refs, (own_ref, other_ref, low_ref, t_scr, w_scr, sem) = refs[:9], refs[9:]
+STEPS = (0, 1, 2, 3, -1, -2, -3, 4)
+
+
+def ring_of(own, axis, fore, aft, cut):
+    fore_going, aft_going = [own], [own]
+    for _ in range(3):
+        fore_going.append(lax.ppermute(fore_going[-1], axis, fore))
+        aft_going.append(lax.ppermute(aft_going[-1], axis, aft))
+    return fore_going + aft_going[1:] + [
+        lax.ppermute(fore_going[3][:cut], axis, fore),
+        lax.ppermute(aft_going[3][cut:], axis, aft),
+    ]
+
+
+def project_kernel(pos_ref, *refs):
+    t_refs, w_refs, refs = refs[:9], refs[9:18], refs[18:]
+    own_ref, other_ref, low_ref, t_scr, w_scr, sem = refs
     n = t_scr.shape[0]
-    half = w_scr.shape[1] // 2
     way = 2 * pos_ref[0] - 1
     copies = []
-    for j, step in enumerate((0, 1, 2, 3, -1, -2, -3, 4)):
-        k = lax.rem(pos_ref[1] + step * way + n, n)
-        parts = [(t_ref.at[k], t_scr.at[j])]
-        if step == 4:
-            parts.append((w_refs[7], w_scr.at[j, pl.ds(0, half)]))
-            parts.append((w_refs[8], w_scr.at[j, pl.ds(half, half)]))
-        else:
-            parts.append((w_refs[j], w_scr.at[j]))
-        copies.append(
-            [pltpu.make_async_copy(a, b, sem.at[3 * j + i]) for i, (a, b) in enumerate(parts)]
-        )
-        for c in copies[j]:
-            c.start()
+    for at, (parts, scr) in enumerate(((t_refs, t_scr), (w_refs, w_scr))):
+        cut = parts[7].shape[0]
+        for j, step in enumerate(STEPS):
+            k = lax.rem(pos_ref[1 + at] + step * way + n, n)
+            if step == 4:
+                pairs = [
+                    (parts[7], scr.at[k, pl.ds(0, cut)]),
+                    (parts[8], scr.at[k, pl.ds(cut, scr.shape[1] - cut)]),
+                ]
+            else:
+                pairs = [(parts[j], scr.at[k])]
+            for i, (a, b) in enumerate(pairs):
+                copies.append(pltpu.make_async_copy(a, b, sem.at[at, j + i]))
+    for c in copies:
+        c.start()
+    for c in copies:
+        c.wait()
     rows = own_ref.shape[0]
     total = jnp.zeros((2 * rows, w_scr.shape[2]), F32)
     low = jnp.zeros((t_scr.shape[1] - 2 * rows, t_scr.shape[2]), F32)
-    for j in range(n):
-        for c in copies[j]:
-            c.wait()
-        total = total + mm(t_scr[j, pl.ds(0, 2 * rows)], w_scr[j], NN)
-        low = low + t_scr[j, pl.ds(2 * rows, low.shape[0])].astype(F32)
+    for k in range(n):
+        total = total + mm(t_scr[k, pl.ds(0, 2 * rows)], w_scr[k], NN)
+        low = low + t_scr[k, pl.ds(2 * rows, low.shape[0])].astype(F32)
     own_ref[...] = total[:rows]
     other_ref[...] = total[rows:]
     low = low[:low.shape[0] // 2] + low[low.shape[0] // 2:]
@@ -225,15 +241,21 @@
 def on_device(tokens, queries, probes, w_key, w_value, down_proj, up_key, up_value, lengths):
     rows, feats = tokens.shape
     row_at = lax.axis_index("row")
-    pos = jnp.stack([row_at % 2, row_at // 8]).astype(jnp.int32)
+    pos = jnp.stack([row_at % 2, lax.axis_index("col"), row_at // 8]).astype(jnp.int32)
 
     def place(y, x, core):
         return ((y % 8) * 4 + x % 4) * 2 + core % 2
 
     sites = [(y, x, core) for y in range(8) for x in range(4) for core in range(2)]
     swap = [(place(y, x, c), place(y, x, 1 - c)) for y, x, c in sites]
-    fore = [(place(y, x, c), place(y + 1 - 2 * c, x, c)) for y, x, c in sites]
-    aft = [(b, a) for a, b in fore]
+    y_fore = [(place(y, x, c), place(y + 1 - 2 * c, x, c)) for y, x, c in sites]
+    y_aft = [(b, a) for a, b in y_fore]
+    z_fore = [
+        (place(y, x, c) * 8 + z, place(y, x, c) * 8 + (z + 1 - 2 * c) % 8)
+        for y, x, c in sites
+        for z in range(8)
+    ]
+    z_aft = [(b, a) for a, b in z_fore]
     y_lines = [[place(y, x, c) for y in range(8)] for x in range(4) for c in range(2)]
     squares = [[place(y, x, c) for x in range(4) for c in range(2)] for y in range(8)]
     x_lines = [[place(y, x, c) for x in range(4)] for y in range(8) for c in range(2)]
@@ -248,7 +270,7 @@
         low_kernel, [((16, feats // 2), BF)], [VMEM, VMEM], [VMEM], tokens, down_proj.T
     )
     pair = jnp.concatenate([mine, swapped, low_part], axis=0)
-    all_tokens = lax.all_gather(pair, "col", axis=0)
+    t_parts = ring_of(pair, ("row", "col"), z_fore, z_aft, rows)
 
     w_both = jnp.concatenate([w_key, w_value], axis=1)
     wide = w_both.shape[1]
@@ -256,26 +278,18 @@
         jnp.broadcast_to(w_both, (4,) + w_both.shape), "row", 0, 0, axis_index_groups=x_lines
     )
     w_own = w_line.reshape(feats // 2, wide)
-    fore_going, aft_going = [w_own], [w_own]
-    for _ in range(3):
-        fore_going.append(lax.ppermute(fore_going[-1], "row", fore))
-        aft_going.append(lax.ppermute(aft_going[-1], "row", aft))
-    middle = feats // 4
-    w_parts = fore_going + aft_going[1:] + [
-        lax.ppermute(fore_going[3][:middle], "row", fore),
-        lax.ppermute(aft_going[3][middle:], "row", aft),
-    ]
+    w_parts = ring_of(w_own, "row", y_fore, y_aft, feats // 4)
 
     own, other, low_half = call(
         project_kernel,
         [((rows, wide), F32), ((rows, wide), F32), ((rows, 64), BF)],
-        [SMEM] + [HBM] * 10,
+        [SMEM] + [HBM] * 18,
         [VMEM] * 3,
-        pos, all_tokens, *w_parts,
+        pos, *t_parts, *w_parts,
         scratch=[
             pltpu.VMEM((8, 2 * rows + 16, feats // 2), BF),
             pltpu.VMEM((8, feats // 2, wide), BF),
-            pltpu.SemaphoreType.DMA((24,)),
+            pltpu.SemaphoreType.DMA((2, 9)),
         ],
         mib=56,
     )

time: 177 us -> 168 us (0.949)
  starting transfers between devices: 40.6 us -> 77 us
  waiting for transfers between devices: 35.5 us -> 15.2 us
  blocking collectives: 67.1 us -> 53.8 us
  between operations: 14.4 us -> 1.29 us
    ppermute x8 -> x16, starting transfers between devices: 24.6 us -> 57.4 us  [the longest x6 28.6 us: ring_of(): fore_going.append(lax.ppermute(fore_going[-1], axis, fore))]
    ppermute x8 -> x16, waiting for transfers between devices: 34.3 us -> 12.6 us  [the longest x6 6.97 us: ring_of(): fore_going.append(lax.ppermute(fore_going[-1], axis, fore))]
    all_to_all x1 -> x0, blocking collectives: 11.6 us -> none  [on_device(): lax.all_to_all(jnp.broadcast_to(w_both, (4,) + w_both.shape), 'row', 0, 0...]
    all_to_all x1, blocking collectives: 18.1 us -> 12.8 us  [on_device(): packs = lax.all_to_all(pack, 'col', 0, 0)]
    all_to_all x0 -> x1, starting transfers between devices: none -> 3.6 us  [on_device(): lax.all_to_all(jnp.broadcast_to(w_both, (4,) + w_both.shape), 'row', 0, 0...]
    all_to_all x1, blocking collectives: 11.8 us -> 14.1 us  [on_device(): term_parts = lax.all_to_all(terms, 'row', 0, 0, axis_index_groups=squares)]
    unnamed x42 -> x62, local copies, waits for them, and re-layouts: 3.72 us -> 4.14 us
  transfers between devices with their start and end apart: 11 -> 19, of which waited for: 8 -> 7; matrix products, arithmetic and copies ran while one was open for 0% -> 1% of each run, Pallas kernels for 0% -> 0%
where the time goes in v4:
time: 168 us; the launch traced here: 167 us
  starting transfers between devices  77 us (46%)
  blocking collectives  53.8 us (32%)
  waiting for transfers between devices  15.2 us (9%)
  Pallas kernels  14.3 us (9%)
  local copies, waits for them, and re-layouts  5.04 us (3%)
    ppermute x6, starting transfers between devices, ring_of(): fore_going.append(lax.ppermute(fore_going[-1], axis, fore))  28.6 us
    all_to_all x1, blocking collectives, on_device(): lax.all_to_all(square, 'row', 0, 0, axis_index_groups=y_lines)  14.7 us
    pallas_call x8, Pallas kernels, call(): pl.pallas_call(kernel, out_shape=[jax.ShapeDtypeStruct(s, d) for s, d in...  14.3 us
    all_to_all x1, blocking collectives, on_device(): term_parts = lax.all_to_all(terms, 'row', 0, 0, axis_index_groups=squares)  14.1 us
    ppermute x6, starting transfers between devices, ring_of(): aft_going.append(lax.ppermute(aft_going[-1], axis, aft))  14.1 us
    all_to_all x1, blocking collectives, on_device(): packs = lax.all_to_all(pack, 'col', 0, 0)  12.8 us
    all_to_all x1, blocking collectives, on_device(): pieces = lax.all_to_all(summed, 'row', 0, 0, axis_index_groups=squares)  12.2 us
    ppermute x2, starting transfers between devices, ring_of(): lax.ppermute(fore_going[3][:cut], axis, fore)  9.59 us
  transfers between devices with their start and end apart: 19, of which 7 were waited for; matrix products, arithmetic and copies ran while one was open for 1% of the time, Pallas kernels for 0%

profile of v4, /device:TPU:1, one launch (start us, length us, event | category | flops | bytes accessed | tf_op | source)
XLA Modules:
  0.0 166.8 jit_solution(5420755704038187225)
XLA Ops:
  0.7 0.1 pad_add_fusion.pos_ref
  0.7 1.0 copy-done
  1.8 0.7 shard_map.112
  2.5 8.8 %collective-permute-start = (bf16[128,1024]{1,0:T(8,128)(2,1)S(1)}, bf16[128,1024]{1,0:T(8,128)(2,1)S(1)}, u32[]{:S(2)}, u32[]{:S(2)}) collective-permute-start(bf16[128,1024]{1,0:T(8,128)(2,1)S(1)} %get-tuple-element.15), channel_id=1, source_target_pairs={{0,8},{8,0},{16,24},{24,16},{32,40},{40,32},{48,56},{56,48},{64,72... | collective-permute-start | bytes 786440 | tf_op jit(solution)/shard_map/ppermute | solution.py:268
  11.3 0.8 broadcast_in_dim.3
  12.2 3.6 %all-to-all-start = ((bf16[4,256,256]{2,1,0:T(8,128)(2,1)}), bf16[4,256,256]{2,1,0:T(8,128)(2,1)S(1)}, u32[]{:S(2)}, u32[]{:S(2)}) async-start(bf16[4,256,256]{2,1,0:T(8,128)(2,1)} %broadcast_in_dim.3), calls=%async_computation | async-start | bytes 1048576 | tf_op jit(solution)/shard_map/all_to_all | solution.py:277
  15.8 0.4 shard_map.113
  16.2 1.9 %collective-permute-start.4 = (bf16[272,1024]{1,0:T(8,128)(2,1)S(1)}, bf16[272,1024]{1,0:T(8,128)(2,1)S(1)}, u32[]{:S(2)}, u32[]{:S(2)}) collective-permute-start(bf16[272,1024]{1,0:T(8,128)(2,1)S(1)} %pad_maximum_fusion.refs_0_), channel_id=1, source_target_pairs={{1,0},{2,1},{3,2},{4,3},{5,4},{6,5},{7,6},{0,7},{15,8},{8,9},{9,10... | collective-permute-start | bytes 1671176 | tf_op jit(solution)/shard_map/ppermute | solution.py:75
  18.2 5.8 %collective-permute-start.1 = (bf16[272,1024]{1,0:T(8,128)(2,1)S(1)}, bf16[272,1024]{1,0:T(8,128)(2,1)S(1)}, u32[]{:S(2)}, u32[]{:S(2)}) collective-permute-start(bf16[272,1024]{1,0:T(8,128)(2,1)S(1)} %pad_maximum_fusion.refs_0_), channel_id=1, source_target_pairs={{0,1},{1,2},{2,3},{3,4},{4,5},{5,6},{6,7},{7,0},{8,15},{9,8},{10,9... | collective-permute-start | bytes 1671176 | tf_op jit(solution)/shard_map/ppermute | solution.py:74
  24.0 1.4 all-to-all-done
  25.4 1.9 %collective-permute-start.12 = (bf16[1024,256]{1,0:T(8,128)(2,1)S(1)}, bf16[1024,256]{1,0:T(8,128)(2,1)S(1)}, u32[]{:S(2)}, u32[]{:S(2)}) collective-permute-start(bf16[1024,256]{1,0:T(8,128)(2,1)S(1)} %bitcast.7), channel_id=1, source_target_pairs={{64,0},{456,8},{80,16},{472,24},{96,32},{488,40},{112,48},{504,56}... | collective-permute-start | bytes 1572872 | tf_op jit(solution)/shard_map/ppermute | solution.py:75
  27.3 4.6 %collective-permute-start.9 = (bf16[1024,256]{1,0:T(8,128)(2,1)S(1)}, bf16[1024,256]{1,0:T(8,128)(2,1)S(1)}, u32[]{:S(2)}, u32[]{:S(2)}) collective-permute-start(bf16[1024,256]{1,0:T(8,128)(2,1)S(1)} %bitcast.8), channel_id=1, source_target_pairs={{0,64},{8,456},{16,80},{24,472},{32,96},{40,488},{48,112},{56,504}... | collective-permute-start | bytes 1572872 | tf_op jit(solution)/shard_map/ppermute | solution.py:74
  31.9 1.9 %collective-permute-start.5 = (bf16[272,1024]{1,0:T(8,128)(2,1)S(1)}, bf16[272,1024]{1,0:T(8,128)(2,1)S(1)}, u32[]{:S(2)}, u32[]{:S(2)}) collective-permute-start(bf16[272,1024]{1,0:T(8,128)(2,1)S(1)} %collective-permute-done.4.refs_4_), channel_id=1, source_target_pairs={{1,0},{2,1},{3,2},{4,3},{5,4},{6,5},{7,6},{0,7},{15,8},{8,9},{9,10... | collective-permute-start | bytes 1671176 | tf_op jit(solution)/shard_map/ppermute | solution.py:75
  33.8 1.4 collective-permute-done.1.refs_1_
  35.2 5.0 %collective-permute-start.2 = (bf16[272,1024]{1,0:T(8,128)(2,1)S(1)}, bf16[272,1024]{1,0:T(8,128)(2,1)S(1)}, u32[]{:S(2)}, u32[]{:S(2)}) collective-permute-start(bf16[272,1024]{1,0:T(8,128)(2,1)S(1)} %collective-permute-done.1.refs_1_), channel_id=1, source_target_pairs={{0,1},{1,2},{2,3},{3,4},{4,5},{5,6},{6,7},{7,0},{8,15},{9,8},{10,9... | collective-permute-start | bytes 1671176 | tf_op jit(solution)/shard_map/ppermute | solution.py:74
  40.3 3.2 %collective-permute-start.13 = (bf16[1024,256]{1,0:T(8,128)(2,1)S(1)}, bf16[1024,256]{1,0:T(8,128)(2,1)S(1)}, u32[]{:S(2)}, u32[]{:S(2)}) collective-permute-start(bf16[1024,256]{1,0:T(8,128)(2,1)S(1)} %collective-permute-done.12.refs_13_), channel_id=1, source_target_pairs={{64,0},{456,8},{80,16},{472,24},{96,32},{488,40},{112,48},{504,56}... | collective-permute-start | bytes 1572872 | tf_op jit(solution)/shard_map/ppermute | solution.py:75
  43.5 4.1 %collective-permute-start.10 = (bf16[1024,256]{1,0:T(8,128)(2,1)S(1)}, bf16[1024,256]{1,0:T(8,128)(2,1)S(1)}, u32[]{:S(2)}, u32[]{:S(2)}) collective-permute-start(bf16[1024,256]{1,0:T(8,128)(2,1)S(1)} %collective-permute-done.9.refs_10_), channel_id=1, source_target_pairs={{0,64},{8,456},{16,80},{24,472},{32,96},{40,488},{48,112},{56,504}... | collective-permute-start | bytes 1572872 | tf_op jit(solution)/shard_map/ppermute | solution.py:74
  47.6 1.9 %collective-permute-start.6 = (bf16[272,1024]{1,0:T(8,128)(2,1)S(1)}, bf16[272,1024]{1,0:T(8,128)(2,1)S(1)}, u32[]{:S(2)}, u32[]{:S(2)}) collective-permute-start(bf16[272,1024]{1,0:T(8,128)(2,1)S(1)} %collective-permute-done.5.refs_5_), channel_id=1, source_target_pairs={{1,0},{2,1},{3,2},{4,3},{5,4},{6,5},{7,6},{0,7},{15,8},{8,9},{9,10... | collective-permute-start | bytes 1671176 | tf_op jit(solution)/shard_map/ppermute | solution.py:75
  49.6 3.1 %collective-permute-done.2.refs_2_ = bf16[272,1024]{1,0:T(8,128)(2,1)S(1)} collective-permute-done((bf16[272,1024]{1,0:T(8,128)(2,1)S(1)}, bf16[272,1024]{1,0:T(8,128)(2,1)S(1)}, u32[]{:S(2)}, u32[]{:S(2)}) %collective-permute-start.2) | collective-permute-done | bytes 557088 | tf_op jit(solution)/shard_map/ppermute | solution.py:74
  52.7 5.2 %collective-permute-start.3 = (bf16[272,1024]{1,0:T(8,128)(2,1)S(1)}, bf16[272,1024]{1,0:T(8,128)(2,1)S(1)}, u32[]{:S(2)}, u32[]{:S(2)}) collective-permute-start(bf16[272,1024]{1,0:T(8,128)(2,1)S(1)} %collective-permute-done.2.refs_2_), channel_id=1, source_target_pairs={{0,1},{1,2},{2,3},{3,4},{4,5},{5,6},{6,7},{7,0},{8,15},{9,8},{10,9... | collective-permute-start | bytes 1671176 | tf_op jit(solution)/shard_map/ppermute | solution.py:74
  57.9 3.2 %collective-permute-start.14 = (bf16[1024,256]{1,0:T(8,128)(2,1)S(1)}, bf16[1024,256]{1,0:T(8,128)(2,1)S(1)}, u32[]{:S(2)}, u32[]{:S(2)}) collective-permute-start(bf16[1024,256]{1,0:T(8,128)(2,1)S(1)} %collective-permute-done.13.refs_14_), channel_id=1, source_target_pairs={{64,0},{456,8},{80,16},{472,24},{96,32},{488,40},{112,48},{504,56}... | collective-permute-start | bytes 1572872 | tf_op jit(solution)/shard_map/ppermute | solution.py:75
  61.2 3.9 %collective-permute-start.11 = (bf16[1024,256]{1,0:T(8,128)(2,1)S(1)}, bf16[1024,256]{1,0:T(8,128)(2,1)S(1)}, u32[]{:S(2)}, u32[]{:S(2)}) collective-permute-start(bf16[1024,256]{1,0:T(8,128)(2,1)S(1)} %collective-permute-done.10.refs_11_), channel_id=1, source_target_pairs={{0,64},{8,456},{16,80},{24,472},{32,96},{40,488},{48,112},{56,504}... | collective-permute-start | bytes 1572872 | tf_op jit(solution)/shard_map/ppermute | solution.py:74
  65.1 1.9 %collective-permute-start.8 = (bf16[144,1024]{1,0:T(8,128)(2,1)S(1)}, bf16[144,1024]{1,0:T(8,128)(2,1)S(1)}, u32[]{:S(2)}, u32[]{:S(2)}) collective-permute-start(bf16[144,1024]{1,0:T(8,128)(2,1)S(1)} %slice.17), channel_id=1, source_target_pairs={{1,0},{2,1},{3,2},{4,3},{5,4},{6,5},{7,6},{0,7},{15,8},{8,9},{9,10... | collective-permute-start | bytes 884744 | tf_op jit(solution)/shard_map/ppermute | solution.py:78
  67.0 2.5 %collective-permute-done.3.refs_3_ = bf16[272,1024]{1,0:T(8,128)(2,1)S(1)} collective-permute-done((bf16[272,1024]{1,0:T(8,128)(2,1)S(1)}, bf16[272,1024]{1,0:T(8,128)(2,1)S(1)}, u32[]{:S(2)}, u32[]{:S(2)}) %collective-permute-start.3) | collective-permute-done | bytes 557088 | tf_op jit(solution)/shard_map/ppermute | solution.py:74
  69.5 5.3 %collective-permute-start.7 = (bf16[128,1024]{1,0:T(8,128)(2,1)S(1)}, bf16[128,1024]{1,0:T(8,128)(2,1)S(1)}, u32[]{:S(2)}, u32[]{:S(2)}) collective-permute-start(bf16[128,1024]{1,0:T(8,128)(2,1)S(1)} %slice.16), channel_id=1, source_target_pairs={{0,1},{1,2},{2,3},{3,4},{4,5},{5,6},{6,7},{7,0},{8,15},{9,8},{10,9... | collective-permute-start | bytes 786440 | tf_op jit(solution)/shard_map/ppermute | solution.py:77
  74.9 3.2 %collective-permute-start.16 = (bf16[512,256]{1,0:T(8,128)(2,1)S(1)}, bf16[512,256]{1,0:T(8,128)(2,1)S(1)}, u32[]{:S(2)}, u32[]{:S(2)}) collective-permute-start(bf16[512,256]{1,0:T(8,128)(2,1)S(1)} %slice.19), channel_id=1, source_target_pairs={{64,0},{456,8},{80,16},{472,24},{96,32},{488,40},{112,48},{504,56}... | collective-permute-start | bytes 786440 | tf_op jit(solution)/shard_map/ppermute | solution.py:78
  78.2 0.0 copy-start.2
  78.2 0.0 copy-start.3
  78.2 0.0 copy-start.7
  78.2 0.0 copy-start.8
  78.2 0.0 copy-start.10
  78.2 4.3 %collective-permute-start.15 = (bf16[512,256]{1,0:T(8,128)(2,1)S(1)}, bf16[512,256]{1,0:T(8,128)(2,1)S(1)}, u32[]{:S(2)}, u32[]{:S(2)}) collective-permute-start(bf16[512,256]{1,0:T(8,128)(2,1)S(1)} %slice.18), channel_id=1, source_target_pairs={{0,64},{8,456},{16,80},{24,472},{32,96},{40,488},{48,112},{56,504}... | collective-permute-start | bytes 786440 | tf_op jit(solution)/shard_map/ppermute | solution.py:77
  82.5 1.8 %collective-permute-done.16.refs_17_ = bf16[512,256]{1,0:T(8,128)(2,1)S(1)} collective-permute-done((bf16[512,256]{1,0:T(8,128)(2,1)S(1)}, bf16[512,256]{1,0:T(8,128)(2,1)S(1)}, u32[]{:S(2)}, u32[]{:S(2)}) %collective-permute-start.16) | collective-permute-done | bytes 262176 | tf_op jit(solution)/shard_map/ppermute | solution.py:78
  84.4 3.8 %collective-permute-done.15.refs_16_ = bf16[512,256]{1,0:T(8,128)(2,1)S(1)} collective-permute-done((bf16[512,256]{1,0:T(8,128)(2,1)S(1)}, bf16[512,256]{1,0:T(8,128)(2,1)S(1)}, u32[]{:S(2)}, u32[]{:S(2)}) %collective-permute-start.15) | collective-permute-done | bytes 262176 | tf_op jit(solution)/shard_map/ppermute | solution.py:77
  88.3 0.6 copy-done.28
  88.9 0.7 copy-done.25
  89.6 6.2 %shard_map.114 = (f32[128,256]{1,0:T(8,128)}, f32[128,256]{1,0:T(8,128)}, bf16[128,64]{1,0:T(8,128)(2,1)}) custom-call(s32[3]{0:T(128)} %copy-done.9, bf16[272,1024]{1,0:T(8,128)(2,1)} %copy-done.11, bf16[272,1024]{1,0:T(8,128)(2,1)} %copy-done.18, bf16[272,1024]{1,0:T(8,128)(2,1)} %copy-done.20, bf16[272,1024]{1,0:T(8,128)(2,1)} %copy-done.14, ...), custom_call_target="tpu_custom_call" | custom-call | tf_op jit(solution)/shard_map/pallas_call | solution.py:231
  95.8 7.3 %collective-permute-start.17 = (f32[128,256]{1,0:T(8,128)}, f32[128,256]{1,0:T(8,128)S(1)}, u32[]{:S(2)}, u32[]{:S(2)}) collective-permute-start(f32[128,256]{1,0:T(8,128)} %get-tuple-element.17), channel_id=1, source_target_pairs={{0,8},{8,0},{16,24},{24,16},{32,40},{40,32},{48,56},{56,48},{64,72... | collective-permute-start | bytes 393224 | tf_op jit(solution)/shard_map/ppermute | solution.py:296
  103.1 1.2 collective-permute-done.17.got_ref
  104.3 0.9 copy-done.5
  105.2 0.8 copy-done.6
  106.0 5.2 %shard_map.115 = (bf16[8,80,128]{2,1,0:T(8,128)(2,1)S(1)}, f32[128,128]{1,0:T(8,128)S(1)}, f32[128,128]{1,0:T(8,128)S(1)}) custom-call(s32[1,8]{1,0:T(1,128)S(1)} %copy-done.10, f32[128,256]{1,0:T(8,128)S(1)} %copy-done.5, f32[128,256]{1,0:T(8,128)S(1)} %collective-permute-done.17.got_ref, bf16[128,64]{1,0:T(8,128)(2,1)S(1)} %copy-done.6, ...), custom_call_target="tpu_custom_call" | custom-call | tf_op jit(solution)/shard_map/pallas_call | solution.py:231
  111.2 12.8 %all_to_all.25.pack_ref = bf16[8,80,128]{2,1,0:T(8,128)(2,1)S(1)} all-to-all(bf16[8,80,128]{2,1,0:T(8,128)(2,1)S(1)} %get-tuple-element.19), channel_id=1, replica_groups=mesh['row'=64,'col'=8] {'col'}, dimensions={0} | all-to-all | bytes 327680 | tf_op jit(solution)/shard_map/all_to_all | solution.py:309
  124.0 0.9 shard_map.116
  124.9 14.1 %all_to_all.26.in_ref = bf16[8,72,256]{2,1,0:T(8,128)(2,1)S(1)} all-to-all(bf16[8,72,256]{2,1,0:T(8,128)(2,1)S(1)} %shard_map.116), channel_id=1, replica_groups={{0,8,16,24,32,40,48,56},{64,72,80,88,96,104,112,120},{128,136,144,152,1..., dimensions={0} | all-to-all | bytes 589824 | tf_op jit(solution)/shard_map/all_to_all | solution.py:315
  139.1 14.7 %all_to_all.27.in_ref = bf16[8,72,256]{2,1,0:T(8,128)(2,1)S(1)} all-to-all(bf16[8,72,256]{2,1,0:T(8,128)(2,1)S(1)} %shard_map.117), channel_id=1, replica_groups={{0,64,128,192,256,320,384,448},{8,72,136,200,264,328,392,456},{16,80,14..., dimensions={0} | all-to-all | bytes 589824 | tf_op jit(solution)/shard_map/all_to_all | solution.py:317
  153.8 12.2 %all_to_all.28.in_ref = bf16[8,72,256]{2,1,0:T(8,128)(2,1)S(1)} all-to-all(bf16[8,72,256]{2,1,0:T(8,128)(2,1)S(1)} %shard_map.118), channel_id=1, replica_groups={{0,8,16,24,32,40,48,56},{64,72,80,88,96,104,112,120},{128,136,144,152,1..., dimensions={0} | all-to-all | bytes 589824 | tf_op jit(solution)/shard_map/all_to_all | solution.py:319
  166.0 0.8 shard_map.119
  (72 shorter events, 0.4 us)
Async XLA Ops:
  0.7 1.0 copy-start
  1.8 10.4 %copy-start.9 = (s32[3]{0:T(128)}, s32[3]{0:T(128)S(1)}, u32[]{:S(2)}) copy-start(s32[3]{0:T(128)S(1)} %pad_add_fusion.pos_ref) | copy-start | bytes 40
  1.8 9.5 %copy-start.29 = (bf16[256,128]{1,0:T(8,128)(2,1)S(1)}, bf16[256,128]{1,0:T(8,128)(2,1)}, u32[]{:S(2)}) copy-start(bf16[256,128]{1,0:T(8,128)(2,1)} %param.13) | copy-start | bytes 196612
  1.8 9.5 %copy-start.30 = (bf16[256,128]{1,0:T(8,128)(2,1)S(1)}, bf16[256,128]{1,0:T(8,128)(2,1)}, u32[]{:S(2)}) copy-start(bf16[256,128]{1,0:T(8,128)(2,1)} %param.12) | copy-start | bytes 196612
  2.5 13.7 %collective-permute-start = (bf16[128,1024]{1,0:T(8,128)(2,1)S(1)}, bf16[128,1024]{1,0:T(8,128)(2,1)S(1)}, u32[]{:S(2)}, u32[]{:S(2)}) collective-permute-start(bf16[128,1024]{1,0:T(8,128)(2,1)S(1)} %get-tuple-element.15), channel_id=1, source_target_pairs={{0,8},{8,0},{16,24},{24,16},{32,40},{40,32},{48,56},{56,48},{64,72... | collective-permute-start | bytes 786440 | tf_op jit(solution)/shard_map/ppermute | solution.py:268
  12.2 3.6 %copy-start.1 = (bf16[128,2048]{1,0:T(8,128)(2,1)S(1)}, bf16[128,2048]{1,0:T(8,128)(2,1)}, u32[]{:S(2)}) copy-start(bf16[128,2048]{1,0:T(8,128)(2,1)} %t_ref.5) | copy-start | bytes 1572868
  12.2 3.6 %copy-start.4 = (bf16[2048,64]{0,1:T(8,128)(2,1)S(1)}, bf16[2048,64]{0,1:T(8,128)(2,1)}, u32[]{:S(2)}) copy-start(bf16[2048,64]{0,1:T(8,128)(2,1)} %param.14) | copy-start | bytes 786436
  12.2 13.2 %all-to-all-start = ((bf16[4,256,256]{2,1,0:T(8,128)(2,1)}), bf16[4,256,256]{2,1,0:T(8,128)(2,1)S(1)}, u32[]{:S(2)}, u32[]{:S(2)}) async-start(bf16[4,256,256]{2,1,0:T(8,128)(2,1)} %broadcast_in_dim.3), calls=%async_computation | async-start | bytes 1048576 | tf_op jit(solution)/shard_map/all_to_all | solution.py:277
  16.2 53.3 %copy-start.11 = (bf16[272,1024]{1,0:T(8,128)(2,1)}, bf16[272,1024]{1,0:T(8,128)(2,1)S(1)}, u32[]{:S(2)}) copy-start(bf16[272,1024]{1,0:T(8,128)(2,1)S(1)} %pad_maximum_fusion.refs_0_) | copy-start | bytes 1671172
  16.2 15.7 %collective-permute-start.4 = (bf16[272,1024]{1,0:T(8,128)(2,1)S(1)}, bf16[272,1024]{1,0:T(8,128)(2,1)S(1)}, u32[]{:S(2)}, u32[]{:S(2)}) collective-permute-start(bf16[272,1024]{1,0:T(8,128)(2,1)S(1)} %pad_maximum_fusion.refs_0_), channel_id=1, source_target_pairs={{1,0},{2,1},{3,2},{4,3},{5,4},{6,5},{7,6},{0,7},{15,8},{8,9},{9,10... | collective-permute-start | bytes 1671176 | tf_op jit(solution)/shard_map/ppermute | solution.py:75
  18.2 17.1 %collective-permute-start.1 = (bf16[272,1024]{1,0:T(8,128)(2,1)S(1)}, bf16[272,1024]{1,0:T(8,128)(2,1)S(1)}, u32[]{:S(2)}, u32[]{:S(2)}) collective-permute-start(bf16[272,1024]{1,0:T(8,128)(2,1)S(1)} %pad_maximum_fusion.refs_0_), channel_id=1, source_target_pairs={{0,1},{1,2},{2,3},{3,4},{4,5},{5,6},{6,7},{7,0},{8,15},{9,8},{10,9... | collective-permute-start | bytes 1671176 | tf_op jit(solution)/shard_map/ppermute | solution.py:74
  25.4 44.1 %copy-start.12 = (bf16[4,256,256]{2,1,0:T(8,128)(2,1)}, bf16[4,256,256]{2,1,0:T(8,128)(2,1)S(1)}, u32[]{:S(2)}) copy-start(bf16[4,256,256]{2,1,0:T(8,128)(2,1)S(1)} %all-to-all-done) | copy-start | bytes 1572868
  25.4 14.9 %collective-permute-start.12 = (bf16[1024,256]{1,0:T(8,128)(2,1)S(1)}, bf16[1024,256]{1,0:T(8,128)(2,1)S(1)}, u32[]{:S(2)}, u32[]{:S(2)}) collective-permute-start(bf16[1024,256]{1,0:T(8,128)(2,1)S(1)} %bitcast.7), channel_id=1, source_target_pairs={{64,0},{456,8},{80,16},{472,24},{96,32},{488,40},{112,48},{504,56}... | collective-permute-start | bytes 1572872 | tf_op jit(solution)/shard_map/ppermute | solution.py:75
  27.3 16.2 %collective-permute-start.9 = (bf16[1024,256]{1,0:T(8,128)(2,1)S(1)}, bf16[1024,256]{1,0:T(8,128)(2,1)S(1)}, u32[]{:S(2)}, u32[]{:S(2)}) collective-permute-start(bf16[1024,256]{1,0:T(8,128)(2,1)S(1)} %bitcast.8), channel_id=1, source_target_pairs={{0,64},{8,456},{16,80},{24,472},{32,96},{40,488},{48,112},{56,504}... | collective-permute-start | bytes 1572872 | tf_op jit(solution)/shard_map/ppermute | solution.py:74
  31.9 56.3 %copy-start.17 = (bf16[272,1024]{1,0:T(8,128)(2,1)}, bf16[272,1024]{1,0:T(8,128)(2,1)S(1)}, u32[]{:S(2)}) copy-start(bf16[272,1024]{1,0:T(8,128)(2,1)S(1)} %collective-permute-done.4.refs_4_) | copy-start | bytes 1671172
  31.9 15.7 %collective-permute-start.5 = (bf16[272,1024]{1,0:T(8,128)(2,1)S(1)}, bf16[272,1024]{1,0:T(8,128)(2,1)S(1)}, u32[]{:S(2)}, u32[]{:S(2)}) collective-permute-start(bf16[272,1024]{1,0:T(8,128)(2,1)S(1)} %collective-permute-done.4.refs_4_), channel_id=1, source_target_pairs={{1,0},{2,1},{3,2},{4,3},{5,4},{6,5},{7,6},{0,7},{15,8},{8,9},{9,10... | collective-permute-start | bytes 1671176 | tf_op jit(solution)/shard_map/ppermute | solution.py:75
  35.2 53.0 %copy-start.18 = (bf16[272,1024]{1,0:T(8,128)(2,1)}, bf16[272,1024]{1,0:T(8,128)(2,1)S(1)}, u32[]{:S(2)}) copy-start(bf16[272,1024]{1,0:T(8,128)(2,1)S(1)} %collective-permute-done.1.refs_1_) | copy-start | bytes 1671172
  35.2 17.4 %collective-permute-start.2 = (bf16[272,1024]{1,0:T(8,128)(2,1)S(1)}, bf16[272,1024]{1,0:T(8,128)(2,1)S(1)}, u32[]{:S(2)}, u32[]{:S(2)}) collective-permute-start(bf16[272,1024]{1,0:T(8,128)(2,1)S(1)} %collective-permute-done.1.refs_1_), channel_id=1, source_target_pairs={{0,1},{1,2},{2,3},{3,4},{4,5},{5,6},{6,7},{7,0},{8,15},{9,8},{10,9... | collective-permute-start | bytes 1671176 | tf_op jit(solution)/shard_map/ppermute | solution.py:74
  40.3 47.9 %copy-start.21 = (bf16[1024,256]{1,0:T(8,128)(2,1)}, bf16[1024,256]{1,0:T(8,128)(2,1)S(1)}, u32[]{:S(2)}) copy-start(bf16[1024,256]{1,0:T(8,128)(2,1)S(1)} %collective-permute-done.12.refs_13_) | copy-start | bytes 1572868
  40.3 17.6 %collective-permute-start.13 = (bf16[1024,256]{1,0:T(8,128)(2,1)S(1)}, bf16[1024,256]{1,0:T(8,128)(2,1)S(1)}, u32[]{:S(2)}, u32[]{:S(2)}) collective-permute-start(bf16[1024,256]{1,0:T(8,128)(2,1)S(1)} %collective-permute-done.12.refs_13_), channel_id=1, source_target_pairs={{64,0},{456,8},{80,16},{472,24},{96,32},{488,40},{112,48},{504,56}... | collective-permute-start | bytes 1572872 | tf_op jit(solution)/shard_map/ppermute | solution.py:75
  43.5 17.6 %copy-start.22 = (bf16[1024,256]{1,0:T(8,128)(2,1)}, bf16[1024,256]{1,0:T(8,128)(2,1)S(1)}, u32[]{:S(2)}) copy-start(bf16[1024,256]{1,0:T(8,128)(2,1)S(1)} %collective-permute-done.9.refs_10_) | copy-start | bytes 1572868
  43.5 17.6 %collective-permute-start.10 = (bf16[1024,256]{1,0:T(8,128)(2,1)S(1)}, bf16[1024,256]{1,0:T(8,128)(2,1)S(1)}, u32[]{:S(2)}, u32[]{:S(2)}) collective-permute-start(bf16[1024,256]{1,0:T(8,128)(2,1)S(1)} %collective-permute-done.9.refs_10_), channel_id=1, source_target_pairs={{0,64},{8,456},{16,80},{24,472},{32,96},{40,488},{48,112},{56,504}... | collective-permute-start | bytes 1572872 | tf_op jit(solution)/shard_map/ppermute | solution.py:74
  47.6 40.6 %copy-start.19 = (bf16[272,1024]{1,0:T(8,128)(2,1)}, bf16[272,1024]{1,0:T(8,128)(2,1)S(1)}, u32[]{:S(2)}) copy-start(bf16[272,1024]{1,0:T(8,128)(2,1)S(1)} %collective-permute-done.5.refs_5_) | copy-start | bytes 1671172
  47.6 17.4 %collective-permute-start.6 = (bf16[272,1024]{1,0:T(8,128)(2,1)S(1)}, bf16[272,1024]{1,0:T(8,128)(2,1)S(1)}, u32[]{:S(2)}, u32[]{:S(2)}) collective-permute-start(bf16[272,1024]{1,0:T(8,128)(2,1)S(1)} %collective-permute-done.5.refs_5_), channel_id=1, source_target_pairs={{1,0},{2,1},{3,2},{4,3},{5,4},{6,5},{7,6},{0,7},{15,8},{8,9},{9,10... | collective-permute-start | bytes 1671176 | tf_op jit(solution)/shard_map/ppermute | solution.py:75
  52.7 35.6 %copy-start.20 = (bf16[272,1024]{1,0:T(8,128)(2,1)}, bf16[272,1024]{1,0:T(8,128)(2,1)S(1)}, u32[]{:S(2)}) copy-start(bf16[272,1024]{1,0:T(8,128)(2,1)S(1)} %collective-permute-done.2.refs_2_) | copy-start | bytes 1671172
  52.7 16.8 %collective-permute-start.3 = (bf16[272,1024]{1,0:T(8,128)(2,1)S(1)}, bf16[272,1024]{1,0:T(8,128)(2,1)S(1)}, u32[]{:S(2)}, u32[]{:S(2)}) collective-permute-start(bf16[272,1024]{1,0:T(8,128)(2,1)S(1)} %collective-permute-done.2.refs_2_), channel_id=1, source_target_pairs={{0,1},{1,2},{2,3},{3,4},{4,5},{5,6},{6,7},{7,0},{8,15},{9,8},{10,9... | collective-permute-start | bytes 1671176 | tf_op jit(solution)/shard_map/ppermute | solution.py:74
  57.9 20.2 %copy-start.23 = (bf16[1024,256]{1,0:T(8,128)(2,1)}, bf16[1024,256]{1,0:T(8,128)(2,1)S(1)}, u32[]{:S(2)}) copy-start(bf16[1024,256]{1,0:T(8,128)(2,1)S(1)} %collective-permute-done.13.refs_14_) | copy-start | bytes 1572868
  57.9 16.9 %collective-permute-start.14 = (bf16[1024,256]{1,0:T(8,128)(2,1)S(1)}, bf16[1024,256]{1,0:T(8,128)(2,1)S(1)}, u32[]{:S(2)}, u32[]{:S(2)}) collective-permute-start(bf16[1024,256]{1,0:T(8,128)(2,1)S(1)} %collective-permute-done.13.refs_14_), channel_id=1, source_target_pairs={{64,0},{456,8},{80,16},{472,24},{96,32},{488,40},{112,48},{504,56}... | collective-permute-start | bytes 1572872 | tf_op jit(solution)/shard_map/ppermute | solution.py:75
  61.1 17.0 %copy-start.24 = (bf16[1024,256]{1,0:T(8,128)(2,1)}, bf16[1024,256]{1,0:T(8,128)(2,1)S(1)}, u32[]{:S(2)}) copy-start(bf16[1024,256]{1,0:T(8,128)(2,1)S(1)} %collective-permute-done.10.refs_11_) | copy-start | bytes 1572868
  61.2 17.0 %collective-permute-start.11 = (bf16[1024,256]{1,0:T(8,128)(2,1)S(1)}, bf16[1024,256]{1,0:T(8,128)(2,1)S(1)}, u32[]{:S(2)}, u32[]{:S(2)}) collective-permute-start(bf16[1024,256]{1,0:T(8,128)(2,1)S(1)} %collective-permute-done.10.refs_11_), channel_id=1, source_target_pairs={{0,64},{8,456},{16,80},{24,472},{32,96},{40,488},{48,112},{56,504}... | collective-permute-start | bytes 1572872 | tf_op jit(solution)/shard_map/ppermute | solution.py:74
  65.0 23.2 %copy-start.13 = (bf16[272,1024]{1,0:T(8,128)(2,1)}, bf16[272,1024]{1,0:T(8,128)(2,1)S(1)}, u32[]{:S(2)}) copy-start(bf16[272,1024]{1,0:T(8,128)(2,1)S(1)} %collective-permute-done.6.refs_6_) | copy-start | bytes 1671172
  65.1 23.1 %collective-permute-start.8 = (bf16[144,1024]{1,0:T(8,128)(2,1)S(1)}, bf16[144,1024]{1,0:T(8,128)(2,1)S(1)}, u32[]{:S(2)}, u32[]{:S(2)}) collective-permute-start(bf16[144,1024]{1,0:T(8,128)(2,1)S(1)} %slice.17), channel_id=1, source_target_pairs={{1,0},{2,1},{3,2},{4,3},{5,4},{6,5},{7,6},{0,7},{15,8},{8,9},{9,10... | collective-permute-start | bytes 884744 | tf_op jit(solution)/shard_map/ppermute | solution.py:78
  69.5 18.8 %copy-start.14 = (bf16[272,1024]{1,0:T(8,128)(2,1)}, bf16[272,1024]{1,0:T(8,128)(2,1)S(1)}, u32[]{:S(2)}) copy-start(bf16[272,1024]{1,0:T(8,128)(2,1)S(1)} %collective-permute-done.3.refs_3_) | copy-start | bytes 1671172
  69.5 13.0 %collective-permute-start.7 = (bf16[128,1024]{1,0:T(8,128)(2,1)S(1)}, bf16[128,1024]{1,0:T(8,128)(2,1)S(1)}, u32[]{:S(2)}, u32[]{:S(2)}) collective-permute-start(bf16[128,1024]{1,0:T(8,128)(2,1)S(1)} %slice.16), channel_id=1, source_target_pairs={{0,1},{1,2},{2,3},{3,4},{4,5},{5,6},{6,7},{7,0},{8,15},{9,8},{10,9... | collective-permute-start | bytes 786440 | tf_op jit(solution)/shard_map/ppermute | solution.py:77
  74.9 13.4 %copy-start.15 = (bf16[1024,256]{1,0:T(8,128)(2,1)}, bf16[1024,256]{1,0:T(8,128)(2,1)S(1)}, u32[]{:S(2)}) copy-start(bf16[1024,256]{1,0:T(8,128)(2,1)S(1)} %collective-permute-done.14.refs_15_) | copy-start | bytes 1572868
  74.9 9.5 %collective-permute-start.16 = (bf16[512,256]{1,0:T(8,128)(2,1)S(1)}, bf16[512,256]{1,0:T(8,128)(2,1)S(1)}, u32[]{:S(2)}, u32[]{:S(2)}) collective-permute-start(bf16[512,256]{1,0:T(8,128)(2,1)S(1)} %slice.19), channel_id=1, source_target_pairs={{64,0},{456,8},{80,16},{472,24},{96,32},{488,40},{112,48},{504,56}... | collective-permute-start | bytes 786440 | tf_op jit(solution)/shard_map/ppermute | solution.py:78
  78.1 10.1 %copy-start.16 = (bf16[1024,256]{1,0:T(8,128)(2,1)}, bf16[1024,256]{1,0:T(8,128)(2,1)S(1)}, u32[]{:S(2)}) copy-start(bf16[1024,256]{1,0:T(8,128)(2,1)S(1)} %collective-permute-done.11.refs_12_) | copy-start | bytes 1572868
  78.2 26.1 %copy-start.2 = (bf16[128,2048]{1,0:T(8,128)(2,1)S(1)}, bf16[128,2048]{1,0:T(8,128)(2,1)}, u32[]{:S(2)}) copy-start(bf16[128,2048]{1,0:T(8,128)(2,1)} %q_ref.1) | copy-start | bytes 1572868
  78.2 26.1 %copy-start.3 = (bf16[128,2048]{1,0:T(8,128)(2,1)S(1)}, bf16[128,2048]{1,0:T(8,128)(2,1)}, u32[]{:S(2)}) copy-start(bf16[128,2048]{1,0:T(8,128)(2,1)} %p_ref.1) | copy-start | bytes 1572868
  78.2 26.1 %copy-start.7 = (bf16[64,128]{1,0:T(8,128)(2,1)S(1)}, bf16[64,128]{1,0:T(8,128)(2,1)}, u32[]{:S(2)}) copy-start(bf16[64,128]{1,0:T(8,128)(2,1)} %upk_ref.1) | copy-start | bytes 49156
  78.2 26.1 %copy-start.8 = (bf16[64,128]{1,0:T(8,128)(2,1)S(1)}, bf16[64,128]{1,0:T(8,128)(2,1)}, u32[]{:S(2)}) copy-start(bf16[64,128]{1,0:T(8,128)(2,1)} %upv_ref.1) | copy-start | bytes 49156
  78.2 26.1 %copy-start.10 = (s32[1,8]{1,0:T(1,128)S(1)}, s32[1,8]{1,0:T(1,128)}, u32[]{:S(2)}) copy-start(s32[1,8]{1,0:T(1,128)} %lengths_ref.3) | copy-start | bytes 100
  78.2 10.0 %collective-permute-start.15 = (bf16[512,256]{1,0:T(8,128)(2,1)S(1)}, bf16[512,256]{1,0:T(8,128)(2,1)S(1)}, u32[]{:S(2)}, u32[]{:S(2)}) collective-permute-start(bf16[512,256]{1,0:T(8,128)(2,1)S(1)} %slice.18), channel_id=1, source_target_pairs={{0,64},{8,456},{16,80},{24,472},{32,96},{40,488},{48,112},{56,504}... | collective-permute-start | bytes 786440 | tf_op jit(solution)/shard_map/ppermute | solution.py:77
  82.5 5.8 %copy-start.26 = (bf16[128,1024]{1,0:T(8,128)(2,1)}, bf16[128,1024]{1,0:T(8,128)(2,1)S(1)}, u32[]{:S(2)}) copy-start(bf16[128,1024]{1,0:T(8,128)(2,1)S(1)} %collective-permute-done.7.refs_7_) | copy-start | bytes 786436
  84.4 3.9 %copy-start.27 = (bf16[512,256]{1,0:T(8,128)(2,1)}, bf16[512,256]{1,0:T(8,128)(2,1)S(1)}, u32[]{:S(2)}) copy-start(bf16[512,256]{1,0:T(8,128)(2,1)S(1)} %collective-permute-done.16.refs_17_) | copy-start | bytes 786436
  95.8 8.5 %collective-permute-start.17 = (f32[128,256]{1,0:T(8,128)}, f32[128,256]{1,0:T(8,128)S(1)}, u32[]{:S(2)}, u32[]{:S(2)}) collective-permute-start(f32[128,256]{1,0:T(8,128)} %get-tuple-element.17), channel_id=1, source_target_pairs={{0,8},{8,0},{16,24},{24,16},{32,40},{40,32},{48,56},{56,48},{64,72... | collective-permute-start | bytes 393224 | tf_op jit(solution)/shard_map/ppermute | solution.py:296
  104.3 0.9 copy-start.5
  105.2 0.8 copy-start.6
  (2 other events, 1.4 us)

commit v5 on v4

--- a/solution.py
+++ b/solution.py
@@ -68,36 +68,25 @@
 STEPS = (0, 1, 2, 3, -1, -2, -3, 4)
 
 
-def ring_of(own, axis, fore, aft, cut):
-    fore_going, aft_going = [own], [own]
+def ring_of(own, axis, fore, swap):
+    near, far, crossed = [own], lax.ppermute(own, "row", swap), []
     for _ in range(3):
-        fore_going.append(lax.ppermute(fore_going[-1], axis, fore))
-        aft_going.append(lax.ppermute(aft_going[-1], axis, aft))
-    return fore_going + aft_going[1:] + [
-        lax.ppermute(fore_going[3][:cut], axis, fore),
-        lax.ppermute(aft_going[3][cut:], axis, aft),
-    ]
+        near.append(lax.ppermute(near[-1], axis, fore))
+        far = lax.ppermute(far, axis, fore)
+        crossed.append(lax.ppermute(far, "row", swap))
+    return near + crossed + [lax.ppermute(near[3], axis, fore)]
 
 
 def project_kernel(pos_ref, *refs):
-    t_refs, w_refs, refs = refs[:9], refs[9:18], refs[18:]
+    t_refs, w_refs, refs = refs[:8], refs[8:16], refs[16:]
     own_ref, other_ref, low_ref, t_scr, w_scr, sem = refs
     n = t_scr.shape[0]
     way = 2 * pos_ref[0] - 1
     copies = []
     for at, (parts, scr) in enumerate(((t_refs, t_scr), (w_refs, w_scr))):
-        cut = parts[7].shape[0]
         for j, step in enumerate(STEPS):
             k = lax.rem(pos_ref[1 + at] + step * way + n, n)
-            if step == 4:
-                pairs = [
-                    (parts[7], scr.at[k, pl.ds(0, cut)]),
-                    (parts[8], scr.at[k, pl.ds(cut, scr.shape[1] - cut)]),
-                ]
-            else:
-                pairs = [(parts[j], scr.at[k])]
-            for i, (a, b) in enumerate(pairs):
-                copies.append(pltpu.make_async_copy(a, b, sem.at[at, j + i]))
+            copies.append(pltpu.make_async_copy(parts[j], scr.at[k], sem.at[at, j]))
     for c in copies:
         c.start()
     for c in copies:
@@ -249,13 +238,11 @@
     sites = [(y, x, core) for y in range(8) for x in range(4) for core in range(2)]
     swap = [(place(y, x, c), place(y, x, 1 - c)) for y, x, c in sites]
     y_fore = [(place(y, x, c), place(y + 1 - 2 * c, x, c)) for y, x, c in sites]
-    y_aft = [(b, a) for a, b in y_fore]
     z_fore = [
         (place(y, x, c) * 8 + z, place(y, x, c) * 8 + (z + 1 - 2 * c) % 8)
         for y, x, c in sites
         for z in range(8)
     ]
-    z_aft = [(b, a) for a, b in z_fore]
     y_lines = [[place(y, x, c) for y in range(8)] for x in range(4) for c in range(2)]
     squares = [[place(y, x, c) for x in range(4) for c in range(2)] for y in range(8)]
     x_lines = [[place(y, x, c) for x in range(4)] for y in range(8) for c in range(2)]
@@ -270,7 +257,7 @@
         low_kernel, [((16, feats // 2), BF)], [VMEM, VMEM], [VMEM], tokens, down_proj.T
     )
     pair = jnp.concatenate([mine, swapped, low_part], axis=0)
-    t_parts = ring_of(pair, ("row", "col"), z_fore, z_aft, rows)
+    t_parts = ring_of(pair, ("row", "col"), z_fore, swap)
 
     w_both = jnp.concatenate([w_key, w_value], axis=1)
     wide = w_both.shape[1]
@@ -278,18 +265,18 @@
         jnp.broadcast_to(w_both, (4,) + w_both.shape), "row", 0, 0, axis_index_groups=x_lines
     )
     w_own = w_line.reshape(feats // 2, wide)
-    w_parts = ring_of(w_own, "row", y_fore, y_aft, feats // 4)
+    w_parts = ring_of(w_own, "row", y_fore, swap)
 
     own, other, low_half = call(
         project_kernel,
         [((rows, wide), F32), ((rows, wide), F32), ((rows, 64), BF)],
-        [SMEM] + [HBM] * 18,
+        [SMEM] + [HBM] * 16,
         [VMEM] * 3,
         pos, *t_parts, *w_parts,
         scratch=[
             pltpu.VMEM((8, 2 * rows + 16, feats // 2), BF),
             pltpu.VMEM((8, feats // 2, wide), BF),
-            pltpu.SemaphoreType.DMA((2, 9)),
+            pltpu.SemaphoreType.DMA((2, 8)),
         ],
         mib=56,
     )

time: 168 us -> 170 us (1.012)
  starting transfers between devices: 77 us -> 85 us
  waiting for transfers between devices: 15.2 us -> 8.43 us
    ppermute x16 -> x22, starting transfers between devices: 57.4 us -> 68.4 us  [the longest x6 23.4 us: ring_of(): near.append(lax.ppermute(near[-1], axis, fore))]
    ppermute x16 -> x22, waiting for transfers between devices: 12.6 us -> 6.12 us  [the longest x2 6.07 us: ring_of(): return near + crossed + [lax.ppermute(near[3], axis, fore)]]
    ppermute x1, starting transfers between devices: 7.28 us -> 4.26 us  [on_device(): got = lax.ppermute(other, 'row', swap)]
    unnamed x62 -> x56, local copies, waits for them, and re-layouts: 4.14 us -> 5.22 us
  transfers between devices with their start and end apart: 19 -> 25, of which waited for: 7 -> 3; matrix products, arithmetic and copies ran while one was open for 1% -> 1% of each run, Pallas kernels for 0% -> 0%
where the time goes in v5:
time: 170 us; the launch traced here: 169 us
  starting transfers between devices  85 us (50%)
  blocking collectives  53.3 us (31%)
  Pallas kernels  14.3 us (8%)
  waiting for transfers between devices  8.43 us (5%)
  local copies, waits for them, and re-layouts  6.05 us (4%)
    ppermute x6, starting transfers between devices, ring_of(): near.append(lax.ppermute(near[-1], axis, fore))  23.4 us
    ppermute x6, starting transfers between devices, ring_of(): far = lax.ppermute(far, axis, fore)  19.4 us
    ppermute x6, starting transfers between devices, ring_of(): crossed.append(lax.ppermute(far, 'row', swap))  15.9 us
    all_to_all x1, blocking collectives, on_device(): lax.all_to_all(square, 'row', 0, 0, axis_index_groups=y_lines)  15.6 us
    pallas_call x8, Pallas kernels, call(): pl.pallas_call(kernel, out_shape=[jax.ShapeDtypeStruct(s, d) for s, d in...  14.3 us
    all_to_all x1, blocking collectives, on_device(): term_parts = lax.all_to_all(terms, 'row', 0, 0, axis_index_groups=squares)  13.1 us
    all_to_all x1, blocking collectives, on_device(): packs = lax.all_to_all(pack, 'col', 0, 0)  12.4 us
    all_to_all x1, blocking collectives, on_device(): pieces = lax.all_to_all(summed, 'row', 0, 0, axis_index_groups=squares)  12.2 us
  transfers between devices with their start and end apart: 25, of which 3 were waited for; matrix products, arithmetic and copies ran while one was open for 1% of the time, Pallas kernels for 0%

profile of v5, /device:TPU:1, one launch (start us, length us, event | category | flops | bytes accessed | tf_op | source)
XLA Modules:
  0.0 168.5 jit_solution(10709263438890033747)
XLA Ops:
  0.7 0.1 pad_add_fusion.pos_ref
  0.7 1.0 copy-done
  1.8 0.7 shard_map.112
  2.5 8.8 %collective-permute-start = (bf16[128,1024]{1,0:T(8,128)(2,1)S(1)}, bf16[128,1024]{1,0:T(8,128)(2,1)S(1)}, u32[]{:S(2)}, u32[]{:S(2)}) collective-permute-start(bf16[128,1024]{1,0:T(8,128)(2,1)S(1)} %get-tuple-element.15), channel_id=1, source_target_pairs={{0,8},{8,0},{16,24},{24,16},{32,40},{40,32},{48,56},{56,48},{64,72... | collective-permute-start | bytes 786440 | tf_op jit(solution)/shard_map/ppermute | solution.py:255
  11.3 0.8 broadcast_in_dim.3
  12.2 3.6 %all-to-all-start = ((bf16[4,256,256]{2,1,0:T(8,128)(2,1)}), bf16[4,256,256]{2,1,0:T(8,128)(2,1)S(1)}, u32[]{:S(2)}, u32[]{:S(2)}) async-start(bf16[4,256,256]{2,1,0:T(8,128)(2,1)} %broadcast_in_dim.3), calls=%async_computation | async-start | bytes 1048576 | tf_op jit(solution)/shard_map/all_to_all | solution.py:264
  15.8 0.4 shard_map.113
  16.2 1.9 %collective-permute-start.4 = (bf16[272,1024]{1,0:T(8,128)(2,1)S(1)}, bf16[272,1024]{1,0:T(8,128)(2,1)S(1)}, u32[]{:S(2)}, u32[]{:S(2)}) collective-permute-start(bf16[272,1024]{1,0:T(8,128)(2,1)S(1)} %pad_maximum_fusion.refs_0_), channel_id=1, source_target_pairs={{0,8},{8,0},{16,24},{24,16},{32,40},{40,32},{48,56},{56,48},{64,72... | collective-permute-start | bytes 1671176 | tf_op jit(solution)/shard_map/ppermute | solution.py:72
  18.2 6.1 %collective-permute-start.1 = (bf16[272,1024]{1,0:T(8,128)(2,1)S(1)}, bf16[272,1024]{1,0:T(8,128)(2,1)S(1)}, u32[]{:S(2)}, u32[]{:S(2)}) collective-permute-start(bf16[272,1024]{1,0:T(8,128)(2,1)S(1)} %pad_maximum_fusion.refs_0_), channel_id=1, source_target_pairs={{0,1},{1,2},{2,3},{3,4},{4,5},{5,6},{6,7},{7,0},{8,15},{9,8},{10,9... | collective-permute-start | bytes 1671176 | tf_op jit(solution)/shard_map/ppermute | solution.py:74
  24.3 1.1 all-to-all-done
  25.4 0.0 copy-start.8
  25.4 0.0 copy-start.10
  25.4 2.8 %collective-permute-start.15 = (bf16[1024,256]{1,0:T(8,128)(2,1)S(1)}, bf16[1024,256]{1,0:T(8,128)(2,1)S(1)}, u32[]{:S(2)}, u32[]{:S(2)}) collective-permute-start(bf16[1024,256]{1,0:T(8,128)(2,1)S(1)} %bitcast.7), channel_id=1, source_target_pairs={{0,8},{8,0},{16,24},{24,16},{32,40},{40,32},{48,56},{56,48},{64,72... | collective-permute-start | bytes 1572872 | tf_op jit(solution)/shard_map/ppermute | solution.py:72
  28.3 5.9 %collective-permute-start.5 = (bf16[272,1024]{1,0:T(8,128)(2,1)S(1)}, bf16[272,1024]{1,0:T(8,128)(2,1)S(1)}, u32[]{:S(2)}, u32[]{:S(2)}) collective-permute-start(bf16[272,1024]{1,0:T(8,128)(2,1)S(1)} %collective-permute-done.4), channel_id=1, source_target_pairs={{0,1},{1,2},{2,3},{3,4},{4,5},{5,6},{6,7},{7,0},{8,15},{9,8},{10,9... | collective-permute-start | bytes 1671176 | tf_op jit(solution)/shard_map/ppermute | solution.py:75
  34.2 2.2 %collective-permute-start.2 = (bf16[272,1024]{1,0:T(8,128)(2,1)S(1)}, bf16[272,1024]{1,0:T(8,128)(2,1)S(1)}, u32[]{:S(2)}, u32[]{:S(2)}) collective-permute-start(bf16[272,1024]{1,0:T(8,128)(2,1)S(1)} %collective-permute-done.1.refs_1_), channel_id=1, source_target_pairs={{0,1},{1,2},{2,3},{3,4},{4,5},{5,6},{6,7},{7,0},{8,15},{9,8},{10,9... | collective-permute-start | bytes 1671176 | tf_op jit(solution)/shard_map/ppermute | solution.py:74
  36.4 5.1 %collective-permute-start.12 = (bf16[1024,256]{1,0:T(8,128)(2,1)S(1)}, bf16[1024,256]{1,0:T(8,128)(2,1)S(1)}, u32[]{:S(2)}, u32[]{:S(2)}) collective-permute-start(bf16[1024,256]{1,0:T(8,128)(2,1)S(1)} %bitcast.8), channel_id=1, source_target_pairs={{0,64},{8,456},{16,80},{24,472},{32,96},{40,488},{48,112},{56,504}... | collective-permute-start | bytes 1572872 | tf_op jit(solution)/shard_map/ppermute | solution.py:74
  41.5 3.0 %collective-permute-start.16 = (bf16[1024,256]{1,0:T(8,128)(2,1)S(1)}, bf16[1024,256]{1,0:T(8,128)(2,1)S(1)}, u32[]{:S(2)}, u32[]{:S(2)}) collective-permute-start(bf16[1024,256]{1,0:T(8,128)(2,1)S(1)} %collective-permute-done.15), channel_id=1, source_target_pairs={{0,64},{8,456},{16,80},{24,472},{32,96},{40,488},{48,112},{56,504}... | collective-permute-start | bytes 1572872 | tf_op jit(solution)/shard_map/ppermute | solution.py:75
  44.5 2.2 %collective-permute-start.7 = (bf16[272,1024]{1,0:T(8,128)(2,1)S(1)}, bf16[272,1024]{1,0:T(8,128)(2,1)S(1)}, u32[]{:S(2)}, u32[]{:S(2)}) collective-permute-start(bf16[272,1024]{1,0:T(8,128)(2,1)S(1)} %collective-permute-done.5), channel_id=1, source_target_pairs={{0,1},{1,2},{2,3},{3,4},{4,5},{5,6},{6,7},{7,0},{8,15},{9,8},{10,9... | collective-permute-start | bytes 1671176 | tf_op jit(solution)/shard_map/ppermute | solution.py:75
  46.7 1.9 %collective-permute-start.6 = (bf16[272,1024]{1,0:T(8,128)(2,1)S(1)}, bf16[272,1024]{1,0:T(8,128)(2,1)S(1)}, u32[]{:S(2)}, u32[]{:S(2)}) collective-permute-start(bf16[272,1024]{1,0:T(8,128)(2,1)S(1)} %collective-permute-done.5), channel_id=1, source_target_pairs={{0,8},{8,0},{16,24},{24,16},{32,40},{40,32},{48,56},{56,48},{64,72... | collective-permute-start | bytes 1671176 | tf_op jit(solution)/shard_map/ppermute | solution.py:76
  48.6 4.1 %collective-permute-start.13 = (bf16[1024,256]{1,0:T(8,128)(2,1)S(1)}, bf16[1024,256]{1,0:T(8,128)(2,1)S(1)}, u32[]{:S(2)}, u32[]{:S(2)}) collective-permute-start(bf16[1024,256]{1,0:T(8,128)(2,1)S(1)} %collective-permute-done.12.refs_9_), channel_id=1, source_target_pairs={{0,64},{8,456},{16,80},{24,472},{32,96},{40,488},{48,112},{56,504}... | collective-permute-start | bytes 1572872 | tf_op jit(solution)/shard_map/ppermute | solution.py:74
  52.7 3.1 %collective-permute-start.3 = (bf16[272,1024]{1,0:T(8,128)(2,1)S(1)}, bf16[272,1024]{1,0:T(8,128)(2,1)S(1)}, u32[]{:S(2)}, u32[]{:S(2)}) collective-permute-start(bf16[272,1024]{1,0:T(8,128)(2,1)S(1)} %collective-permute-done.2.refs_2_), channel_id=1, source_target_pairs={{0,1},{1,2},{2,3},{3,4},{4,5},{5,6},{6,7},{7,0},{8,15},{9,8},{10,9... | collective-permute-start | bytes 1671176 | tf_op jit(solution)/shard_map/ppermute | solution.py:74
  55.8 3.0 %collective-permute-start.18 = (bf16[1024,256]{1,0:T(8,128)(2,1)S(1)}, bf16[1024,256]{1,0:T(8,128)(2,1)S(1)}, u32[]{:S(2)}, u32[]{:S(2)}) collective-permute-start(bf16[1024,256]{1,0:T(8,128)(2,1)S(1)} %collective-permute-done.16), channel_id=1, source_target_pairs={{0,64},{8,456},{16,80},{24,472},{32,96},{40,488},{48,112},{56,504}... | collective-permute-start | bytes 1572872 | tf_op jit(solution)/shard_map/ppermute | solution.py:75
  58.8 2.4 %collective-permute-start.9 = (bf16[272,1024]{1,0:T(8,128)(2,1)S(1)}, bf16[272,1024]{1,0:T(8,128)(2,1)S(1)}, u32[]{:S(2)}, u32[]{:S(2)}) collective-permute-start(bf16[272,1024]{1,0:T(8,128)(2,1)S(1)} %collective-permute-done.7), channel_id=1, source_target_pairs={{0,1},{1,2},{2,3},{3,4},{4,5},{5,6},{6,7},{7,0},{8,15},{9,8},{10,9... | collective-permute-start | bytes 1671176 | tf_op jit(solution)/shard_map/ppermute | solution.py:75
  61.2 3.1 %collective-permute-start.17 = (bf16[1024,256]{1,0:T(8,128)(2,1)S(1)}, bf16[1024,256]{1,0:T(8,128)(2,1)}, u32[]{:S(2)}, u32[]{:S(2)}) collective-permute-start(bf16[1024,256]{1,0:T(8,128)(2,1)S(1)} %collective-permute-done.16), channel_id=1, source_target_pairs={{0,8},{8,0},{16,24},{24,16},{32,40},{40,32},{48,56},{56,48},{64,72... | collective-permute-start | bytes 1572872 | tf_op jit(solution)/shard_map/ppermute | solution.py:76
  64.4 2.8 %collective-permute-start.14 = (bf16[1024,256]{1,0:T(8,128)(2,1)S(1)}, bf16[1024,256]{1,0:T(8,128)(2,1)S(1)}, u32[]{:S(2)}, u32[]{:S(2)}) collective-permute-start(bf16[1024,256]{1,0:T(8,128)(2,1)S(1)} %collective-permute-done.13.refs_10_), channel_id=1, source_target_pairs={{0,64},{8,456},{16,80},{24,472},{32,96},{40,488},{48,112},{56,504}... | collective-permute-start | bytes 1572872 | tf_op jit(solution)/shard_map/ppermute | solution.py:74
  67.3 3.0 %collective-permute-start.20 = (bf16[1024,256]{1,0:T(8,128)(2,1)S(1)}, bf16[1024,256]{1,0:T(8,128)(2,1)S(1)}, u32[]{:S(2)}, u32[]{:S(2)}) collective-permute-start(bf16[1024,256]{1,0:T(8,128)(2,1)S(1)} %collective-permute-done.18), channel_id=1, source_target_pairs={{0,64},{8,456},{16,80},{24,472},{32,96},{40,488},{48,112},{56,504}... | collective-permute-start | bytes 1572872 | tf_op jit(solution)/shard_map/ppermute | solution.py:75
  70.3 3.0 %collective-permute-start.19 = (bf16[1024,256]{1,0:T(8,128)(2,1)S(1)}, bf16[1024,256]{1,0:T(8,128)(2,1)S(1)}, u32[]{:S(2)}, u32[]{:S(2)}) collective-permute-start(bf16[1024,256]{1,0:T(8,128)(2,1)S(1)} %collective-permute-done.18), channel_id=1, source_target_pairs={{0,8},{8,0},{16,24},{24,16},{32,40},{40,32},{48,56},{56,48},{64,72... | collective-permute-start | bytes 1572872 | tf_op jit(solution)/shard_map/ppermute | solution.py:76
  73.3 1.9 %collective-permute-start.8 = (bf16[272,1024]{1,0:T(8,128)(2,1)S(1)}, bf16[272,1024]{1,0:T(8,128)(2,1)S(1)}, u32[]{:S(2)}, u32[]{:S(2)}) collective-permute-start(bf16[272,1024]{1,0:T(8,128)(2,1)S(1)} %collective-permute-done.7), channel_id=1, source_target_pairs={{0,8},{8,0},{16,24},{24,16},{32,40},{40,32},{48,56},{56,48},{64,72... | collective-permute-start | bytes 1671176 | tf_op jit(solution)/shard_map/ppermute | solution.py:76
  75.3 2.9 %collective-permute-start.11 = (bf16[272,1024]{1,0:T(8,128)(2,1)S(1)}, bf16[272,1024]{1,0:T(8,128)(2,1)S(1)}, u32[]{:S(2)}, u32[]{:S(2)}) collective-permute-start(bf16[272,1024]{1,0:T(8,128)(2,1)S(1)} %collective-permute-done.3.refs_3_), channel_id=1, source_target_pairs={{0,1},{1,2},{2,3},{3,4},{4,5},{5,6},{6,7},{7,0},{8,15},{9,8},{10,9... | collective-permute-start | bytes 1671176 | tf_op jit(solution)/shard_map/ppermute | solution.py:77
  78.2 3.8 %collective-permute-start.10 = (bf16[272,1024]{1,0:T(8,128)(2,1)S(1)}, bf16[272,1024]{1,0:T(8,128)(2,1)S(1)}, u32[]{:S(2)}, u32[]{:S(2)}) collective-permute-start(bf16[272,1024]{1,0:T(8,128)(2,1)S(1)} %collective-permute-done.9), channel_id=1, source_target_pairs={{0,8},{8,0},{16,24},{24,16},{32,40},{40,32},{48,56},{56,48},{64,72... | collective-permute-start | bytes 1671176 | tf_op jit(solution)/shard_map/ppermute | solution.py:76
  82.0 2.0 %collective-permute-start.22 = (bf16[1024,256]{1,0:T(8,128)(2,1)S(1)}, bf16[1024,256]{1,0:T(8,128)(2,1)S(1)}, u32[]{:S(2)}, u32[]{:S(2)}) collective-permute-start(bf16[1024,256]{1,0:T(8,128)(2,1)S(1)} %collective-permute-done.14.refs_11_), channel_id=1, source_target_pairs={{0,64},{8,456},{16,80},{24,472},{32,96},{40,488},{48,112},{56,504}... | collective-permute-start | bytes 1572872 | tf_op jit(solution)/shard_map/ppermute | solution.py:77
  84.0 2.1 %collective-permute-start.21 = (bf16[1024,256]{1,0:T(8,128)(2,1)S(1)}, bf16[1024,256]{1,0:T(8,128)(2,1)S(1)}, u32[]{:S(2)}, u32[]{:S(2)}) collective-permute-start(bf16[1024,256]{1,0:T(8,128)(2,1)S(1)} %collective-permute-done.20), channel_id=1, source_target_pairs={{0,8},{8,0},{16,24},{24,16},{32,40},{40,32},{48,56},{56,48},{64,72... | collective-permute-start | bytes 1572872 | tf_op jit(solution)/shard_map/ppermute | solution.py:76
  86.2 6.1 %collective-permute-done.22.refs_15_ = bf16[1024,256]{1,0:T(8,128)(2,1)S(1)} collective-permute-done((bf16[1024,256]{1,0:T(8,128)(2,1)S(1)}, bf16[1024,256]{1,0:T(8,128)(2,1)S(1)}, u32[]{:S(2)}, u32[]{:S(2)}) %collective-permute-start.22) | collective-permute-done | bytes 524320 | tf_op jit(solution)/shard_map/ppermute | solution.py:77
  92.3 0.8 copy-done.24
  93.1 0.8 copy-done.25
  94.0 0.8 copy-done.19
  94.8 6.2 %shard_map.114 = (f32[128,256]{1,0:T(8,128)}, f32[128,256]{1,0:T(8,128)}, bf16[128,64]{1,0:T(8,128)(2,1)}) custom-call(s32[3]{0:T(128)} %copy-done.9, bf16[272,1024]{1,0:T(8,128)(2,1)} %copy-done.11, bf16[272,1024]{1,0:T(8,128)(2,1)} %copy-done.13, bf16[272,1024]{1,0:T(8,128)(2,1)} %copy-done.14, bf16[272,1024]{1,0:T(8,128)(2,1)} %copy-done.16, ...), custom_call_target="tpu_custom_call" | custom-call | tf_op jit(solution)/shard_map/pallas_call | solution.py:220
  101.1 4.3 %collective-permute-start.23 = (f32[128,256]{1,0:T(8,128)}, f32[128,256]{1,0:T(8,128)S(1)}, u32[]{:S(2)}, u32[]{:S(2)}) collective-permute-start(f32[128,256]{1,0:T(8,128)} %get-tuple-element.17), channel_id=1, source_target_pairs={{0,8},{8,0},{16,24},{24,16},{32,40},{40,32},{48,56},{56,48},{64,72... | collective-permute-start | bytes 393224 | tf_op jit(solution)/shard_map/ppermute | solution.py:283
  105.3 1.2 collective-permute-done.23.got_ref
  106.5 0.9 copy-done.5
  107.4 0.8 copy-done.6
  108.2 5.2 %shard_map.115 = (bf16[8,80,128]{2,1,0:T(8,128)(2,1)S(1)}, f32[128,128]{1,0:T(8,128)S(1)}, f32[128,128]{1,0:T(8,128)S(1)}) custom-call(s32[1,8]{1,0:T(1,128)S(1)} %copy-done.10, f32[128,256]{1,0:T(8,128)S(1)} %copy-done.5, f32[128,256]{1,0:T(8,128)S(1)} %collective-permute-done.23.got_ref, bf16[128,64]{1,0:T(8,128)(2,1)S(1)} %copy-done.6, ...), custom_call_target="tpu_custom_call" | custom-call | tf_op jit(solution)/shard_map/pallas_call | solution.py:220
  113.4 12.4 %all_to_all.25.pack_ref = bf16[8,80,128]{2,1,0:T(8,128)(2,1)S(1)} all-to-all(bf16[8,80,128]{2,1,0:T(8,128)(2,1)S(1)} %get-tuple-element.19), channel_id=1, replica_groups=mesh['row'=64,'col'=8] {'col'}, dimensions={0} | all-to-all | bytes 327680 | tf_op jit(solution)/shard_map/all_to_all | solution.py:296
  125.7 0.9 shard_map.116
  126.7 13.1 %all_to_all.26.in_ref = bf16[8,72,256]{2,1,0:T(8,128)(2,1)S(1)} all-to-all(bf16[8,72,256]{2,1,0:T(8,128)(2,1)S(1)} %shard_map.116), channel_id=1, replica_groups={{0,8,16,24,32,40,48,56},{64,72,80,88,96,104,112,120},{128,136,144,152,1..., dimensions={0} | all-to-all | bytes 589824 | tf_op jit(solution)/shard_map/all_to_all | solution.py:302
  139.9 15.6 %all_to_all.27.in_ref = bf16[8,72,256]{2,1,0:T(8,128)(2,1)S(1)} all-to-all(bf16[8,72,256]{2,1,0:T(8,128)(2,1)S(1)} %shard_map.117), channel_id=1, replica_groups={{0,64,128,192,256,320,384,448},{8,72,136,200,264,328,392,456},{16,80,14..., dimensions={0} | all-to-all | bytes 589824 | tf_op jit(solution)/shard_map/all_to_all | solution.py:304
  155.5 12.2 %all_to_all.28.in_ref = bf16[8,72,256]{2,1,0:T(8,128)(2,1)S(1)} all-to-all(bf16[8,72,256]{2,1,0:T(8,128)(2,1)S(1)} %shard_map.118), channel_id=1, replica_groups={{0,8,16,24,32,40,48,56},{64,72,80,88,96,104,112,120},{128,136,144,152,1..., dimensions={0} | all-to-all | bytes 589824 | tf_op jit(solution)/shard_map/all_to_all | solution.py:306
  167.7 0.8 shard_map.119
  (74 shorter events, 0.3 us)
Async XLA Ops:
  0.7 1.0 copy-start
  1.8 10.4 %copy-start.9 = (s32[3]{0:T(128)}, s32[3]{0:T(128)S(1)}, u32[]{:S(2)}) copy-start(s32[3]{0:T(128)S(1)} %pad_add_fusion.pos_ref) | copy-start | bytes 40
  1.8 9.5 %copy-start.26 = (bf16[256,128]{1,0:T(8,128)(2,1)S(1)}, bf16[256,128]{1,0:T(8,128)(2,1)}, u32[]{:S(2)}) copy-start(bf16[256,128]{1,0:T(8,128)(2,1)} %param.13) | copy-start | bytes 196612
  1.8 9.5 %copy-start.27 = (bf16[256,128]{1,0:T(8,128)(2,1)S(1)}, bf16[256,128]{1,0:T(8,128)(2,1)}, u32[]{:S(2)}) copy-start(bf16[256,128]{1,0:T(8,128)(2,1)} %param.12) | copy-start | bytes 196612
  2.5 13.7 %collective-permute-start = (bf16[128,1024]{1,0:T(8,128)(2,1)S(1)}, bf16[128,1024]{1,0:T(8,128)(2,1)S(1)}, u32[]{:S(2)}, u32[]{:S(2)}) collective-permute-start(bf16[128,1024]{1,0:T(8,128)(2,1)S(1)} %get-tuple-element.15), channel_id=1, source_target_pairs={{0,8},{8,0},{16,24},{24,16},{32,40},{40,32},{48,56},{56,48},{64,72... | collective-permute-start | bytes 786440 | tf_op jit(solution)/shard_map/ppermute | solution.py:255
  12.2 3.6 %copy-start.1 = (bf16[128,2048]{1,0:T(8,128)(2,1)S(1)}, bf16[128,2048]{1,0:T(8,128)(2,1)}, u32[]{:S(2)}) copy-start(bf16[128,2048]{1,0:T(8,128)(2,1)} %t_ref.5) | copy-start | bytes 1572868
  12.2 3.6 %copy-start.4 = (bf16[2048,64]{0,1:T(8,128)(2,1)S(1)}, bf16[2048,64]{0,1:T(8,128)(2,1)}, u32[]{:S(2)}) copy-start(bf16[2048,64]{0,1:T(8,128)(2,1)} %param.14) | copy-start | bytes 786436
  12.2 13.2 %all-to-all-start = ((bf16[4,256,256]{2,1,0:T(8,128)(2,1)}), bf16[4,256,256]{2,1,0:T(8,128)(2,1)S(1)}, u32[]{:S(2)}, u32[]{:S(2)}) async-start(bf16[4,256,256]{2,1,0:T(8,128)(2,1)} %broadcast_in_dim.3), calls=%async_computation | async-start | bytes 1048576 | tf_op jit(solution)/shard_map/all_to_all | solution.py:264
  16.2 77.7 %copy-start.11 = (bf16[272,1024]{1,0:T(8,128)(2,1)}, bf16[272,1024]{1,0:T(8,128)(2,1)S(1)}, u32[]{:S(2)}) copy-start(bf16[272,1024]{1,0:T(8,128)(2,1)S(1)} %pad_maximum_fusion.refs_0_) | copy-start | bytes 1671172
  16.2 12.0 %collective-permute-start.4 = (bf16[272,1024]{1,0:T(8,128)(2,1)S(1)}, bf16[272,1024]{1,0:T(8,128)(2,1)S(1)}, u32[]{:S(2)}, u32[]{:S(2)}) collective-permute-start(bf16[272,1024]{1,0:T(8,128)(2,1)S(1)} %pad_maximum_fusion.refs_0_), channel_id=1, source_target_pairs={{0,8},{8,0},{16,24},{24,16},{32,40},{40,32},{48,56},{56,48},{64,72... | collective-permute-start | bytes 1671176 | tf_op jit(solution)/shard_map/ppermute | solution.py:72
  18.2 16.0 %collective-permute-start.1 = (bf16[272,1024]{1,0:T(8,128)(2,1)S(1)}, bf16[272,1024]{1,0:T(8,128)(2,1)S(1)}, u32[]{:S(2)}, u32[]{:S(2)}) collective-permute-start(bf16[272,1024]{1,0:T(8,128)(2,1)S(1)} %pad_maximum_fusion.refs_0_), channel_id=1, source_target_pairs={{0,1},{1,2},{2,3},{3,4},{4,5},{5,6},{6,7},{7,0},{8,15},{9,8},{10,9... | collective-permute-start | bytes 1671176 | tf_op jit(solution)/shard_map/ppermute | solution.py:74
  25.4 68.6 %copy-start.12 = (bf16[4,256,256]{2,1,0:T(8,128)(2,1)}, bf16[4,256,256]{2,1,0:T(8,128)(2,1)S(1)}, u32[]{:S(2)}) copy-start(bf16[4,256,256]{2,1,0:T(8,128)(2,1)S(1)} %all-to-all-done) | copy-start | bytes 1572868
  25.4 81.1 %copy-start.2 = (bf16[128,2048]{1,0:T(8,128)(2,1)S(1)}, bf16[128,2048]{1,0:T(8,128)(2,1)}, u32[]{:S(2)}) copy-start(bf16[128,2048]{1,0:T(8,128)(2,1)} %q_ref.1) | copy-start | bytes 1572868
  25.4 81.1 %copy-start.3 = (bf16[128,2048]{1,0:T(8,128)(2,1)S(1)}, bf16[128,2048]{1,0:T(8,128)(2,1)}, u32[]{:S(2)}) copy-start(bf16[128,2048]{1,0:T(8,128)(2,1)} %p_ref.1) | copy-start | bytes 1572868
  25.4 81.1 %copy-start.7 = (bf16[64,128]{1,0:T(8,128)(2,1)S(1)}, bf16[64,128]{1,0:T(8,128)(2,1)}, u32[]{:S(2)}) copy-start(bf16[64,128]{1,0:T(8,128)(2,1)} %upk_ref.1) | copy-start | bytes 49156
  25.4 81.1 %copy-start.8 = (bf16[64,128]{1,0:T(8,128)(2,1)S(1)}, bf16[64,128]{1,0:T(8,128)(2,1)}, u32[]{:S(2)}) copy-start(bf16[64,128]{1,0:T(8,128)(2,1)} %upv_ref.1) | copy-start | bytes 49156
  25.4 81.1 %copy-start.10 = (s32[1,8]{1,0:T(1,128)S(1)}, s32[1,8]{1,0:T(1,128)}, u32[]{:S(2)}) copy-start(s32[1,8]{1,0:T(1,128)} %lengths_ref.3) | copy-start | bytes 100
  25.4 16.0 %collective-permute-start.15 = (bf16[1024,256]{1,0:T(8,128)(2,1)S(1)}, bf16[1024,256]{1,0:T(8,128)(2,1)S(1)}, u32[]{:S(2)}, u32[]{:S(2)}) collective-permute-start(bf16[1024,256]{1,0:T(8,128)(2,1)S(1)} %bitcast.7), channel_id=1, source_target_pairs={{0,8},{8,0},{16,24},{24,16},{32,40},{40,32},{48,56},{56,48},{64,72... | collective-permute-start | bytes 1572872 | tf_op jit(solution)/shard_map/ppermute | solution.py:72
  28.3 16.2 %collective-permute-start.5 = (bf16[272,1024]{1,0:T(8,128)(2,1)S(1)}, bf16[272,1024]{1,0:T(8,128)(2,1)S(1)}, u32[]{:S(2)}, u32[]{:S(2)}) collective-permute-start(bf16[272,1024]{1,0:T(8,128)(2,1)S(1)} %collective-permute-done.4), channel_id=1, source_target_pairs={{0,1},{1,2},{2,3},{3,4},{4,5},{5,6},{6,7},{7,0},{8,15},{9,8},{10,9... | collective-permute-start | bytes 1671176 | tf_op jit(solution)/shard_map/ppermute | solution.py:75
  34.2 59.8 %copy-start.13 = (bf16[272,1024]{1,0:T(8,128)(2,1)}, bf16[272,1024]{1,0:T(8,128)(2,1)S(1)}, u32[]{:S(2)}) copy-start(bf16[272,1024]{1,0:T(8,128)(2,1)S(1)} %collective-permute-done.1.refs_1_) | copy-start | bytes 1671172
  34.2 18.5 %collective-permute-start.2 = (bf16[272,1024]{1,0:T(8,128)(2,1)S(1)}, bf16[272,1024]{1,0:T(8,128)(2,1)S(1)}, u32[]{:S(2)}, u32[]{:S(2)}) collective-permute-start(bf16[272,1024]{1,0:T(8,128)(2,1)S(1)} %collective-permute-done.1.refs_1_), channel_id=1, source_target_pairs={{0,1},{1,2},{2,3},{3,4},{4,5},{5,6},{6,7},{7,0},{8,15},{9,8},{10,9... | collective-permute-start | bytes 1671176 | tf_op jit(solution)/shard_map/ppermute | solution.py:74
  36.4 12.2 %collective-permute-start.12 = (bf16[1024,256]{1,0:T(8,128)(2,1)S(1)}, bf16[1024,256]{1,0:T(8,128)(2,1)S(1)}, u32[]{:S(2)}, u32[]{:S(2)}) collective-permute-start(bf16[1024,256]{1,0:T(8,128)(2,1)S(1)} %bitcast.8), channel_id=1, source_target_pairs={{0,64},{8,456},{16,80},{24,472},{32,96},{40,488},{48,112},{56,504}... | collective-permute-start | bytes 1572872 | tf_op jit(solution)/shard_map/ppermute | solution.py:74
  41.5 14.3 %collective-permute-start.16 = (bf16[1024,256]{1,0:T(8,128)(2,1)S(1)}, bf16[1024,256]{1,0:T(8,128)(2,1)S(1)}, u32[]{:S(2)}, u32[]{:S(2)}) collective-permute-start(bf16[1024,256]{1,0:T(8,128)(2,1)S(1)} %collective-permute-done.15), channel_id=1, source_target_pairs={{0,64},{8,456},{16,80},{24,472},{32,96},{40,488},{48,112},{56,504}... | collective-permute-start | bytes 1572872 | tf_op jit(solution)/shard_map/ppermute | solution.py:75
  44.5 14.3 %collective-permute-start.7 = (bf16[272,1024]{1,0:T(8,128)(2,1)S(1)}, bf16[272,1024]{1,0:T(8,128)(2,1)S(1)}, u32[]{:S(2)}, u32[]{:S(2)}) collective-permute-start(bf16[272,1024]{1,0:T(8,128)(2,1)S(1)} %collective-permute-done.5), channel_id=1, source_target_pairs={{0,1},{1,2},{2,3},{3,4},{4,5},{5,6},{6,7},{7,0},{8,15},{9,8},{10,9... | collective-permute-start | bytes 1671176 | tf_op jit(solution)/shard_map/ppermute | solution.py:75
  46.7 17.7 %collective-permute-start.6 = (bf16[272,1024]{1,0:T(8,128)(2,1)S(1)}, bf16[272,1024]{1,0:T(8,128)(2,1)S(1)}, u32[]{:S(2)}, u32[]{:S(2)}) collective-permute-start(bf16[272,1024]{1,0:T(8,128)(2,1)S(1)} %collective-permute-done.5), channel_id=1, source_target_pairs={{0,8},{8,0},{16,24},{24,16},{32,40},{40,32},{48,56},{56,48},{64,72... | collective-permute-start | bytes 1671176 | tf_op jit(solution)/shard_map/ppermute | solution.py:76
  48.6 45.4 %copy-start.20 = (bf16[1024,256]{1,0:T(8,128)(2,1)}, bf16[1024,256]{1,0:T(8,128)(2,1)S(1)}, u32[]{:S(2)}) copy-start(bf16[1024,256]{1,0:T(8,128)(2,1)S(1)} %collective-permute-done.12.refs_9_) | copy-start | bytes 1572868
  48.6 12.6 %collective-permute-start.13 = (bf16[1024,256]{1,0:T(8,128)(2,1)S(1)}, bf16[1024,256]{1,0:T(8,128)(2,1)S(1)}, u32[]{:S(2)}, u32[]{:S(2)}) collective-permute-start(bf16[1024,256]{1,0:T(8,128)(2,1)S(1)} %collective-permute-done.12.refs_9_), channel_id=1, source_target_pairs={{0,64},{8,456},{16,80},{24,472},{32,96},{40,488},{48,112},{56,504}... | collective-permute-start | bytes 1572872 | tf_op jit(solution)/shard_map/ppermute | solution.py:74
  52.7 41.3 %copy-start.14 = (bf16[272,1024]{1,0:T(8,128)(2,1)}, bf16[272,1024]{1,0:T(8,128)(2,1)S(1)}, u32[]{:S(2)}) copy-start(bf16[272,1024]{1,0:T(8,128)(2,1)S(1)} %collective-permute-done.2.refs_2_) | copy-start | bytes 1671172
  52.7 17.6 %collective-permute-start.3 = (bf16[272,1024]{1,0:T(8,128)(2,1)S(1)}, bf16[272,1024]{1,0:T(8,128)(2,1)S(1)}, u32[]{:S(2)}, u32[]{:S(2)}) collective-permute-start(bf16[272,1024]{1,0:T(8,128)(2,1)S(1)} %collective-permute-done.2.refs_2_), channel_id=1, source_target_pairs={{0,1},{1,2},{2,3},{3,4},{4,5},{5,6},{6,7},{7,0},{8,15},{9,8},{10,9... | collective-permute-start | bytes 1671176 | tf_op jit(solution)/shard_map/ppermute | solution.py:74
  55.8 11.5 %collective-permute-start.18 = (bf16[1024,256]{1,0:T(8,128)(2,1)S(1)}, bf16[1024,256]{1,0:T(8,128)(2,1)S(1)}, u32[]{:S(2)}, u32[]{:S(2)}) collective-permute-start(bf16[1024,256]{1,0:T(8,128)(2,1)S(1)} %collective-permute-done.16), channel_id=1, source_target_pairs={{0,64},{8,456},{16,80},{24,472},{32,96},{40,488},{48,112},{56,504}... | collective-permute-start | bytes 1572872 | tf_op jit(solution)/shard_map/ppermute | solution.py:75
  58.8 19.4 %collective-permute-start.9 = (bf16[272,1024]{1,0:T(8,128)(2,1)S(1)}, bf16[272,1024]{1,0:T(8,128)(2,1)S(1)}, u32[]{:S(2)}, u32[]{:S(2)}) collective-permute-start(bf16[272,1024]{1,0:T(8,128)(2,1)S(1)} %collective-permute-done.7), channel_id=1, source_target_pairs={{0,1},{1,2},{2,3},{3,4},{4,5},{5,6},{6,7},{7,0},{8,15},{9,8},{10,9... | collective-permute-start | bytes 1671176 | tf_op jit(solution)/shard_map/ppermute | solution.py:75
  61.2 32.7 %copy-start.21 = (bf16[1024,256]{1,0:T(8,128)(2,1)}, bf16[1024,256]{1,0:T(8,128)(2,1)S(1)}, u32[]{:S(2)}) copy-start(bf16[1024,256]{1,0:T(8,128)(2,1)S(1)} %collective-permute-done.13.refs_10_) | copy-start | bytes 1572868
  61.2 12.0 %collective-permute-start.17 = (bf16[1024,256]{1,0:T(8,128)(2,1)S(1)}, bf16[1024,256]{1,0:T(8,128)(2,1)}, u32[]{:S(2)}, u32[]{:S(2)}) collective-permute-start(bf16[1024,256]{1,0:T(8,128)(2,1)S(1)} %collective-permute-done.16), channel_id=1, source_target_pairs={{0,8},{8,0},{16,24},{24,16},{32,40},{40,32},{48,56},{56,48},{64,72... | collective-permute-start | bytes 1572872 | tf_op jit(solution)/shard_map/ppermute | solution.py:76
  64.4 29.6 %copy-start.15 = (bf16[272,1024]{1,0:T(8,128)(2,1)}, bf16[272,1024]{1,0:T(8,128)(2,1)S(1)}, u32[]{:S(2)}) copy-start(bf16[272,1024]{1,0:T(8,128)(2,1)S(1)} %collective-permute-done.6.refs_4_) | copy-start | bytes 1671172
  64.4 10.8 %collective-permute-start.14 = (bf16[1024,256]{1,0:T(8,128)(2,1)S(1)}, bf16[1024,256]{1,0:T(8,128)(2,1)S(1)}, u32[]{:S(2)}, u32[]{:S(2)}) collective-permute-start(bf16[1024,256]{1,0:T(8,128)(2,1)S(1)} %collective-permute-done.13.refs_10_), channel_id=1, source_target_pairs={{0,64},{8,456},{16,80},{24,472},{32,96},{40,488},{48,112},{56,504}... | collective-permute-start | bytes 1572872 | tf_op jit(solution)/shard_map/ppermute | solution.py:74
  67.3 14.7 %collective-permute-start.20 = (bf16[1024,256]{1,0:T(8,128)(2,1)S(1)}, bf16[1024,256]{1,0:T(8,128)(2,1)S(1)}, u32[]{:S(2)}, u32[]{:S(2)}) collective-permute-start(bf16[1024,256]{1,0:T(8,128)(2,1)S(1)} %collective-permute-done.18), channel_id=1, source_target_pairs={{0,64},{8,456},{16,80},{24,472},{32,96},{40,488},{48,112},{56,504}... | collective-permute-start | bytes 1572872 | tf_op jit(solution)/shard_map/ppermute | solution.py:75
  70.3 23.7 %copy-start.16 = (bf16[272,1024]{1,0:T(8,128)(2,1)}, bf16[272,1024]{1,0:T(8,128)(2,1)S(1)}, u32[]{:S(2)}) copy-start(bf16[272,1024]{1,0:T(8,128)(2,1)S(1)} %collective-permute-done.3.refs_3_) | copy-start | bytes 1671172
  70.3 13.7 %collective-permute-start.19 = (bf16[1024,256]{1,0:T(8,128)(2,1)S(1)}, bf16[1024,256]{1,0:T(8,128)(2,1)S(1)}, u32[]{:S(2)}, u32[]{:S(2)}) collective-permute-start(bf16[1024,256]{1,0:T(8,128)(2,1)S(1)} %collective-permute-done.18), channel_id=1, source_target_pairs={{0,8},{8,0},{16,24},{24,16},{32,40},{40,32},{48,56},{56,48},{64,72... | collective-permute-start | bytes 1572872 | tf_op jit(solution)/shard_map/ppermute | solution.py:76
  73.3 19.0 %collective-permute-start.8 = (bf16[272,1024]{1,0:T(8,128)(2,1)S(1)}, bf16[272,1024]{1,0:T(8,128)(2,1)S(1)}, u32[]{:S(2)}, u32[]{:S(2)}) collective-permute-start(bf16[272,1024]{1,0:T(8,128)(2,1)S(1)} %collective-permute-done.7), channel_id=1, source_target_pairs={{0,8},{8,0},{16,24},{24,16},{32,40},{40,32},{48,56},{56,48},{64,72... | collective-permute-start | bytes 1671176 | tf_op jit(solution)/shard_map/ppermute | solution.py:76
  75.2 17.0 %copy-start.22 = (bf16[1024,256]{1,0:T(8,128)(2,1)}, bf16[1024,256]{1,0:T(8,128)(2,1)S(1)}, u32[]{:S(2)}) copy-start(bf16[1024,256]{1,0:T(8,128)(2,1)S(1)} %collective-permute-done.14.refs_11_) | copy-start | bytes 1572868
  75.3 17.0 %collective-permute-start.11 = (bf16[272,1024]{1,0:T(8,128)(2,1)S(1)}, bf16[272,1024]{1,0:T(8,128)(2,1)S(1)}, u32[]{:S(2)}, u32[]{:S(2)}) collective-permute-start(bf16[272,1024]{1,0:T(8,128)(2,1)S(1)} %collective-permute-done.3.refs_3_), channel_id=1, source_target_pairs={{0,1},{1,2},{2,3},{3,4},{4,5},{5,6},{6,7},{7,0},{8,15},{9,8},{10,9... | collective-permute-start | bytes 1671176 | tf_op jit(solution)/shard_map/ppermute | solution.py:77
  78.2 15.7 %collective-permute-start.10 = (bf16[272,1024]{1,0:T(8,128)(2,1)S(1)}, bf16[272,1024]{1,0:T(8,128)(2,1)S(1)}, u32[]{:S(2)}, u32[]{:S(2)}) collective-permute-start(bf16[272,1024]{1,0:T(8,128)(2,1)S(1)} %collective-permute-done.9), channel_id=1, source_target_pairs={{0,8},{8,0},{16,24},{24,16},{32,40},{40,32},{48,56},{56,48},{64,72... | collective-permute-start | bytes 1671176 | tf_op jit(solution)/shard_map/ppermute | solution.py:76
  82.0 10.2 %collective-permute-start.22 = (bf16[1024,256]{1,0:T(8,128)(2,1)S(1)}, bf16[1024,256]{1,0:T(8,128)(2,1)S(1)}, u32[]{:S(2)}, u32[]{:S(2)}) collective-permute-start(bf16[1024,256]{1,0:T(8,128)(2,1)S(1)} %collective-permute-done.14.refs_11_), channel_id=1, source_target_pairs={{0,64},{8,456},{16,80},{24,472},{32,96},{40,488},{48,112},{56,504}... | collective-permute-start | bytes 1572872 | tf_op jit(solution)/shard_map/ppermute | solution.py:77
  84.0 8.3 %copy-start.23 = (bf16[1024,256]{1,0:T(8,128)(2,1)}, bf16[1024,256]{1,0:T(8,128)(2,1)S(1)}, u32[]{:S(2)}) copy-start(bf16[1024,256]{1,0:T(8,128)(2,1)S(1)} %collective-permute-done.19.refs_13_) | copy-start | bytes 1572868
  84.0 8.3 %collective-permute-start.21 = (bf16[1024,256]{1,0:T(8,128)(2,1)S(1)}, bf16[1024,256]{1,0:T(8,128)(2,1)S(1)}, u32[]{:S(2)}, u32[]{:S(2)}) collective-permute-start(bf16[1024,256]{1,0:T(8,128)(2,1)S(1)} %collective-permute-done.20), channel_id=1, source_target_pairs={{0,8},{8,0},{16,24},{24,16},{32,40},{40,32},{48,56},{56,48},{64,72... | collective-permute-start | bytes 1572872 | tf_op jit(solution)/shard_map/ppermute | solution.py:76
  92.3 1.8 %copy-start.17 = (bf16[272,1024]{1,0:T(8,128)(2,1)}, bf16[272,1024]{1,0:T(8,128)(2,1)S(1)}, u32[]{:S(2)}) copy-start(bf16[272,1024]{1,0:T(8,128)(2,1)S(1)} %collective-permute-done.8.refs_5_) | copy-start | bytes 1671172
  92.3 1.7 %copy-start.18 = (bf16[272,1024]{1,0:T(8,128)(2,1)}, bf16[272,1024]{1,0:T(8,128)(2,1)S(1)}, u32[]{:S(2)}) copy-start(bf16[272,1024]{1,0:T(8,128)(2,1)S(1)} %collective-permute-done.11.refs_7_) | copy-start | bytes 1671172
  101.1 5.4 %collective-permute-start.23 = (f32[128,256]{1,0:T(8,128)}, f32[128,256]{1,0:T(8,128)S(1)}, u32[]{:S(2)}, u32[]{:S(2)}) collective-permute-start(f32[128,256]{1,0:T(8,128)} %get-tuple-element.17), channel_id=1, source_target_pairs={{0,8},{8,0},{16,24},{24,16},{32,40},{40,32},{48,56},{56,48},{64,72... | collective-permute-start | bytes 393224 | tf_op jit(solution)/shard_map/ppermute | solution.py:283
  (5 other events, 4.2 us)

commit v6 on v5

--- a/solution.py
+++ b/solution.py
@@ -43,14 +43,17 @@
     return ids
 
 
-def split_kernel(pos_ref, t_ref, mine_ref, theirs_ref, sem):
+def spread_kernel(pos_ref, t_ref, out_ref, sem):
     copies = []
-    for i in range(t_ref.shape[1] // 512):
-        to = pl.ds(i * 256, 256)
-        for k, ref in enumerate((mine_ref, theirs_ref)):
-            core = lax.rem(pos_ref[0] + k, 2)
-            at = pl.ds(pl.multiple_of(i * 512 + core * 256, 256), 256)
-            copies.append(pltpu.make_async_copy(t_ref.at[:, at], ref.at[:, to], sem.at[2 * i + k]))
+    for slot in range(4):
+        for i in range(2):
+            x = slot // 2 + 2 * lax.rem(pos_ref[3] + i, 2)
+            at = pl.ds(pl.multiple_of(x * 512 + slot % 2 * 256, 256), 256)
+            copies.append(
+                pltpu.make_async_copy(
+                    t_ref.at[:, at], out_ref.at[slot, :, pl.ds(i * 256, 256)], sem.at[2 * slot + i]
+                )
+            )
     for c in copies:
         c.start()
     for c in copies:
@@ -78,36 +81,34 @@
 
 
 def project_kernel(pos_ref, *refs):
-    t_refs, w_refs, refs = refs[:8], refs[8:16], refs[16:]
-    own_ref, other_ref, low_ref, t_scr, w_scr, sem = refs
+    t_refs, (w_ref, out_ref, low_ref, t_scr, w_scr, t_sem, w_sem) = refs[:8], refs[8:]
     n = t_scr.shape[0]
+    slots, rows, wide = out_ref.shape
     way = 2 * pos_ref[0] - 1
-    copies = []
-    for at, (parts, scr) in enumerate(((t_refs, t_scr), (w_refs, w_scr))):
-        for j, step in enumerate(STEPS):
-            k = lax.rem(pos_ref[1 + at] + step * way + n, n)
-            copies.append(pltpu.make_async_copy(parts[j], scr.at[k], sem.at[at, j]))
+    copies = [pltpu.make_async_copy(w_ref, w_scr, w_sem)]
+    for j, step in enumerate(STEPS):
+        k = lax.rem(pos_ref[1] + step * way + n, n)
+        copies.append(pltpu.make_async_copy(t_refs[j], t_scr.at[k], t_sem.at[j]))
     for c in copies:
         c.start()
     for c in copies:
         c.wait()
-    rows = own_ref.shape[0]
-    total = jnp.zeros((2 * rows, w_scr.shape[2]), F32)
-    low = jnp.zeros((t_scr.shape[1] - 2 * rows, t_scr.shape[2]), F32)
+    total = jnp.zeros((slots * rows, wide), F32)
+    low = jnp.zeros((t_scr.shape[1] - slots * rows, t_scr.shape[2]), F32)
     for k in range(n):
-        total = total + mm(t_scr[k, pl.ds(0, 2 * rows)], w_scr[k], NN)
-        low = low + t_scr[k, pl.ds(2 * rows, low.shape[0])].astype(F32)
-    own_ref[...] = total[:rows]
-    other_ref[...] = total[rows:]
+        total = total + mm(t_scr[k, pl.ds(0, slots * rows)], w_scr[k], NN)
+        low = low + t_scr[k, pl.ds(slots * rows, low.shape[0])].astype(F32)
+    for i in range(slots):
+        out_ref[i] = total[i * rows:(i + 1) * rows].astype(BF)
     low = low[:low.shape[0] // 2] + low[low.shape[0] // 2:]
     low_ref[...] = unfold(low, low_ref.shape[1]).astype(BF)
 
 
 def attend_kernel(
-    lengths_ref, own_ref, got_ref, low_ref, upk_ref, upv_ref, q_ref, p_ref,
+    lengths_ref, full_ref, low_ref, upk_ref, upv_ref, q_ref, p_ref,
     pack_ref, gk_ref, gv_ref, q_scr, p_scr, sem,
 ):
-    rows = own_ref.shape[0]
+    rows = q_ref.shape[0]
     heads = q_ref.shape[1] // HD
     batch = 4
     copies = []
@@ -120,7 +121,9 @@
     score_scale = HD ** (-0.5)
     probe_scale = (q_ref.shape[1] * pack_ref.shape[0]) ** (-0.5)
     low_half = low_ref[...]
-    full = own_ref[...] + got_ref[...]
+    full = full_ref[0].astype(F32)
+    for i in range(1, full_ref.shape[0]):
+        full = full + full_ref[i].astype(F32)
     key_full, value_full = full[:, :HD], full[:, HD:]
     key_pol = (key_full + mm(low_half, upk_ref[...], NN)).astype(BF)
     value_pol = (value_full + mm(low_half, upv_ref[...], NN)).astype(BF)
@@ -230,14 +233,13 @@
 def on_device(tokens, queries, probes, w_key, w_value, down_proj, up_key, up_value, lengths):
     rows, feats = tokens.shape
     row_at = lax.axis_index("row")
-    pos = jnp.stack([row_at % 2, lax.axis_index("col"), row_at // 8]).astype(jnp.int32)
+    pos = jnp.stack([row_at % 2, lax.axis_index("col"), row_at // 8, row_at // 4 % 2]).astype(jnp.int32)
 
     def place(y, x, core):
         return ((y % 8) * 4 + x % 4) * 2 + core % 2
 
     sites = [(y, x, core) for y in range(8) for x in range(4) for core in range(2)]
     swap = [(place(y, x, c), place(y, x, 1 - c)) for y, x, c in sites]
-    y_fore = [(place(y, x, c), place(y + 1 - 2 * c, x, c)) for y, x, c in sites]
     z_fore = [
         (place(y, x, c) * 8 + z, place(y, x, c) * 8 + (z + 1 - 2 * c) % 8)
         for y, x, c in sites
@@ -245,48 +247,53 @@
     ]
     y_lines = [[place(y, x, c) for y in range(8)] for x in range(4) for c in range(2)]
     squares = [[place(y, x, c) for x in range(4) for c in range(2)] for y in range(8)]
-    x_lines = [[place(y, x, c) for x in range(4)] for y in range(8) for c in range(2)]
-
-    half = (rows, feats // 2)
-    mine, theirs = call(
-        split_kernel, [(half, BF), (half, BF)], [SMEM, HBM], [VMEM, VMEM], pos, tokens,
-        scratch=[pltpu.SemaphoreType.DMA((feats // 256,))],
-    )
-    swapped = lax.ppermute(theirs, "row", swap)
+    pairs = [
+        [place(y, 2 * h + x, c) for x in range(2) for c in range(2)]
+        for y in range(8)
+        for h in range(2)
+    ]
+    across = [(place(y, x, c), place(y, x + 2, c)) for y, x, c in sites]
+
+    quarter = feats // 4
+    (spread,) = call(
+        spread_kernel, [((4, rows, quarter), BF)], [SMEM, HBM], [VMEM], pos, tokens,
+        scratch=[pltpu.SemaphoreType.DMA((8,))],
+    )
+    paired = lax.all_to_all(spread, "row", 0, 0, axis_index_groups=pairs)
     (low_part,) = call(
-        low_kernel, [((16, feats // 2), BF)], [VMEM, VMEM], [VMEM], tokens, down_proj.T
-    )
-    pair = jnp.concatenate([mine, swapped, low_part], axis=0)
-    t_parts = ring_of(pair, ("row", "col"), z_fore, swap)
+        low_kernel, [((32, quarter), BF)], [VMEM, VMEM], [VMEM], tokens, down_proj.T
+    )
+    block = jnp.concatenate([paired.reshape(4 * rows, quarter), low_part], axis=0)
+    t_parts = ring_of(block, ("row", "col"), z_fore, swap)
 
     w_both = jnp.concatenate([w_key, w_value], axis=1)
     wide = w_both.shape[1]
-    w_line = lax.all_to_all(
-        jnp.broadcast_to(w_both, (4,) + w_both.shape), "row", 0, 0, axis_index_groups=x_lines
-    )
-    w_own = w_line.reshape(feats // 2, wide)
-    w_parts = ring_of(w_own, "row", y_fore, swap)
-
-    own, other, low_half = call(
+    w_own = jnp.concatenate([w_both, lax.ppermute(w_both, "row", across)], axis=0)
+    w_all = lax.all_to_all(
+        jnp.broadcast_to(w_own, (8,) + w_own.shape), "row", 0, 0, axis_index_groups=y_lines
+    )
+
+    shares, low_half = call(
         project_kernel,
-        [((rows, wide), F32), ((rows, wide), F32), ((rows, 64), BF)],
-        [SMEM] + [HBM] * 16,
-        [VMEM] * 3,
-        pos, *t_parts, *w_parts,
+        [((4, rows, wide), BF), ((rows, 64), BF)],
+        [SMEM] + [HBM] * 9,
+        [VMEM] * 2,
+        pos, *t_parts, w_all,
         scratch=[
-            pltpu.VMEM((8, 2 * rows + 16, feats // 2), BF),
-            pltpu.VMEM((8, feats // 2, wide), BF),
-            pltpu.SemaphoreType.DMA((2, 8)),
+            pltpu.VMEM((8,) + block.shape, BF),
+            pltpu.VMEM(w_all.shape, BF),
+            pltpu.SemaphoreType.DMA((8,)),
+            pltpu.SemaphoreType.DMA,
         ],
         mib=56,
     )
-    got = lax.ppermute(other, "row", swap)
+    full_parts = lax.all_to_all(shares, "row", 0, 0, axis_index_groups=pairs)
     pack, gk, gv = call(
         attend_kernel,
         [((8, 80, 128), BF), ((rows, HD), F32), ((rows, HD), F32)],
-        [SMEM] + [VMEM] * 5 + [HBM] * 2,
+        [SMEM] + [VMEM] * 4 + [HBM] * 2,
         [VMEM] * 3,
-        lengths, own, got, low_half, up_key, up_value, queries, probes,
+        lengths, full_parts, low_half, up_key, up_value, queries, probes,
         scratch=[
             pltpu.VMEM((rows, feats), BF),
             pltpu.VMEM((rows, feats), BF),

time: 170 us -> 168 us (0.988)
  starting transfers between devices: 85 us -> 65 us
  blocking collectives: 53.3 us -> 63.7 us
  waiting for transfers between devices: 8.43 us -> 17.4 us
    all_to_all x1 -> x2, starting transfers between devices: 3.6 us -> 15.4 us  [the longest x1 10.3 us: on_device(): paired = lax.all_to_all(spread, 'row', 0, 0, axis_index_groups=pairs)]
    ppermute x2 -> x1, starting transfers between devices: 13 us -> 1.92 us  [on_device(): lax.ppermute(w_both, 'row', across)]
    all_to_all x0 -> x1, blocking collectives: none -> 10.5 us  [on_device(): full_parts = lax.all_to_all(shares, 'row', 0, 0, axis_index_groups=pairs)]
    ppermute x6 -> x3, starting transfers between devices: 15.9 us -> 7.4 us  [ring_of(): crossed.append(lax.ppermute(far, 'row', swap))]
    ppermute x6 -> x3, starting transfers between devices: 19.4 us -> 13 us  [ring_of(): far = lax.ppermute(far, axis, fore)]
    ppermute x2 -> x1, waiting for transfers between devices: 1.18 us -> 6.94 us  [on_device(): lax.ppermute(w_both, 'row', across)]
    ppermute x6 -> x3, waiting for transfers between devices: 0.02 us -> 4.81 us  [ring_of(): near.append(lax.ppermute(near[-1], axis, fore))]
    all_to_all x1, blocking collectives: 15.6 us -> 17.8 us  [on_device(): lax.all_to_all(square, 'row', 0, 0, axis_index_groups=y_lines)]
  transfers between devices with their start and end apart: 25 -> 14, of which waited for: 3 -> 6; matrix products, arithmetic and copies ran while one was open for 1% -> 0% of each run, Pallas kernels for 0% -> 0%
where the time goes in v6:
time: 168 us; the launch traced here: 167 us
  starting transfers between devices  65 us (39%)
  blocking collectives  63.7 us (38%)
  waiting for transfers between devices  17.4 us (10%)
  Pallas kernels  14.4 us (9%)
  local copies, waits for them, and re-layouts  5.04 us (3%)
    ppermute x3, starting transfers between devices, ring_of(): near.append(lax.ppermute(near[-1], axis, fore))  21.5 us
    all_to_all x1, blocking collectives, on_device(): lax.all_to_all(square, 'row', 0, 0, axis_index_groups=y_lines)  17.8 us
    pallas_call x8, Pallas kernels, call(): pl.pallas_call(kernel, out_shape=[jax.ShapeDtypeStruct(s, d) for s, d in...  14.4 us
    ppermute x3, starting transfers between devices, ring_of(): far = lax.ppermute(far, axis, fore)  13 us
    all_to_all x1, blocking collectives, on_device(): term_parts = lax.all_to_all(terms, 'row', 0, 0, axis_index_groups=squares)  12.4 us
    all_to_all x1, blocking collectives, on_device(): pieces = lax.all_to_all(summed, 'row', 0, 0, axis_index_groups=squares)  12.2 us
    all_to_all x1, blocking collectives, on_device(): packs = lax.all_to_all(pack, 'col', 0, 0)  10.9 us
    all_to_all x1, blocking collectives, on_device(): full_parts = lax.all_to_all(shares, 'row', 0, 0, axis_index_groups=pairs)  10.5 us
  transfers between devices with their start and end apart: 14, of which 6 were waited for; matrix products, arithmetic and copies ran while one was open for 0% of the time, Pallas kernels for 0%

profile of v6, /device:TPU:1, one launch (start us, length us, event | category | flops | bytes accessed | tf_op | source)
XLA Modules:
  0.0 166.8 jit_solution(16085298684093631529)
XLA Ops:
  0.7 0.1 pad_add_fusion.pos_ref
  0.8 1.0 copy-done
  1.8 1.5 shard_map.112
  3.3 10.3 %all-to-all-start = ((bf16[4,128,512]{2,1,0:T(8,128)(2,1)}), bf16[4,128,512]{2,1,0:T(8,128)(2,1)S(1)}, u32[]{:S(2)}, u32[]{:S(2)}) async-start(bf16[4,128,512]{2,1,0:T(8,128)(2,1)} %shard_map.112), calls=%async_computation | async-start | bytes 1048576 | tf_op jit(solution)/shard_map/all_to_all | solution.py:262
  13.7 1.9 %collective-permute-start.11 = (bf16[256,256]{1,0:T(8,128)(2,1)S(1)}, bf16[256,256]{1,0:T(8,128)(2,1)S(1)}, u32[]{:S(2)}, u32[]{:S(2)}) collective-permute-start(bf16[256,256]{1,0:T(8,128)(2,1)S(1)} %constant_dynamic-update-slice_fusion), channel_id=1, source_target_pairs={{0,32},{8,40},{16,48},{24,56},{32,0},{40,8},{48,16},{56,24},{64,96... | collective-permute-start | bytes 393224 | tf_op jit(solution)/shard_map/ppermute | solution.py:271
  15.7 6.9 %collective-permute-done.11 = bf16[256,256]{1,0:T(8,128)(2,1)S(1)} collective-permute-done((bf16[256,256]{1,0:T(8,128)(2,1)S(1)}, bf16[256,256]{1,0:T(8,128)(2,1)S(1)}, u32[]{:S(2)}, u32[]{:S(2)}) %collective-permute-start.11) | collective-permute-done | bytes 131104 | tf_op jit(solution)/shard_map/ppermute | solution.py:271
  22.6 1.5 broadcast_in_dim.3
  24.1 5.1 %all-to-all-start.1 = ((bf16[8,512,256]{2,1,0:T(8,128)(2,1)}), bf16[8,512,256]{2,1,0:T(8,128)(2,1)}, u32[]{:S(2)}, u32[]{:S(2)}) async-start(bf16[8,512,256]{2,1,0:T(8,128)(2,1)} %broadcast_in_dim.3), calls=%async_computation.1 | async-start | bytes 4194304 | tf_op jit(solution)/shard_map/all_to_all | solution.py:272
  29.2 0.4 shard_map.113
  29.6 0.0 copy-start.2
  29.6 0.0 copy-start.3
  29.6 0.0 copy-start.6
  29.6 0.0 copy-start.7
  29.6 0.0 copy-start.9
  29.6 2.9 %collective-permute-start.3 = (bf16[544,512]{1,0:T(8,128)(2,1)S(1)}, bf16[544,512]{1,0:T(8,128)(2,1)S(1)}, u32[]{:S(2)}, u32[]{:S(2)}) collective-permute-start(bf16[544,512]{1,0:T(8,128)(2,1)S(1)} %pad_maximum_fusion.refs_0_), channel_id=1, source_target_pairs={{0,8},{8,0},{16,24},{24,16},{32,40},{40,32},{48,56},{56,48},{64,72... | collective-permute-start | bytes 1671176 | tf_op jit(solution)/shard_map/ppermute | solution.py:75
  32.6 10.7 %collective-permute-start = (bf16[544,512]{1,0:T(8,128)(2,1)S(1)}, bf16[544,512]{1,0:T(8,128)(2,1)S(1)}, u32[]{:S(2)}, u32[]{:S(2)}) collective-permute-start(bf16[544,512]{1,0:T(8,128)(2,1)S(1)} %pad_maximum_fusion.refs_0_), channel_id=1, source_target_pairs={{0,1},{1,2},{2,3},{3,4},{4,5},{5,6},{6,7},{7,0},{8,15},{9,8},{10,9... | collective-permute-start | bytes 1671176 | tf_op jit(solution)/shard_map/ppermute | solution.py:77
  43.3 0.0 collective-permute-done.3
  43.3 2.2 %collective-permute-start.4 = (bf16[544,512]{1,0:T(8,128)(2,1)S(1)}, bf16[544,512]{1,0:T(8,128)(2,1)S(1)}, u32[]{:S(2)}, u32[]{:S(2)}) collective-permute-start(bf16[544,512]{1,0:T(8,128)(2,1)S(1)} %collective-permute-done.3), channel_id=1, source_target_pairs={{0,1},{1,2},{2,3},{3,4},{4,5},{5,6},{6,7},{7,0},{8,15},{9,8},{10,9... | collective-permute-start | bytes 1671176 | tf_op jit(solution)/shard_map/ppermute | solution.py:78
  45.5 4.3 %collective-permute-done.refs_1_ = bf16[544,512]{1,0:T(8,128)(2,1)S(1)} collective-permute-done((bf16[544,512]{1,0:T(8,128)(2,1)S(1)}, bf16[544,512]{1,0:T(8,128)(2,1)S(1)}, u32[]{:S(2)}, u32[]{:S(2)}) %collective-permute-start) | collective-permute-done | bytes 557088 | tf_op jit(solution)/shard_map/ppermute | solution.py:77
  49.7 5.4 %collective-permute-start.1 = (bf16[544,512]{1,0:T(8,128)(2,1)S(1)}, bf16[544,512]{1,0:T(8,128)(2,1)S(1)}, u32[]{:S(2)}, u32[]{:S(2)}) collective-permute-start(bf16[544,512]{1,0:T(8,128)(2,1)S(1)} %collective-permute-done.refs_1_), channel_id=1, source_target_pairs={{0,1},{1,2},{2,3},{3,4},{4,5},{5,6},{6,7},{7,0},{8,15},{9,8},{10,9... | collective-permute-start | bytes 1671176 | tf_op jit(solution)/shard_map/ppermute | solution.py:77
  55.1 0.5 collective-permute-done.4
  55.7 5.4 %collective-permute-start.6 = (bf16[544,512]{1,0:T(8,128)(2,1)S(1)}, bf16[544,512]{1,0:T(8,128)(2,1)S(1)}, u32[]{:S(2)}, u32[]{:S(2)}) collective-permute-start(bf16[544,512]{1,0:T(8,128)(2,1)S(1)} %collective-permute-done.4), channel_id=1, source_target_pairs={{0,1},{1,2},{2,3},{3,4},{4,5},{5,6},{6,7},{7,0},{8,15},{9,8},{10,9... | collective-permute-start | bytes 1671176 | tf_op jit(solution)/shard_map/ppermute | solution.py:78
  61.1 0.5 collective-permute-done.1.refs_2_
  61.7 5.4 %collective-permute-start.2 = (bf16[544,512]{1,0:T(8,128)(2,1)S(1)}, bf16[544,512]{1,0:T(8,128)(2,1)S(1)}, u32[]{:S(2)}, u32[]{:S(2)}) collective-permute-start(bf16[544,512]{1,0:T(8,128)(2,1)S(1)} %collective-permute-done.1.refs_2_), channel_id=1, source_target_pairs={{0,1},{1,2},{2,3},{3,4},{4,5},{5,6},{6,7},{7,0},{8,15},{9,8},{10,9... | collective-permute-start | bytes 1671176 | tf_op jit(solution)/shard_map/ppermute | solution.py:77
  67.1 0.5 collective-permute-done.6
  67.6 5.4 %collective-permute-start.8 = (bf16[544,512]{1,0:T(8,128)(2,1)S(1)}, bf16[544,512]{1,0:T(8,128)(2,1)S(1)}, u32[]{:S(2)}, u32[]{:S(2)}) collective-permute-start(bf16[544,512]{1,0:T(8,128)(2,1)S(1)} %collective-permute-done.6), channel_id=1, source_target_pairs={{0,1},{1,2},{2,3},{3,4},{4,5},{5,6},{6,7},{7,0},{8,15},{9,8},{10,9... | collective-permute-start | bytes 1671176 | tf_op jit(solution)/shard_map/ppermute | solution.py:78
  73.0 1.9 %collective-permute-start.5 = (bf16[544,512]{1,0:T(8,128)(2,1)S(1)}, bf16[544,512]{1,0:T(8,128)(2,1)S(1)}, u32[]{:S(2)}, u32[]{:S(2)}) collective-permute-start(bf16[544,512]{1,0:T(8,128)(2,1)S(1)} %collective-permute-done.4), channel_id=1, source_target_pairs={{0,8},{8,0},{16,24},{24,16},{32,40},{40,32},{48,56},{56,48},{64,72... | collective-permute-start | bytes 1671176 | tf_op jit(solution)/shard_map/ppermute | solution.py:79
  75.0 2.4 %collective-permute-start.7 = (bf16[544,512]{1,0:T(8,128)(2,1)S(1)}, bf16[544,512]{1,0:T(8,128)(2,1)S(1)}, u32[]{:S(2)}, u32[]{:S(2)}) collective-permute-start(bf16[544,512]{1,0:T(8,128)(2,1)S(1)} %collective-permute-done.6), channel_id=1, source_target_pairs={{0,8},{8,0},{16,24},{24,16},{32,40},{40,32},{48,56},{56,48},{64,72... | collective-permute-start | bytes 1671176 | tf_op jit(solution)/shard_map/ppermute | solution.py:79
  77.4 0.0 collective-permute-done.2.refs_3_
  77.4 0.8 copy-done.13
  78.2 2.9 %collective-permute-start.10 = (bf16[544,512]{1,0:T(8,128)(2,1)S(1)}, bf16[544,512]{1,0:T(8,128)(2,1)S(1)}, u32[]{:S(2)}, u32[]{:S(2)}) collective-permute-start(bf16[544,512]{1,0:T(8,128)(2,1)S(1)} %collective-permute-done.2.refs_3_), channel_id=1, source_target_pairs={{0,1},{1,2},{2,3},{3,4},{4,5},{5,6},{6,7},{7,0},{8,15},{9,8},{10,9... | collective-permute-start | bytes 1671176 | tf_op jit(solution)/shard_map/ppermute | solution.py:80
  81.1 3.1 %collective-permute-start.9 = (bf16[544,512]{1,0:T(8,128)(2,1)S(1)}, bf16[544,512]{1,0:T(8,128)(2,1)}, u32[]{:S(2)}, u32[]{:S(2)}) collective-permute-start(bf16[544,512]{1,0:T(8,128)(2,1)S(1)} %collective-permute-done.8), channel_id=1, source_target_pairs={{0,8},{8,0},{16,24},{24,16},{32,40},{40,32},{48,56},{56,48},{64,72... | collective-permute-start | bytes 1671176 | tf_op jit(solution)/shard_map/ppermute | solution.py:79
  84.2 0.0 collective-permute-done.5.refs_4_
  84.2 0.0 collective-permute-done.7.refs_5_
  84.2 4.6 %collective-permute-done.10.refs_7_ = bf16[544,512]{1,0:T(8,128)(2,1)S(1)} collective-permute-done((bf16[544,512]{1,0:T(8,128)(2,1)S(1)}, bf16[544,512]{1,0:T(8,128)(2,1)S(1)}, u32[]{:S(2)}, u32[]{:S(2)}) %collective-permute-start.10) | collective-permute-done | bytes 557088 | tf_op jit(solution)/shard_map/ppermute | solution.py:80
  88.8 0.9 copy-done.16
  89.6 0.0 collective-permute-done.9.refs_6_
  89.7 5.5 %shard_map.114 = (bf16[4,128,256]{2,1,0:T(8,128)(2,1)}, bf16[128,64]{1,0:T(8,128)(2,1)}) custom-call(s32[4]{0:T(128)} %copy-done.8, bf16[544,512]{1,0:T(8,128)(2,1)} %copy-done.10, bf16[544,512]{1,0:T(8,128)(2,1)} %copy-done.11, bf16[544,512]{1,0:T(8,128)(2,1)} %copy-done.12, bf16[544,512]{1,0:T(8,128)(2,1)} %copy-done.13, bf16[544,512]{1,0:T(8,128)(2,1)} %copy-done.14, ...), custom_call_target="tpu_custom_call" | custom-call | tf_op jit(solution)/shard_map/pallas_call | solution.py:223
  95.2 10.5 %all_to_all.35.full_ref = bf16[4,128,256]{2,1,0:T(8,128)(2,1)S(1)} all-to-all(bf16[4,128,256]{2,1,0:T(8,128)(2,1)} %get-tuple-element.11), channel_id=1, replica_groups={{0,8,16,24},{32,40,48,56},{64,72,80,88},{96,104,112,120},{128,136,144,1..., dimensions={0} | all-to-all | bytes 524288 | tf_op jit(solution)/shard_map/all_to_all | solution.py:290
  105.7 0.0 copy-start.5
  105.7 0.7 copy-done.5
  106.5 5.1 %shard_map.115 = (bf16[8,80,128]{2,1,0:T(8,128)(2,1)S(1)}, f32[128,128]{1,0:T(8,128)S(1)}, f32[128,128]{1,0:T(8,128)S(1)}) custom-call(s32[1,8]{1,0:T(1,128)S(1)} %copy-done.9, bf16[4,128,256]{2,1,0:T(8,128)(2,1)S(1)} %all_to_all.35.full_ref, bf16[128,64]{1,0:T(8,128)(2,1)S(1)} %copy-done.5, bf16[64,128]{1,0:T(8,128)(2,1)S(1)} %copy-done.6, ...), custom_call_target="tpu_custom_call" | custom-call | tf_op jit(solution)/shard_map/pallas_call | solution.py:223
  111.6 10.9 %all_to_all.36.pack_ref = bf16[8,80,128]{2,1,0:T(8,128)(2,1)S(1)} all-to-all(bf16[8,80,128]{2,1,0:T(8,128)(2,1)S(1)} %get-tuple-element.13), channel_id=1, replica_groups=mesh['row'=64,'col'=8] {'col'}, dimensions={0} | all-to-all | bytes 327680 | tf_op jit(solution)/shard_map/all_to_all | solution.py:303
  122.5 0.9 shard_map.116
  123.5 12.4 %all_to_all.37.in_ref = bf16[8,72,256]{2,1,0:T(8,128)(2,1)S(1)} all-to-all(bf16[8,72,256]{2,1,0:T(8,128)(2,1)S(1)} %shard_map.116), channel_id=1, replica_groups={{0,8,16,24,32,40,48,56},{64,72,80,88,96,104,112,120},{128,136,144,152,1..., dimensions={0} | all-to-all | bytes 589824 | tf_op jit(solution)/shard_map/all_to_all | solution.py:309
  135.9 17.8 %all_to_all.38.in_ref = bf16[8,72,256]{2,1,0:T(8,128)(2,1)S(1)} all-to-all(bf16[8,72,256]{2,1,0:T(8,128)(2,1)S(1)} %shard_map.117), channel_id=1, replica_groups={{0,64,128,192,256,320,384,448},{8,72,136,200,264,328,392,456},{16,80,14..., dimensions={0} | all-to-all | bytes 589824 | tf_op jit(solution)/shard_map/all_to_all | solution.py:311
  153.8 12.2 %all_to_all.39.in_ref = bf16[8,72,256]{2,1,0:T(8,128)(2,1)S(1)} all-to-all(bf16[8,72,256]{2,1,0:T(8,128)(2,1)S(1)} %shard_map.118), channel_id=1, replica_groups={{0,8,16,24,32,40,48,56},{64,72,80,88,96,104,112,120},{128,136,144,152,1..., dimensions={0} | all-to-all | bytes 589824 | tf_op jit(solution)/shard_map/all_to_all | solution.py:313
  165.9 0.8 shard_map.119
  (37 shorter events, 0.2 us)
Async XLA Ops:
  0.6 13.0 %copy-start.17 = (bf16[256,128]{1,0:T(8,128)(2,1)S(1)}, bf16[256,128]{1,0:T(8,128)(2,1)}, u32[]{:S(2)}) copy-start(bf16[256,128]{1,0:T(8,128)(2,1)} %param.12) | copy-start | bytes 196612
  0.8 1.0 copy-start
  1.8 11.9 %copy-start.8 = (s32[4]{0:T(128)}, s32[4]{0:T(128)S(1)}, u32[]{:S(2)}) copy-start(s32[4]{0:T(128)S(1)} %pad_add_fusion.pos_ref) | copy-start | bytes 52
  1.8 11.9 %copy-start.18 = (bf16[256,128]{1,0:T(8,128)(2,1)S(1)}, bf16[256,128]{1,0:T(8,128)(2,1)}, u32[]{:S(2)}) copy-start(bf16[256,128]{1,0:T(8,128)(2,1)} %param.13) | copy-start | bytes 196612
  3.3 19.3 %all-to-all-start = ((bf16[4,128,512]{2,1,0:T(8,128)(2,1)}), bf16[4,128,512]{2,1,0:T(8,128)(2,1)S(1)}, u32[]{:S(2)}, u32[]{:S(2)}) async-start(bf16[4,128,512]{2,1,0:T(8,128)(2,1)} %shard_map.112), calls=%async_computation | async-start | bytes 1048576 | tf_op jit(solution)/shard_map/all_to_all | solution.py:262
  13.7 8.9 %collective-permute-start.11 = (bf16[256,256]{1,0:T(8,128)(2,1)S(1)}, bf16[256,256]{1,0:T(8,128)(2,1)S(1)}, u32[]{:S(2)}, u32[]{:S(2)}) collective-permute-start(bf16[256,256]{1,0:T(8,128)(2,1)S(1)} %constant_dynamic-update-slice_fusion), channel_id=1, source_target_pairs={{0,32},{8,40},{16,48},{24,56},{32,0},{40,8},{48,16},{56,24},{64,96... | collective-permute-start | bytes 393224 | tf_op jit(solution)/shard_map/ppermute | solution.py:271
  24.1 5.1 %copy-start.1 = (bf16[128,2048]{1,0:T(8,128)(2,1)S(1)}, bf16[128,2048]{1,0:T(8,128)(2,1)}, u32[]{:S(2)}) copy-start(bf16[128,2048]{1,0:T(8,128)(2,1)} %t_ref.5) | copy-start | bytes 1572868
  24.1 5.1 %copy-start.4 = (bf16[2048,64]{0,1:T(8,128)(2,1)S(1)}, bf16[2048,64]{0,1:T(8,128)(2,1)}, u32[]{:S(2)}) copy-start(bf16[2048,64]{0,1:T(8,128)(2,1)} %param.14) | copy-start | bytes 786436
  24.1 65.5 %all-to-all-start.1 = ((bf16[8,512,256]{2,1,0:T(8,128)(2,1)}), bf16[8,512,256]{2,1,0:T(8,128)(2,1)}, u32[]{:S(2)}, u32[]{:S(2)}) async-start(bf16[8,512,256]{2,1,0:T(8,128)(2,1)} %broadcast_in_dim.3), calls=%async_computation.1 | async-start | bytes 4194304 | tf_op jit(solution)/shard_map/all_to_all | solution.py:272
  29.6 60.1 %copy-start.10 = (bf16[544,512]{1,0:T(8,128)(2,1)}, bf16[544,512]{1,0:T(8,128)(2,1)S(1)}, u32[]{:S(2)}) copy-start(bf16[544,512]{1,0:T(8,128)(2,1)S(1)} %pad_maximum_fusion.refs_0_) | copy-start | bytes 1671172
  29.6 76.1 %copy-start.2 = (bf16[128,2048]{1,0:T(8,128)(2,1)S(1)}, bf16[128,2048]{1,0:T(8,128)(2,1)}, u32[]{:S(2)}) copy-start(bf16[128,2048]{1,0:T(8,128)(2,1)} %q_ref.1) | copy-start | bytes 1572868
  29.6 76.1 %copy-start.3 = (bf16[128,2048]{1,0:T(8,128)(2,1)S(1)}, bf16[128,2048]{1,0:T(8,128)(2,1)}, u32[]{:S(2)}) copy-start(bf16[128,2048]{1,0:T(8,128)(2,1)} %p_ref.1) | copy-start | bytes 1572868
  29.6 76.1 %copy-start.6 = (bf16[64,128]{1,0:T(8,128)(2,1)S(1)}, bf16[64,128]{1,0:T(8,128)(2,1)}, u32[]{:S(2)}) copy-start(bf16[64,128]{1,0:T(8,128)(2,1)} %upk_ref.1) | copy-start | bytes 49156
  29.6 76.1 %copy-start.7 = (bf16[64,128]{1,0:T(8,128)(2,1)S(1)}, bf16[64,128]{1,0:T(8,128)(2,1)}, u32[]{:S(2)}) copy-start(bf16[64,128]{1,0:T(8,128)(2,1)} %upv_ref.1) | copy-start | bytes 49156
  29.6 76.1 %copy-start.9 = (s32[1,8]{1,0:T(1,128)S(1)}, s32[1,8]{1,0:T(1,128)}, u32[]{:S(2)}) copy-start(s32[1,8]{1,0:T(1,128)} %lengths_ref.3) | copy-start | bytes 100
  29.6 13.6 %collective-permute-start.3 = (bf16[544,512]{1,0:T(8,128)(2,1)S(1)}, bf16[544,512]{1,0:T(8,128)(2,1)S(1)}, u32[]{:S(2)}, u32[]{:S(2)}) collective-permute-start(bf16[544,512]{1,0:T(8,128)(2,1)S(1)} %pad_maximum_fusion.refs_0_), channel_id=1, source_target_pairs={{0,8},{8,0},{16,24},{24,16},{32,40},{40,32},{48,56},{56,48},{64,72... | collective-permute-start | bytes 1671176 | tf_op jit(solution)/shard_map/ppermute | solution.py:75
  32.6 17.1 %collective-permute-start = (bf16[544,512]{1,0:T(8,128)(2,1)S(1)}, bf16[544,512]{1,0:T(8,128)(2,1)S(1)}, u32[]{:S(2)}, u32[]{:S(2)}) collective-permute-start(bf16[544,512]{1,0:T(8,128)(2,1)S(1)} %pad_maximum_fusion.refs_0_), channel_id=1, source_target_pairs={{0,1},{1,2},{2,3},{3,4},{4,5},{5,6},{6,7},{7,0},{8,15},{9,8},{10,9... | collective-permute-start | bytes 1671176 | tf_op jit(solution)/shard_map/ppermute | solution.py:77
  43.3 12.4 %collective-permute-start.4 = (bf16[544,512]{1,0:T(8,128)(2,1)S(1)}, bf16[544,512]{1,0:T(8,128)(2,1)S(1)}, u32[]{:S(2)}, u32[]{:S(2)}) collective-permute-start(bf16[544,512]{1,0:T(8,128)(2,1)S(1)} %collective-permute-done.3), channel_id=1, source_target_pairs={{0,1},{1,2},{2,3},{3,4},{4,5},{5,6},{6,7},{7,0},{8,15},{9,8},{10,9... | collective-permute-start | bytes 1671176 | tf_op jit(solution)/shard_map/ppermute | solution.py:78
  49.7 39.9 %copy-start.11 = (bf16[544,512]{1,0:T(8,128)(2,1)}, bf16[544,512]{1,0:T(8,128)(2,1)S(1)}, u32[]{:S(2)}) copy-start(bf16[544,512]{1,0:T(8,128)(2,1)S(1)} %collective-permute-done.refs_1_) | copy-start | bytes 1671172
  49.7 11.9 %collective-permute-start.1 = (bf16[544,512]{1,0:T(8,128)(2,1)S(1)}, bf16[544,512]{1,0:T(8,128)(2,1)S(1)}, u32[]{:S(2)}, u32[]{:S(2)}) collective-permute-start(bf16[544,512]{1,0:T(8,128)(2,1)S(1)} %collective-permute-done.refs_1_), channel_id=1, source_target_pairs={{0,1},{1,2},{2,3},{3,4},{4,5},{5,6},{6,7},{7,0},{8,15},{9,8},{10,9... | collective-permute-start | bytes 1671176 | tf_op jit(solution)/shard_map/ppermute | solution.py:77
  55.7 11.9 %collective-permute-start.6 = (bf16[544,512]{1,0:T(8,128)(2,1)S(1)}, bf16[544,512]{1,0:T(8,128)(2,1)S(1)}, u32[]{:S(2)}, u32[]{:S(2)}) collective-permute-start(bf16[544,512]{1,0:T(8,128)(2,1)S(1)} %collective-permute-done.4), channel_id=1, source_target_pairs={{0,1},{1,2},{2,3},{3,4},{4,5},{5,6},{6,7},{7,0},{8,15},{9,8},{10,9... | collective-permute-start | bytes 1671176 | tf_op jit(solution)/shard_map/ppermute | solution.py:78
  61.6 28.0 %copy-start.12 = (bf16[544,512]{1,0:T(8,128)(2,1)}, bf16[544,512]{1,0:T(8,128)(2,1)S(1)}, u32[]{:S(2)}) copy-start(bf16[544,512]{1,0:T(8,128)(2,1)S(1)} %collective-permute-done.1.refs_2_) | copy-start | bytes 1671172
  61.7 15.7 %collective-permute-start.2 = (bf16[544,512]{1,0:T(8,128)(2,1)S(1)}, bf16[544,512]{1,0:T(8,128)(2,1)S(1)}, u32[]{:S(2)}, u32[]{:S(2)}) collective-permute-start(bf16[544,512]{1,0:T(8,128)(2,1)S(1)} %collective-permute-done.1.refs_2_), channel_id=1, source_target_pairs={{0,1},{1,2},{2,3},{3,4},{4,5},{5,6},{6,7},{7,0},{8,15},{9,8},{10,9... | collective-permute-start | bytes 1671176 | tf_op jit(solution)/shard_map/ppermute | solution.py:77
  67.6 13.5 %collective-permute-start.8 = (bf16[544,512]{1,0:T(8,128)(2,1)S(1)}, bf16[544,512]{1,0:T(8,128)(2,1)S(1)}, u32[]{:S(2)}, u32[]{:S(2)}) collective-permute-start(bf16[544,512]{1,0:T(8,128)(2,1)S(1)} %collective-permute-done.6), channel_id=1, source_target_pairs={{0,1},{1,2},{2,3},{3,4},{4,5},{5,6},{6,7},{7,0},{8,15},{9,8},{10,9... | collective-permute-start | bytes 1671176 | tf_op jit(solution)/shard_map/ppermute | solution.py:78
  73.0 11.1 %collective-permute-start.5 = (bf16[544,512]{1,0:T(8,128)(2,1)S(1)}, bf16[544,512]{1,0:T(8,128)(2,1)S(1)}, u32[]{:S(2)}, u32[]{:S(2)}) collective-permute-start(bf16[544,512]{1,0:T(8,128)(2,1)S(1)} %collective-permute-done.4), channel_id=1, source_target_pairs={{0,8},{8,0},{16,24},{24,16},{32,40},{40,32},{48,56},{56,48},{64,72... | collective-permute-start | bytes 1671176 | tf_op jit(solution)/shard_map/ppermute | solution.py:79
  75.0 9.2 %collective-permute-start.7 = (bf16[544,512]{1,0:T(8,128)(2,1)S(1)}, bf16[544,512]{1,0:T(8,128)(2,1)S(1)}, u32[]{:S(2)}, u32[]{:S(2)}) collective-permute-start(bf16[544,512]{1,0:T(8,128)(2,1)S(1)} %collective-permute-done.6), channel_id=1, source_target_pairs={{0,8},{8,0},{16,24},{24,16},{32,40},{40,32},{48,56},{56,48},{64,72... | collective-permute-start | bytes 1671176 | tf_op jit(solution)/shard_map/ppermute | solution.py:79
  77.4 0.8 copy-start.13
  78.2 10.6 %collective-permute-start.10 = (bf16[544,512]{1,0:T(8,128)(2,1)S(1)}, bf16[544,512]{1,0:T(8,128)(2,1)S(1)}, u32[]{:S(2)}, u32[]{:S(2)}) collective-permute-start(bf16[544,512]{1,0:T(8,128)(2,1)S(1)} %collective-permute-done.2.refs_3_), channel_id=1, source_target_pairs={{0,1},{1,2},{2,3},{3,4},{4,5},{5,6},{6,7},{7,0},{8,15},{9,8},{10,9... | collective-permute-start | bytes 1671176 | tf_op jit(solution)/shard_map/ppermute | solution.py:80
  81.1 8.5 %collective-permute-start.9 = (bf16[544,512]{1,0:T(8,128)(2,1)S(1)}, bf16[544,512]{1,0:T(8,128)(2,1)}, u32[]{:S(2)}, u32[]{:S(2)}) collective-permute-start(bf16[544,512]{1,0:T(8,128)(2,1)S(1)} %collective-permute-done.8), channel_id=1, source_target_pairs={{0,8},{8,0},{16,24},{24,16},{32,40},{40,32},{48,56},{56,48},{64,72... | collective-permute-start | bytes 1671176 | tf_op jit(solution)/shard_map/ppermute | solution.py:79
  84.2 4.6 %copy-start.14 = (bf16[544,512]{1,0:T(8,128)(2,1)}, bf16[544,512]{1,0:T(8,128)(2,1)S(1)}, u32[]{:S(2)}) copy-start(bf16[544,512]{1,0:T(8,128)(2,1)S(1)} %collective-permute-done.5.refs_4_) | copy-start | bytes 1671172
  84.2 4.6 %copy-start.15 = (bf16[544,512]{1,0:T(8,128)(2,1)}, bf16[544,512]{1,0:T(8,128)(2,1)S(1)}, u32[]{:S(2)}) copy-start(bf16[544,512]{1,0:T(8,128)(2,1)S(1)} %collective-permute-done.7.refs_5_) | copy-start | bytes 1671172
  88.8 0.9 copy-start.16
  105.7 0.8 copy-start.5

commit v7 on v6

--- a/solution.py
+++ b/solution.py
@@ -43,12 +43,11 @@
     return ids
 
 
-def spread_kernel(pos_ref, t_ref, out_ref, sem):
+def spread_kernel(t_ref, out_ref, sem):
     copies = []
     for slot in range(4):
         for i in range(2):
-            x = slot // 2 + 2 * lax.rem(pos_ref[3] + i, 2)
-            at = pl.ds(pl.multiple_of(x * 512 + slot % 2 * 256, 256), 256)
+            at = pl.ds((slot // 2 + 2 * i) * 512 + slot % 2 * 256, 256)
             copies.append(
                 pltpu.make_async_copy(
                     t_ref.at[:, at], out_ref.at[slot, :, pl.ds(i * 256, 256)], sem.at[2 * slot + i]
@@ -61,11 +60,7 @@
 
 
 def low_kernel(t_ref, down_ref, out_ref):
-    low = mm(t_ref[...], down_ref[...], NT)
-    rows, wide = out_ref.shape
-    low = fold(low, rows // 2)
-    high = low.astype(BF).astype(F32)
-    out_ref[...] = jnp.concatenate([high, low - high], axis=0).astype(BF)
+    out_ref[...] = fold(mm(t_ref[...], down_ref[...], NT), out_ref.shape[0]).astype(BF)
 
 
 STEPS = (0, 1, 2, 3, -1, -2, -3, 4)
@@ -80,28 +75,47 @@
     return near + crossed + [lax.ppermute(near[3], axis, fore)]
 
 
+def block_at(pos_ref, step, n):
+    return lax.rem(pos_ref[1] + step * (2 * pos_ref[0] - 1) + n, n)
+
+
 def project_kernel(pos_ref, *refs):
-    t_refs, (w_ref, out_ref, low_ref, t_scr, w_scr, t_sem, w_sem) = refs[:8], refs[8:]
-    n = t_scr.shape[0]
-    slots, rows, wide = out_ref.shape
-    way = 2 * pos_ref[0] - 1
+    t_refs, (w_ref, total_ref, low_ref, t_scr, w_scr, t_sem, w_sem) = refs[:7], refs[7:]
+    rows = total_ref.shape[0]
     copies = [pltpu.make_async_copy(w_ref, w_scr, w_sem)]
-    for j, step in enumerate(STEPS):
-        k = lax.rem(pos_ref[1] + step * way + n, n)
-        copies.append(pltpu.make_async_copy(t_refs[j], t_scr.at[k], t_sem.at[j]))
+    for j, t_ref in enumerate(t_refs):
+        copies.append(pltpu.make_async_copy(t_ref, t_scr.at[j], t_sem.at[j]))
     for c in copies:
         c.start()
+    copies[0].wait()
+    total = jnp.zeros(total_ref.shape, F32)
+    low = jnp.zeros(low_ref.shape, F32)
+    for j, step in enumerate(STEPS[:7]):
+        copies[1 + j].wait()
+        w = w_scr[block_at(pos_ref, step, w_scr.shape[0])]
+        total = total + mm(t_scr[j, pl.ds(0, rows)], w, NN)
+        low = low + t_scr[j, pl.ds(rows, low.shape[0])].astype(F32)
+    total_ref[...] = total
+    low_ref[...] = low
+
+
+def finish_kernel(
+    pos_ref, total_ref, low_ref, t_ref, w_ref, out_ref, low_half_ref,
+    total_scr, low_scr, t_scr, w_scr, sem,
+):
+    k = block_at(pos_ref, STEPS[7], w_ref.shape[0])
+    pairs = ((t_ref, t_scr), (w_ref.at[k], w_scr), (total_ref, total_scr), (low_ref, low_scr))
+    copies = [pltpu.make_async_copy(a, b, sem.at[i]) for i, (a, b) in enumerate(pairs)]
+    for c in copies:
+        c.start()
     for c in copies:
         c.wait()
-    total = jnp.zeros((slots * rows, wide), F32)
-    low = jnp.zeros((t_scr.shape[1] - slots * rows, t_scr.shape[2]), F32)
-    for k in range(n):
-        total = total + mm(t_scr[k, pl.ds(0, slots * rows)], w_scr[k], NN)
-        low = low + t_scr[k, pl.ds(slots * rows, low.shape[0])].astype(F32)
+    slots, rows, _ = out_ref.shape
+    total = total_scr[...] + mm(t_scr[pl.ds(0, slots * rows)], w_scr[...], NN)
     for i in range(slots):
         out_ref[i] = total[i * rows:(i + 1) * rows].astype(BF)
-    low = low[:low.shape[0] // 2] + low[low.shape[0] // 2:]
-    low_ref[...] = unfold(low, low_ref.shape[1]).astype(BF)
+    low = low_scr[...] + t_scr[pl.ds(slots * rows, low_scr.shape[0])].astype(F32)
+    low_half_ref[...] = unfold(low, low_half_ref.shape[1]).astype(BF)
 
 
 def attend_kernel(
@@ -219,13 +233,16 @@
         upv_ref[pl.ds(j * deep, deep)] = up[:, HD:]
 
 
-def call(kernel, outs, in_specs, out_specs, *args, scratch=(), mib=8):
+def call(kernel, outs, in_specs, out_specs, *args, scratch=(), mib=8, cost=None):
     return pl.pallas_call(
         kernel,
         out_shape=[jax.ShapeDtypeStruct(s, d) for s, d in outs],
         in_specs=in_specs,
         out_specs=out_specs,
         scratch_shapes=list(scratch),
+        cost_estimate=cost and pl.CostEstimate(
+            flops=cost[0], bytes_accessed=cost[1], transcendentals=0
+        ),
         compiler_params=pltpu.CompilerParams(vmem_limit_bytes=mib * 1024 * 1024),
     )(*args)
 
@@ -233,7 +250,7 @@
 def on_device(tokens, queries, probes, w_key, w_value, down_proj, up_key, up_value, lengths):
     rows, feats = tokens.shape
     row_at = lax.axis_index("row")
-    pos = jnp.stack([row_at % 2, lax.axis_index("col"), row_at // 8, row_at // 4 % 2]).astype(jnp.int32)
+    pos = jnp.stack([row_at % 2, lax.axis_index("col"), row_at // 8]).astype(jnp.int32)
 
     def place(y, x, core):
         return ((y % 8) * 4 + x % 4) * 2 + core % 2
@@ -252,40 +269,60 @@
         for y in range(8)
         for h in range(2)
     ]
-    across = [(place(y, x, c), place(y, x + 2, c)) for y, x, c in sites]
+    sixteens = [
+        [place(y, x + 2 * i, c) for y in range(8) for i in range(2)]
+        for x in range(2)
+        for c in range(2)
+    ]
 
     quarter = feats // 4
     (spread,) = call(
-        spread_kernel, [((4, rows, quarter), BF)], [SMEM, HBM], [VMEM], pos, tokens,
-        scratch=[pltpu.SemaphoreType.DMA((8,))],
+        spread_kernel, [((4, rows, quarter), BF)], [HBM], [VMEM], tokens,
+        scratch=[pltpu.SemaphoreType.DMA((8,))], mib=56,
     )
     paired = lax.all_to_all(spread, "row", 0, 0, axis_index_groups=pairs)
     (low_part,) = call(
-        low_kernel, [((32, quarter), BF)], [VMEM, VMEM], [VMEM], tokens, down_proj.T
+        low_kernel, [((16, quarter), BF)], [VMEM, VMEM], [VMEM], tokens, down_proj.T
     )
     block = jnp.concatenate([paired.reshape(4 * rows, quarter), low_part], axis=0)
     t_parts = ring_of(block, ("row", "col"), z_fore, swap)
 
     w_both = jnp.concatenate([w_key, w_value], axis=1)
     wide = w_both.shape[1]
-    w_own = jnp.concatenate([w_both, lax.ppermute(w_both, "row", across)], axis=0)
     w_all = lax.all_to_all(
-        jnp.broadcast_to(w_own, (8,) + w_own.shape), "row", 0, 0, axis_index_groups=y_lines
-    )
-
-    shares, low_half = call(
+        jnp.broadcast_to(w_both, (16,) + w_both.shape), "row", 0, 0, axis_index_groups=sixteens
+    )
+    w_all = w_all.reshape(8, quarter, wide)
+
+    total, low_sum = call(
         project_kernel,
-        [((4, rows, wide), BF), ((rows, 64), BF)],
-        [SMEM] + [HBM] * 9,
+        [((4 * rows, wide), F32), ((16, quarter), F32)],
+        [SMEM] + [HBM] * 8,
         [VMEM] * 2,
-        pos, *t_parts, w_all,
+        pos, *t_parts[:7], w_all,
         scratch=[
-            pltpu.VMEM((8,) + block.shape, BF),
+            pltpu.VMEM((7,) + block.shape, BF),
             pltpu.VMEM(w_all.shape, BF),
-            pltpu.SemaphoreType.DMA((8,)),
+            pltpu.SemaphoreType.DMA((7,)),
             pltpu.SemaphoreType.DMA,
         ],
-        mib=56,
+        mib=52,
+        cost=(2 * 28 * rows * quarter * wide, 7 * 2 * block.size + 2 * w_all.size),
+    )
+    shares, low_half = call(
+        finish_kernel,
+        [((4, rows, wide), BF), ((rows, 64), BF)],
+        [SMEM] + [HBM] * 4,
+        [VMEM] * 2,
+        pos, total, low_sum, t_parts[7], w_all,
+        scratch=[
+            pltpu.VMEM(total.shape, F32),
+            pltpu.VMEM(low_sum.shape, F32),
+            pltpu.VMEM(block.shape, BF),
+            pltpu.VMEM((quarter, wide), BF),
+            pltpu.SemaphoreType.DMA((4,)),
+        ],
+        mib=52,
     )
     full_parts = lax.all_to_all(shares, "row", 0, 0, axis_index_groups=pairs)
     pack, gk, gv = call(

time: 168 us -> 167 us (level)
  blocking collectives: 63.7 us -> 67.4 us
  local copies, waits for them, and re-layouts: 5.04 us -> 1.55 us
    ppermute x3, starting transfers between devices: 21.5 us -> 13 us  [ring_of(): near.append(lax.ppermute(near[-1], axis, fore))]
    ppermute x3, starting transfers between devices: 13 us -> 21.3 us  [ring_of(): far = lax.ppermute(far, axis, fore)]
    all_to_all x1, waiting for transfers between devices: 0.01 us -> 7.95 us  [on_device(): paired = lax.all_to_all(spread, 'row', 0, 0, axis_index_groups=pairs)]
    ppermute x1 -> x0, waiting for transfers between devices: 6.94 us -> none  [on_device(): lax.ppermute(w_both, 'row', across)]
    ppermute x3, waiting for transfers between devices: 4.81 us -> 0.95 us  [ring_of(): near.append(lax.ppermute(near[-1], axis, fore))]
    ppermute x3, waiting for transfers between devices: 1.09 us -> 4.9 us  [ring_of(): far = lax.ppermute(far, axis, fore)]
    unnamed x39 -> x22, local copies, waits for them, and re-layouts: 3.55 us -> 0.04 us
    ppermute x1, waiting for transfers between devices: 4.55 us -> 1.65 us  [ring_of(): return near + crossed + [lax.ppermute(near[3], axis, fore)]]
  transfers between devices with their start and end apart: 14 -> 13, of which waited for: 6 -> 8; matrix products, arithmetic and copies ran while one was open for 0% -> 0% of each run, Pallas kernels for 0% -> 3%
where the time goes in v7:
time: 167 us; the launch traced here: 166 us
  blocking collectives  67.4 us (40%)
  starting transfers between devices  63.6 us (38%)
  waiting for transfers between devices  17 us (10%)
  Pallas kernels  15.7 us (9%)
    ppermute x3, starting transfers between devices, ring_of(): far = lax.ppermute(far, axis, fore)  21.3 us
    all_to_all x1, blocking collectives, on_device(): lax.all_to_all(square, 'row', 0, 0, axis_index_groups=y_lines)  17.2 us
    pallas_call x9, Pallas kernels, call(): pl.pallas_call(kernel, out_shape=[jax.ShapeDtypeStruct(s, d) for s, d in...  15.7 us
    all_to_all x1, blocking collectives, on_device(): term_parts = lax.all_to_all(terms, 'row', 0, 0, axis_index_groups=squares)  14.5 us
    ppermute x3, starting transfers between devices, ring_of(): near.append(lax.ppermute(near[-1], axis, fore))  13 us
    all_to_all x1, blocking collectives, on_device(): pieces = lax.all_to_all(summed, 'row', 0, 0, axis_index_groups=squares)  12.2 us
    all_to_all x1, blocking collectives, on_device(): packs = lax.all_to_all(pack, 'col', 0, 0)  12 us
    all_to_all x1, blocking collectives, on_device(): full_parts = lax.all_to_all(shares, 'row', 0, 0, axis_index_groups=pairs)  11.5 us
  transfers between devices with their start and end apart: 13, of which 8 were waited for; matrix products, arithmetic and copies ran while one was open for 0% of the time, Pallas kernels for 3%

profile of v7, /device:TPU:1, one launch (start us, length us, event | category | flops | bytes accessed | tf_op | source)
XLA Modules:
  0.0 166.4 jit_solution(5786552350738167819)
XLA Ops:
  0.6 0.0 copy-start.10
  0.6 0.0 copy-start.9
  0.7 2.0 %shard_map.112 = bf16[4,128,512]{2,1,0:T(8,128)(2,1)} custom-call(bf16[128,2048]{1,0:T(8,128)(2,1)} %t_ref.5), custom_call_target="tpu_custom_call" | custom-call | tf_op jit(solution)/shard_map/pallas_call | solution.py:237
  2.6 10.3 %all-to-all-start = ((bf16[4,128,512]{2,1,0:T(8,128)(2,1)}), bf16[4,128,512]{2,1,0:T(8,128)(2,1)S(1)}, u32[]{:S(2)}, u32[]{:S(2)}) async-start(bf16[4,128,512]{2,1,0:T(8,128)(2,1)} %shard_map.112), calls=%async_computation | async-start | bytes 1048576 | tf_op jit(solution)/shard_map/all_to_all | solution.py:283
  13.0 0.0 copy-done.10
  13.0 0.0 copy-done.9
  13.0 8.0 %all-to-all-done = bf16[4,128,512]{2,1,0:T(8,128)(2,1)S(1)} async-done(((bf16[4,128,512]{2,1,0:T(8,128)(2,1)}), bf16[4,128,512]{2,1,0:T(8,128)(2,1)S(1)}, u32[]{:S(2)}, u32[]{:S(2)}) %all-to-all-start) | async-done | bytes 524320 | tf_op jit(solution)/shard_map/all_to_all | solution.py:283
  20.9 1.5 broadcast_in_dim.3
  22.4 4.6 %all-to-all-start.1 = ((bf16[16,256,256]{2,1,0:T(8,128)(2,1)}), bf16[16,256,256]{2,1,0:T(8,128)(2,1)}, u32[]{:S(2)}, u32[]{:S(2)}) async-start(bf16[16,256,256]{2,1,0:T(8,128)(2,1)} %broadcast_in_dim.3), calls=%async_computation.1 | async-start | bytes 4194304 | tf_op jit(solution)/shard_map/all_to_all | solution.py:292
  27.0 0.0 copy-done
  27.0 0.0 copy-done.3
  27.0 0.3 shard_map.113
  27.4 2.8 %collective-permute-start.3 = (bf16[528,512]{1,0:T(8,128)(2,1)S(1)}, bf16[528,512]{1,0:T(8,128)(2,1)S(1)}, u32[]{:S(2)}, u32[]{:S(2)}) collective-permute-start(bf16[528,512]{1,0:T(8,128)(2,1)S(1)} %pad_maximum_fusion.refs_0_), channel_id=1, source_target_pairs={{0,8},{8,0},{16,24},{24,16},{32,40},{40,32},{48,56},{56,48},{64,72... | collective-permute-start | bytes 1622024 | tf_op jit(solution)/shard_map/ppermute | solution.py:70
  30.2 1.5 collective-permute-done.3
  31.8 10.6 %collective-permute-start.4 = (bf16[528,512]{1,0:T(8,128)(2,1)S(1)}, bf16[528,512]{1,0:T(8,128)(2,1)}, u32[]{:S(2)}, u32[]{:S(2)}) collective-permute-start(bf16[528,512]{1,0:T(8,128)(2,1)S(1)} %collective-permute-done.3), channel_id=1, source_target_pairs={{0,1},{1,2},{2,3},{3,4},{4,5},{5,6},{6,7},{7,0},{8,15},{9,8},{10,9... | collective-permute-start | bytes 1622024 | tf_op jit(solution)/shard_map/ppermute | solution.py:73
  42.3 2.2 %collective-permute-start = (bf16[528,512]{1,0:T(8,128)(2,1)S(1)}, bf16[528,512]{1,0:T(8,128)(2,1)S(1)}, u32[]{:S(2)}, u32[]{:S(2)}) collective-permute-start(bf16[528,512]{1,0:T(8,128)(2,1)S(1)} %pad_maximum_fusion.refs_0_), channel_id=1, source_target_pairs={{0,1},{1,2},{2,3},{3,4},{4,5},{5,6},{6,7},{7,0},{8,15},{9,8},{10,9... | collective-permute-start | bytes 1622024 | tf_op jit(solution)/shard_map/ppermute | solution.py:72
  44.5 4.1 %collective-permute-done.4 = bf16[528,512]{1,0:T(8,128)(2,1)} collective-permute-done((bf16[528,512]{1,0:T(8,128)(2,1)S(1)}, bf16[528,512]{1,0:T(8,128)(2,1)}, u32[]{:S(2)}, u32[]{:S(2)}) %collective-permute-start.4) | collective-permute-done | bytes 540704 | tf_op jit(solution)/shard_map/ppermute | solution.py:73
  48.6 5.4 %collective-permute-start.6 = (bf16[528,512]{1,0:T(8,128)(2,1)}, bf16[528,512]{1,0:T(8,128)(2,1)}, u32[]{:S(2)}, u32[]{:S(2)}) collective-permute-start(bf16[528,512]{1,0:T(8,128)(2,1)} %collective-permute-done.4), channel_id=1, source_target_pairs={{0,1},{1,2},{2,3},{3,4},{4,5},{5,6},{6,7},{7,0},{8,15},{9,8},{10,9... | collective-permute-start | bytes 1622024 | tf_op jit(solution)/shard_map/ppermute | solution.py:73
  54.0 0.4 collective-permute-done.refs_1_
  54.4 5.4 %collective-permute-start.1 = (bf16[528,512]{1,0:T(8,128)(2,1)S(1)}, bf16[528,512]{1,0:T(8,128)(2,1)S(1)}, u32[]{:S(2)}, u32[]{:S(2)}) collective-permute-start(bf16[528,512]{1,0:T(8,128)(2,1)S(1)} %collective-permute-done.refs_1_), channel_id=1, source_target_pairs={{0,1},{1,2},{2,3},{3,4},{4,5},{5,6},{6,7},{7,0},{8,15},{9,8},{10,9... | collective-permute-start | bytes 1622024 | tf_op jit(solution)/shard_map/ppermute | solution.py:72
  59.8 0.8 collective-permute-done.6
  60.6 5.3 %collective-permute-start.8 = (bf16[528,512]{1,0:T(8,128)(2,1)}, bf16[528,512]{1,0:T(8,128)(2,1)}, u32[]{:S(2)}, u32[]{:S(2)}) collective-permute-start(bf16[528,512]{1,0:T(8,128)(2,1)} %collective-permute-done.6), channel_id=1, source_target_pairs={{0,1},{1,2},{2,3},{3,4},{4,5},{5,6},{6,7},{7,0},{8,15},{9,8},{10,9... | collective-permute-start | bytes 1622024 | tf_op jit(solution)/shard_map/ppermute | solution.py:73
  66.0 0.4 collective-permute-done.1.refs_2_
  66.3 5.4 %collective-permute-start.2 = (bf16[528,512]{1,0:T(8,128)(2,1)S(1)}, bf16[528,512]{1,0:T(8,128)(2,1)S(1)}, u32[]{:S(2)}, u32[]{:S(2)}) collective-permute-start(bf16[528,512]{1,0:T(8,128)(2,1)S(1)} %collective-permute-done.1.refs_2_), channel_id=1, source_target_pairs={{0,1},{1,2},{2,3},{3,4},{4,5},{5,6},{6,7},{7,0},{8,15},{9,8},{10,9... | collective-permute-start | bytes 1622024 | tf_op jit(solution)/shard_map/ppermute | solution.py:72
  71.7 1.9 %collective-permute-start.5 = (bf16[528,512]{1,0:T(8,128)(2,1)}, bf16[528,512]{1,0:T(8,128)(2,1)}, u32[]{:S(2)}, u32[]{:S(2)}) collective-permute-start(bf16[528,512]{1,0:T(8,128)(2,1)} %collective-permute-done.4), channel_id=1, source_target_pairs={{0,8},{8,0},{16,24},{24,16},{32,40},{40,32},{48,56},{56,48},{64,72... | collective-permute-start | bytes 1622024 | tf_op jit(solution)/shard_map/ppermute | solution.py:74
  73.7 2.4 %collective-permute-start.7 = (bf16[528,512]{1,0:T(8,128)(2,1)}, bf16[528,512]{1,0:T(8,128)(2,1)}, u32[]{:S(2)}, u32[]{:S(2)}) collective-permute-start(bf16[528,512]{1,0:T(8,128)(2,1)} %collective-permute-done.6), channel_id=1, source_target_pairs={{0,8},{8,0},{16,24},{24,16},{32,40},{40,32},{48,56},{56,48},{64,72... | collective-permute-start | bytes 1622024 | tf_op jit(solution)/shard_map/ppermute | solution.py:74
  76.1 0.0 collective-permute-done.8
  76.1 1.9 %collective-permute-start.9 = (bf16[528,512]{1,0:T(8,128)(2,1)}, bf16[528,512]{1,0:T(8,128)(2,1)}, u32[]{:S(2)}, u32[]{:S(2)}) collective-permute-start(bf16[528,512]{1,0:T(8,128)(2,1)} %collective-permute-done.8), channel_id=1, source_target_pairs={{0,8},{8,0},{16,24},{24,16},{32,40},{40,32},{48,56},{56,48},{64,72... | collective-permute-start | bytes 1622024 | tf_op jit(solution)/shard_map/ppermute | solution.py:74
  78.0 0.2 collective-permute-done.2.refs_3_
  78.2 5.4 %collective-permute-start.10 = (bf16[528,512]{1,0:T(8,128)(2,1)S(1)}, bf16[528,512]{1,0:T(8,128)(2,1)S(1)}, u32[]{:S(2)}, u32[]{:S(2)}) collective-permute-start(bf16[528,512]{1,0:T(8,128)(2,1)S(1)} %collective-permute-done.2.refs_3_), channel_id=1, source_target_pairs={{0,1},{1,2},{2,3},{3,4},{4,5},{5,6},{6,7},{7,0},{8,15},{9,8},{10,9... | collective-permute-start | bytes 1622024 | tf_op jit(solution)/shard_map/ppermute | solution.py:75
  83.7 0.1 pad_add_fusion.pos_ref
  83.8 0.0 collective-permute-done.5.refs_4_
  83.8 0.0 collective-permute-done.7.refs_5_
  83.8 0.0 collective-permute-done.9.refs_6_
  83.8 0.0 all-to-all-done.1
  83.8 0.0 copy-done.7
  83.8 4.5 %shard_map.114 = (f32[512,256]{1,0:T(8,128)S(1)}, f32[16,512]{1,0:T(8,128)S(1)}) custom-call(s32[3]{0:T(128)S(1)} %pad_add_fusion.pos_ref, bf16[528,512]{1,0:T(8,128)(2,1)S(1)} %pad_maximum_fusion.refs_0_, bf16[528,512]{1,0:T(8,128)(2,1)S(1)} %collective-permute-done.refs_1_, bf16[528,512]{1,0:T(8,128)(2,1)} %copy-done.7, bf16[528,512]{1,0:T(8,128)(2,1)} %copy-done.8, ...), custom_call_target="tpu_custom_call" | custom-call | flops 939524096 | bytes 5881856 | tf_op jit(solution)/shard_map/pallas_call | solution.py:237
  88.3 1.6 collective-permute-done.10.t_ref
  90.0 1.9 %shard_map.115 = (bf16[4,128,256]{2,1,0:T(8,128)(2,1)S(1)}, bf16[128,64]{1,0:T(8,128)(2,1)S(1)}) custom-call(s32[3]{0:T(128)S(1)} %pad_add_fusion.pos_ref, f32[512,256]{1,0:T(8,128)S(1)} %get-tuple-element.13.total_ref, f32[16,512]{1,0:T(8,128)S(1)} %get-tuple-element.14.low_ref, bf16[528,512]{1,0:T(8,128)(2,1)S(1)} %collective-permute-done.10.t_ref, ...), custom_call_target="tpu_custom_call" | custom-call | tf_op jit(solution)/shard_map/pallas_call | solution.py:237
  91.9 11.5 %all_to_all.35.full_ref = bf16[4,128,256]{2,1,0:T(8,128)(2,1)S(1)} all-to-all(bf16[4,128,256]{2,1,0:T(8,128)(2,1)S(1)} %get-tuple-element.15), channel_id=1, replica_groups={{0,8,16,24},{32,40,48,56},{64,72,80,88},{96,104,112,120},{128,136,144,1..., dimensions={0} | all-to-all | bytes 524288 | tf_op jit(solution)/shard_map/all_to_all | solution.py:327
  103.4 0.0 copy-done.2
  103.4 5.2 %shard_map.116 = (bf16[8,80,128]{2,1,0:T(8,128)(2,1)S(1)}, f32[128,128]{1,0:T(8,128)S(1)}, f32[128,128]{1,0:T(8,128)S(1)}) custom-call(s32[1,8]{1,0:T(1,128)S(1)} %copy-done.6, bf16[4,128,256]{2,1,0:T(8,128)(2,1)S(1)} %all_to_all.35.full_ref, bf16[128,64]{1,0:T(8,128)(2,1)S(1)} %get-tuple-element.16.low_ref.low_half_ref, bf16[64,128]{1,0:T(8,128)(2,1)S(1)} %copy-done.4, ...), custom_call_target="tpu_custom_call" | custom-call | tf_op jit(solution)/shard_map/pallas_call | solution.py:237
  108.6 12.0 %all_to_all.36.pack_ref = bf16[8,80,128]{2,1,0:T(8,128)(2,1)S(1)} all-to-all(bf16[8,80,128]{2,1,0:T(8,128)(2,1)S(1)} %get-tuple-element.17), channel_id=1, replica_groups=mesh['row'=64,'col'=8] {'col'}, dimensions={0} | all-to-all | bytes 327680 | tf_op jit(solution)/shard_map/all_to_all | solution.py:340
  120.6 0.9 shard_map.117
  121.6 14.5 %all_to_all.37.in_ref = bf16[8,72,256]{2,1,0:T(8,128)(2,1)S(1)} all-to-all(bf16[8,72,256]{2,1,0:T(8,128)(2,1)S(1)} %shard_map.117), channel_id=1, replica_groups={{0,8,16,24,32,40,48,56},{64,72,80,88,96,104,112,120},{128,136,144,152,1..., dimensions={0} | all-to-all | bytes 589824 | tf_op jit(solution)/shard_map/all_to_all | solution.py:346
  136.1 17.2 %all_to_all.38.in_ref = bf16[8,72,256]{2,1,0:T(8,128)(2,1)S(1)} all-to-all(bf16[8,72,256]{2,1,0:T(8,128)(2,1)S(1)} %shard_map.118), channel_id=1, replica_groups={{0,64,128,192,256,320,384,448},{8,72,136,200,264,328,392,456},{16,80,14..., dimensions={0} | all-to-all | bytes 589824 | tf_op jit(solution)/shard_map/all_to_all | solution.py:348
  153.4 12.2 %all_to_all.39.in_ref = bf16[8,72,256]{2,1,0:T(8,128)(2,1)S(1)} all-to-all(bf16[8,72,256]{2,1,0:T(8,128)(2,1)S(1)} %shard_map.119), channel_id=1, replica_groups={{0,8,16,24,32,40,48,56},{64,72,80,88,96,104,112,120},{128,136,144,152,1..., dimensions={0} | all-to-all | bytes 589824 | tf_op jit(solution)/shard_map/all_to_all | solution.py:350
  165.5 0.8 shard_map.120
  (18 shorter events, 0.2 us)
Async XLA Ops:
  0.6 12.3 %copy-start.10 = (bf16[256,128]{1,0:T(8,128)(2,1)S(1)}, bf16[256,128]{1,0:T(8,128)(2,1)}, u32[]{:S(2)}) copy-start(bf16[256,128]{1,0:T(8,128)(2,1)} %param.12) | copy-start | bytes 196612
  0.6 12.3 %copy-start.9 = (bf16[256,128]{1,0:T(8,128)(2,1)S(1)}, bf16[256,128]{1,0:T(8,128)(2,1)}, u32[]{:S(2)}) copy-start(bf16[256,128]{1,0:T(8,128)(2,1)} %param.13) | copy-start | bytes 196612
  2.6 18.3 %all-to-all-start = ((bf16[4,128,512]{2,1,0:T(8,128)(2,1)}), bf16[4,128,512]{2,1,0:T(8,128)(2,1)S(1)}, u32[]{:S(2)}, u32[]{:S(2)}) async-start(bf16[4,128,512]{2,1,0:T(8,128)(2,1)} %shard_map.112), calls=%async_computation | async-start | bytes 1048576 | tf_op jit(solution)/shard_map/all_to_all | solution.py:283
  22.4 4.6 %copy-start = (bf16[128,2048]{1,0:T(8,128)(2,1)S(1)}, bf16[128,2048]{1,0:T(8,128)(2,1)}, u32[]{:S(2)}) copy-start(bf16[128,2048]{1,0:T(8,128)(2,1)} %t_ref.5) | copy-start | bytes 1572868
  22.4 4.6 %copy-start.3 = (bf16[2048,64]{0,1:T(8,128)(2,1)S(1)}, bf16[2048,64]{0,1:T(8,128)(2,1)}, u32[]{:S(2)}) copy-start(bf16[2048,64]{0,1:T(8,128)(2,1)} %param.14) | copy-start | bytes 786436
  22.4 61.3 %all-to-all-start.1 = ((bf16[16,256,256]{2,1,0:T(8,128)(2,1)}), bf16[16,256,256]{2,1,0:T(8,128)(2,1)}, u32[]{:S(2)}, u32[]{:S(2)}) async-start(bf16[16,256,256]{2,1,0:T(8,128)(2,1)} %broadcast_in_dim.3), calls=%async_computation.1 | async-start | bytes 4194304 | tf_op jit(solution)/shard_map/all_to_all | solution.py:292
  27.4 4.3 %collective-permute-start.3 = (bf16[528,512]{1,0:T(8,128)(2,1)S(1)}, bf16[528,512]{1,0:T(8,128)(2,1)S(1)}, u32[]{:S(2)}, u32[]{:S(2)}) collective-permute-start(bf16[528,512]{1,0:T(8,128)(2,1)S(1)} %pad_maximum_fusion.refs_0_), channel_id=1, source_target_pairs={{0,8},{8,0},{16,24},{24,16},{32,40},{40,32},{48,56},{56,48},{64,72... | collective-permute-start | bytes 1622024 | tf_op jit(solution)/shard_map/ppermute | solution.py:70
  31.8 16.9 %collective-permute-start.4 = (bf16[528,512]{1,0:T(8,128)(2,1)S(1)}, bf16[528,512]{1,0:T(8,128)(2,1)}, u32[]{:S(2)}, u32[]{:S(2)}) collective-permute-start(bf16[528,512]{1,0:T(8,128)(2,1)S(1)} %collective-permute-done.3), channel_id=1, source_target_pairs={{0,1},{1,2},{2,3},{3,4},{4,5},{5,6},{6,7},{7,0},{8,15},{9,8},{10,9... | collective-permute-start | bytes 1622024 | tf_op jit(solution)/shard_map/ppermute | solution.py:73
  42.3 12.1 %collective-permute-start = (bf16[528,512]{1,0:T(8,128)(2,1)S(1)}, bf16[528,512]{1,0:T(8,128)(2,1)S(1)}, u32[]{:S(2)}, u32[]{:S(2)}) collective-permute-start(bf16[528,512]{1,0:T(8,128)(2,1)S(1)} %pad_maximum_fusion.refs_0_), channel_id=1, source_target_pairs={{0,1},{1,2},{2,3},{3,4},{4,5},{5,6},{6,7},{7,0},{8,15},{9,8},{10,9... | collective-permute-start | bytes 1622024 | tf_op jit(solution)/shard_map/ppermute | solution.py:72
  48.6 12.0 %collective-permute-start.6 = (bf16[528,512]{1,0:T(8,128)(2,1)}, bf16[528,512]{1,0:T(8,128)(2,1)}, u32[]{:S(2)}, u32[]{:S(2)}) collective-permute-start(bf16[528,512]{1,0:T(8,128)(2,1)} %collective-permute-done.4), channel_id=1, source_target_pairs={{0,1},{1,2},{2,3},{3,4},{4,5},{5,6},{6,7},{7,0},{8,15},{9,8},{10,9... | collective-permute-start | bytes 1622024 | tf_op jit(solution)/shard_map/ppermute | solution.py:73
  54.4 11.9 %collective-permute-start.1 = (bf16[528,512]{1,0:T(8,128)(2,1)S(1)}, bf16[528,512]{1,0:T(8,128)(2,1)S(1)}, u32[]{:S(2)}, u32[]{:S(2)}) collective-permute-start(bf16[528,512]{1,0:T(8,128)(2,1)S(1)} %collective-permute-done.refs_1_), channel_id=1, source_target_pairs={{0,1},{1,2},{2,3},{3,4},{4,5},{5,6},{6,7},{7,0},{8,15},{9,8},{10,9... | collective-permute-start | bytes 1622024 | tf_op jit(solution)/shard_map/ppermute | solution.py:72
  60.6 15.5 %collective-permute-start.8 = (bf16[528,512]{1,0:T(8,128)(2,1)}, bf16[528,512]{1,0:T(8,128)(2,1)}, u32[]{:S(2)}, u32[]{:S(2)}) collective-permute-start(bf16[528,512]{1,0:T(8,128)(2,1)} %collective-permute-done.6), channel_id=1, source_target_pairs={{0,1},{1,2},{2,3},{3,4},{4,5},{5,6},{6,7},{7,0},{8,15},{9,8},{10,9... | collective-permute-start | bytes 1622024 | tf_op jit(solution)/shard_map/ppermute | solution.py:73
  66.3 17.5 %copy-start.7 = (bf16[528,512]{1,0:T(8,128)(2,1)}, bf16[528,512]{1,0:T(8,128)(2,1)S(1)}, u32[]{:S(2)}) copy-start(bf16[528,512]{1,0:T(8,128)(2,1)S(1)} %collective-permute-done.1.refs_2_) | copy-start | bytes 1622020
  66.3 11.9 %collective-permute-start.2 = (bf16[528,512]{1,0:T(8,128)(2,1)S(1)}, bf16[528,512]{1,0:T(8,128)(2,1)S(1)}, u32[]{:S(2)}, u32[]{:S(2)}) collective-permute-start(bf16[528,512]{1,0:T(8,128)(2,1)S(1)} %collective-permute-done.1.refs_2_), channel_id=1, source_target_pairs={{0,1},{1,2},{2,3},{3,4},{4,5},{5,6},{6,7},{7,0},{8,15},{9,8},{10,9... | collective-permute-start | bytes 1622024 | tf_op jit(solution)/shard_map/ppermute | solution.py:72
  71.7 12.0 %collective-permute-start.5 = (bf16[528,512]{1,0:T(8,128)(2,1)}, bf16[528,512]{1,0:T(8,128)(2,1)}, u32[]{:S(2)}, u32[]{:S(2)}) collective-permute-start(bf16[528,512]{1,0:T(8,128)(2,1)} %collective-permute-done.4), channel_id=1, source_target_pairs={{0,8},{8,0},{16,24},{24,16},{32,40},{40,32},{48,56},{56,48},{64,72... | collective-permute-start | bytes 1622024 | tf_op jit(solution)/shard_map/ppermute | solution.py:74
  73.7 10.1 %collective-permute-start.7 = (bf16[528,512]{1,0:T(8,128)(2,1)}, bf16[528,512]{1,0:T(8,128)(2,1)}, u32[]{:S(2)}, u32[]{:S(2)}) collective-permute-start(bf16[528,512]{1,0:T(8,128)(2,1)} %collective-permute-done.6), channel_id=1, source_target_pairs={{0,8},{8,0},{16,24},{24,16},{32,40},{40,32},{48,56},{56,48},{64,72... | collective-permute-start | bytes 1622024 | tf_op jit(solution)/shard_map/ppermute | solution.py:74
  76.1 7.7 %collective-permute-start.9 = (bf16[528,512]{1,0:T(8,128)(2,1)}, bf16[528,512]{1,0:T(8,128)(2,1)}, u32[]{:S(2)}, u32[]{:S(2)}) collective-permute-start(bf16[528,512]{1,0:T(8,128)(2,1)} %collective-permute-done.8), channel_id=1, source_target_pairs={{0,8},{8,0},{16,24},{24,16},{32,40},{40,32},{48,56},{56,48},{64,72... | collective-permute-start | bytes 1622024 | tf_op jit(solution)/shard_map/ppermute | solution.py:74
  78.2 5.6 %copy-start.8 = (bf16[528,512]{1,0:T(8,128)(2,1)}, bf16[528,512]{1,0:T(8,128)(2,1)S(1)}, u32[]{:S(2)}) copy-start(bf16[528,512]{1,0:T(8,128)(2,1)S(1)} %collective-permute-done.2.refs_3_) | copy-start | bytes 1622020
  78.2 11.7 %collective-permute-start.10 = (bf16[528,512]{1,0:T(8,128)(2,1)S(1)}, bf16[528,512]{1,0:T(8,128)(2,1)S(1)}, u32[]{:S(2)}, u32[]{:S(2)}) collective-permute-start(bf16[528,512]{1,0:T(8,128)(2,1)S(1)} %collective-permute-done.2.refs_3_), channel_id=1, source_target_pairs={{0,1},{1,2},{2,3},{3,4},{4,5},{5,6},{6,7},{7,0},{8,15},{9,8},{10,9... | collective-permute-start | bytes 1622024 | tf_op jit(solution)/shard_map/ppermute | solution.py:75
  89.9 13.5 %copy-start.1 = (bf16[128,2048]{1,0:T(8,128)(2,1)S(1)}, bf16[128,2048]{1,0:T(8,128)(2,1)}, u32[]{:S(2)}) copy-start(bf16[128,2048]{1,0:T(8,128)(2,1)} %q_ref.1) | copy-start | bytes 1572868
  89.9 13.5 %copy-start.2 = (bf16[128,2048]{1,0:T(8,128)(2,1)S(1)}, bf16[128,2048]{1,0:T(8,128)(2,1)}, u32[]{:S(2)}) copy-start(bf16[128,2048]{1,0:T(8,128)(2,1)} %p_ref.1) | copy-start | bytes 1572868
  89.9 13.5 %copy-start.4 = (bf16[64,128]{1,0:T(8,128)(2,1)S(1)}, bf16[64,128]{1,0:T(8,128)(2,1)}, u32[]{:S(2)}) copy-start(bf16[64,128]{1,0:T(8,128)(2,1)} %upk_ref.1) | copy-start | bytes 49156
  89.9 13.5 %copy-start.5 = (bf16[64,128]{1,0:T(8,128)(2,1)S(1)}, bf16[64,128]{1,0:T(8,128)(2,1)}, u32[]{:S(2)}) copy-start(bf16[64,128]{1,0:T(8,128)(2,1)} %upv_ref.1) | copy-start | bytes 49156
  89.9 13.5 %copy-start.6 = (s32[1,8]{1,0:T(1,128)S(1)}, s32[1,8]{1,0:T(1,128)}, u32[]{:S(2)}) copy-start(s32[1,8]{1,0:T(1,128)} %lengths_ref.3) | copy-start | bytes 100

commit v8 on v7

--- a/solution.py
+++ b/solution.py
@@ -43,14 +43,18 @@
     return ids
 
 
-def spread_kernel(t_ref, out_ref, sem):
+def spread_kernel(pos_ref, t_ref, *refs):
+    out_refs, sem = refs[:4], refs[4]
     copies = []
     for slot in range(4):
+        x = lax.rem(pos_ref[3] + slot // 2, 2)
+        core = lax.rem(pos_ref[0] + slot % 2, 2)
         for i in range(2):
-            at = pl.ds((slot // 2 + 2 * i) * 512 + slot % 2 * 256, 256)
+            far = lax.rem(pos_ref[4] + i, 2)
+            at = pl.ds(pl.multiple_of((x + 2 * far) * 512 + core * 256, 256), 256)
             copies.append(
                 pltpu.make_async_copy(
-                    t_ref.at[:, at], out_ref.at[slot, :, pl.ds(i * 256, 256)], sem.at[2 * slot + i]
+                    t_ref.at[:, at], out_refs[slot].at[:, pl.ds(i * 256, 256)], sem.at[2 * slot + i]
                 )
             )
     for c in copies:
@@ -61,6 +65,14 @@
 
 def low_kernel(t_ref, down_ref, out_ref):
     out_ref[...] = fold(mm(t_ref[...], down_ref[...], NT), out_ref.shape[0]).astype(BF)
+
+
+def join_kernel(*refs):
+    parts, out_ref = refs[:-1], refs[-1]
+    at = 0
+    for part in parts:
+        out_ref[pl.ds(at, part.shape[0])] = part[...]
+        at += part.shape[0]
 
 
 STEPS = (0, 1, 2, 3, -1, -2, -3, 4)
@@ -113,7 +125,9 @@
     slots, rows, _ = out_ref.shape
     total = total_scr[...] + mm(t_scr[pl.ds(0, slots * rows)], w_scr[...], NN)
     for i in range(slots):
-        out_ref[i] = total[i * rows:(i + 1) * rows].astype(BF)
+        x = lax.rem(pos_ref[3] + i // 2, 2)
+        core = lax.rem(pos_ref[0] + i % 2, 2)
+        out_ref[2 * x + core] = total[i * rows:(i + 1) * rows].astype(BF)
     low = low_scr[...] + t_scr[pl.ds(slots * rows, low_scr.shape[0])].astype(F32)
     low_half_ref[...] = unfold(low, low_half_ref.shape[1]).astype(BF)
 
@@ -250,7 +264,8 @@
 def on_device(tokens, queries, probes, w_key, w_value, down_proj, up_key, up_value, lengths):
     rows, feats = tokens.shape
     row_at = lax.axis_index("row")
-    pos = jnp.stack([row_at % 2, lax.axis_index("col"), row_at // 8]).astype(jnp.int32)
+    pos = jnp.stack([row_at % 2, lax.axis_index("col"), row_at // 8, row_at // 2 % 2, row_at // 4 % 2])
+    pos = pos.astype(jnp.int32)
 
     def place(y, x, core):
         return ((y % 8) * 4 + x % 4) * 2 + core % 2
@@ -269,6 +284,23 @@
         for y in range(8)
         for h in range(2)
     ]
+    beside = [(place(y, x, c), place(y, x ^ 1, c)) for y, x, c in sites]
+    across = [(place(y, x, c), place(y, x ^ 1, 1 - c)) for y, x, c in sites]
+    opposite = [(place(y, x, c), place(y, x + 2, c)) for y, x, c in sites]
+    z_fore = [
+        (place(y, x, c) * 8 + z, place(y, x, c) * 8 + (z + 1 - 2 * c) % 8)
+        for y, x, c in sites
+        for z in range(8)
+    ]
+    y_lines = [[place(y, x, c) for y in range(8)] for x in range(4) for c in range(2)]
+    squares = [[place(y, x, c) for x in range(4) for c in range(2)] for y in range(8)]
+    pairs = [
+        [place(y, 2 * h + x, c) for x in range(2) for c in range(2)]
+        for y in range(8)
+        for h in range(2)
+    ]
+    beside = [(place(y, x, c), place(y, x ^ 1, c)) for y, x, c in sites]
+    across = [(place(y, x, c), place(y, x ^ 1, 1 - c)) for y, x, c in sites]
     sixteens = [
         [place(y, x + 2 * i, c) for y in range(8) for i in range(2)]
         for x in range(2)
@@ -276,23 +308,30 @@
     ]
 
     quarter = feats // 4
-    (spread,) = call(
-        spread_kernel, [((4, rows, quarter), BF)], [HBM], [VMEM], tokens,
+    mine, *others = call(
+        spread_kernel, [((rows, quarter), BF)] * 4, [SMEM, HBM], [VMEM] * 4, pos, tokens,
         scratch=[pltpu.SemaphoreType.DMA((8,))], mib=56,
     )
-    paired = lax.all_to_all(spread, "row", 0, 0, axis_index_groups=pairs)
+    paired = [
+        lax.ppermute(part, "row", way) for part, way in zip(others, (swap, beside, across))
+    ]
     (low_part,) = call(
         low_kernel, [((16, quarter), BF)], [VMEM, VMEM], [VMEM], tokens, down_proj.T
     )
-    block = jnp.concatenate([paired.reshape(4 * rows, quarter), low_part], axis=0)
-    t_parts = ring_of(block, ("row", "col"), z_fore, swap)
 
     w_both = jnp.concatenate([w_key, w_value], axis=1)
     wide = w_both.shape[1]
+    w_far = lax.ppermute(w_both, "row", opposite)
+    paired, w_far = lax.optimization_barrier((paired, w_far))
+    (block,) = call(
+        join_kernel, [((4 * rows + 16, quarter), BF)], [VMEM] * 5, [VMEM],
+        mine, *paired, low_part,
+    )
+    t_parts = ring_of(block, ("row", "col"), z_fore, swap)
+    w_own = jnp.concatenate([w_both, w_far], axis=0)
     w_all = lax.all_to_all(
-        jnp.broadcast_to(w_both, (16,) + w_both.shape), "row", 0, 0, axis_index_groups=sixteens
-    )
-    w_all = w_all.reshape(8, quarter, wide)
+        jnp.broadcast_to(w_own, (8,) + w_own.shape), "row", 0, 0, axis_index_groups=y_lines
+    )
 
     total, low_sum = call(
         project_kernel,

time: 167 us -> 172 us (1.030)
  starting transfers between devices: 63.6 us -> 66.9 us
  local copies, waits for them, and re-layouts: 1.55 us -> 3.84 us
  waiting for transfers between devices: 17 us -> 15 us
    ppermute x0 -> x4, starting transfers between devices: none -> 16.2 us  [the longest x3 14.2 us: on_device(): lax.ppermute(part, 'row', way)]
    all_to_all x2 -> x1, starting transfers between devices: 14.9 us -> 4.48 us  [on_device(): lax.all_to_all(jnp.broadcast_to(w_own, (8,) + w_own.shape), 'row', 0, 0,...]
    all_to_all x2 -> x1, waiting for transfers between devices: 7.96 us -> 0.01 us  [on_device(): lax.all_to_all(jnp.broadcast_to(w_own, (8,) + w_own.shape), 'row', 0, 0,...]
    ppermute x0 -> x4, waiting for transfers between devices: none -> 6.34 us  [the longest x1 5.16 us: on_device(): w_far = lax.ppermute(w_both, 'row', opposite)]
    ppermute x3, starting transfers between devices: 21.3 us -> 18.9 us  [ring_of(): far = lax.ppermute(far, axis, fore)]
    pallas_call x9 -> x10, Pallas kernels: 15.7 us -> 16.4 us  [call(): pl.pallas_call(kernel, out_shape=[jax.ShapeDtypeStruct(s, d) for s, d in...]
  transfers between devices with their start and end apart: 13 -> 16, of which waited for: 8 -> 8; matrix products, arithmetic and copies ran while one was open for 0% -> 1% of each run, Pallas kernels for 3% -> 3%
where the time goes in v8:
time: 172 us; the launch traced here: 171 us
  blocking collectives  67.4 us (39%)
  starting transfers between devices  66.9 us (39%)
  Pallas kernels  16.4 us (10%)
  waiting for transfers between devices  15 us (9%)
  local copies, waits for them, and re-layouts  3.84 us (2%)
    ppermute x3, starting transfers between devices, ring_of(): far = lax.ppermute(far, axis, fore)  18.9 us
    all_to_all x1, blocking collectives, on_device(): lax.all_to_all(square, 'row', 0, 0, axis_index_groups=y_lines)  17.8 us
    pallas_call x10, Pallas kernels, call(): pl.pallas_call(kernel, out_shape=[jax.ShapeDtypeStruct(s, d) for s, d in...  16.4 us
    ppermute x3, starting transfers between devices, on_device(): lax.ppermute(part, 'row', way)  14.2 us
    all_to_all x1, blocking collectives, on_device(): term_parts = lax.all_to_all(terms, 'row', 0, 0, axis_index_groups=squares)  13.9 us
    ppermute x3, starting transfers between devices, ring_of(): near.append(lax.ppermute(near[-1], axis, fore))  12.8 us
    all_to_all x1, blocking collectives, on_device(): pieces = lax.all_to_all(summed, 'row', 0, 0, axis_index_groups=squares)  12.2 us
    all_to_all x1, blocking collectives, on_device(): packs = lax.all_to_all(pack, 'col', 0, 0)  12.1 us
  transfers between devices with their start and end apart: 16, of which 8 were waited for; matrix products, arithmetic and copies ran while one was open for 1% of the time, Pallas kernels for 3%

profile of v8, /device:TPU:1, one launch (start us, length us, event | category | flops | bytes accessed | tf_op | source)
XLA Modules:
  0.0 170.7 jit_solution(15687155052937944246)
XLA Ops:
  0.7 0.6 stack.23.pos_ref
  1.3 2.6 %shard_map.112 = (bf16[128,512]{1,0:T(8,128)(2,1)}, bf16[128,512]{1,0:T(8,128)(2,1)}, bf16[128,512]{1,0:T(8,128)(2,1)}, bf16[128,512]{1,0:T(8,128)(2,1)}) custom-call(s32[5]{0:T(128)} %stack.23.pos_ref, bf16[128,2048]{1,0:T(8,128)(2,1)} %t_ref.5), custom_call_target="tpu_custom_call" | custom-call | tf_op jit(solution)/shard_map/pallas_call | solution.py:251
  3.9 8.8 %collective-permute-start = (bf16[128,512]{1,0:T(8,128)(2,1)}, bf16[128,512]{1,0:T(8,128)(2,1)S(1)}, u32[]{:S(2)}, u32[]{:S(2)}) collective-permute-start(bf16[128,512]{1,0:T(8,128)(2,1)} %get-tuple-element.22), channel_id=1, source_target_pairs={{0,8},{8,0},{16,24},{24,16},{32,40},{40,32},{48,56},{56,48},{64,72... | collective-permute-start | bytes 393224 | tf_op jit(solution)/shard_map/ppermute | solution.py:316
  12.7 1.9 %collective-permute-start.1 = (bf16[128,512]{1,0:T(8,128)(2,1)}, bf16[128,512]{1,0:T(8,128)(2,1)S(1)}, u32[]{:S(2)}, u32[]{:S(2)}) collective-permute-start(bf16[128,512]{1,0:T(8,128)(2,1)} %get-tuple-element.23), channel_id=1, source_target_pairs={{0,16},{8,24},{16,0},{24,8},{32,48},{40,56},{48,32},{56,40},{64,80... | collective-permute-start | bytes 393224 | tf_op jit(solution)/shard_map/ppermute | solution.py:316
  14.6 3.5 %collective-permute-start.2 = (bf16[128,512]{1,0:T(8,128)(2,1)}, bf16[128,512]{1,0:T(8,128)(2,1)S(1)}, u32[]{:S(2)}, u32[]{:S(2)}) collective-permute-start(bf16[128,512]{1,0:T(8,128)(2,1)} %get-tuple-element.24), channel_id=1, source_target_pairs={{0,24},{8,16},{16,8},{24,0},{32,56},{40,48},{48,40},{56,32},{64,88... | collective-permute-start | bytes 393224 | tf_op jit(solution)/shard_map/ppermute | solution.py:316
  18.2 0.9 constant_dynamic-update-slice_fusion.1
  19.0 0.9 constant_dynamic-update-slice_fusion
  19.9 1.9 %collective-permute-start.3 = (bf16[256,256]{1,0:T(8,128)(2,1)S(1)}, bf16[256,256]{1,0:T(8,128)(2,1)S(1)}, u32[]{:S(2)}, u32[]{:S(2)}) collective-permute-start(bf16[256,256]{1,0:T(8,128)(2,1)S(1)} %constant_dynamic-update-slice_fusion), channel_id=1, source_target_pairs={{0,32},{8,40},{16,48},{24,56},{32,0},{40,8},{48,16},{56,24},{64,96... | collective-permute-start | bytes 393224 | tf_op jit(solution)/shard_map/ppermute | solution.py:324
  21.9 1.2 collective-permute-done.2.refs_3_
  23.0 5.2 %collective-permute-done.3 = bf16[256,256]{1,0:T(8,128)(2,1)S(1)} collective-permute-done((bf16[256,256]{1,0:T(8,128)(2,1)S(1)}, bf16[256,256]{1,0:T(8,128)(2,1)S(1)}, u32[]{:S(2)}, u32[]{:S(2)}) %collective-permute-start.3) | collective-permute-done | bytes 131104 | tf_op jit(solution)/shard_map/ppermute | solution.py:324
  28.2 1.5 broadcast_in_dim.3
  29.7 4.5 %all-to-all-start = ((bf16[8,512,256]{2,1,0:T(8,128)(2,1)}), bf16[8,512,256]{2,1,0:T(8,128)(2,1)}, u32[]{:S(2)}, u32[]{:S(2)}) async-start(bf16[8,512,256]{2,1,0:T(8,128)(2,1)} %broadcast_in_dim.3), calls=%async_computation | async-start | bytes 4194304 | tf_op jit(solution)/shard_map/all_to_all | solution.py:332
  34.2 0.4 shard_map.113.refs_4_
  34.6 2.9 %collective-permute-start.7 = (bf16[528,512]{1,0:T(8,128)(2,1)S(1)}, bf16[528,512]{1,0:T(8,128)(2,1)S(1)}, u32[]{:S(2)}, u32[]{:S(2)}) collective-permute-start(bf16[528,512]{1,0:T(8,128)(2,1)S(1)} %shard_map.114.refs_0_), channel_id=1, source_target_pairs={{0,8},{8,0},{16,24},{24,16},{32,40},{40,32},{48,56},{56,48},{64,72... | collective-permute-start | bytes 1622024 | tf_op jit(solution)/shard_map/ppermute | solution.py:82
  37.5 1.5 collective-permute-done.7
  39.1 8.0 %collective-permute-start.8 = (bf16[528,512]{1,0:T(8,128)(2,1)S(1)}, bf16[528,512]{1,0:T(8,128)(2,1)S(1)}, u32[]{:S(2)}, u32[]{:S(2)}) collective-permute-start(bf16[528,512]{1,0:T(8,128)(2,1)S(1)} %collective-permute-done.7), channel_id=1, source_target_pairs={{0,1},{1,2},{2,3},{3,4},{4,5},{5,6},{6,7},{7,0},{8,15},{9,8},{10,9... | collective-permute-start | bytes 1622024 | tf_op jit(solution)/shard_map/ppermute | solution.py:85
  47.1 2.2 %collective-permute-start.4 = (bf16[528,512]{1,0:T(8,128)(2,1)S(1)}, bf16[528,512]{1,0:T(8,128)(2,1)S(1)}, u32[]{:S(2)}, u32[]{:S(2)}) collective-permute-start(bf16[528,512]{1,0:T(8,128)(2,1)S(1)} %shard_map.114.refs_0_), channel_id=1, source_target_pairs={{0,1},{1,2},{2,3},{3,4},{4,5},{5,6},{6,7},{7,0},{8,15},{9,8},{10,9... | collective-permute-start | bytes 1622024 | tf_op jit(solution)/shard_map/ppermute | solution.py:84
  49.3 4.1 %collective-permute-done.8 = bf16[528,512]{1,0:T(8,128)(2,1)S(1)} collective-permute-done((bf16[528,512]{1,0:T(8,128)(2,1)S(1)}, bf16[528,512]{1,0:T(8,128)(2,1)S(1)}, u32[]{:S(2)}, u32[]{:S(2)}) %collective-permute-start.8) | collective-permute-done | bytes 540704 | tf_op jit(solution)/shard_map/ppermute | solution.py:85
  53.4 5.4 %collective-permute-start.10 = (bf16[528,512]{1,0:T(8,128)(2,1)S(1)}, bf16[528,512]{1,0:T(8,128)(2,1)S(1)}, u32[]{:S(2)}, u32[]{:S(2)}) collective-permute-start(bf16[528,512]{1,0:T(8,128)(2,1)S(1)} %collective-permute-done.8), channel_id=1, source_target_pairs={{0,1},{1,2},{2,3},{3,4},{4,5},{5,6},{6,7},{7,0},{8,15},{9,8},{10,9... | collective-permute-start | bytes 1622024 | tf_op jit(solution)/shard_map/ppermute | solution.py:85
  58.8 0.4 collective-permute-done.4.refs_1_
  59.2 5.3 %collective-permute-start.5 = (bf16[528,512]{1,0:T(8,128)(2,1)S(1)}, bf16[528,512]{1,0:T(8,128)(2,1)S(1)}, u32[]{:S(2)}, u32[]{:S(2)}) collective-permute-start(bf16[528,512]{1,0:T(8,128)(2,1)S(1)} %collective-permute-done.4.refs_1_), channel_id=1, source_target_pairs={{0,1},{1,2},{2,3},{3,4},{4,5},{5,6},{6,7},{7,0},{8,15},{9,8},{10,9... | collective-permute-start | bytes 1622024 | tf_op jit(solution)/shard_map/ppermute | solution.py:84
  64.5 0.6 collective-permute-done.10
  65.1 5.4 %collective-permute-start.12 = (bf16[528,512]{1,0:T(8,128)(2,1)S(1)}, bf16[528,512]{1,0:T(8,128)(2,1)S(1)}, u32[]{:S(2)}, u32[]{:S(2)}) collective-permute-start(bf16[528,512]{1,0:T(8,128)(2,1)S(1)} %collective-permute-done.10), channel_id=1, source_target_pairs={{0,1},{1,2},{2,3},{3,4},{4,5},{5,6},{6,7},{7,0},{8,15},{9,8},{10,9... | collective-permute-start | bytes 1622024 | tf_op jit(solution)/shard_map/ppermute | solution.py:85
  70.5 0.4 collective-permute-done.5.refs_2_
  70.9 5.4 %collective-permute-start.6 = (bf16[528,512]{1,0:T(8,128)(2,1)S(1)}, bf16[528,512]{1,0:T(8,128)(2,1)S(1)}, u32[]{:S(2)}, u32[]{:S(2)}) collective-permute-start(bf16[528,512]{1,0:T(8,128)(2,1)S(1)} %collective-permute-done.5.refs_2_), channel_id=1, source_target_pairs={{0,1},{1,2},{2,3},{3,4},{4,5},{5,6},{6,7},{7,0},{8,15},{9,8},{10,9... | collective-permute-start | bytes 1622024 | tf_op jit(solution)/shard_map/ppermute | solution.py:84
  76.3 1.9 %collective-permute-start.9 = (bf16[528,512]{1,0:T(8,128)(2,1)S(1)}, bf16[528,512]{1,0:T(8,128)(2,1)}, u32[]{:S(2)}, u32[]{:S(2)}) collective-permute-start(bf16[528,512]{1,0:T(8,128)(2,1)S(1)} %collective-permute-done.8), channel_id=1, source_target_pairs={{0,8},{8,0},{16,24},{24,16},{32,40},{40,32},{48,56},{56,48},{64,72... | collective-permute-start | bytes 1622024 | tf_op jit(solution)/shard_map/ppermute | solution.py:86
  78.2 2.4 %collective-permute-start.11 = (bf16[528,512]{1,0:T(8,128)(2,1)S(1)}, bf16[528,512]{1,0:T(8,128)(2,1)}, u32[]{:S(2)}, u32[]{:S(2)}) collective-permute-start(bf16[528,512]{1,0:T(8,128)(2,1)S(1)} %collective-permute-done.10), channel_id=1, source_target_pairs={{0,8},{8,0},{16,24},{24,16},{32,40},{40,32},{48,56},{56,48},{64,72... | collective-permute-start | bytes 1622024 | tf_op jit(solution)/shard_map/ppermute | solution.py:86
  80.7 0.0 collective-permute-done.12
  80.7 1.9 %collective-permute-start.13 = (bf16[528,512]{1,0:T(8,128)(2,1)S(1)}, bf16[528,512]{1,0:T(8,128)(2,1)}, u32[]{:S(2)}, u32[]{:S(2)}) collective-permute-start(bf16[528,512]{1,0:T(8,128)(2,1)S(1)} %collective-permute-done.12), channel_id=1, source_target_pairs={{0,8},{8,0},{16,24},{24,16},{32,40},{40,32},{48,56},{56,48},{64,72... | collective-permute-start | bytes 1622024 | tf_op jit(solution)/shard_map/ppermute | solution.py:86
  82.6 0.0 collective-permute-done.6.refs_3_
  82.6 5.4 %collective-permute-start.14 = (bf16[528,512]{1,0:T(8,128)(2,1)S(1)}, bf16[528,512]{1,0:T(8,128)(2,1)S(1)}, u32[]{:S(2)}, u32[]{:S(2)}) collective-permute-start(bf16[528,512]{1,0:T(8,128)(2,1)S(1)} %collective-permute-done.6.refs_3_), channel_id=1, source_target_pairs={{0,1},{1,2},{2,3},{3,4},{4,5},{5,6},{6,7},{7,0},{8,15},{9,8},{10,9... | collective-permute-start | bytes 1622024 | tf_op jit(solution)/shard_map/ppermute | solution.py:87
  88.0 0.0 collective-permute-done.11.refs_5_
  88.1 4.5 %shard_map.115 = (f32[512,256]{1,0:T(8,128)S(1)}, f32[16,512]{1,0:T(8,128)S(1)}) custom-call(s32[5]{0:T(128)S(1)} %copy-done.7, bf16[528,512]{1,0:T(8,128)(2,1)S(1)} %shard_map.114.refs_0_, bf16[528,512]{1,0:T(8,128)(2,1)S(1)} %collective-permute-done.4.refs_1_, bf16[528,512]{1,0:T(8,128)(2,1)} %copy-done.9, bf16[528,512]{1,0:T(8,128)(2,1)} %copy-done.10, ...), custom_call_target="tpu_custom_call" | custom-call | flops 939524096 | bytes 5881856 | tf_op jit(solution)/shard_map/pallas_call | solution.py:251
  92.6 0.0 copy-start.1
  92.6 0.0 copy-start.2
  92.6 0.0 copy-start.5
  92.6 0.0 copy-start.6
  92.6 0.0 copy-start.8
  92.6 1.7 collective-permute-done.14.t_ref
  94.3 1.9 %shard_map.116 = (bf16[4,128,256]{2,1,0:T(8,128)(2,1)S(1)}, bf16[128,64]{1,0:T(8,128)(2,1)S(1)}) custom-call(s32[5]{0:T(128)S(1)} %copy-done.7, f32[512,256]{1,0:T(8,128)S(1)} %get-tuple-element.29.total_ref, f32[16,512]{1,0:T(8,128)S(1)} %get-tuple-element.30.low_ref, bf16[528,512]{1,0:T(8,128)(2,1)S(1)} %collective-permute-done.14.t_ref, ...), custom_call_target="tpu_custom_call" | custom-call | tf_op jit(solution)/shard_map/pallas_call | solution.py:251
  96.2 11.5 %all_to_all.30.full_ref = bf16[4,128,256]{2,1,0:T(8,128)(2,1)S(1)} all-to-all(bf16[4,128,256]{2,1,0:T(8,128)(2,1)S(1)} %get-tuple-element.31), channel_id=1, replica_groups={{0,8,16,24},{32,40,48,56},{64,72,80,88},{96,104,112,120},{128,136,144,1..., dimensions={0} | all-to-all | bytes 524288 | tf_op jit(solution)/shard_map/all_to_all | solution.py:366
  107.7 5.1 %shard_map.117 = (bf16[8,80,128]{2,1,0:T(8,128)(2,1)S(1)}, f32[128,128]{1,0:T(8,128)S(1)}, f32[128,128]{1,0:T(8,128)S(1)}) custom-call(s32[1,8]{1,0:T(1,128)S(1)} %copy-done.8, bf16[4,128,256]{2,1,0:T(8,128)(2,1)S(1)} %all_to_all.30.full_ref, bf16[128,64]{1,0:T(8,128)(2,1)S(1)} %get-tuple-element.32.low_ref.low_half_ref, bf16[64,128]{1,0:T(8,128)(2,1)S(1)} %copy-done.5, ...), custom_call_target="tpu_custom_call" | custom-call | tf_op jit(solution)/shard_map/pallas_call | solution.py:251
  112.9 12.1 %all_to_all.31.pack_ref = bf16[8,80,128]{2,1,0:T(8,128)(2,1)S(1)} all-to-all(bf16[8,80,128]{2,1,0:T(8,128)(2,1)S(1)} %get-tuple-element.33), channel_id=1, replica_groups=mesh['row'=64,'col'=8] {'col'}, dimensions={0} | all-to-all | bytes 327680 | tf_op jit(solution)/shard_map/all_to_all | solution.py:379
  124.9 0.9 shard_map.118
  125.9 13.9 %all_to_all.32.in_ref = bf16[8,72,256]{2,1,0:T(8,128)(2,1)S(1)} all-to-all(bf16[8,72,256]{2,1,0:T(8,128)(2,1)S(1)} %shard_map.118), channel_id=1, replica_groups={{0,8,16,24,32,40,48,56},{64,72,80,88,96,104,112,120},{128,136,144,152,1..., dimensions={0} | all-to-all | bytes 589824 | tf_op jit(solution)/shard_map/all_to_all | solution.py:385
  139.9 17.8 %all_to_all.33.in_ref = bf16[8,72,256]{2,1,0:T(8,128)(2,1)S(1)} all-to-all(bf16[8,72,256]{2,1,0:T(8,128)(2,1)S(1)} %shard_map.119), channel_id=1, replica_groups={{0,64,128,192,256,320,384,448},{8,72,136,200,264,328,392,456},{16,80,14..., dimensions={0} | all-to-all | bytes 589824 | tf_op jit(solution)/shard_map/all_to_all | solution.py:387
  157.7 12.2 %all_to_all.34.in_ref = bf16[8,72,256]{2,1,0:T(8,128)(2,1)S(1)} all-to-all(bf16[8,72,256]{2,1,0:T(8,128)(2,1)S(1)} %shard_map.120), channel_id=1, replica_groups={{0,8,16,24,32,40,48,56},{64,72,80,88,96,104,112,120},{128,136,144,152,1..., dimensions={0} | all-to-all | bytes 589824 | tf_op jit(solution)/shard_map/all_to_all | solution.py:389
  169.8 0.8 shard_map.121
  (26 shorter events, 0.2 us)
Async XLA Ops:
  3.9 17.9 %collective-permute-start = (bf16[128,512]{1,0:T(8,128)(2,1)}, bf16[128,512]{1,0:T(8,128)(2,1)S(1)}, u32[]{:S(2)}, u32[]{:S(2)}) collective-permute-start(bf16[128,512]{1,0:T(8,128)(2,1)} %get-tuple-element.22), channel_id=1, source_target_pairs={{0,8},{8,0},{16,24},{24,16},{32,40},{40,32},{48,56},{56,48},{64,72... | collective-permute-start | bytes 393224 | tf_op jit(solution)/shard_map/ppermute | solution.py:316
  12.7 9.1 %collective-permute-start.1 = (bf16[128,512]{1,0:T(8,128)(2,1)}, bf16[128,512]{1,0:T(8,128)(2,1)S(1)}, u32[]{:S(2)}, u32[]{:S(2)}) collective-permute-start(bf16[128,512]{1,0:T(8,128)(2,1)} %get-tuple-element.23), channel_id=1, source_target_pairs={{0,16},{8,24},{16,0},{24,8},{32,48},{40,56},{48,32},{56,40},{64,80... | collective-permute-start | bytes 393224 | tf_op jit(solution)/shard_map/ppermute | solution.py:316
  14.6 8.4 %collective-permute-start.2 = (bf16[128,512]{1,0:T(8,128)(2,1)}, bf16[128,512]{1,0:T(8,128)(2,1)S(1)}, u32[]{:S(2)}, u32[]{:S(2)}) collective-permute-start(bf16[128,512]{1,0:T(8,128)(2,1)} %get-tuple-element.24), channel_id=1, source_target_pairs={{0,24},{8,16},{16,8},{24,0},{32,56},{40,48},{48,40},{56,32},{64,88... | collective-permute-start | bytes 393224 | tf_op jit(solution)/shard_map/ppermute | solution.py:316
  19.9 8.3 %collective-permute-start.3 = (bf16[256,256]{1,0:T(8,128)(2,1)S(1)}, bf16[256,256]{1,0:T(8,128)(2,1)S(1)}, u32[]{:S(2)}, u32[]{:S(2)}) collective-permute-start(bf16[256,256]{1,0:T(8,128)(2,1)S(1)} %constant_dynamic-update-slice_fusion), channel_id=1, source_target_pairs={{0,32},{8,40},{16,48},{24,56},{32,0},{40,8},{48,16},{56,24},{64,96... | collective-permute-start | bytes 393224 | tf_op jit(solution)/shard_map/ppermute | solution.py:324
  29.7 4.5 %copy-start = (bf16[128,2048]{1,0:T(8,128)(2,1)S(1)}, bf16[128,2048]{1,0:T(8,128)(2,1)}, u32[]{:S(2)}) copy-start(bf16[128,2048]{1,0:T(8,128)(2,1)} %t_ref.5) | copy-start | bytes 1572868
  29.7 4.5 %copy-start.3 = (bf16[2048,64]{0,1:T(8,128)(2,1)S(1)}, bf16[2048,64]{0,1:T(8,128)(2,1)}, u32[]{:S(2)}) copy-start(bf16[2048,64]{0,1:T(8,128)(2,1)} %param.14) | copy-start | bytes 786436
  29.7 4.9 %copy-start.4 = (bf16[128,512]{1,0:T(8,128)(2,1)S(1)}, bf16[128,512]{1,0:T(8,128)(2,1)}, u32[]{:S(2)}) copy-start(bf16[128,512]{1,0:T(8,128)(2,1)} %get-tuple-element.21.refs_0_) | copy-start | bytes 393220
  29.7 58.4 %copy-start.7 = (s32[5]{0:T(128)S(1)}, s32[5]{0:T(128)}, u32[]{:S(2)}) copy-start(s32[5]{0:T(128)} %stack.23.pos_ref) | copy-start | bytes 64
  29.7 58.4 %all-to-all-start = ((bf16[8,512,256]{2,1,0:T(8,128)(2,1)}), bf16[8,512,256]{2,1,0:T(8,128)(2,1)}, u32[]{:S(2)}, u32[]{:S(2)}) async-start(bf16[8,512,256]{2,1,0:T(8,128)(2,1)} %broadcast_in_dim.3), calls=%async_computation | async-start | bytes 4194304 | tf_op jit(solution)/shard_map/all_to_all | solution.py:332
  34.6 4.5 %collective-permute-start.7 = (bf16[528,512]{1,0:T(8,128)(2,1)S(1)}, bf16[528,512]{1,0:T(8,128)(2,1)S(1)}, u32[]{:S(2)}, u32[]{:S(2)}) collective-permute-start(bf16[528,512]{1,0:T(8,128)(2,1)S(1)} %shard_map.114.refs_0_), channel_id=1, source_target_pairs={{0,8},{8,0},{16,24},{24,16},{32,40},{40,32},{48,56},{56,48},{64,72... | collective-permute-start | bytes 1622024 | tf_op jit(solution)/shard_map/ppermute | solution.py:82
  39.1 14.3 %collective-permute-start.8 = (bf16[528,512]{1,0:T(8,128)(2,1)S(1)}, bf16[528,512]{1,0:T(8,128)(2,1)S(1)}, u32[]{:S(2)}, u32[]{:S(2)}) collective-permute-start(bf16[528,512]{1,0:T(8,128)(2,1)S(1)} %collective-permute-done.7), channel_id=1, source_target_pairs={{0,1},{1,2},{2,3},{3,4},{4,5},{5,6},{6,7},{7,0},{8,15},{9,8},{10,9... | collective-permute-start | bytes 1622024 | tf_op jit(solution)/shard_map/ppermute | solution.py:85
  47.1 12.1 %collective-permute-start.4 = (bf16[528,512]{1,0:T(8,128)(2,1)S(1)}, bf16[528,512]{1,0:T(8,128)(2,1)S(1)}, u32[]{:S(2)}, u32[]{:S(2)}) collective-permute-start(bf16[528,512]{1,0:T(8,128)(2,1)S(1)} %shard_map.114.refs_0_), channel_id=1, source_target_pairs={{0,1},{1,2},{2,3},{3,4},{4,5},{5,6},{6,7},{7,0},{8,15},{9,8},{10,9... | collective-permute-start | bytes 1622024 | tf_op jit(solution)/shard_map/ppermute | solution.py:84
  53.4 11.7 %collective-permute-start.10 = (bf16[528,512]{1,0:T(8,128)(2,1)S(1)}, bf16[528,512]{1,0:T(8,128)(2,1)S(1)}, u32[]{:S(2)}, u32[]{:S(2)}) collective-permute-start(bf16[528,512]{1,0:T(8,128)(2,1)S(1)} %collective-permute-done.8), channel_id=1, source_target_pairs={{0,1},{1,2},{2,3},{3,4},{4,5},{5,6},{6,7},{7,0},{8,15},{9,8},{10,9... | collective-permute-start | bytes 1622024 | tf_op jit(solution)/shard_map/ppermute | solution.py:85
  59.2 11.7 %collective-permute-start.5 = (bf16[528,512]{1,0:T(8,128)(2,1)S(1)}, bf16[528,512]{1,0:T(8,128)(2,1)S(1)}, u32[]{:S(2)}, u32[]{:S(2)}) collective-permute-start(bf16[528,512]{1,0:T(8,128)(2,1)S(1)} %collective-permute-done.4.refs_1_), channel_id=1, source_target_pairs={{0,1},{1,2},{2,3},{3,4},{4,5},{5,6},{6,7},{7,0},{8,15},{9,8},{10,9... | collective-permute-start | bytes 1622024 | tf_op jit(solution)/shard_map/ppermute | solution.py:84
  65.1 15.6 %collective-permute-start.12 = (bf16[528,512]{1,0:T(8,128)(2,1)S(1)}, bf16[528,512]{1,0:T(8,128)(2,1)S(1)}, u32[]{:S(2)}, u32[]{:S(2)}) collective-permute-start(bf16[528,512]{1,0:T(8,128)(2,1)S(1)} %collective-permute-done.10), channel_id=1, source_target_pairs={{0,1},{1,2},{2,3},{3,4},{4,5},{5,6},{6,7},{7,0},{8,15},{9,8},{10,9... | collective-permute-start | bytes 1622024 | tf_op jit(solution)/shard_map/ppermute | solution.py:85
  70.9 17.2 %copy-start.9 = (bf16[528,512]{1,0:T(8,128)(2,1)}, bf16[528,512]{1,0:T(8,128)(2,1)S(1)}, u32[]{:S(2)}) copy-start(bf16[528,512]{1,0:T(8,128)(2,1)S(1)} %collective-permute-done.5.refs_2_) | copy-start | bytes 1622020
  70.9 11.7 %collective-permute-start.6 = (bf16[528,512]{1,0:T(8,128)(2,1)S(1)}, bf16[528,512]{1,0:T(8,128)(2,1)S(1)}, u32[]{:S(2)}, u32[]{:S(2)}) collective-permute-start(bf16[528,512]{1,0:T(8,128)(2,1)S(1)} %collective-permute-done.5.refs_2_), channel_id=1, source_target_pairs={{0,1},{1,2},{2,3},{3,4},{4,5},{5,6},{6,7},{7,0},{8,15},{9,8},{10,9... | collective-permute-start | bytes 1622024 | tf_op jit(solution)/shard_map/ppermute | solution.py:84
  76.3 11.7 %collective-permute-start.9 = (bf16[528,512]{1,0:T(8,128)(2,1)S(1)}, bf16[528,512]{1,0:T(8,128)(2,1)}, u32[]{:S(2)}, u32[]{:S(2)}) collective-permute-start(bf16[528,512]{1,0:T(8,128)(2,1)S(1)} %collective-permute-done.8), channel_id=1, source_target_pairs={{0,8},{8,0},{16,24},{24,16},{32,40},{40,32},{48,56},{56,48},{64,72... | collective-permute-start | bytes 1622024 | tf_op jit(solution)/shard_map/ppermute | solution.py:86
  78.2 9.8 %collective-permute-start.11 = (bf16[528,512]{1,0:T(8,128)(2,1)S(1)}, bf16[528,512]{1,0:T(8,128)(2,1)}, u32[]{:S(2)}, u32[]{:S(2)}) collective-permute-start(bf16[528,512]{1,0:T(8,128)(2,1)S(1)} %collective-permute-done.10), channel_id=1, source_target_pairs={{0,8},{8,0},{16,24},{24,16},{32,40},{40,32},{48,56},{56,48},{64,72... | collective-permute-start | bytes 1622024 | tf_op jit(solution)/shard_map/ppermute | solution.py:86
  80.7 7.4 %collective-permute-start.13 = (bf16[528,512]{1,0:T(8,128)(2,1)S(1)}, bf16[528,512]{1,0:T(8,128)(2,1)}, u32[]{:S(2)}, u32[]{:S(2)}) collective-permute-start(bf16[528,512]{1,0:T(8,128)(2,1)S(1)} %collective-permute-done.12), channel_id=1, source_target_pairs={{0,8},{8,0},{16,24},{24,16},{32,40},{40,32},{48,56},{56,48},{64,72... | collective-permute-start | bytes 1622024 | tf_op jit(solution)/shard_map/ppermute | solution.py:86
  82.6 5.5 %copy-start.10 = (bf16[528,512]{1,0:T(8,128)(2,1)}, bf16[528,512]{1,0:T(8,128)(2,1)S(1)}, u32[]{:S(2)}) copy-start(bf16[528,512]{1,0:T(8,128)(2,1)S(1)} %collective-permute-done.6.refs_3_) | copy-start | bytes 1622020
  82.6 11.7 %collective-permute-start.14 = (bf16[528,512]{1,0:T(8,128)(2,1)S(1)}, bf16[528,512]{1,0:T(8,128)(2,1)S(1)}, u32[]{:S(2)}, u32[]{:S(2)}) collective-permute-start(bf16[528,512]{1,0:T(8,128)(2,1)S(1)} %collective-permute-done.6.refs_3_), channel_id=1, source_target_pairs={{0,1},{1,2},{2,3},{3,4},{4,5},{5,6},{6,7},{7,0},{8,15},{9,8},{10,9... | collective-permute-start | bytes 1622024 | tf_op jit(solution)/shard_map/ppermute | solution.py:87
  92.6 15.1 %copy-start.1 = (bf16[128,2048]{1,0:T(8,128)(2,1)S(1)}, bf16[128,2048]{1,0:T(8,128)(2,1)}, u32[]{:S(2)}) copy-start(bf16[128,2048]{1,0:T(8,128)(2,1)} %q_ref.1) | copy-start | bytes 1572868
  92.6 15.1 %copy-start.2 = (bf16[128,2048]{1,0:T(8,128)(2,1)S(1)}, bf16[128,2048]{1,0:T(8,128)(2,1)}, u32[]{:S(2)}) copy-start(bf16[128,2048]{1,0:T(8,128)(2,1)} %p_ref.1) | copy-start | bytes 1572868
  92.6 15.1 %copy-start.5 = (bf16[64,128]{1,0:T(8,128)(2,1)S(1)}, bf16[64,128]{1,0:T(8,128)(2,1)}, u32[]{:S(2)}) copy-start(bf16[64,128]{1,0:T(8,128)(2,1)} %upk_ref.1) | copy-start | bytes 49156
  92.6 15.1 %copy-start.6 = (bf16[64,128]{1,0:T(8,128)(2,1)S(1)}, bf16[64,128]{1,0:T(8,128)(2,1)}, u32[]{:S(2)}) copy-start(bf16[64,128]{1,0:T(8,128)(2,1)} %upv_ref.1) | copy-start | bytes 49156
  92.6 15.1 %copy-start.8 = (s32[1,8]{1,0:T(1,128)S(1)}, s32[1,8]{1,0:T(1,128)}, u32[]{:S(2)}) copy-start(s32[1,8]{1,0:T(1,128)} %lengths_ref.3) | copy-start | bytes 100

commit v9 on v4

--- a/solution.py
+++ b/solution.py
@@ -11,6 +11,7 @@
 BF = jnp.bfloat16
 F32 = jnp.float32
 npo_beta = 0.5
+LOG2E = 1.4426950408889634
 
 VMEM = pl.BlockSpec(memory_space=pltpu.VMEM)
 SMEM = pl.BlockSpec(memory_space=pltpu.SMEM)
@@ -79,39 +80,69 @@
     ]
 
 
+def block_at(pos_ref, axis, step, n):
+    return lax.rem(pos_ref[1 + axis] + step * (2 * pos_ref[0] - 1) + n, n)
+
+
 def project_kernel(pos_ref, *refs):
-    t_refs, w_refs, refs = refs[:9], refs[9:18], refs[18:]
-    own_ref, other_ref, low_ref, t_scr, w_scr, sem = refs
+    t_refs, w_refs, refs = refs[:7], refs[7:14], refs[14:]
+    total_ref, low_ref, t_left_ref, w_left_ref, t_scr, w_scr, sem = refs
     n = t_scr.shape[0]
-    way = 2 * pos_ref[0] - 1
     copies = []
-    for at, (parts, scr) in enumerate(((t_refs, t_scr), (w_refs, w_scr))):
-        cut = parts[7].shape[0]
-        for j, step in enumerate(STEPS):
-            k = lax.rem(pos_ref[1 + at] + step * way + n, n)
-            if step == 4:
-                pairs = [
-                    (parts[7], scr.at[k, pl.ds(0, cut)]),
-                    (parts[8], scr.at[k, pl.ds(cut, scr.shape[1] - cut)]),
-                ]
-            else:
-                pairs = [(parts[j], scr.at[k])]
-            for i, (a, b) in enumerate(pairs):
-                copies.append(pltpu.make_async_copy(a, b, sem.at[at, j + i]))
+    for axis, (parts, scr) in enumerate(((t_refs, t_scr), (w_refs, w_scr))):
+        for j, part in enumerate(parts):
+            k = block_at(pos_ref, axis, STEPS[j], n)
+            copies.append(pltpu.make_async_copy(part, scr.at[k], sem.at[axis, j]))
+    for c in copies:
+        c.start()
+    t_far, w_far = (block_at(pos_ref, axis, STEPS[7], n) for axis in range(2))
+    t_scr[t_far] = jnp.zeros(t_scr.shape[1:], BF)
+    w_scr[w_far] = jnp.zeros(w_scr.shape[1:], BF)
+    for c in copies:
+        c.wait()
+    rows = total_ref.shape[0]
+    total = jnp.zeros(total_ref.shape, F32)
+    low = jnp.zeros(low_ref.shape, F32)
+    for k in range(n):
+        total = total + mm(t_scr[k, pl.ds(0, rows)], w_scr[k], NN)
+        low = low + t_scr[k, pl.ds(rows, low.shape[0])].astype(F32)
+    total_ref[...] = total
+    low_ref[...] = low
+    t_left_ref[...] = t_scr[w_far, pl.ds(0, rows)]
+    w_left_ref[...] = w_scr[t_far]
+
+
+def finish_kernel(
+    pos_ref, t1_ref, t2_ref, w1_ref, w2_ref, total_ref, low_ref, t_left_ref, w_left_ref,
+    own_ref, other_ref, low_half_ref,
+    t_scr, w_scr, total_scr, low_scr, t_left_scr, w_left_scr, sem,
+):
+    pairs = [
+        (t1_ref, t_scr.at[pl.ds(0, t1_ref.shape[0])]),
+        (t2_ref, t_scr.at[pl.ds(t1_ref.shape[0], t2_ref.shape[0])]),
+        (w1_ref, w_scr.at[pl.ds(0, w1_ref.shape[0])]),
+        (w2_ref, w_scr.at[pl.ds(w1_ref.shape[0], w2_ref.shape[0])]),
+        (total_ref, total_scr),
+        (low_ref, low_scr),
+        (t_left_ref, t_left_scr),
+        (w_left_ref, w_left_scr),
+    ]
+    copies = [pltpu.make_async_copy(a, b, sem.at[i]) for i, (a, b) in enumerate(pairs)]
     for c in copies:
         c.start()
     for c in copies:
         c.wait()
     rows = own_ref.shape[0]
-    total = jnp.zeros((2 * rows, w_scr.shape[2]), F32)
-    low = jnp.zeros((t_scr.shape[1] - 2 * rows, t_scr.shape[2]), F32)
-    for k in range(n):
-        total = total + mm(t_scr[k, pl.ds(0, 2 * rows)], w_scr[k], NN)
-        low = low + t_scr[k, pl.ds(2 * rows, low.shape[0])].astype(F32)
+    same = pos_ref[1] == pos_ref[2]
+    w_late = w_scr[...]
+    w_match = jnp.where(same, w_late, w_left_scr[...])
+    total = total_scr[...] + mm(t_scr[pl.ds(0, 2 * rows)], w_match, NN)
+    total = total + mm(t_left_scr[...], w_late, NN)
     own_ref[...] = total[:rows]
     other_ref[...] = total[rows:]
+    low = low_scr[...] + t_scr[pl.ds(2 * rows, low_scr.shape[0])].astype(F32)
     low = low[:low.shape[0] // 2] + low[low.shape[0] // 2:]
-    low_ref[...] = unfold(low, low_ref.shape[1]).astype(BF)
+    low_half_ref[...] = unfold(low, low_half_ref.shape[1]).astype(BF)
 
 
 def attend_kernel(
@@ -143,11 +174,11 @@
     t_at = lax.broadcasted_iota(jnp.int32, (rows, rows), 1)
     allowed = (doc_s == doc_t) & (t_at >= s_at)
 
-    def probs_of(scores):
-        scores = jnp.where(allowed, scores * score_scale, -1e30)
+    def raised(scores):
+        scores = jnp.where(allowed, scores, -1e30)
         peak = jnp.max(scores, axis=0, keepdims=True)
-        e = jnp.exp(scores - peak)
-        return e / jnp.sum(e, axis=0, keepdims=True)
+        e = jnp.exp2((scores - peak) * (score_scale * LOG2E))
+        return e, 1.0 / jnp.sum(e, axis=0, keepdims=True)
 
     gk = jnp.zeros((rows, HD), F32)
     gv = jnp.zeros((rows, HD), F32)
@@ -160,11 +191,12 @@
         probe = p_scr[:, pl.ds(h * HD, HD)]
         scores = mm(keys, q, NT)
         grads = mm(values, probe, NT)
-        pol = probs_of(scores[:rows])
-        ref = probs_of(scores[rows:])
+        pol, share = raised(scores[:rows])
+        pol = pol * share
+        ref, share = raised(scores[rows:])
         grad_pol = grads[:rows]
         mean_pol = jnp.sum(pol * grad_pol, axis=0, keepdims=True)
-        mean_ref = jnp.sum(ref * grads[rows:], axis=0, keepdims=True)
+        mean_ref = jnp.sum(ref * grads[rows:], axis=0, keepdims=True) * share
         gap = gap + (mean_pol - mean_ref)
         grad_scores = (pol * (grad_pol - mean_pol)).astype(BF)
         gk = gk + mm(grad_scores, q, NN)
@@ -227,13 +259,16 @@
         upv_ref[pl.ds(j * deep, deep)] = up[:, HD:]
 
 
-def call(kernel, outs, in_specs, out_specs, *args, scratch=(), mib=8):
+def call(kernel, outs, in_specs, out_specs, *args, scratch=(), mib=8, cost=None):
     return pl.pallas_call(
         kernel,
         out_shape=[jax.ShapeDtypeStruct(s, d) for s, d in outs],
         in_specs=in_specs,
         out_specs=out_specs,
         scratch_shapes=list(scratch),
+        cost_estimate=cost and pl.CostEstimate(
+            flops=cost[0], bytes_accessed=cost[1], transcendentals=0
+        ),
         compiler_params=pltpu.CompilerParams(vmem_limit_bytes=mib * 1024 * 1024),
     )(*args)
 
@@ -270,7 +305,6 @@
         low_kernel, [((16, feats // 2), BF)], [VMEM, VMEM], [VMEM], tokens, down_proj.T
     )
     pair = jnp.concatenate([mine, swapped, low_part], axis=0)
-    t_parts = ring_of(pair, ("row", "col"), z_fore, z_aft, rows)
 
     w_both = jnp.concatenate([w_key, w_value], axis=1)
     wide = w_both.shape[1]
@@ -278,20 +312,40 @@
         jnp.broadcast_to(w_both, (4,) + w_both.shape), "row", 0, 0, axis_index_groups=x_lines
     )
     w_own = w_line.reshape(feats // 2, wide)
+    t_parts = ring_of(pair, ("row", "col"), z_fore, z_aft, rows)
     w_parts = ring_of(w_own, "row", y_fore, y_aft, feats // 4)
 
+    deep = feats // 2
+    total, low_sum, t_left, w_left = call(
+        project_kernel,
+        [((2 * rows, wide), F32), ((16, deep), F32), ((2 * rows, deep), BF), (w_own.shape, BF)],
+        [SMEM] + [HBM] * 14,
+        [VMEM] * 4,
+        pos, *t_parts[:7], *w_parts[:7],
+        scratch=[
+            pltpu.VMEM((8,) + pair.shape, BF),
+            pltpu.VMEM((8,) + w_own.shape, BF),
+            pltpu.SemaphoreType.DMA((2, 7)),
+        ],
+        mib=52,
+        cost=(2 * 16 * rows * deep * wide, 14 * (pair.size + w_own.size)),
+    )
     own, other, low_half = call(
-        project_kernel,
+        finish_kernel,
         [((rows, wide), F32), ((rows, wide), F32), ((rows, 64), BF)],
-        [SMEM] + [HBM] * 18,
+        [SMEM] + [HBM] * 8,
         [VMEM] * 3,
-        pos, *t_parts, *w_parts,
+        pos, *t_parts[7:], *w_parts[7:], total, low_sum, t_left, w_left,
         scratch=[
-            pltpu.VMEM((8, 2 * rows + 16, feats // 2), BF),
-            pltpu.VMEM((8, feats // 2, wide), BF),
-            pltpu.SemaphoreType.DMA((2, 9)),
+            pltpu.VMEM(pair.shape, BF),
+            pltpu.VMEM(w_own.shape, BF),
+            pltpu.VMEM(total.shape, F32),
+            pltpu.VMEM(low_sum.shape, F32),
+            pltpu.VMEM(t_left.shape, BF),
+            pltpu.VMEM(w_left.shape, BF),
+            pltpu.SemaphoreType.DMA((8,)),
         ],
-        mib=56,
+        mib=52,
     )
     got = lax.ppermute(other, "row", swap)
     pack, gk, gv = call(

time: 168 us -> 162 us (0.964)
  starting transfers between devices: 77 us -> 72.7 us
  waiting for transfers between devices: 15.2 us -> 11.7 us
  blocking collectives: 53.8 us -> 56.6 us
    ppermute x2, waiting for transfers between devices: 3.82 us -> 0.01 us  [ring_of(): lax.ppermute(fore_going[3][:cut], axis, fore)]
    ppermute x1, starting transfers between devices: 7.28 us -> 4.23 us  [on_device(): got = lax.ppermute(other, 'row', swap)]
    all_to_all x1, blocking collectives: 14.7 us -> 17.5 us  [on_device(): lax.all_to_all(square, 'row', 0, 0, axis_index_groups=y_lines)]
    ppermute x6, starting transfers between devices: 14.1 us -> 11.5 us  [ring_of(): aft_going.append(lax.ppermute(aft_going[-1], axis, aft))]
    ppermute x6, starting transfers between devices: 28.6 us -> 30.3 us  [ring_of(): fore_going.append(lax.ppermute(fore_going[-1], axis, fore))]
    unnamed x62 -> x50, local copies, waits for them, and re-layouts: 4.14 us -> 2.73 us
    pallas_call x8 -> x9, Pallas kernels: 14.3 us -> 15.5 us  [call(): pl.pallas_call(kernel, out_shape=[jax.ShapeDtypeStruct(s, d) for s, d in...]
  transfers between devices with their start and end apart: 19 -> 19, of which waited for: 7 -> 6; matrix products, arithmetic and copies ran while one was open for 1% -> 1% of each run, Pallas kernels for 0% -> 3%
where the time goes in v9:
time: 162 us
  starting transfers between devices  72.7 us (45%)
  blocking collectives  56.6 us (35%)
  Pallas kernels  15.5 us (10%)
  waiting for transfers between devices  11.7 us (7%)
  local copies, waits for them, and re-layouts  3.63 us (2%)
    ppermute x6, starting transfers between devices, ring_of(): fore_going.append(lax.ppermute(fore_going[-1], axis, fore))  30.3 us
    all_to_all x1, blocking collectives, on_device(): lax.all_to_all(square, 'row', 0, 0, axis_index_groups=y_lines)  17.5 us
    pallas_call x9, Pallas kernels, call(): pl.pallas_call(kernel, out_shape=[jax.ShapeDtypeStruct(s, d) for s, d in...  15.5 us
    all_to_all x1, blocking collectives, on_device(): term_parts = lax.all_to_all(terms, 'row', 0, 0, axis_index_groups=squares)  14.3 us
    all_to_all x1, blocking collectives, on_device(): packs = lax.all_to_all(pack, 'col', 0, 0)  12.6 us
    all_to_all x1, blocking collectives, on_device(): pieces = lax.all_to_all(summed, 'row', 0, 0, axis_index_groups=squares)  12.2 us
    ppermute x6, starting transfers between devices, ring_of(): aft_going.append(lax.ppermute(aft_going[-1], axis, aft))  11.5 us
    ppermute x2, starting transfers between devices, ring_of(): lax.ppermute(fore_going[3][:cut], axis, fore)  10.4 us
  transfers between devices with their start and end apart: 19, of which 6 were waited for; matrix products, arithmetic and copies ran while one was open for 1% of the time, Pallas kernels for 3%

profile of v9, /device:TPU:1, one launch (start us, length us, event | category | flops | bytes accessed | tf_op | source)
XLA Modules:
  0.0 161.5 jit_solution(10218809980803998924)
XLA Ops:
  0.7 0.1 pad_add_fusion.pos_ref
  0.7 1.0 copy-done
  1.8 0.7 shard_map.112
  2.5 8.8 %collective-permute-start = (bf16[128,1024]{1,0:T(8,128)(2,1)S(1)}, bf16[128,1024]{1,0:T(8,128)(2,1)S(1)}, u32[]{:S(2)}, u32[]{:S(2)}) collective-permute-start(bf16[128,1024]{1,0:T(8,128)(2,1)S(1)} %get-tuple-element.19), channel_id=1, source_target_pairs={{0,8},{8,0},{16,24},{24,16},{32,40},{40,32},{48,56},{56,48},{64,72... | collective-permute-start | bytes 786440 | tf_op jit(solution)/shard_map/ppermute | solution.py:303
  11.3 0.8 broadcast_in_dim.3
  12.2 3.6 %all-to-all-start = ((bf16[4,256,256]{2,1,0:T(8,128)(2,1)}), bf16[4,256,256]{2,1,0:T(8,128)(2,1)S(1)}, u32[]{:S(2)}, u32[]{:S(2)}) async-start(bf16[4,256,256]{2,1,0:T(8,128)(2,1)} %broadcast_in_dim.3), calls=%async_computation | async-start | bytes 1048576 | tf_op jit(solution)/shard_map/all_to_all | solution.py:311
  15.8 0.4 shard_map.113
  16.2 0.0 collective-permute-done
  16.2 1.9 %collective-permute-start.5 = (bf16[272,1024]{1,0:T(8,128)(2,1)S(1)}, bf16[272,1024]{1,0:T(8,128)(2,1)S(1)}, u32[]{:S(2)}, u32[]{:S(2)}) collective-permute-start(bf16[272,1024]{1,0:T(8,128)(2,1)S(1)} %pad_maximum_fusion.refs_0_), channel_id=1, source_target_pairs={{1,0},{2,1},{3,2},{4,3},{5,4},{6,5},{7,6},{0,7},{15,8},{8,9},{9,10... | collective-permute-start | bytes 1671176 | tf_op jit(solution)/shard_map/ppermute | solution.py:76
  18.2 5.8 %collective-permute-start.1 = (bf16[272,1024]{1,0:T(8,128)(2,1)S(1)}, bf16[272,1024]{1,0:T(8,128)(2,1)S(1)}, u32[]{:S(2)}, u32[]{:S(2)}) collective-permute-start(bf16[272,1024]{1,0:T(8,128)(2,1)S(1)} %pad_maximum_fusion.refs_0_), channel_id=1, source_target_pairs={{0,1},{1,2},{2,3},{3,4},{4,5},{5,6},{6,7},{7,0},{8,15},{9,8},{10,9... | collective-permute-start | bytes 1671176 | tf_op jit(solution)/shard_map/ppermute | solution.py:75
  24.0 1.4 all-to-all-done
  25.4 3.7 %collective-permute-start.9 = (bf16[1024,256]{1,0:T(8,128)(2,1)S(1)}, bf16[1024,256]{1,0:T(8,128)(2,1)S(1)}, u32[]{:S(2)}, u32[]{:S(2)}) collective-permute-start(bf16[1024,256]{1,0:T(8,128)(2,1)S(1)} %bitcast.6), channel_id=1, source_target_pairs={{0,64},{8,456},{16,80},{24,472},{32,96},{40,488},{48,112},{56,504}... | collective-permute-start | bytes 1572872 | tf_op jit(solution)/shard_map/ppermute | solution.py:75
  29.1 1.9 %collective-permute-start.13 = (bf16[1024,256]{1,0:T(8,128)(2,1)S(1)}, bf16[1024,256]{1,0:T(8,128)(2,1)S(1)}, u32[]{:S(2)}, u32[]{:S(2)}) collective-permute-start(bf16[1024,256]{1,0:T(8,128)(2,1)S(1)} %bitcast.7), channel_id=1, source_target_pairs={{64,0},{456,8},{80,16},{472,24},{96,32},{488,40},{112,48},{504,56}... | collective-permute-start | bytes 1572872 | tf_op jit(solution)/shard_map/ppermute | solution.py:76
  31.0 1.9 %collective-permute-start.6 = (bf16[272,1024]{1,0:T(8,128)(2,1)S(1)}, bf16[272,1024]{1,0:T(8,128)(2,1)S(1)}, u32[]{:S(2)}, u32[]{:S(2)}) collective-permute-start(bf16[272,1024]{1,0:T(8,128)(2,1)S(1)} %collective-permute-done.5.refs_4_), channel_id=1, source_target_pairs={{1,0},{2,1},{3,2},{4,3},{5,4},{6,5},{7,6},{0,7},{15,8},{8,9},{9,10... | collective-permute-start | bytes 1671176 | tf_op jit(solution)/shard_map/ppermute | solution.py:76
  33.0 2.3 %collective-permute-done.1.refs_1_ = bf16[272,1024]{1,0:T(8,128)(2,1)S(1)} collective-permute-done((bf16[272,1024]{1,0:T(8,128)(2,1)S(1)}, bf16[272,1024]{1,0:T(8,128)(2,1)S(1)}, u32[]{:S(2)}, u32[]{:S(2)}) %collective-permute-start.1) | collective-permute-done | bytes 557088 | tf_op jit(solution)/shard_map/ppermute | solution.py:75
  35.2 5.3 %collective-permute-start.2 = (bf16[272,1024]{1,0:T(8,128)(2,1)S(1)}, bf16[272,1024]{1,0:T(8,128)(2,1)S(1)}, u32[]{:S(2)}, u32[]{:S(2)}) collective-permute-start(bf16[272,1024]{1,0:T(8,128)(2,1)S(1)} %collective-permute-done.1.refs_1_), channel_id=1, source_target_pairs={{0,1},{1,2},{2,3},{3,4},{4,5},{5,6},{6,7},{7,0},{8,15},{9,8},{10,9... | collective-permute-start | bytes 1671176 | tf_op jit(solution)/shard_map/ppermute | solution.py:75
  40.5 0.0 collective-permute-done.9.refs_8_
  40.6 0.0 copy-start.19
  40.6 5.1 %collective-permute-start.10 = (bf16[1024,256]{1,0:T(8,128)(2,1)S(1)}, bf16[1024,256]{1,0:T(8,128)(2,1)S(1)}, u32[]{:S(2)}, u32[]{:S(2)}) collective-permute-start(bf16[1024,256]{1,0:T(8,128)(2,1)S(1)} %collective-permute-done.9.refs_8_), channel_id=1, source_target_pairs={{0,64},{8,456},{16,80},{24,472},{32,96},{40,488},{48,112},{56,504}... | collective-permute-start | bytes 1572872 | tf_op jit(solution)/shard_map/ppermute | solution.py:75
  45.7 0.0 collective-permute-done.13.refs_11_
  45.7 1.9 %collective-permute-start.14 = (bf16[1024,256]{1,0:T(8,128)(2,1)S(1)}, bf16[1024,256]{1,0:T(8,128)(2,1)S(1)}, u32[]{:S(2)}, u32[]{:S(2)}) collective-permute-start(bf16[1024,256]{1,0:T(8,128)(2,1)S(1)} %collective-permute-done.13.refs_11_), channel_id=1, source_target_pairs={{64,0},{456,8},{80,16},{472,24},{96,32},{488,40},{112,48},{504,56}... | collective-permute-start | bytes 1572872 | tf_op jit(solution)/shard_map/ppermute | solution.py:76
  47.6 0.0 collective-permute-done.6.refs_5_
  47.6 1.9 %collective-permute-start.7 = (bf16[272,1024]{1,0:T(8,128)(2,1)S(1)}, bf16[272,1024]{1,0:T(8,128)(2,1)S(1)}, u32[]{:S(2)}, u32[]{:S(2)}) collective-permute-start(bf16[272,1024]{1,0:T(8,128)(2,1)S(1)} %collective-permute-done.6.refs_5_), channel_id=1, source_target_pairs={{1,0},{2,1},{3,2},{4,3},{5,4},{6,5},{7,6},{0,7},{15,8},{8,9},{9,10... | collective-permute-start | bytes 1671176 | tf_op jit(solution)/shard_map/ppermute | solution.py:76
  49.6 3.1 %collective-permute-done.2.refs_2_ = bf16[272,1024]{1,0:T(8,128)(2,1)S(1)} collective-permute-done((bf16[272,1024]{1,0:T(8,128)(2,1)S(1)}, bf16[272,1024]{1,0:T(8,128)(2,1)S(1)}, u32[]{:S(2)}, u32[]{:S(2)}) %collective-permute-start.2) | collective-permute-done | bytes 557088 | tf_op jit(solution)/shard_map/ppermute | solution.py:75
  52.6 5.3 %collective-permute-start.3 = (bf16[272,1024]{1,0:T(8,128)(2,1)S(1)}, bf16[272,1024]{1,0:T(8,128)(2,1)S(1)}, u32[]{:S(2)}, u32[]{:S(2)}) collective-permute-start(bf16[272,1024]{1,0:T(8,128)(2,1)S(1)} %collective-permute-done.2.refs_2_), channel_id=1, source_target_pairs={{0,1},{1,2},{2,3},{3,4},{4,5},{5,6},{6,7},{7,0},{8,15},{9,8},{10,9... | collective-permute-start | bytes 1671176 | tf_op jit(solution)/shard_map/ppermute | solution.py:75
  58.0 5.1 %collective-permute-start.11 = (bf16[1024,256]{1,0:T(8,128)(2,1)S(1)}, bf16[1024,256]{1,0:T(8,128)(2,1)S(1)}, u32[]{:S(2)}, u32[]{:S(2)}) collective-permute-start(bf16[1024,256]{1,0:T(8,128)(2,1)S(1)} %collective-permute-done.10.refs_9_), channel_id=1, source_target_pairs={{0,64},{8,456},{16,80},{24,472},{32,96},{40,488},{48,112},{56,504}... | collective-permute-start | bytes 1572872 | tf_op jit(solution)/shard_map/ppermute | solution.py:75
  63.1 1.9 %collective-permute-start.15 = (bf16[1024,256]{1,0:T(8,128)(2,1)S(1)}, bf16[1024,256]{1,0:T(8,128)(2,1)S(1)}, u32[]{:S(2)}, u32[]{:S(2)}) collective-permute-start(bf16[1024,256]{1,0:T(8,128)(2,1)S(1)} %collective-permute-done.14.refs_12_), channel_id=1, source_target_pairs={{64,0},{456,8},{80,16},{472,24},{96,32},{488,40},{112,48},{504,56}... | collective-permute-start | bytes 1572872 | tf_op jit(solution)/shard_map/ppermute | solution.py:76
  65.1 1.9 %collective-permute-start.8 = (bf16[144,1024]{1,0:T(8,128)(2,1)S(1)}, bf16[144,1024]{1,0:T(8,128)(2,1)S(1)}, u32[]{:S(2)}, u32[]{:S(2)}) collective-permute-start(bf16[144,1024]{1,0:T(8,128)(2,1)S(1)} %slice.17), channel_id=1, source_target_pairs={{1,0},{2,1},{3,2},{4,3},{5,4},{6,5},{7,6},{0,7},{15,8},{8,9},{9,10... | collective-permute-start | bytes 884744 | tf_op jit(solution)/shard_map/ppermute | solution.py:79
  67.0 2.8 %collective-permute-done.3.refs_3_ = bf16[272,1024]{1,0:T(8,128)(2,1)S(1)} collective-permute-done((bf16[272,1024]{1,0:T(8,128)(2,1)S(1)}, bf16[272,1024]{1,0:T(8,128)(2,1)S(1)}, u32[]{:S(2)}, u32[]{:S(2)}) %collective-permute-start.3) | collective-permute-done | bytes 557088 | tf_op jit(solution)/shard_map/ppermute | solution.py:75
  69.8 5.3 %collective-permute-start.4 = (bf16[128,1024]{1,0:T(8,128)(2,1)S(1)}, bf16[128,1024]{1,0:T(8,128)(2,1)S(1)}, u32[]{:S(2)}, u32[]{:S(2)}) collective-permute-start(bf16[128,1024]{1,0:T(8,128)(2,1)S(1)} %slice.16), channel_id=1, source_target_pairs={{0,1},{1,2},{2,3},{3,4},{4,5},{5,6},{6,7},{7,0},{8,15},{9,8},{10,9... | collective-permute-start | bytes 786440 | tf_op jit(solution)/shard_map/ppermute | solution.py:78
  75.2 5.1 %collective-permute-start.12 = (bf16[512,256]{1,0:T(8,128)(2,1)S(1)}, bf16[512,256]{1,0:T(8,128)(2,1)S(1)}, u32[]{:S(2)}, u32[]{:S(2)}) collective-permute-start(bf16[512,256]{1,0:T(8,128)(2,1)S(1)} %slice.18), channel_id=1, source_target_pairs={{0,64},{8,456},{16,80},{24,472},{32,96},{40,488},{48,112},{56,504}... | collective-permute-start | bytes 786440 | tf_op jit(solution)/shard_map/ppermute | solution.py:78
  80.4 1.9 %collective-permute-start.16 = (bf16[512,256]{1,0:T(8,128)(2,1)S(1)}, bf16[512,256]{1,0:T(8,128)(2,1)S(1)}, u32[]{:S(2)}, u32[]{:S(2)}) collective-permute-start(bf16[512,256]{1,0:T(8,128)(2,1)S(1)} %slice.19), channel_id=1, source_target_pairs={{64,0},{456,8},{80,16},{472,24},{96,32},{488,40},{112,48},{504,56}... | collective-permute-start | bytes 786440 | tf_op jit(solution)/shard_map/ppermute | solution.py:79
  82.4 5.0 %shard_map.114 = (f32[256,256]{1,0:T(8,128)S(1)}, f32[16,1024]{1,0:T(8,128)S(1)}, bf16[256,1024]{1,0:T(8,128)(2,1)S(1)}, bf16[1024,256]{1,0:T(8,128)(2,1)S(1)}) custom-call(s32[3]{0:T(128)S(1)} %pad_add_fusion.pos_ref, bf16[272,1024]{1,0:T(8,128)(2,1)} %copy-done.10, bf16[272,1024]{1,0:T(8,128)(2,1)} %copy-done.16, bf16[272,1024]{1,0:T(8,128)(2,1)} %copy-done.18, ...), custom_call_target="tpu_custom_call" | custom-call | flops 1073741824 | bytes 7569408 | tf_op jit(solution)/shard_map/pallas_call | solution.py:263
  87.4 0.0 copy-start.4
  87.5 0.8 copy-done.4
  88.2 0.8 copy-done.5
  89.1 1.2 collective-permute-done.16.w2_ref
  90.3 0.0 copy-start.9
  90.3 2.5 %shard_map.115 = (f32[128,256]{1,0:T(8,128)S(1)}, f32[128,256]{1,0:T(8,128)S(1)}, bf16[128,64]{1,0:T(8,128)(2,1)S(1)}) custom-call(s32[3]{0:T(128)S(1)} %pad_add_fusion.pos_ref, bf16[128,1024]{1,0:T(8,128)(2,1)S(1)} %collective-permute-done.4.t1_ref, bf16[144,1024]{1,0:T(8,128)(2,1)S(1)} %collective-permute-done.8.t2_ref, ...), custom_call_target="tpu_custom_call" | custom-call | tf_op jit(solution)/shard_map/pallas_call | solution.py:263
  92.8 4.2 %collective-permute-start.17 = (f32[128,256]{1,0:T(8,128)S(1)}, f32[128,256]{1,0:T(8,128)S(1)}, u32[]{:S(2)}, u32[]{:S(2)}) collective-permute-start(f32[128,256]{1,0:T(8,128)S(1)} %get-tuple-element.25), channel_id=1, source_target_pairs={{0,8},{8,0},{16,24},{24,16},{32,40},{40,32},{48,56},{56,48},{64,72... | collective-permute-start | bytes 393224 | tf_op jit(solution)/shard_map/ppermute | solution.py:350
  97.0 1.0 collective-permute-done.17.got_ref
  98.0 5.0 %shard_map.116 = (bf16[8,80,128]{2,1,0:T(8,128)(2,1)S(1)}, f32[128,128]{1,0:T(8,128)S(1)}, f32[128,128]{1,0:T(8,128)S(1)}) custom-call(s32[1,8]{1,0:T(1,128)S(1)} %copy-done.9, f32[128,256]{1,0:T(8,128)S(1)} %get-tuple-element.24.own_ref, f32[128,256]{1,0:T(8,128)S(1)} %collective-permute-done.17.got_ref, ...), custom_call_target="tpu_custom_call" | custom-call | tf_op jit(solution)/shard_map/pallas_call | solution.py:263
  103.1 12.6 %all_to_all.25.pack_ref = bf16[8,80,128]{2,1,0:T(8,128)(2,1)S(1)} all-to-all(bf16[8,80,128]{2,1,0:T(8,128)(2,1)S(1)} %get-tuple-element.27), channel_id=1, replica_groups=mesh['row'=64,'col'=8] {'col'}, dimensions={0} | all-to-all | bytes 327680 | tf_op jit(solution)/shard_map/all_to_all | solution.py:363
  115.7 0.9 shard_map.117
  116.6 14.3 %all_to_all.26.in_ref = bf16[8,72,256]{2,1,0:T(8,128)(2,1)S(1)} all-to-all(bf16[8,72,256]{2,1,0:T(8,128)(2,1)S(1)} %shard_map.117), channel_id=1, replica_groups={{0,8,16,24,32,40,48,56},{64,72,80,88,96,104,112,120},{128,136,144,152,1..., dimensions={0} | all-to-all | bytes 589824 | tf_op jit(solution)/shard_map/all_to_all | solution.py:369
  131.0 17.5 %all_to_all.27.in_ref = bf16[8,72,256]{2,1,0:T(8,128)(2,1)S(1)} all-to-all(bf16[8,72,256]{2,1,0:T(8,128)(2,1)S(1)} %shard_map.118), channel_id=1, replica_groups={{0,64,128,192,256,320,384,448},{8,72,136,200,264,328,392,456},{16,80,14..., dimensions={0} | all-to-all | bytes 589824 | tf_op jit(solution)/shard_map/all_to_all | solution.py:371
  148.5 12.2 %all_to_all.28.in_ref = bf16[8,72,256]{2,1,0:T(8,128)(2,1)S(1)} all-to-all(bf16[8,72,256]{2,1,0:T(8,128)(2,1)S(1)} %shard_map.119), channel_id=1, replica_groups={{0,8,16,24,32,40,48,56},{64,72,80,88,96,104,112,120},{128,136,144,152,1..., dimensions={0} | all-to-all | bytes 589824 | tf_op jit(solution)/shard_map/all_to_all | solution.py:373
  160.7 0.8 shard_map.120
  (61 shorter events, 0.3 us)
Async XLA Ops:
  0.7 1.0 copy-start
  1.8 9.5 %copy-start.23 = (bf16[256,128]{1,0:T(8,128)(2,1)S(1)}, bf16[256,128]{1,0:T(8,128)(2,1)}, u32[]{:S(2)}) copy-start(bf16[256,128]{1,0:T(8,128)(2,1)} %param.13) | copy-start | bytes 196612
  1.8 9.5 %copy-start.24 = (bf16[256,128]{1,0:T(8,128)(2,1)S(1)}, bf16[256,128]{1,0:T(8,128)(2,1)}, u32[]{:S(2)}) copy-start(bf16[256,128]{1,0:T(8,128)(2,1)} %param.12) | copy-start | bytes 196612
  2.5 13.7 %collective-permute-start = (bf16[128,1024]{1,0:T(8,128)(2,1)S(1)}, bf16[128,1024]{1,0:T(8,128)(2,1)S(1)}, u32[]{:S(2)}, u32[]{:S(2)}) collective-permute-start(bf16[128,1024]{1,0:T(8,128)(2,1)S(1)} %get-tuple-element.19), channel_id=1, source_target_pairs={{0,8},{8,0},{16,24},{24,16},{32,40},{40,32},{48,56},{56,48},{64,72... | collective-permute-start | bytes 786440 | tf_op jit(solution)/shard_map/ppermute | solution.py:303
  12.2 3.6 %copy-start.1 = (bf16[128,2048]{1,0:T(8,128)(2,1)S(1)}, bf16[128,2048]{1,0:T(8,128)(2,1)}, u32[]{:S(2)}) copy-start(bf16[128,2048]{1,0:T(8,128)(2,1)} %t_ref.5) | copy-start | bytes 1572868
  12.2 3.6 %copy-start.6 = (bf16[2048,64]{0,1:T(8,128)(2,1)S(1)}, bf16[2048,64]{0,1:T(8,128)(2,1)}, u32[]{:S(2)}) copy-start(bf16[2048,64]{0,1:T(8,128)(2,1)} %param.14) | copy-start | bytes 786436
  12.2 13.2 %all-to-all-start = ((bf16[4,256,256]{2,1,0:T(8,128)(2,1)}), bf16[4,256,256]{2,1,0:T(8,128)(2,1)S(1)}, u32[]{:S(2)}, u32[]{:S(2)}) async-start(bf16[4,256,256]{2,1,0:T(8,128)(2,1)} %broadcast_in_dim.3), calls=%async_computation | async-start | bytes 1048576 | tf_op jit(solution)/shard_map/all_to_all | solution.py:311
  16.2 53.6 %copy-start.10 = (bf16[272,1024]{1,0:T(8,128)(2,1)}, bf16[272,1024]{1,0:T(8,128)(2,1)S(1)}, u32[]{:S(2)}) copy-start(bf16[272,1024]{1,0:T(8,128)(2,1)S(1)} %pad_maximum_fusion.refs_0_) | copy-start | bytes 1671172
  16.2 14.8 %collective-permute-start.5 = (bf16[272,1024]{1,0:T(8,128)(2,1)S(1)}, bf16[272,1024]{1,0:T(8,128)(2,1)S(1)}, u32[]{:S(2)}, u32[]{:S(2)}) collective-permute-start(bf16[272,1024]{1,0:T(8,128)(2,1)S(1)} %pad_maximum_fusion.refs_0_), channel_id=1, source_target_pairs={{1,0},{2,1},{3,2},{4,3},{5,4},{6,5},{7,6},{0,7},{15,8},{8,9},{9,10... | collective-permute-start | bytes 1671176 | tf_op jit(solution)/shard_map/ppermute | solution.py:76
  18.2 17.1 %collective-permute-start.1 = (bf16[272,1024]{1,0:T(8,128)(2,1)S(1)}, bf16[272,1024]{1,0:T(8,128)(2,1)S(1)}, u32[]{:S(2)}, u32[]{:S(2)}) collective-permute-start(bf16[272,1024]{1,0:T(8,128)(2,1)S(1)} %pad_maximum_fusion.refs_0_), channel_id=1, source_target_pairs={{0,1},{1,2},{2,3},{3,4},{4,5},{5,6},{6,7},{7,0},{8,15},{9,8},{10,9... | collective-permute-start | bytes 1671176 | tf_op jit(solution)/shard_map/ppermute | solution.py:75
  25.4 15.2 %collective-permute-start.9 = (bf16[1024,256]{1,0:T(8,128)(2,1)S(1)}, bf16[1024,256]{1,0:T(8,128)(2,1)S(1)}, u32[]{:S(2)}, u32[]{:S(2)}) collective-permute-start(bf16[1024,256]{1,0:T(8,128)(2,1)S(1)} %bitcast.6), channel_id=1, source_target_pairs={{0,64},{8,456},{16,80},{24,472},{32,96},{40,488},{48,112},{56,504}... | collective-permute-start | bytes 1572872 | tf_op jit(solution)/shard_map/ppermute | solution.py:75
  29.1 16.6 %collective-permute-start.13 = (bf16[1024,256]{1,0:T(8,128)(2,1)S(1)}, bf16[1024,256]{1,0:T(8,128)(2,1)S(1)}, u32[]{:S(2)}, u32[]{:S(2)}) collective-permute-start(bf16[1024,256]{1,0:T(8,128)(2,1)S(1)} %bitcast.7), channel_id=1, source_target_pairs={{64,0},{456,8},{80,16},{472,24},{96,32},{488,40},{112,48},{504,56}... | collective-permute-start | bytes 1572872 | tf_op jit(solution)/shard_map/ppermute | solution.py:76
  31.0 51.3 %copy-start.15 = (bf16[272,1024]{1,0:T(8,128)(2,1)}, bf16[272,1024]{1,0:T(8,128)(2,1)S(1)}, u32[]{:S(2)}) copy-start(bf16[272,1024]{1,0:T(8,128)(2,1)S(1)} %collective-permute-done.5.refs_4_) | copy-start | bytes 1671172
  31.0 16.6 %collective-permute-start.6 = (bf16[272,1024]{1,0:T(8,128)(2,1)S(1)}, bf16[272,1024]{1,0:T(8,128)(2,1)S(1)}, u32[]{:S(2)}, u32[]{:S(2)}) collective-permute-start(bf16[272,1024]{1,0:T(8,128)(2,1)S(1)} %collective-permute-done.5.refs_4_), channel_id=1, source_target_pairs={{1,0},{2,1},{3,2},{4,3},{5,4},{6,5},{7,6},{0,7},{15,8},{8,9},{9,10... | collective-permute-start | bytes 1671176 | tf_op jit(solution)/shard_map/ppermute | solution.py:76
  35.2 47.1 %copy-start.16 = (bf16[272,1024]{1,0:T(8,128)(2,1)}, bf16[272,1024]{1,0:T(8,128)(2,1)S(1)}, u32[]{:S(2)}) copy-start(bf16[272,1024]{1,0:T(8,128)(2,1)S(1)} %collective-permute-done.1.refs_1_) | copy-start | bytes 1671172
  35.2 17.4 %collective-permute-start.2 = (bf16[272,1024]{1,0:T(8,128)(2,1)S(1)}, bf16[272,1024]{1,0:T(8,128)(2,1)S(1)}, u32[]{:S(2)}, u32[]{:S(2)}) collective-permute-start(bf16[272,1024]{1,0:T(8,128)(2,1)S(1)} %collective-permute-done.1.refs_1_), channel_id=1, source_target_pairs={{0,1},{1,2},{2,3},{3,4},{4,5},{5,6},{6,7},{7,0},{8,15},{9,8},{10,9... | collective-permute-start | bytes 1671176 | tf_op jit(solution)/shard_map/ppermute | solution.py:75
  40.6 41.8 %copy-start.19 = (bf16[1024,256]{1,0:T(8,128)(2,1)}, bf16[1024,256]{1,0:T(8,128)(2,1)S(1)}, u32[]{:S(2)}) copy-start(bf16[1024,256]{1,0:T(8,128)(2,1)S(1)} %collective-permute-done.9.refs_8_) | copy-start | bytes 1572868
  40.6 17.4 %collective-permute-start.10 = (bf16[1024,256]{1,0:T(8,128)(2,1)S(1)}, bf16[1024,256]{1,0:T(8,128)(2,1)S(1)}, u32[]{:S(2)}, u32[]{:S(2)}) collective-permute-start(bf16[1024,256]{1,0:T(8,128)(2,1)S(1)} %collective-permute-done.9.refs_8_), channel_id=1, source_target_pairs={{0,64},{8,456},{16,80},{24,472},{32,96},{40,488},{48,112},{56,504}... | collective-permute-start | bytes 1572872 | tf_op jit(solution)/shard_map/ppermute | solution.py:75
  45.7 36.7 %copy-start.20 = (bf16[1024,256]{1,0:T(8,128)(2,1)}, bf16[1024,256]{1,0:T(8,128)(2,1)S(1)}, u32[]{:S(2)}) copy-start(bf16[1024,256]{1,0:T(8,128)(2,1)S(1)} %collective-permute-done.13.refs_11_) | copy-start | bytes 1572868
  45.7 17.4 %collective-permute-start.14 = (bf16[1024,256]{1,0:T(8,128)(2,1)S(1)}, bf16[1024,256]{1,0:T(8,128)(2,1)S(1)}, u32[]{:S(2)}, u32[]{:S(2)}) collective-permute-start(bf16[1024,256]{1,0:T(8,128)(2,1)S(1)} %collective-permute-done.13.refs_11_), channel_id=1, source_target_pairs={{64,0},{456,8},{80,16},{472,24},{96,32},{488,40},{112,48},{504,56}... | collective-permute-start | bytes 1572872 | tf_op jit(solution)/shard_map/ppermute | solution.py:76
  47.6 34.7 %copy-start.17 = (bf16[272,1024]{1,0:T(8,128)(2,1)}, bf16[272,1024]{1,0:T(8,128)(2,1)S(1)}, u32[]{:S(2)}) copy-start(bf16[272,1024]{1,0:T(8,128)(2,1)S(1)} %collective-permute-done.6.refs_5_) | copy-start | bytes 1671172
  47.6 17.4 %collective-permute-start.7 = (bf16[272,1024]{1,0:T(8,128)(2,1)S(1)}, bf16[272,1024]{1,0:T(8,128)(2,1)S(1)}, u32[]{:S(2)}, u32[]{:S(2)}) collective-permute-start(bf16[272,1024]{1,0:T(8,128)(2,1)S(1)} %collective-permute-done.6.refs_5_), channel_id=1, source_target_pairs={{1,0},{2,1},{3,2},{4,3},{5,4},{6,5},{7,6},{0,7},{15,8},{8,9},{9,10... | collective-permute-start | bytes 1671176 | tf_op jit(solution)/shard_map/ppermute | solution.py:76
  52.6 29.7 %copy-start.18 = (bf16[272,1024]{1,0:T(8,128)(2,1)}, bf16[272,1024]{1,0:T(8,128)(2,1)S(1)}, u32[]{:S(2)}) copy-start(bf16[272,1024]{1,0:T(8,128)(2,1)S(1)} %collective-permute-done.2.refs_2_) | copy-start | bytes 1671172
  52.6 17.2 %collective-permute-start.3 = (bf16[272,1024]{1,0:T(8,128)(2,1)S(1)}, bf16[272,1024]{1,0:T(8,128)(2,1)S(1)}, u32[]{:S(2)}, u32[]{:S(2)}) collective-permute-start(bf16[272,1024]{1,0:T(8,128)(2,1)S(1)} %collective-permute-done.2.refs_2_), channel_id=1, source_target_pairs={{0,1},{1,2},{2,3},{3,4},{4,5},{5,6},{6,7},{7,0},{8,15},{9,8},{10,9... | collective-permute-start | bytes 1671176 | tf_op jit(solution)/shard_map/ppermute | solution.py:75
  57.9 24.4 %copy-start.21 = (bf16[1024,256]{1,0:T(8,128)(2,1)}, bf16[1024,256]{1,0:T(8,128)(2,1)S(1)}, u32[]{:S(2)}) copy-start(bf16[1024,256]{1,0:T(8,128)(2,1)S(1)} %collective-permute-done.10.refs_9_) | copy-start | bytes 1572868
  58.0 17.2 %collective-permute-start.11 = (bf16[1024,256]{1,0:T(8,128)(2,1)S(1)}, bf16[1024,256]{1,0:T(8,128)(2,1)S(1)}, u32[]{:S(2)}, u32[]{:S(2)}) collective-permute-start(bf16[1024,256]{1,0:T(8,128)(2,1)S(1)} %collective-permute-done.10.refs_9_), channel_id=1, source_target_pairs={{0,64},{8,456},{16,80},{24,472},{32,96},{40,488},{48,112},{56,504}... | collective-permute-start | bytes 1572872 | tf_op jit(solution)/shard_map/ppermute | solution.py:75
  63.1 19.3 %copy-start.22 = (bf16[1024,256]{1,0:T(8,128)(2,1)}, bf16[1024,256]{1,0:T(8,128)(2,1)S(1)}, u32[]{:S(2)}) copy-start(bf16[1024,256]{1,0:T(8,128)(2,1)S(1)} %collective-permute-done.14.refs_12_) | copy-start | bytes 1572868
  63.1 17.2 %collective-permute-start.15 = (bf16[1024,256]{1,0:T(8,128)(2,1)S(1)}, bf16[1024,256]{1,0:T(8,128)(2,1)S(1)}, u32[]{:S(2)}, u32[]{:S(2)}) collective-permute-start(bf16[1024,256]{1,0:T(8,128)(2,1)S(1)} %collective-permute-done.14.refs_12_), channel_id=1, source_target_pairs={{64,0},{456,8},{80,16},{472,24},{96,32},{488,40},{112,48},{504,56}... | collective-permute-start | bytes 1572872 | tf_op jit(solution)/shard_map/ppermute | solution.py:76
  65.0 4.8 %copy-start.11 = (bf16[272,1024]{1,0:T(8,128)(2,1)}, bf16[272,1024]{1,0:T(8,128)(2,1)S(1)}, u32[]{:S(2)}) copy-start(bf16[272,1024]{1,0:T(8,128)(2,1)S(1)} %collective-permute-done.7.refs_6_) | copy-start | bytes 1671172
  65.1 24.0 %collective-permute-start.8 = (bf16[144,1024]{1,0:T(8,128)(2,1)S(1)}, bf16[144,1024]{1,0:T(8,128)(2,1)S(1)}, u32[]{:S(2)}, u32[]{:S(2)}) collective-permute-start(bf16[144,1024]{1,0:T(8,128)(2,1)S(1)} %slice.17), channel_id=1, source_target_pairs={{1,0},{2,1},{3,2},{4,3},{5,4},{6,5},{7,6},{0,7},{15,8},{8,9},{9,10... | collective-permute-start | bytes 884744 | tf_op jit(solution)/shard_map/ppermute | solution.py:79
  69.8 10.6 %copy-start.12 = (bf16[272,1024]{1,0:T(8,128)(2,1)}, bf16[272,1024]{1,0:T(8,128)(2,1)S(1)}, u32[]{:S(2)}) copy-start(bf16[272,1024]{1,0:T(8,128)(2,1)S(1)} %collective-permute-done.3.refs_3_) | copy-start | bytes 1671172
  69.8 19.2 %collective-permute-start.4 = (bf16[128,1024]{1,0:T(8,128)(2,1)S(1)}, bf16[128,1024]{1,0:T(8,128)(2,1)S(1)}, u32[]{:S(2)}, u32[]{:S(2)}) collective-permute-start(bf16[128,1024]{1,0:T(8,128)(2,1)S(1)} %slice.16), channel_id=1, source_target_pairs={{0,1},{1,2},{2,3},{3,4},{4,5},{5,6},{6,7},{7,0},{8,15},{9,8},{10,9... | collective-permute-start | bytes 786440 | tf_op jit(solution)/shard_map/ppermute | solution.py:78
  75.2 7.2 %copy-start.13 = (bf16[1024,256]{1,0:T(8,128)(2,1)}, bf16[1024,256]{1,0:T(8,128)(2,1)S(1)}, u32[]{:S(2)}) copy-start(bf16[1024,256]{1,0:T(8,128)(2,1)S(1)} %collective-permute-done.11.refs_10_) | copy-start | bytes 1572868
  75.2 13.8 %collective-permute-start.12 = (bf16[512,256]{1,0:T(8,128)(2,1)S(1)}, bf16[512,256]{1,0:T(8,128)(2,1)S(1)}, u32[]{:S(2)}, u32[]{:S(2)}) collective-permute-start(bf16[512,256]{1,0:T(8,128)(2,1)S(1)} %slice.18), channel_id=1, source_target_pairs={{0,64},{8,456},{16,80},{24,472},{32,96},{40,488},{48,112},{56,504}... | collective-permute-start | bytes 786440 | tf_op jit(solution)/shard_map/ppermute | solution.py:78
  80.3 2.1 %copy-start.14 = (bf16[1024,256]{1,0:T(8,128)(2,1)}, bf16[1024,256]{1,0:T(8,128)(2,1)S(1)}, u32[]{:S(2)}) copy-start(bf16[1024,256]{1,0:T(8,128)(2,1)S(1)} %collective-permute-done.15.refs_13_) | copy-start | bytes 1572868
  80.4 9.9 %collective-permute-start.16 = (bf16[512,256]{1,0:T(8,128)(2,1)S(1)}, bf16[512,256]{1,0:T(8,128)(2,1)S(1)}, u32[]{:S(2)}, u32[]{:S(2)}) collective-permute-start(bf16[512,256]{1,0:T(8,128)(2,1)S(1)} %slice.19), channel_id=1, source_target_pairs={{64,0},{456,8},{80,16},{472,24},{96,32},{488,40},{112,48},{504,56}... | collective-permute-start | bytes 786440 | tf_op jit(solution)/shard_map/ppermute | solution.py:79
  87.4 0.8 copy-start.4
  88.2 0.8 copy-start.5
  90.3 7.7 %copy-start.2 = (bf16[128,2048]{1,0:T(8,128)(2,1)S(1)}, bf16[128,2048]{1,0:T(8,128)(2,1)}, u32[]{:S(2)}) copy-start(bf16[128,2048]{1,0:T(8,128)(2,1)} %q_ref.1) | copy-start | bytes 1572868
  90.3 7.7 %copy-start.3 = (bf16[128,2048]{1,0:T(8,128)(2,1)S(1)}, bf16[128,2048]{1,0:T(8,128)(2,1)}, u32[]{:S(2)}) copy-start(bf16[128,2048]{1,0:T(8,128)(2,1)} %p_ref.1) | copy-start | bytes 1572868
  90.3 7.7 %copy-start.7 = (bf16[64,128]{1,0:T(8,128)(2,1)S(1)}, bf16[64,128]{1,0:T(8,128)(2,1)}, u32[]{:S(2)}) copy-start(bf16[64,128]{1,0:T(8,128)(2,1)} %upk_ref.1) | copy-start | bytes 49156
  90.3 7.7 %copy-start.8 = (bf16[64,128]{1,0:T(8,128)(2,1)S(1)}, bf16[64,128]{1,0:T(8,128)(2,1)}, u32[]{:S(2)}) copy-start(bf16[64,128]{1,0:T(8,128)(2,1)} %upv_ref.1) | copy-start | bytes 49156
  90.3 7.7 %copy-start.9 = (s32[1,8]{1,0:T(1,128)S(1)}, s32[1,8]{1,0:T(1,128)}, u32[]{:S(2)}) copy-start(s32[1,8]{1,0:T(1,128)} %lengths_ref.3) | copy-start | bytes 100
  92.8 5.2 %collective-permute-start.17 = (f32[128,256]{1,0:T(8,128)S(1)}, f32[128,256]{1,0:T(8,128)S(1)}, u32[]{:S(2)}, u32[]{:S(2)}) collective-permute-start(f32[128,256]{1,0:T(8,128)S(1)} %get-tuple-element.25), channel_id=1, source_target_pairs={{0,8},{8,0},{16,24},{24,16},{32,40},{40,32},{48,56},{56,48},{64,72... | collective-permute-start | bytes 393224 | tf_op jit(solution)/shard_map/ppermute | solution.py:350

commit v10 on v9

--- a/solution.py
+++ b/solution.py
@@ -69,15 +69,21 @@
 STEPS = (0, 1, 2, 3, -1, -2, -3, 4)
 
 
-def ring_of(own, axis, fore, aft, cut):
-    fore_going, aft_going = [own], [own]
-    for _ in range(3):
-        fore_going.append(lax.ppermute(fore_going[-1], axis, fore))
-        aft_going.append(lax.ppermute(aft_going[-1], axis, aft))
-    return fore_going + aft_going[1:] + [
-        lax.ppermute(fore_going[3][:cut], axis, fore),
-        lax.ppermute(aft_going[3][cut:], axis, aft),
-    ]
+def rings_of(owns, axes, fores, afts, cuts):
+    both = range(2)
+    going = [list(owns), list(owns)]
+    blocks = [[[own] for own in owns] for _ in going]
+    for step in range(4):
+        for side, ways in enumerate((fores, afts)):
+            now = going[side]
+            if step == 0 and side == 1:
+                now = lax.optimization_barrier(tuple(now))
+            if step == 3:
+                now = [now[i][:cuts[i]] if side == 0 else now[i][cuts[i]:] for i in both]
+            going[side] = [lax.ppermute(now[i], axes[i], ways[i]) for i in both]
+            for i in both:
+                blocks[side][i].append(going[side][i])
+    return [blocks[0][i][:4] + blocks[1][i][1:4] + [blocks[0][i][4], blocks[1][i][4]] for i in both]
 
 
 def block_at(pos_ref, axis, step, n):
@@ -101,15 +107,21 @@
     for c in copies:
         c.wait()
     rows = total_ref.shape[0]
+    left = [
+        pltpu.make_async_copy(t_scr.at[w_far, pl.ds(0, rows)], t_left_ref, sem.at[0, 7]),
+        pltpu.make_async_copy(w_scr.at[t_far], w_left_ref, sem.at[1, 7]),
+    ]
+    for c in left:
+        c.start()
     total = jnp.zeros(total_ref.shape, F32)
     low = jnp.zeros(low_ref.shape, F32)
     for k in range(n):
-        total = total + mm(t_scr[k, pl.ds(0, rows)], w_scr[k], NN)
+        total = total + mm(t_scr[k, pl.ds(0, rows)], w_scr[k, pl.ds(0, t_scr.shape[2])], NN)
         low = low + t_scr[k, pl.ds(rows, low.shape[0])].astype(F32)
     total_ref[...] = total
     low_ref[...] = low
-    t_left_ref[...] = t_scr[w_far, pl.ds(0, rows)]
-    w_left_ref[...] = w_scr[t_far]
+    for c in left:
+        c.wait()
 
 
 def finish_kernel(
@@ -134,8 +146,8 @@
         c.wait()
     rows = own_ref.shape[0]
     same = pos_ref[1] == pos_ref[2]
-    w_late = w_scr[...]
-    w_match = jnp.where(same, w_late, w_left_scr[...])
+    w_late = w_scr[pl.ds(0, t_left_scr.shape[1])]
+    w_match = jnp.where(same, w_late, w_left_scr[pl.ds(0, t_left_scr.shape[1])])
     total = total_scr[...] + mm(t_scr[pl.ds(0, 2 * rows)], w_match, NN)
     total = total + mm(t_left_scr[...], w_late, NN)
     own_ref[...] = total[:rows]
@@ -312,20 +324,23 @@
         jnp.broadcast_to(w_both, (4,) + w_both.shape), "row", 0, 0, axis_index_groups=x_lines
     )
     w_own = w_line.reshape(feats // 2, wide)
-    t_parts = ring_of(pair, ("row", "col"), z_fore, z_aft, rows)
-    w_parts = ring_of(w_own, "row", y_fore, y_aft, feats // 4)
+    w_own = jnp.pad(w_own, ((0, pair.size // wide - w_own.shape[0]), (0, 0)))
+    t_parts, w_parts = rings_of(
+        (pair, w_own), (("row", "col"), "row"), (z_fore, y_fore), (z_aft, y_aft),
+        (rows, w_own.shape[0] // 2),
+    )
 
     deep = feats // 2
     total, low_sum, t_left, w_left = call(
         project_kernel,
         [((2 * rows, wide), F32), ((16, deep), F32), ((2 * rows, deep), BF), (w_own.shape, BF)],
         [SMEM] + [HBM] * 14,
-        [VMEM] * 4,
+        [VMEM] * 2 + [HBM] * 2,
         pos, *t_parts[:7], *w_parts[:7],
         scratch=[
             pltpu.VMEM((8,) + pair.shape, BF),
             pltpu.VMEM((8,) + w_own.shape, BF),
-            pltpu.SemaphoreType.DMA((2, 7)),
+            pltpu.SemaphoreType.DMA((2, 8)),
         ],
         mib=52,
         cost=(2 * 16 * rows * deep * wide, 14 * (pair.size + w_own.size)),

time: 162 us -> 163 us (level)
  starting transfers between devices: 72.7 us -> 83.5 us
  waiting for transfers between devices: 11.7 us -> 1.83 us
    ppermute x16, waiting for transfers between devices: 9.36 us -> 0.09 us  [rings_of(): going[side] = [lax.ppermute(now[i], axes[i], ways[i]) for i in both]]
    ppermute x16, starting transfers between devices: 56.1 us -> 64.7 us  [rings_of(): going[side] = [lax.ppermute(now[i], axes[i], ways[i]) for i in both]]
    all_to_all x1, blocking collectives: 12.6 us -> 16.1 us  [on_device(): packs = lax.all_to_all(pack, 'col', 0, 0)]
    all_to_all x1, blocking collectives: 14.3 us -> 11.8 us  [on_device(): term_parts = lax.all_to_all(terms, 'row', 0, 0, axis_index_groups=squares)]
    ppermute x1, starting transfers between devices: 4.23 us -> 6.41 us  [on_device(): got = lax.ppermute(other, 'row', swap)]
    all_to_all x1, blocking collectives: 17.5 us -> 15.8 us  [on_device(): lax.all_to_all(square, 'row', 0, 0, axis_index_groups=y_lines)]
  transfers between devices with their start and end apart: 19 -> 19, of which waited for: 6 -> 2; matrix products, arithmetic and copies ran while one was open for 1% -> 0% of each run, Pallas kernels for 3% -> 4%
where the time goes in v10:
time: 163 us; the launch traced here: 162 us
  starting transfers between devices  83.5 us (51%)
  blocking collectives  55.8 us (34%)
  Pallas kernels  15.8 us (10%)
  local copies, waits for them, and re-layouts  2.63 us (2%)
  waiting for transfers between devices  1.83 us (1%)
    ppermute x16, starting transfers between devices, rings_of(): going[side] = [lax.ppermute(now[i], axes[i], ways[i]) for i in both]  64.7 us
    all_to_all x1, blocking collectives, on_device(): packs = lax.all_to_all(pack, 'col', 0, 0)  16.1 us
    all_to_all x1, blocking collectives, on_device(): lax.all_to_all(square, 'row', 0, 0, axis_index_groups=y_lines)  15.8 us
    pallas_call x9, Pallas kernels, call(): pl.pallas_call(kernel, out_shape=[jax.ShapeDtypeStruct(s, d) for s, d in...  15.8 us
    all_to_all x1, blocking collectives, on_device(): pieces = lax.all_to_all(summed, 'row', 0, 0, axis_index_groups=squares)  12.2 us
    all_to_all x1, blocking collectives, on_device(): term_parts = lax.all_to_all(terms, 'row', 0, 0, axis_index_groups=squares)  11.8 us
    ppermute x1, starting transfers between devices, on_device(): swapped = lax.ppermute(theirs, 'row', swap)  7.46 us
    ppermute x1, starting transfers between devices, on_device(): got = lax.ppermute(other, 'row', swap)  6.41 us
  transfers between devices with their start and end apart: 19, of which 2 were waited for; matrix products, arithmetic and copies ran while one was open for 0% of the time, Pallas kernels for 4%

profile of v10, /device:TPU:1, one launch (start us, length us, event | category | flops | bytes accessed | tf_op | source)
XLA Modules:
  0.0 161.8 jit_solution(6951631314560683226)
XLA Ops:
  0.6 0.9 pad_maximum_fusion.1
  1.5 0.8 broadcast_in_dim.3
  2.4 5.0 %all-to-all-start = ((bf16[4,256,256]{2,1,0:T(8,128)(2,1)}), bf16[4,256,256]{2,1,0:T(8,128)(2,1)S(1)}, u32[]{:S(2)}, u32[]{:S(2)}) async-start(bf16[4,256,256]{2,1,0:T(8,128)(2,1)} %broadcast_in_dim.3), calls=%async_computation | async-start | bytes 1048576 | tf_op jit(solution)/shard_map/all_to_all | solution.py:323
  7.3 0.1 pad_add_fusion.pos_ref
  7.4 0.7 shard_map.112
  8.1 7.5 %collective-permute-start = (bf16[128,1024]{1,0:T(8,128)(2,1)S(1)}, bf16[128,1024]{1,0:T(8,128)(2,1)S(1)}, u32[]{:S(2)}, u32[]{:S(2)}) collective-permute-start(bf16[128,1024]{1,0:T(8,128)(2,1)S(1)} %get-tuple-element.21), channel_id=1, source_target_pairs={{0,8},{8,0},{16,24},{24,16},{32,40},{40,32},{48,56},{56,48},{64,72... | collective-permute-start | bytes 786440 | tf_op jit(solution)/shard_map/ppermute | solution.py:315
  15.6 0.4 shard_map.113
  16.0 0.8 collective-permute-done
  16.9 2.8 %collective-permute-start.5 = (bf16[272,1024]{1,0:T(8,128)(2,1)S(1)}, bf16[272,1024]{1,0:T(8,128)(2,1)S(1)}, u32[]{:S(2)}, u32[]{:S(2)}) collective-permute-start(bf16[272,1024]{1,0:T(8,128)(2,1)S(1)} %pad_maximum_fusion.refs_0_), channel_id=1, source_target_pairs={{1,0},{2,1},{3,2},{4,3},{5,4},{6,5},{7,6},{0,7},{15,8},{8,9},{9,10... | collective-permute-start | bytes 1671176 | tf_op jit(solution)/shard_map/ppermute | solution.py:83
  19.7 3.2 %collective-permute-start.13 = (bf16[1088,256]{1,0:T(8,128)(2,1)S(1)}, bf16[1088,256]{1,0:T(8,128)(2,1)S(1)}, u32[]{:S(2)}, u32[]{:S(2)}) collective-permute-start(bf16[1088,256]{1,0:T(8,128)(2,1)S(1)} %pad.4.refs_7_), channel_id=1, source_target_pairs={{64,0},{456,8},{80,16},{472,24},{96,32},{488,40},{112,48},{504,56}... | collective-permute-start | bytes 1671176 | tf_op jit(solution)/shard_map/ppermute | solution.py:83
  22.9 3.8 %collective-permute-start.9 = (bf16[1088,256]{1,0:T(8,128)(2,1)S(1)}, bf16[1088,256]{1,0:T(8,128)(2,1)S(1)}, u32[]{:S(2)}, u32[]{:S(2)}) collective-permute-start(bf16[1088,256]{1,0:T(8,128)(2,1)S(1)} %pad.4.refs_7_), channel_id=1, source_target_pairs={{0,64},{8,456},{16,80},{24,472},{32,96},{40,488},{48,112},{56,504}... | collective-permute-start | bytes 1671176 | tf_op jit(solution)/shard_map/ppermute | solution.py:83
  26.7 8.6 %collective-permute-start.1 = (bf16[272,1024]{1,0:T(8,128)(2,1)S(1)}, bf16[272,1024]{1,0:T(8,128)(2,1)S(1)}, u32[]{:S(2)}, u32[]{:S(2)}) collective-permute-start(bf16[272,1024]{1,0:T(8,128)(2,1)S(1)} %pad_maximum_fusion.refs_0_), channel_id=1, source_target_pairs={{0,1},{1,2},{2,3},{3,4},{4,5},{5,6},{6,7},{7,0},{8,15},{9,8},{10,9... | collective-permute-start | bytes 1671176 | tf_op jit(solution)/shard_map/ppermute | solution.py:83
  35.3 1.9 %collective-permute-start.6 = (bf16[272,1024]{1,0:T(8,128)(2,1)S(1)}, bf16[272,1024]{1,0:T(8,128)(2,1)S(1)}, u32[]{:S(2)}, u32[]{:S(2)}) collective-permute-start(bf16[272,1024]{1,0:T(8,128)(2,1)S(1)} %collective-permute-done.5.refs_4_), channel_id=1, source_target_pairs={{1,0},{2,1},{3,2},{4,3},{5,4},{6,5},{7,6},{0,7},{15,8},{8,9},{9,10... | collective-permute-start | bytes 1671176 | tf_op jit(solution)/shard_map/ppermute | solution.py:83
  37.2 0.0 collective-permute-done.13.refs_11_
  37.3 1.9 %collective-permute-start.14 = (bf16[1088,256]{1,0:T(8,128)(2,1)S(1)}, bf16[1088,256]{1,0:T(8,128)(2,1)S(1)}, u32[]{:S(2)}, u32[]{:S(2)}) collective-permute-start(bf16[1088,256]{1,0:T(8,128)(2,1)S(1)} %collective-permute-done.13.refs_11_), channel_id=1, source_target_pairs={{64,0},{456,8},{80,16},{472,24},{96,32},{488,40},{112,48},{504,56}... | collective-permute-start | bytes 1671176 | tf_op jit(solution)/shard_map/ppermute | solution.py:83
  39.2 0.0 collective-permute-done.9.refs_8_
  39.2 4.6 %collective-permute-start.10 = (bf16[1088,256]{1,0:T(8,128)(2,1)S(1)}, bf16[1088,256]{1,0:T(8,128)(2,1)S(1)}, u32[]{:S(2)}, u32[]{:S(2)}) collective-permute-start(bf16[1088,256]{1,0:T(8,128)(2,1)S(1)} %collective-permute-done.9.refs_8_), channel_id=1, source_target_pairs={{0,64},{8,456},{16,80},{24,472},{32,96},{40,488},{48,112},{56,504}... | collective-permute-start | bytes 1671176 | tf_op jit(solution)/shard_map/ppermute | solution.py:83
  43.8 0.0 collective-permute-done.1.refs_1_
  43.8 8.0 %collective-permute-start.2 = (bf16[272,1024]{1,0:T(8,128)(2,1)S(1)}, bf16[272,1024]{1,0:T(8,128)(2,1)S(1)}, u32[]{:S(2)}, u32[]{:S(2)}) collective-permute-start(bf16[272,1024]{1,0:T(8,128)(2,1)S(1)} %collective-permute-done.1.refs_1_), channel_id=1, source_target_pairs={{0,1},{1,2},{2,3},{3,4},{4,5},{5,6},{6,7},{7,0},{8,15},{9,8},{10,9... | collective-permute-start | bytes 1671176 | tf_op jit(solution)/shard_map/ppermute | solution.py:83
  51.8 0.0 collective-permute-done.6.refs_5_
  51.8 1.9 %collective-permute-start.7 = (bf16[272,1024]{1,0:T(8,128)(2,1)S(1)}, bf16[272,1024]{1,0:T(8,128)(2,1)S(1)}, u32[]{:S(2)}, u32[]{:S(2)}) collective-permute-start(bf16[272,1024]{1,0:T(8,128)(2,1)S(1)} %collective-permute-done.6.refs_5_), channel_id=1, source_target_pairs={{1,0},{2,1},{3,2},{4,3},{5,4},{6,5},{7,6},{0,7},{15,8},{8,9},{9,10... | collective-permute-start | bytes 1671176 | tf_op jit(solution)/shard_map/ppermute | solution.py:83
  53.7 0.0 collective-permute-done.14.refs_12_
  53.8 1.9 %collective-permute-start.15 = (bf16[1088,256]{1,0:T(8,128)(2,1)S(1)}, bf16[1088,256]{1,0:T(8,128)(2,1)S(1)}, u32[]{:S(2)}, u32[]{:S(2)}) collective-permute-start(bf16[1088,256]{1,0:T(8,128)(2,1)S(1)} %collective-permute-done.14.refs_12_), channel_id=1, source_target_pairs={{64,0},{456,8},{80,16},{472,24},{96,32},{488,40},{112,48},{504,56}... | collective-permute-start | bytes 1671176 | tf_op jit(solution)/shard_map/ppermute | solution.py:83
  55.7 4.6 %collective-permute-start.11 = (bf16[1088,256]{1,0:T(8,128)(2,1)S(1)}, bf16[1088,256]{1,0:T(8,128)(2,1)S(1)}, u32[]{:S(2)}, u32[]{:S(2)}) collective-permute-start(bf16[1088,256]{1,0:T(8,128)(2,1)S(1)} %collective-permute-done.10.refs_9_), channel_id=1, source_target_pairs={{0,64},{8,456},{16,80},{24,472},{32,96},{40,488},{48,112},{56,504}... | collective-permute-start | bytes 1671176 | tf_op jit(solution)/shard_map/ppermute | solution.py:83
  60.3 7.0 %collective-permute-start.3 = (bf16[272,1024]{1,0:T(8,128)(2,1)S(1)}, bf16[272,1024]{1,0:T(8,128)(2,1)S(1)}, u32[]{:S(2)}, u32[]{:S(2)}) collective-permute-start(bf16[272,1024]{1,0:T(8,128)(2,1)S(1)} %collective-permute-done.2.refs_2_), channel_id=1, source_target_pairs={{0,1},{1,2},{2,3},{3,4},{4,5},{5,6},{6,7},{7,0},{8,15},{9,8},{10,9... | collective-permute-start | bytes 1671176 | tf_op jit(solution)/shard_map/ppermute | solution.py:83
  67.3 0.0 collective-permute-done.7.refs_6_
  67.4 1.9 %collective-permute-start.8 = (bf16[144,1024]{1,0:T(8,128)(2,1)S(1)}, bf16[144,1024]{1,0:T(8,128)(2,1)S(1)}, u32[]{:S(2)}, u32[]{:S(2)}) collective-permute-start(bf16[144,1024]{1,0:T(8,128)(2,1)S(1)} %slice.17), channel_id=1, source_target_pairs={{1,0},{2,1},{3,2},{4,3},{5,4},{6,5},{7,6},{0,7},{15,8},{8,9},{9,10... | collective-permute-start | bytes 884744 | tf_op jit(solution)/shard_map/ppermute | solution.py:83
  69.4 1.9 %collective-permute-start.16 = (bf16[544,256]{1,0:T(8,128)(2,1)S(1)}, bf16[544,256]{1,0:T(8,128)(2,1)S(1)}, u32[]{:S(2)}, u32[]{:S(2)}) collective-permute-start(bf16[544,256]{1,0:T(8,128)(2,1)S(1)} %slice.19), channel_id=1, source_target_pairs={{64,0},{456,8},{80,16},{472,24},{96,32},{488,40},{112,48},{504,56}... | collective-permute-start | bytes 835592 | tf_op jit(solution)/shard_map/ppermute | solution.py:83
  71.4 4.6 %collective-permute-start.12 = (bf16[544,256]{1,0:T(8,128)(2,1)S(1)}, bf16[544,256]{1,0:T(8,128)(2,1)S(1)}, u32[]{:S(2)}, u32[]{:S(2)}) collective-permute-start(bf16[544,256]{1,0:T(8,128)(2,1)S(1)} %slice.18), channel_id=1, source_target_pairs={{0,64},{8,456},{16,80},{24,472},{32,96},{40,488},{48,112},{56,504}... | collective-permute-start | bytes 835592 | tf_op jit(solution)/shard_map/ppermute | solution.py:83
  76.0 6.0 %collective-permute-start.4 = (bf16[128,1024]{1,0:T(8,128)(2,1)S(1)}, bf16[128,1024]{1,0:T(8,128)(2,1)S(1)}, u32[]{:S(2)}, u32[]{:S(2)}) collective-permute-start(bf16[128,1024]{1,0:T(8,128)(2,1)S(1)} %slice.16), channel_id=1, source_target_pairs={{0,1},{1,2},{2,3},{3,4},{4,5},{5,6},{6,7},{7,0},{8,15},{9,8},{10,9... | collective-permute-start | bytes 786440 | tf_op jit(solution)/shard_map/ppermute | solution.py:83
  82.2 5.2 %shard_map.114 = (f32[256,256]{1,0:T(8,128)S(1)}, f32[16,1024]{1,0:T(8,128)S(1)}, bf16[256,1024]{1,0:T(8,128)(2,1)S(1)}, bf16[1088,256]{1,0:T(8,128)(2,1)S(1)}) custom-call(s32[3]{0:T(128)S(1)} %pad_add_fusion.pos_ref, bf16[272,1024]{1,0:T(8,128)(2,1)S(1)} %pad_maximum_fusion.refs_0_, bf16[272,1024]{1,0:T(8,128)(2,1)} %copy-done.17, ...), custom_call_target="tpu_custom_call" | custom-call | flops 1073741824 | bytes 7798784 | tf_op jit(solution)/shard_map/pallas_call | solution.py:275
  87.4 0.8 copy-done.1
  88.2 0.8 copy-done.4
  89.0 0.0 copy-start.2
  89.0 0.0 copy-start.3
  89.1 0.0 copy-start.6
  89.1 0.0 copy-start.7
  89.1 0.0 copy-start.8
  89.1 2.5 %shard_map.115 = (f32[128,256]{1,0:T(8,128)S(1)}, f32[128,256]{1,0:T(8,128)S(1)}, bf16[128,64]{1,0:T(8,128)(2,1)S(1)}) custom-call(s32[3]{0:T(128)S(1)} %pad_add_fusion.pos_ref, bf16[128,1024]{1,0:T(8,128)(2,1)S(1)} %collective-permute-done.4.t1_ref, bf16[144,1024]{1,0:T(8,128)(2,1)S(1)} %collective-permute-done.8.t2_ref, ...), custom_call_target="tpu_custom_call" | custom-call | tf_op jit(solution)/shard_map/pallas_call | solution.py:275
  91.6 6.4 %collective-permute-start.17 = (f32[128,256]{1,0:T(8,128)S(1)}, f32[128,256]{1,0:T(8,128)S(1)}, u32[]{:S(2)}, u32[]{:S(2)}) collective-permute-start(f32[128,256]{1,0:T(8,128)S(1)} %get-tuple-element.29), channel_id=1, source_target_pairs={{0,8},{8,0},{16,24},{24,16},{32,40},{40,32},{48,56},{56,48},{64,72... | collective-permute-start | bytes 393224 | tf_op jit(solution)/shard_map/ppermute | solution.py:365
  98.1 1.0 collective-permute-done.17.got_ref
  99.0 5.0 %shard_map.116 = (bf16[8,80,128]{2,1,0:T(8,128)(2,1)S(1)}, f32[128,128]{1,0:T(8,128)S(1)}, f32[128,128]{1,0:T(8,128)S(1)}) custom-call(s32[1,8]{1,0:T(1,128)S(1)} %copy-done.8, f32[128,256]{1,0:T(8,128)S(1)} %get-tuple-element.28.own_ref, f32[128,256]{1,0:T(8,128)S(1)} %collective-permute-done.17.got_ref, ...), custom_call_target="tpu_custom_call" | custom-call | tf_op jit(solution)/shard_map/pallas_call | solution.py:275
  104.1 16.1 %all_to_all.25.pack_ref = bf16[8,80,128]{2,1,0:T(8,128)(2,1)S(1)} all-to-all(bf16[8,80,128]{2,1,0:T(8,128)(2,1)S(1)} %get-tuple-element.31), channel_id=1, replica_groups=mesh['row'=64,'col'=8] {'col'}, dimensions={0} | all-to-all | bytes 327680 | tf_op jit(solution)/shard_map/all_to_all | solution.py:378
  120.2 0.9 shard_map.117
  121.1 11.8 %all_to_all.26.in_ref = bf16[8,72,256]{2,1,0:T(8,128)(2,1)S(1)} all-to-all(bf16[8,72,256]{2,1,0:T(8,128)(2,1)S(1)} %shard_map.117), channel_id=1, replica_groups={{0,8,16,24,32,40,48,56},{64,72,80,88,96,104,112,120},{128,136,144,152,1..., dimensions={0} | all-to-all | bytes 589824 | tf_op jit(solution)/shard_map/all_to_all | solution.py:384
  133.0 15.8 %all_to_all.27.in_ref = bf16[8,72,256]{2,1,0:T(8,128)(2,1)S(1)} all-to-all(bf16[8,72,256]{2,1,0:T(8,128)(2,1)S(1)} %shard_map.118), channel_id=1, replica_groups={{0,64,128,192,256,320,384,448},{8,72,136,200,264,328,392,456},{16,80,14..., dimensions={0} | all-to-all | bytes 589824 | tf_op jit(solution)/shard_map/all_to_all | solution.py:386
  148.8 12.2 %all_to_all.28.in_ref = bf16[8,72,256]{2,1,0:T(8,128)(2,1)S(1)} all-to-all(bf16[8,72,256]{2,1,0:T(8,128)(2,1)S(1)} %shard_map.119), channel_id=1, replica_groups={{0,8,16,24,32,40,48,56},{64,72,80,88,96,104,112,120},{128,136,144,152,1..., dimensions={0} | all-to-all | bytes 589824 | tf_op jit(solution)/shard_map/all_to_all | solution.py:388
  161.0 0.8 shard_map.120
  (56 shorter events, 0.3 us)
Async XLA Ops:
  2.3 5.1 %copy-start = (bf16[128,2048]{1,0:T(8,128)(2,1)S(1)}, bf16[128,2048]{1,0:T(8,128)(2,1)}, u32[]{:S(2)}) copy-start(bf16[128,2048]{1,0:T(8,128)(2,1)} %t_ref.5) | copy-start | bytes 1572868
  2.4 14.4 %all-to-all-start = ((bf16[4,256,256]{2,1,0:T(8,128)(2,1)}), bf16[4,256,256]{2,1,0:T(8,128)(2,1)S(1)}, u32[]{:S(2)}, u32[]{:S(2)}) async-start(bf16[4,256,256]{2,1,0:T(8,128)(2,1)} %broadcast_in_dim.3), calls=%async_computation | async-start | bytes 1048576 | tf_op jit(solution)/shard_map/all_to_all | solution.py:323
  7.3 8.3 %copy-start.5 = (bf16[2048,64]{0,1:T(8,128)(2,1)S(1)}, bf16[2048,64]{0,1:T(8,128)(2,1)}, u32[]{:S(2)}) copy-start(bf16[2048,64]{0,1:T(8,128)(2,1)} %param.14) | copy-start | bytes 786436
  8.1 8.6 %collective-permute-start = (bf16[128,1024]{1,0:T(8,128)(2,1)S(1)}, bf16[128,1024]{1,0:T(8,128)(2,1)S(1)}, u32[]{:S(2)}, u32[]{:S(2)}) collective-permute-start(bf16[128,1024]{1,0:T(8,128)(2,1)S(1)} %get-tuple-element.21), channel_id=1, source_target_pairs={{0,8},{8,0},{16,24},{24,16},{32,40},{40,32},{48,56},{56,48},{64,72... | collective-permute-start | bytes 786440 | tf_op jit(solution)/shard_map/ppermute | solution.py:315
  16.8 52.6 %copy-start.9 = (bf16[1088,256]{1,0:T(8,128)(2,1)}, bf16[1088,256]{1,0:T(8,128)(2,1)S(1)}, u32[]{:S(2)}) copy-start(bf16[1088,256]{1,0:T(8,128)(2,1)S(1)} %pad.4.refs_7_) | copy-start | bytes 1671172
  16.9 18.4 %collective-permute-start.5 = (bf16[272,1024]{1,0:T(8,128)(2,1)S(1)}, bf16[272,1024]{1,0:T(8,128)(2,1)S(1)}, u32[]{:S(2)}, u32[]{:S(2)}) collective-permute-start(bf16[272,1024]{1,0:T(8,128)(2,1)S(1)} %pad_maximum_fusion.refs_0_), channel_id=1, source_target_pairs={{1,0},{2,1},{3,2},{4,3},{5,4},{6,5},{7,6},{0,7},{15,8},{8,9},{9,10... | collective-permute-start | bytes 1671176 | tf_op jit(solution)/shard_map/ppermute | solution.py:83
  19.7 17.6 %collective-permute-start.13 = (bf16[1088,256]{1,0:T(8,128)(2,1)S(1)}, bf16[1088,256]{1,0:T(8,128)(2,1)S(1)}, u32[]{:S(2)}, u32[]{:S(2)}) collective-permute-start(bf16[1088,256]{1,0:T(8,128)(2,1)S(1)} %pad.4.refs_7_), channel_id=1, source_target_pairs={{64,0},{456,8},{80,16},{472,24},{96,32},{488,40},{112,48},{504,56}... | collective-permute-start | bytes 1671176 | tf_op jit(solution)/shard_map/ppermute | solution.py:83
  22.9 16.3 %collective-permute-start.9 = (bf16[1088,256]{1,0:T(8,128)(2,1)S(1)}, bf16[1088,256]{1,0:T(8,128)(2,1)S(1)}, u32[]{:S(2)}, u32[]{:S(2)}) collective-permute-start(bf16[1088,256]{1,0:T(8,128)(2,1)S(1)} %pad.4.refs_7_), channel_id=1, source_target_pairs={{0,64},{8,456},{16,80},{24,472},{32,96},{40,488},{48,112},{56,504}... | collective-permute-start | bytes 1671176 | tf_op jit(solution)/shard_map/ppermute | solution.py:83
  26.7 17.1 %collective-permute-start.1 = (bf16[272,1024]{1,0:T(8,128)(2,1)S(1)}, bf16[272,1024]{1,0:T(8,128)(2,1)S(1)}, u32[]{:S(2)}, u32[]{:S(2)}) collective-permute-start(bf16[272,1024]{1,0:T(8,128)(2,1)S(1)} %pad_maximum_fusion.refs_0_), channel_id=1, source_target_pairs={{0,1},{1,2},{2,3},{3,4},{4,5},{5,6},{6,7},{7,0},{8,15},{9,8},{10,9... | collective-permute-start | bytes 1671176 | tf_op jit(solution)/shard_map/ppermute | solution.py:83
  35.3 46.8 %copy-start.14 = (bf16[272,1024]{1,0:T(8,128)(2,1)}, bf16[272,1024]{1,0:T(8,128)(2,1)S(1)}, u32[]{:S(2)}) copy-start(bf16[272,1024]{1,0:T(8,128)(2,1)S(1)} %collective-permute-done.5.refs_4_) | copy-start | bytes 1671172
  35.3 16.5 %collective-permute-start.6 = (bf16[272,1024]{1,0:T(8,128)(2,1)S(1)}, bf16[272,1024]{1,0:T(8,128)(2,1)S(1)}, u32[]{:S(2)}, u32[]{:S(2)}) collective-permute-start(bf16[272,1024]{1,0:T(8,128)(2,1)S(1)} %collective-permute-done.5.refs_4_), channel_id=1, source_target_pairs={{1,0},{2,1},{3,2},{4,3},{5,4},{6,5},{7,6},{0,7},{15,8},{8,9},{9,10... | collective-permute-start | bytes 1671176 | tf_op jit(solution)/shard_map/ppermute | solution.py:83
  37.2 44.8 %copy-start.15 = (bf16[1088,256]{1,0:T(8,128)(2,1)}, bf16[1088,256]{1,0:T(8,128)(2,1)S(1)}, u32[]{:S(2)}) copy-start(bf16[1088,256]{1,0:T(8,128)(2,1)S(1)} %collective-permute-done.13.refs_11_) | copy-start | bytes 1671172
  37.3 16.5 %collective-permute-start.14 = (bf16[1088,256]{1,0:T(8,128)(2,1)S(1)}, bf16[1088,256]{1,0:T(8,128)(2,1)S(1)}, u32[]{:S(2)}, u32[]{:S(2)}) collective-permute-start(bf16[1088,256]{1,0:T(8,128)(2,1)S(1)} %collective-permute-done.13.refs_11_), channel_id=1, source_target_pairs={{64,0},{456,8},{80,16},{472,24},{96,32},{488,40},{112,48},{504,56}... | collective-permute-start | bytes 1671176 | tf_op jit(solution)/shard_map/ppermute | solution.py:83
  39.2 42.9 %copy-start.16 = (bf16[1088,256]{1,0:T(8,128)(2,1)}, bf16[1088,256]{1,0:T(8,128)(2,1)S(1)}, u32[]{:S(2)}) copy-start(bf16[1088,256]{1,0:T(8,128)(2,1)S(1)} %collective-permute-done.9.refs_8_) | copy-start | bytes 1671172
  39.2 16.5 %collective-permute-start.10 = (bf16[1088,256]{1,0:T(8,128)(2,1)S(1)}, bf16[1088,256]{1,0:T(8,128)(2,1)S(1)}, u32[]{:S(2)}, u32[]{:S(2)}) collective-permute-start(bf16[1088,256]{1,0:T(8,128)(2,1)S(1)} %collective-permute-done.9.refs_8_), channel_id=1, source_target_pairs={{0,64},{8,456},{16,80},{24,472},{32,96},{40,488},{48,112},{56,504}... | collective-permute-start | bytes 1671176 | tf_op jit(solution)/shard_map/ppermute | solution.py:83
  43.8 38.3 %copy-start.17 = (bf16[272,1024]{1,0:T(8,128)(2,1)}, bf16[272,1024]{1,0:T(8,128)(2,1)S(1)}, u32[]{:S(2)}) copy-start(bf16[272,1024]{1,0:T(8,128)(2,1)S(1)} %collective-permute-done.1.refs_1_) | copy-start | bytes 1671172
  43.8 16.5 %collective-permute-start.2 = (bf16[272,1024]{1,0:T(8,128)(2,1)S(1)}, bf16[272,1024]{1,0:T(8,128)(2,1)S(1)}, u32[]{:S(2)}, u32[]{:S(2)}) collective-permute-start(bf16[272,1024]{1,0:T(8,128)(2,1)S(1)} %collective-permute-done.1.refs_1_), channel_id=1, source_target_pairs={{0,1},{1,2},{2,3},{3,4},{4,5},{5,6},{6,7},{7,0},{8,15},{9,8},{10,9... | collective-permute-start | bytes 1671176 | tf_op jit(solution)/shard_map/ppermute | solution.py:83
  51.8 30.3 %copy-start.18 = (bf16[272,1024]{1,0:T(8,128)(2,1)}, bf16[272,1024]{1,0:T(8,128)(2,1)S(1)}, u32[]{:S(2)}) copy-start(bf16[272,1024]{1,0:T(8,128)(2,1)S(1)} %collective-permute-done.6.refs_5_) | copy-start | bytes 1671172
  51.8 15.6 %collective-permute-start.7 = (bf16[272,1024]{1,0:T(8,128)(2,1)S(1)}, bf16[272,1024]{1,0:T(8,128)(2,1)S(1)}, u32[]{:S(2)}, u32[]{:S(2)}) collective-permute-start(bf16[272,1024]{1,0:T(8,128)(2,1)S(1)} %collective-permute-done.6.refs_5_), channel_id=1, source_target_pairs={{1,0},{2,1},{3,2},{4,3},{5,4},{6,5},{7,6},{0,7},{15,8},{8,9},{9,10... | collective-permute-start | bytes 1671176 | tf_op jit(solution)/shard_map/ppermute | solution.py:83
  53.7 28.4 %copy-start.19 = (bf16[1088,256]{1,0:T(8,128)(2,1)}, bf16[1088,256]{1,0:T(8,128)(2,1)S(1)}, u32[]{:S(2)}) copy-start(bf16[1088,256]{1,0:T(8,128)(2,1)S(1)} %collective-permute-done.14.refs_12_) | copy-start | bytes 1671172
  53.8 15.6 %collective-permute-start.15 = (bf16[1088,256]{1,0:T(8,128)(2,1)S(1)}, bf16[1088,256]{1,0:T(8,128)(2,1)S(1)}, u32[]{:S(2)}, u32[]{:S(2)}) collective-permute-start(bf16[1088,256]{1,0:T(8,128)(2,1)S(1)} %collective-permute-done.14.refs_12_), channel_id=1, source_target_pairs={{64,0},{456,8},{80,16},{472,24},{96,32},{488,40},{112,48},{504,56}... | collective-permute-start | bytes 1671176 | tf_op jit(solution)/shard_map/ppermute | solution.py:83
  55.7 26.4 %copy-start.20 = (bf16[1088,256]{1,0:T(8,128)(2,1)}, bf16[1088,256]{1,0:T(8,128)(2,1)S(1)}, u32[]{:S(2)}) copy-start(bf16[1088,256]{1,0:T(8,128)(2,1)S(1)} %collective-permute-done.10.refs_9_) | copy-start | bytes 1671172
  55.7 15.6 %collective-permute-start.11 = (bf16[1088,256]{1,0:T(8,128)(2,1)S(1)}, bf16[1088,256]{1,0:T(8,128)(2,1)S(1)}, u32[]{:S(2)}, u32[]{:S(2)}) collective-permute-start(bf16[1088,256]{1,0:T(8,128)(2,1)S(1)} %collective-permute-done.10.refs_9_), channel_id=1, source_target_pairs={{0,64},{8,456},{16,80},{24,472},{32,96},{40,488},{48,112},{56,504}... | collective-permute-start | bytes 1671176 | tf_op jit(solution)/shard_map/ppermute | solution.py:83
  60.3 21.8 %copy-start.21 = (bf16[272,1024]{1,0:T(8,128)(2,1)}, bf16[272,1024]{1,0:T(8,128)(2,1)S(1)}, u32[]{:S(2)}) copy-start(bf16[272,1024]{1,0:T(8,128)(2,1)S(1)} %collective-permute-done.2.refs_2_) | copy-start | bytes 1671172
  60.3 15.7 %collective-permute-start.3 = (bf16[272,1024]{1,0:T(8,128)(2,1)S(1)}, bf16[272,1024]{1,0:T(8,128)(2,1)S(1)}, u32[]{:S(2)}, u32[]{:S(2)}) collective-permute-start(bf16[272,1024]{1,0:T(8,128)(2,1)S(1)} %collective-permute-done.2.refs_2_), channel_id=1, source_target_pairs={{0,1},{1,2},{2,3},{3,4},{4,5},{5,6},{6,7},{7,0},{8,15},{9,8},{10,9... | collective-permute-start | bytes 1671176 | tf_op jit(solution)/shard_map/ppermute | solution.py:83
  67.4 2.0 %copy-start.10 = (bf16[272,1024]{1,0:T(8,128)(2,1)}, bf16[272,1024]{1,0:T(8,128)(2,1)S(1)}, u32[]{:S(2)}) copy-start(bf16[272,1024]{1,0:T(8,128)(2,1)S(1)} %collective-permute-done.7.refs_6_) | copy-start | bytes 1671172
  67.4 21.6 %collective-permute-start.8 = (bf16[144,1024]{1,0:T(8,128)(2,1)S(1)}, bf16[144,1024]{1,0:T(8,128)(2,1)S(1)}, u32[]{:S(2)}, u32[]{:S(2)}) collective-permute-start(bf16[144,1024]{1,0:T(8,128)(2,1)S(1)} %slice.17), channel_id=1, source_target_pairs={{1,0},{2,1},{3,2},{4,3},{5,4},{6,5},{7,6},{0,7},{15,8},{8,9},{9,10... | collective-permute-start | bytes 884744 | tf_op jit(solution)/shard_map/ppermute | solution.py:83
  69.4 2.0 %copy-start.11 = (bf16[1088,256]{1,0:T(8,128)(2,1)}, bf16[1088,256]{1,0:T(8,128)(2,1)S(1)}, u32[]{:S(2)}) copy-start(bf16[1088,256]{1,0:T(8,128)(2,1)S(1)} %collective-permute-done.15.refs_13_) | copy-start | bytes 1671172
  69.4 19.6 %collective-permute-start.16 = (bf16[544,256]{1,0:T(8,128)(2,1)S(1)}, bf16[544,256]{1,0:T(8,128)(2,1)S(1)}, u32[]{:S(2)}, u32[]{:S(2)}) collective-permute-start(bf16[544,256]{1,0:T(8,128)(2,1)S(1)} %slice.19), channel_id=1, source_target_pairs={{64,0},{456,8},{80,16},{472,24},{96,32},{488,40},{112,48},{504,56}... | collective-permute-start | bytes 835592 | tf_op jit(solution)/shard_map/ppermute | solution.py:83
  71.4 10.8 %copy-start.12 = (bf16[1088,256]{1,0:T(8,128)(2,1)}, bf16[1088,256]{1,0:T(8,128)(2,1)S(1)}, u32[]{:S(2)}) copy-start(bf16[1088,256]{1,0:T(8,128)(2,1)S(1)} %collective-permute-done.11.refs_10_) | copy-start | bytes 1671172
  71.4 17.6 %collective-permute-start.12 = (bf16[544,256]{1,0:T(8,128)(2,1)S(1)}, bf16[544,256]{1,0:T(8,128)(2,1)S(1)}, u32[]{:S(2)}, u32[]{:S(2)}) collective-permute-start(bf16[544,256]{1,0:T(8,128)(2,1)S(1)} %slice.18), channel_id=1, source_target_pairs={{0,64},{8,456},{16,80},{24,472},{32,96},{40,488},{48,112},{56,504}... | collective-permute-start | bytes 835592 | tf_op jit(solution)/shard_map/ppermute | solution.py:83
  76.0 6.2 %copy-start.13 = (bf16[272,1024]{1,0:T(8,128)(2,1)}, bf16[272,1024]{1,0:T(8,128)(2,1)S(1)}, u32[]{:S(2)}) copy-start(bf16[272,1024]{1,0:T(8,128)(2,1)S(1)} %collective-permute-done.3.refs_3_) | copy-start | bytes 1671172
  76.0 13.0 %collective-permute-start.4 = (bf16[128,1024]{1,0:T(8,128)(2,1)S(1)}, bf16[128,1024]{1,0:T(8,128)(2,1)S(1)}, u32[]{:S(2)}, u32[]{:S(2)}) collective-permute-start(bf16[128,1024]{1,0:T(8,128)(2,1)S(1)} %slice.16), channel_id=1, source_target_pairs={{0,1},{1,2},{2,3},{3,4},{4,5},{5,6},{6,7},{7,0},{8,15},{9,8},{10,9... | collective-permute-start | bytes 786440 | tf_op jit(solution)/shard_map/ppermute | solution.py:83
  87.4 0.8 copy-start.1
  88.2 0.8 copy-start.4
  89.0 10.0 %copy-start.2 = (bf16[128,2048]{1,0:T(8,128)(2,1)S(1)}, bf16[128,2048]{1,0:T(8,128)(2,1)}, u32[]{:S(2)}) copy-start(bf16[128,2048]{1,0:T(8,128)(2,1)} %q_ref.1) | copy-start | bytes 1572868
  89.0 10.0 %copy-start.3 = (bf16[128,2048]{1,0:T(8,128)(2,1)S(1)}, bf16[128,2048]{1,0:T(8,128)(2,1)}, u32[]{:S(2)}) copy-start(bf16[128,2048]{1,0:T(8,128)(2,1)} %p_ref.1) | copy-start | bytes 1572868
  89.1 10.0 %copy-start.6 = (bf16[64,128]{1,0:T(8,128)(2,1)S(1)}, bf16[64,128]{1,0:T(8,128)(2,1)}, u32[]{:S(2)}) copy-start(bf16[64,128]{1,0:T(8,128)(2,1)} %upk_ref.1) | copy-start | bytes 49156
  89.1 10.0 %copy-start.7 = (bf16[64,128]{1,0:T(8,128)(2,1)S(1)}, bf16[64,128]{1,0:T(8,128)(2,1)}, u32[]{:S(2)}) copy-start(bf16[64,128]{1,0:T(8,128)(2,1)} %upv_ref.1) | copy-start | bytes 49156
  89.1 10.0 %copy-start.8 = (s32[1,8]{1,0:T(1,128)S(1)}, s32[1,8]{1,0:T(1,128)}, u32[]{:S(2)}) copy-start(s32[1,8]{1,0:T(1,128)} %lengths_ref.3) | copy-start | bytes 100
  91.6 7.4 %collective-permute-start.17 = (f32[128,256]{1,0:T(8,128)S(1)}, f32[128,256]{1,0:T(8,128)S(1)}, u32[]{:S(2)}, u32[]{:S(2)}) collective-permute-start(f32[128,256]{1,0:T(8,128)S(1)} %get-tuple-element.29), channel_id=1, source_target_pairs={{0,8},{8,0},{16,24},{24,16},{32,40},{40,32},{48,56},{56,48},{64,72... | collective-permute-start | bytes 393224 | tf_op jit(solution)/shard_map/ppermute | solution.py:365

commit v11 on v9

--- a/solution.py
+++ b/solution.py
@@ -173,22 +173,26 @@
     s_at = lax.broadcasted_iota(jnp.int32, (rows, rows), 0)
     t_at = lax.broadcasted_iota(jnp.int32, (rows, rows), 1)
     allowed = (doc_s == doc_t) & (t_at >= s_at)
+    banned = jnp.where(allowed, 0.0, -1e30)
+    banned = jnp.concatenate([banned, banned], axis=1)
 
     def raised(scores):
-        scores = jnp.where(allowed, scores, -1e30)
+        scores = jnp.where(banned < 0.0, -1e30, scores)
         peak = jnp.max(scores, axis=0, keepdims=True)
         e = jnp.exp2((scores - peak) * (score_scale * LOG2E))
         return e, 1.0 / jnp.sum(e, axis=0, keepdims=True)
 
     gk = jnp.zeros((rows, HD), F32)
     gv = jnp.zeros((rows, HD), F32)
-    gap = jnp.zeros((1, rows), F32)
-    for h in range(heads):
+    gap = jnp.zeros((1, 2 * rows), F32)
+    for h in range(0, heads, 2):
         if h % batch == 0:
             for c in copies[2 * h // batch:2 * h // batch + 2]:
                 c.wait()
-        q = q_scr[:, pl.ds(h * HD, HD)]
-        probe = p_scr[:, pl.ds(h * HD, HD)]
+        q, probe = (
+            jnp.concatenate([scr[:, pl.ds((h + i) * HD, HD)] for i in range(2)], axis=0)
+            for scr in (q_scr, p_scr)
+        )
         scores = mm(keys, q, NT)
         grads = mm(values, probe, NT)
         pol, share = raised(scores[:rows])
@@ -201,6 +205,7 @@
         grad_scores = (pol * (grad_pol - mean_pol)).astype(BF)
         gk = gk + mm(grad_scores, q, NN)
         gv = gv + mm(pol.astype(BF), probe, NN)
+    gap = gap[:, :rows] + gap[:, rows:]
     gk = gk * (score_scale * probe_scale)
     gv = gv * probe_scale
     gap = gap * probe_scale
@@ -219,7 +224,9 @@
         pack_ref[i, pl.ds(64, 16)] = tail
 
 
-def weigh_kernel(lengths_ref, pack_ref, low_half_ref, gk_ref, gv_ref, t_ref, out_ref):
+def weigh_kernel(
+    pos_ref, lengths_ref, pack_ref, low_half_ref, gk_ref, gv_ref, t_ref, keep_ref, give_ref, up_ref
+):
     rows = gk_ref.shape[0]
     total = pack_ref[0].astype(F32)
     for i in range(1, pack_ref.shape[0]):
@@ -232,12 +239,29 @@
     back_half = (unfold(total[:64], 64) * weight).astype(BF)
     down = mm(back_half, t_ref[...], TN).astype(BF)
     both = jnp.concatenate([gk_ref[...] * weight, gv_ref[...] * weight], axis=1).astype(BF)
-    up = mm(low_half_ref[...], both, TN).astype(BF)
-    slots = out_ref.shape[0]
-    wide, deep = t_ref.shape[1] // slots, up.shape[0] // slots
-    for j in range(slots):
-        out_ref[j, pl.ds(0, 64)] = down[:, j * wide:(j + 1) * wide]
-        out_ref[j, pl.ds(64, deep)] = up[j * deep:(j + 1) * deep]
+    up_ref[...] = mm(low_half_ref[...], both, TN)
+    half = keep_ref.shape[1]
+    for core in range(2):
+
+        @pl.when(pos_ref[0] == core)
+        def _():
+            keep_ref[...] = down[:, core * half:(core + 1) * half]
+            give_ref[...] = down[:, (1 - core) * half:(2 - core) * half]
+
+
+def tiles():
+    for s in range(32):
+        yield s, s // 4 * 128, s % 4 * 16, s // 16 * 128, s // 4 % 4 * 16 + s % 4 * 4
+
+
+def slot_kernel(keep_ref, got_ref, up_ref, out_ref):
+    down = (keep_ref[...].astype(F32) + got_ref[...].astype(F32)).astype(BF)
+    up = up_ref[...]
+    blank = jnp.zeros((4, 128), F32)
+    for s, lane, row, up_lane, up_row in tiles():
+        out_ref[s, pl.ds(0, 16)] = down[row:row + 16, lane:lane + 128]
+        piece = jnp.concatenate([up[up_row:up_row + 4, up_lane:up_lane + 128], blank], axis=0)
+        out_ref[s, pl.ds(16, 8)] = piece.astype(BF)
 
 
 def sum_kernel(in_ref, out_ref):
@@ -249,14 +273,21 @@
         out_ref[i] = total
 
 
-def place_kernel(in_ref, down_ref, upk_ref, upv_ref):
-    slots, _, wide = in_ref.shape
-    deep = upk_ref.shape[0] // slots
-    for j in range(slots):
-        down_ref[:, pl.ds(j * wide, wide)] = in_ref[j, pl.ds(0, 64)].astype(F32)
-        up = in_ref[j, pl.ds(64, deep)].astype(F32)
-        upk_ref[pl.ds(j * deep, deep)] = up[:, :HD]
-        upv_ref[pl.ds(j * deep, deep)] = up[:, HD:]
+def place_kernel(pos_ref, mine_ref, theirs_ref, down_ref, upk_ref, upv_ref):
+    half = down_ref.shape[1] // 2
+    for core in range(2):
+
+        @pl.when(pos_ref[0] == core)
+        def _():
+            for s, lane, row, _, _ in tiles():
+                for k, ref in ((core, mine_ref), (1 - core, theirs_ref)):
+                    to = pl.ds(k * half + lane, 128)
+                    down_ref[pl.ds(row, 16), to] = ref[s, pl.ds(0, 16)].astype(F32)
+
+    for s, _, _, up_lane, up_row in tiles():
+        up = mine_ref[s, pl.ds(16, 8)].astype(F32) + theirs_ref[s, pl.ds(16, 8)].astype(F32)
+        to = upk_ref if up_lane == 0 else upv_ref
+        to[pl.ds(up_row, 4)] = up[:4]
 
 
 def call(kernel, outs, in_specs, out_specs, *args, scratch=(), mib=8, cost=None):
@@ -291,8 +322,7 @@
         for z in range(8)
     ]
     z_aft = [(b, a) for a, b in z_fore]
-    y_lines = [[place(y, x, c) for y in range(8)] for x in range(4) for c in range(2)]
-    squares = [[place(y, x, c) for x in range(4) for c in range(2)] for y in range(8)]
+    kinds = [[place(y, x, c) for y in range(8) for x in range(4)] for c in range(2)]
     x_lines = [[place(y, x, c) for x in range(4)] for y in range(8) for c in range(2)]
 
     half = (rows, feats // 2)
@@ -361,20 +391,23 @@
         ],
     )
     packs = lax.all_to_all(pack, "col", 0, 0)
-    slot = (8, 64 + 8, 2 * HD)
+    keep, give, up = call(
+        weigh_kernel,
+        [((64, feats // 2), BF), ((64, feats // 2), BF), ((64, 2 * HD), F32)],
+        [SMEM] * 2 + [VMEM] * 5, [VMEM] * 3,
+        pos, lengths, packs, low_half, gk, gv, tokens,
+    )
+    slots = (32, 24, 128)
     (terms,) = call(
-        weigh_kernel, [(slot, BF)], [SMEM] + [VMEM] * 5, [VMEM],
-        lengths, packs, low_half, gk, gv, tokens,
-    )
-    term_parts = lax.all_to_all(terms, "row", 0, 0, axis_index_groups=squares)
-    (square,) = call(sum_kernel, [(slot, BF)], [VMEM], [VMEM], term_parts)
-    square_parts = lax.all_to_all(square, "row", 0, 0, axis_index_groups=y_lines)
-    (summed,) = call(sum_kernel, [(slot, BF)], [VMEM], [VMEM], square_parts)
-    pieces = lax.all_to_all(summed, "row", 0, 0, axis_index_groups=squares)
+        slot_kernel, [(slots, BF)], [VMEM] * 3, [VMEM], keep, lax.ppermute(give, "row", swap), up
+    )
+    term_parts = lax.all_to_all(terms, "row", 0, 0, axis_index_groups=kinds)
+    (summed,) = call(sum_kernel, [(slots, BF)], [VMEM], [VMEM], term_parts)
+    pieces = lax.all_to_all(summed, "row", 0, 0, axis_index_groups=kinds)
     grad_down, grad_up_key, grad_up_value = call(
         place_kernel,
         [((64, feats), F32), ((64, HD), F32), ((64, HD), F32)],
-        [VMEM], [VMEM] * 3, pieces,
+        [SMEM] + [VMEM] * 2, [VMEM] * 3, pos, pieces, lax.ppermute(pieces, "row", swap),
     )
     return grad_down.T, grad_up_key, grad_up_value
 

time: 162 us -> 163 us (level)
  blocking collectives: 56.6 us -> 47.1 us
  starting transfers between devices: 72.7 us -> 81.6 us
  waiting for transfers between devices: 11.7 us -> 13.8 us
    all_to_all x3 -> x2, blocking collectives: 44 us -> 34.4 us  [the longest x1 20.6 us: on_device(): term_parts = lax.all_to_all(terms, 'row', 0, 0, axis_index_groups=kinds)]
    ppermute x0 -> x2, starting transfers between devices: none -> 8.91 us  [the longest x1 4.89 us: on_device(): lax.ppermute(pieces, 'row', swap)]
    ppermute x0 -> x2, waiting for transfers between devices: none -> 2.01 us  [the longest x1 1.05 us: on_device(): lax.ppermute(pieces, 'row', swap)]
  transfers between devices with their start and end apart: 19 -> 21, of which waited for: 6 -> 8; matrix products, arithmetic and copies ran while one was open for 1% -> 1% of each run, Pallas kernels for 3% -> 3%
where the time goes in v11:
time: 163 us; the launch traced here: 162 us
  starting transfers between devices  81.6 us (50%)
  blocking collectives  47.1 us (29%)
  Pallas kernels  14.9 us (9%)
  waiting for transfers between devices  13.8 us (8%)
  local copies, waits for them, and re-layouts  3.62 us (2%)
    ppermute x6, starting transfers between devices, ring_of(): fore_going.append(lax.ppermute(fore_going[-1], axis, fore))  30.3 us
    all_to_all x1, blocking collectives, on_device(): term_parts = lax.all_to_all(terms, 'row', 0, 0, axis_index_groups=kinds)  20.6 us
    pallas_call x9, Pallas kernels, call(): pl.pallas_call(kernel, out_shape=[jax.ShapeDtypeStruct(s, d) for s, d in...  14.9 us
    all_to_all x1, blocking collectives, on_device(): pieces = lax.all_to_all(summed, 'row', 0, 0, axis_index_groups=kinds)  13.8 us
    all_to_all x1, blocking collectives, on_device(): packs = lax.all_to_all(pack, 'col', 0, 0)  12.6 us
    ppermute x6, starting transfers between devices, ring_of(): aft_going.append(lax.ppermute(aft_going[-1], axis, aft))  11.5 us
    ppermute x2, starting transfers between devices, ring_of(): lax.ppermute(fore_going[3][:cut], axis, fore)  10.4 us
    ppermute x1, starting transfers between devices, on_device(): swapped = lax.ppermute(theirs, 'row', swap)  8.79 us
  transfers between devices with their start and end apart: 21, of which 8 were waited for; matrix products, arithmetic and copies ran while one was open for 1% of the time, Pallas kernels for 3%

profile of v11, /device:TPU:1, one launch (start us, length us, event | category | flops | bytes accessed | tf_op | source)
XLA Modules:
  0.0 162.4 jit_solution(7840609097603656860)
XLA Ops:
  0.7 0.1 pad_add_fusion.pos_ref
  0.7 1.0 copy-done
  1.8 0.7 shard_map.112
  2.5 8.8 %collective-permute-start = (bf16[128,1024]{1,0:T(8,128)(2,1)S(1)}, bf16[128,1024]{1,0:T(8,128)(2,1)S(1)}, u32[]{:S(2)}, u32[]{:S(2)}) collective-permute-start(bf16[128,1024]{1,0:T(8,128)(2,1)S(1)} %get-tuple-element.22), channel_id=1, source_target_pairs={{0,8},{8,0},{16,24},{24,16},{32,40},{40,32},{48,56},{56,48},{64,72... | collective-permute-start | bytes 786440 | tf_op jit(solution)/shard_map/ppermute | solution.py:333
  11.3 0.8 broadcast_in_dim.3
  12.2 3.6 %all-to-all-start = ((bf16[4,256,256]{2,1,0:T(8,128)(2,1)}), bf16[4,256,256]{2,1,0:T(8,128)(2,1)S(1)}, u32[]{:S(2)}, u32[]{:S(2)}) async-start(bf16[4,256,256]{2,1,0:T(8,128)(2,1)} %broadcast_in_dim.3), calls=%async_computation | async-start | bytes 1048576 | tf_op jit(solution)/shard_map/all_to_all | solution.py:341
  15.8 0.4 shard_map.113
  16.2 0.0 collective-permute-done
  16.2 1.9 %collective-permute-start.5 = (bf16[272,1024]{1,0:T(8,128)(2,1)S(1)}, bf16[272,1024]{1,0:T(8,128)(2,1)S(1)}, u32[]{:S(2)}, u32[]{:S(2)}) collective-permute-start(bf16[272,1024]{1,0:T(8,128)(2,1)S(1)} %pad_maximum_fusion.refs_0_), channel_id=1, source_target_pairs={{1,0},{2,1},{3,2},{4,3},{5,4},{6,5},{7,6},{0,7},{15,8},{8,9},{9,10... | collective-permute-start | bytes 1671176 | tf_op jit(solution)/shard_map/ppermute | solution.py:76
  18.2 5.8 %collective-permute-start.1 = (bf16[272,1024]{1,0:T(8,128)(2,1)S(1)}, bf16[272,1024]{1,0:T(8,128)(2,1)S(1)}, u32[]{:S(2)}, u32[]{:S(2)}) collective-permute-start(bf16[272,1024]{1,0:T(8,128)(2,1)S(1)} %pad_maximum_fusion.refs_0_), channel_id=1, source_target_pairs={{0,1},{1,2},{2,3},{3,4},{4,5},{5,6},{6,7},{7,0},{8,15},{9,8},{10,9... | collective-permute-start | bytes 1671176 | tf_op jit(solution)/shard_map/ppermute | solution.py:75
  24.0 1.4 all-to-all-done
  25.4 3.7 %collective-permute-start.9 = (bf16[1024,256]{1,0:T(8,128)(2,1)S(1)}, bf16[1024,256]{1,0:T(8,128)(2,1)S(1)}, u32[]{:S(2)}, u32[]{:S(2)}) collective-permute-start(bf16[1024,256]{1,0:T(8,128)(2,1)S(1)} %bitcast.6), channel_id=1, source_target_pairs={{0,64},{8,456},{16,80},{24,472},{32,96},{40,488},{48,112},{56,504}... | collective-permute-start | bytes 1572872 | tf_op jit(solution)/shard_map/ppermute | solution.py:75
  29.1 1.9 %collective-permute-start.13 = (bf16[1024,256]{1,0:T(8,128)(2,1)S(1)}, bf16[1024,256]{1,0:T(8,128)(2,1)S(1)}, u32[]{:S(2)}, u32[]{:S(2)}) collective-permute-start(bf16[1024,256]{1,0:T(8,128)(2,1)S(1)} %bitcast.7), channel_id=1, source_target_pairs={{64,0},{456,8},{80,16},{472,24},{96,32},{488,40},{112,48},{504,56}... | collective-permute-start | bytes 1572872 | tf_op jit(solution)/shard_map/ppermute | solution.py:76
  31.0 1.9 %collective-permute-start.6 = (bf16[272,1024]{1,0:T(8,128)(2,1)S(1)}, bf16[272,1024]{1,0:T(8,128)(2,1)S(1)}, u32[]{:S(2)}, u32[]{:S(2)}) collective-permute-start(bf16[272,1024]{1,0:T(8,128)(2,1)S(1)} %collective-permute-done.5.refs_4_), channel_id=1, source_target_pairs={{1,0},{2,1},{3,2},{4,3},{5,4},{6,5},{7,6},{0,7},{15,8},{8,9},{9,10... | collective-permute-start | bytes 1671176 | tf_op jit(solution)/shard_map/ppermute | solution.py:76
  33.0 2.3 %collective-permute-done.1.refs_1_ = bf16[272,1024]{1,0:T(8,128)(2,1)S(1)} collective-permute-done((bf16[272,1024]{1,0:T(8,128)(2,1)S(1)}, bf16[272,1024]{1,0:T(8,128)(2,1)S(1)}, u32[]{:S(2)}, u32[]{:S(2)}) %collective-permute-start.1) | collective-permute-done | bytes 557088 | tf_op jit(solution)/shard_map/ppermute | solution.py:75
  35.2 5.3 %collective-permute-start.2 = (bf16[272,1024]{1,0:T(8,128)(2,1)S(1)}, bf16[272,1024]{1,0:T(8,128)(2,1)S(1)}, u32[]{:S(2)}, u32[]{:S(2)}) collective-permute-start(bf16[272,1024]{1,0:T(8,128)(2,1)S(1)} %collective-permute-done.1.refs_1_), channel_id=1, source_target_pairs={{0,1},{1,2},{2,3},{3,4},{4,5},{5,6},{6,7},{7,0},{8,15},{9,8},{10,9... | collective-permute-start | bytes 1671176 | tf_op jit(solution)/shard_map/ppermute | solution.py:75
  40.6 0.0 copy-start.19
  40.6 5.1 %collective-permute-start.10 = (bf16[1024,256]{1,0:T(8,128)(2,1)S(1)}, bf16[1024,256]{1,0:T(8,128)(2,1)S(1)}, u32[]{:S(2)}, u32[]{:S(2)}) collective-permute-start(bf16[1024,256]{1,0:T(8,128)(2,1)S(1)} %collective-permute-done.9.refs_8_), channel_id=1, source_target_pairs={{0,64},{8,456},{16,80},{24,472},{32,96},{40,488},{48,112},{56,504}... | collective-permute-start | bytes 1572872 | tf_op jit(solution)/shard_map/ppermute | solution.py:75
  45.7 1.9 %collective-permute-start.14 = (bf16[1024,256]{1,0:T(8,128)(2,1)S(1)}, bf16[1024,256]{1,0:T(8,128)(2,1)S(1)}, u32[]{:S(2)}, u32[]{:S(2)}) collective-permute-start(bf16[1024,256]{1,0:T(8,128)(2,1)S(1)} %collective-permute-done.13.refs_11_), channel_id=1, source_target_pairs={{64,0},{456,8},{80,16},{472,24},{96,32},{488,40},{112,48},{504,56}... | collective-permute-start | bytes 1572872 | tf_op jit(solution)/shard_map/ppermute | solution.py:76
  47.6 1.9 %collective-permute-start.7 = (bf16[272,1024]{1,0:T(8,128)(2,1)S(1)}, bf16[272,1024]{1,0:T(8,128)(2,1)S(1)}, u32[]{:S(2)}, u32[]{:S(2)}) collective-permute-start(bf16[272,1024]{1,0:T(8,128)(2,1)S(1)} %collective-permute-done.6.refs_5_), channel_id=1, source_target_pairs={{1,0},{2,1},{3,2},{4,3},{5,4},{6,5},{7,6},{0,7},{15,8},{8,9},{9,10... | collective-permute-start | bytes 1671176 | tf_op jit(solution)/shard_map/ppermute | solution.py:76
  49.6 3.1 %collective-permute-done.2.refs_2_ = bf16[272,1024]{1,0:T(8,128)(2,1)S(1)} collective-permute-done((bf16[272,1024]{1,0:T(8,128)(2,1)S(1)}, bf16[272,1024]{1,0:T(8,128)(2,1)S(1)}, u32[]{:S(2)}, u32[]{:S(2)}) %collective-permute-start.2) | collective-permute-done | bytes 557088 | tf_op jit(solution)/shard_map/ppermute | solution.py:75
  52.6 5.3 %collective-permute-start.3 = (bf16[272,1024]{1,0:T(8,128)(2,1)S(1)}, bf16[272,1024]{1,0:T(8,128)(2,1)S(1)}, u32[]{:S(2)}, u32[]{:S(2)}) collective-permute-start(bf16[272,1024]{1,0:T(8,128)(2,1)S(1)} %collective-permute-done.2.refs_2_), channel_id=1, source_target_pairs={{0,1},{1,2},{2,3},{3,4},{4,5},{5,6},{6,7},{7,0},{8,15},{9,8},{10,9... | collective-permute-start | bytes 1671176 | tf_op jit(solution)/shard_map/ppermute | solution.py:75
  58.0 5.1 %collective-permute-start.11 = (bf16[1024,256]{1,0:T(8,128)(2,1)S(1)}, bf16[1024,256]{1,0:T(8,128)(2,1)S(1)}, u32[]{:S(2)}, u32[]{:S(2)}) collective-permute-start(bf16[1024,256]{1,0:T(8,128)(2,1)S(1)} %collective-permute-done.10.refs_9_), channel_id=1, source_target_pairs={{0,64},{8,456},{16,80},{24,472},{32,96},{40,488},{48,112},{56,504}... | collective-permute-start | bytes 1572872 | tf_op jit(solution)/shard_map/ppermute | solution.py:75
  63.1 1.9 %collective-permute-start.15 = (bf16[1024,256]{1,0:T(8,128)(2,1)S(1)}, bf16[1024,256]{1,0:T(8,128)(2,1)S(1)}, u32[]{:S(2)}, u32[]{:S(2)}) collective-permute-start(bf16[1024,256]{1,0:T(8,128)(2,1)S(1)} %collective-permute-done.14.refs_12_), channel_id=1, source_target_pairs={{64,0},{456,8},{80,16},{472,24},{96,32},{488,40},{112,48},{504,56}... | collective-permute-start | bytes 1572872 | tf_op jit(solution)/shard_map/ppermute | solution.py:76
  65.1 1.9 %collective-permute-start.8 = (bf16[144,1024]{1,0:T(8,128)(2,1)S(1)}, bf16[144,1024]{1,0:T(8,128)(2,1)S(1)}, u32[]{:S(2)}, u32[]{:S(2)}) collective-permute-start(bf16[144,1024]{1,0:T(8,128)(2,1)S(1)} %slice.17), channel_id=1, source_target_pairs={{1,0},{2,1},{3,2},{4,3},{5,4},{6,5},{7,6},{0,7},{15,8},{8,9},{9,10... | collective-permute-start | bytes 884744 | tf_op jit(solution)/shard_map/ppermute | solution.py:79
  67.0 2.8 %collective-permute-done.3.refs_3_ = bf16[272,1024]{1,0:T(8,128)(2,1)S(1)} collective-permute-done((bf16[272,1024]{1,0:T(8,128)(2,1)S(1)}, bf16[272,1024]{1,0:T(8,128)(2,1)S(1)}, u32[]{:S(2)}, u32[]{:S(2)}) %collective-permute-start.3) | collective-permute-done | bytes 557088 | tf_op jit(solution)/shard_map/ppermute | solution.py:75
  69.8 5.3 %collective-permute-start.4 = (bf16[128,1024]{1,0:T(8,128)(2,1)S(1)}, bf16[128,1024]{1,0:T(8,128)(2,1)S(1)}, u32[]{:S(2)}, u32[]{:S(2)}) collective-permute-start(bf16[128,1024]{1,0:T(8,128)(2,1)S(1)} %slice.16), channel_id=1, source_target_pairs={{0,1},{1,2},{2,3},{3,4},{4,5},{5,6},{6,7},{7,0},{8,15},{9,8},{10,9... | collective-permute-start | bytes 786440 | tf_op jit(solution)/shard_map/ppermute | solution.py:78
  75.2 5.1 %collective-permute-start.12 = (bf16[512,256]{1,0:T(8,128)(2,1)S(1)}, bf16[512,256]{1,0:T(8,128)(2,1)S(1)}, u32[]{:S(2)}, u32[]{:S(2)}) collective-permute-start(bf16[512,256]{1,0:T(8,128)(2,1)S(1)} %slice.18), channel_id=1, source_target_pairs={{0,64},{8,456},{16,80},{24,472},{32,96},{40,488},{48,112},{56,504}... | collective-permute-start | bytes 786440 | tf_op jit(solution)/shard_map/ppermute | solution.py:78
  80.4 1.9 %collective-permute-start.16 = (bf16[512,256]{1,0:T(8,128)(2,1)S(1)}, bf16[512,256]{1,0:T(8,128)(2,1)S(1)}, u32[]{:S(2)}, u32[]{:S(2)}) collective-permute-start(bf16[512,256]{1,0:T(8,128)(2,1)S(1)} %slice.19), channel_id=1, source_target_pairs={{64,0},{456,8},{80,16},{472,24},{96,32},{488,40},{112,48},{504,56}... | collective-permute-start | bytes 786440 | tf_op jit(solution)/shard_map/ppermute | solution.py:79
  82.4 5.0 %shard_map.114 = (f32[256,256]{1,0:T(8,128)S(1)}, f32[16,1024]{1,0:T(8,128)S(1)}, bf16[256,1024]{1,0:T(8,128)(2,1)S(1)}, bf16[1024,256]{1,0:T(8,128)(2,1)S(1)}) custom-call(s32[3]{0:T(128)S(1)} %pad_add_fusion.pos_ref, bf16[272,1024]{1,0:T(8,128)(2,1)} %copy-done.10, bf16[272,1024]{1,0:T(8,128)(2,1)} %copy-done.16, bf16[272,1024]{1,0:T(8,128)(2,1)} %copy-done.18, ...), custom_call_target="tpu_custom_call" | custom-call | flops 1073741824 | bytes 7569408 | tf_op jit(solution)/shard_map/pallas_call | solution.py:294
  87.4 0.0 copy-start.4
  87.5 0.8 copy-done.4
  88.2 0.8 copy-done.5
  89.0 1.2 collective-permute-done.16.w2_ref
  90.3 0.0 copy-start.9
  90.3 2.5 %shard_map.115 = (f32[128,256]{1,0:T(8,128)S(1)}, f32[128,256]{1,0:T(8,128)S(1)}, bf16[128,64]{1,0:T(8,128)(2,1)S(1)}) custom-call(s32[3]{0:T(128)S(1)} %pad_add_fusion.pos_ref, bf16[128,1024]{1,0:T(8,128)(2,1)S(1)} %collective-permute-done.4.t1_ref, bf16[144,1024]{1,0:T(8,128)(2,1)S(1)} %collective-permute-done.8.t2_ref, ...), custom_call_target="tpu_custom_call" | custom-call | tf_op jit(solution)/shard_map/pallas_call | solution.py:294
  92.8 4.2 %collective-permute-start.17 = (f32[128,256]{1,0:T(8,128)S(1)}, f32[128,256]{1,0:T(8,128)S(1)}, u32[]{:S(2)}, u32[]{:S(2)}) collective-permute-start(f32[128,256]{1,0:T(8,128)S(1)} %get-tuple-element.28), channel_id=1, source_target_pairs={{0,8},{8,0},{16,24},{24,16},{32,40},{40,32},{48,56},{56,48},{64,72... | collective-permute-start | bytes 393224 | tf_op jit(solution)/shard_map/ppermute | solution.py:380
  97.0 1.0 collective-permute-done.17.got_ref
  98.0 3.9 %shard_map.116 = (bf16[8,80,128]{2,1,0:T(8,128)(2,1)S(1)}, f32[128,128]{1,0:T(8,128)S(1)}, f32[128,128]{1,0:T(8,128)S(1)}) custom-call(s32[1,8]{1,0:T(1,128)S(1)} %copy-done.9, f32[128,256]{1,0:T(8,128)S(1)} %get-tuple-element.27.own_ref, f32[128,256]{1,0:T(8,128)S(1)} %collective-permute-done.17.got_ref, ...), custom_call_target="tpu_custom_call" | custom-call | tf_op jit(solution)/shard_map/pallas_call | solution.py:294
  101.9 12.6 %all_to_all.20.pack_ref = bf16[8,80,128]{2,1,0:T(8,128)(2,1)S(1)} all-to-all(bf16[8,80,128]{2,1,0:T(8,128)(2,1)S(1)} %get-tuple-element.30), channel_id=1, replica_groups=mesh['row'=64,'col'=8] {'col'}, dimensions={0} | all-to-all | bytes 327680 | tf_op jit(solution)/shard_map/all_to_all | solution.py:393
  114.5 1.0 shard_map.117
  115.5 4.0 %collective-permute-start.18 = (bf16[64,1024]{1,0:T(8,128)(2,1)S(1)}, bf16[64,1024]{1,0:T(8,128)(2,1)S(1)}, u32[]{:S(2)}, u32[]{:S(2)}) collective-permute-start(bf16[64,1024]{1,0:T(8,128)(2,1)S(1)} %get-tuple-element.34), channel_id=1, source_target_pairs={{0,8},{8,0},{16,24},{24,16},{32,40},{40,32},{48,56},{56,48},{64,72... | collective-permute-start | bytes 393224 | tf_op jit(solution)/shard_map/ppermute | solution.py:402
  119.5 1.0 collective-permute-done.18.got_ref
  120.5 20.6 %all_to_all.21.in_ref = bf16[32,24,128]{2,1,0:T(8,128)(2,1)S(1)} all-to-all(bf16[32,24,128]{2,1,0:T(8,128)(2,1)S(1)} %shard_map.118), channel_id=1, replica_groups={{0,16,32,48,64,80,96,112,128,144,160,176,192,208,224,240,256,272,288,30..., dimensions={0} | all-to-all | bytes 393216 | tf_op jit(solution)/shard_map/all_to_all | solution.py:404
  141.2 13.8 %all_to_all.22.mine_ref = bf16[32,24,128]{2,1,0:T(8,128)(2,1)S(1)} all-to-all(bf16[32,24,128]{2,1,0:T(8,128)(2,1)S(1)} %shard_map.119), channel_id=1, replica_groups={{0,16,32,48,64,80,96,112,128,144,160,176,192,208,224,240,256,272,288,30..., dimensions={0} | all-to-all | bytes 393216 | tf_op jit(solution)/shard_map/all_to_all | solution.py:406
  155.0 4.9 %collective-permute-start.19 = (bf16[32,24,128]{2,1,0:T(8,128)(2,1)S(1)}, bf16[32,24,128]{2,1,0:T(8,128)(2,1)S(1)}, u32[]{:S(2)}, u32[]{:S(2)}) collective-permute-start(bf16[32,24,128]{2,1,0:T(8,128)(2,1)S(1)} %all_to_all.22.mine_ref), channel_id=1, source_target_pairs={{0,8},{8,0},{16,24},{24,16},{32,40},{40,32},{48,56},{56,48},{64,72... | collective-permute-start | bytes 589832 | tf_op jit(solution)/shard_map/ppermute | solution.py:410
  159.9 1.0 collective-permute-done.19.theirs_ref
  161.0 1.4 shard_map.120
  (64 shorter events, 0.3 us)
Async XLA Ops:
  0.7 1.0 copy-start
  1.8 9.5 %copy-start.23 = (bf16[256,128]{1,0:T(8,128)(2,1)S(1)}, bf16[256,128]{1,0:T(8,128)(2,1)}, u32[]{:S(2)}) copy-start(bf16[256,128]{1,0:T(8,128)(2,1)} %param.13) | copy-start | bytes 196612
  1.8 9.5 %copy-start.24 = (bf16[256,128]{1,0:T(8,128)(2,1)S(1)}, bf16[256,128]{1,0:T(8,128)(2,1)}, u32[]{:S(2)}) copy-start(bf16[256,128]{1,0:T(8,128)(2,1)} %param.12) | copy-start | bytes 196612
  2.5 13.7 %collective-permute-start = (bf16[128,1024]{1,0:T(8,128)(2,1)S(1)}, bf16[128,1024]{1,0:T(8,128)(2,1)S(1)}, u32[]{:S(2)}, u32[]{:S(2)}) collective-permute-start(bf16[128,1024]{1,0:T(8,128)(2,1)S(1)} %get-tuple-element.22), channel_id=1, source_target_pairs={{0,8},{8,0},{16,24},{24,16},{32,40},{40,32},{48,56},{56,48},{64,72... | collective-permute-start | bytes 786440 | tf_op jit(solution)/shard_map/ppermute | solution.py:333
  12.2 3.6 %copy-start.1 = (bf16[128,2048]{1,0:T(8,128)(2,1)S(1)}, bf16[128,2048]{1,0:T(8,128)(2,1)}, u32[]{:S(2)}) copy-start(bf16[128,2048]{1,0:T(8,128)(2,1)} %t_ref.5) | copy-start | bytes 1572868
  12.2 3.6 %copy-start.6 = (bf16[2048,64]{0,1:T(8,128)(2,1)S(1)}, bf16[2048,64]{0,1:T(8,128)(2,1)}, u32[]{:S(2)}) copy-start(bf16[2048,64]{0,1:T(8,128)(2,1)} %param.14) | copy-start | bytes 786436
  12.2 13.2 %all-to-all-start = ((bf16[4,256,256]{2,1,0:T(8,128)(2,1)}), bf16[4,256,256]{2,1,0:T(8,128)(2,1)S(1)}, u32[]{:S(2)}, u32[]{:S(2)}) async-start(bf16[4,256,256]{2,1,0:T(8,128)(2,1)} %broadcast_in_dim.3), calls=%async_computation | async-start | bytes 1048576 | tf_op jit(solution)/shard_map/all_to_all | solution.py:341
  16.2 53.6 %copy-start.10 = (bf16[272,1024]{1,0:T(8,128)(2,1)}, bf16[272,1024]{1,0:T(8,128)(2,1)S(1)}, u32[]{:S(2)}) copy-start(bf16[272,1024]{1,0:T(8,128)(2,1)S(1)} %pad_maximum_fusion.refs_0_) | copy-start | bytes 1671172
  16.2 14.8 %collective-permute-start.5 = (bf16[272,1024]{1,0:T(8,128)(2,1)S(1)}, bf16[272,1024]{1,0:T(8,128)(2,1)S(1)}, u32[]{:S(2)}, u32[]{:S(2)}) collective-permute-start(bf16[272,1024]{1,0:T(8,128)(2,1)S(1)} %pad_maximum_fusion.refs_0_), channel_id=1, source_target_pairs={{1,0},{2,1},{3,2},{4,3},{5,4},{6,5},{7,6},{0,7},{15,8},{8,9},{9,10... | collective-permute-start | bytes 1671176 | tf_op jit(solution)/shard_map/ppermute | solution.py:76
  18.2 17.1 %collective-permute-start.1 = (bf16[272,1024]{1,0:T(8,128)(2,1)S(1)}, bf16[272,1024]{1,0:T(8,128)(2,1)S(1)}, u32[]{:S(2)}, u32[]{:S(2)}) collective-permute-start(bf16[272,1024]{1,0:T(8,128)(2,1)S(1)} %pad_maximum_fusion.refs_0_), channel_id=1, source_target_pairs={{0,1},{1,2},{2,3},{3,4},{4,5},{5,6},{6,7},{7,0},{8,15},{9,8},{10,9... | collective-permute-start | bytes 1671176 | tf_op jit(solution)/shard_map/ppermute | solution.py:75
  25.4 15.2 %collective-permute-start.9 = (bf16[1024,256]{1,0:T(8,128)(2,1)S(1)}, bf16[1024,256]{1,0:T(8,128)(2,1)S(1)}, u32[]{:S(2)}, u32[]{:S(2)}) collective-permute-start(bf16[1024,256]{1,0:T(8,128)(2,1)S(1)} %bitcast.6), channel_id=1, source_target_pairs={{0,64},{8,456},{16,80},{24,472},{32,96},{40,488},{48,112},{56,504}... | collective-permute-start | bytes 1572872 | tf_op jit(solution)/shard_map/ppermute | solution.py:75
  29.1 16.6 %collective-permute-start.13 = (bf16[1024,256]{1,0:T(8,128)(2,1)S(1)}, bf16[1024,256]{1,0:T(8,128)(2,1)S(1)}, u32[]{:S(2)}, u32[]{:S(2)}) collective-permute-start(bf16[1024,256]{1,0:T(8,128)(2,1)S(1)} %bitcast.7), channel_id=1, source_target_pairs={{64,0},{456,8},{80,16},{472,24},{96,32},{488,40},{112,48},{504,56}... | collective-permute-start | bytes 1572872 | tf_op jit(solution)/shard_map/ppermute | solution.py:76
  31.0 51.3 %copy-start.15 = (bf16[272,1024]{1,0:T(8,128)(2,1)}, bf16[272,1024]{1,0:T(8,128)(2,1)S(1)}, u32[]{:S(2)}) copy-start(bf16[272,1024]{1,0:T(8,128)(2,1)S(1)} %collective-permute-done.5.refs_4_) | copy-start | bytes 1671172
  31.0 16.6 %collective-permute-start.6 = (bf16[272,1024]{1,0:T(8,128)(2,1)S(1)}, bf16[272,1024]{1,0:T(8,128)(2,1)S(1)}, u32[]{:S(2)}, u32[]{:S(2)}) collective-permute-start(bf16[272,1024]{1,0:T(8,128)(2,1)S(1)} %collective-permute-done.5.refs_4_), channel_id=1, source_target_pairs={{1,0},{2,1},{3,2},{4,3},{5,4},{6,5},{7,6},{0,7},{15,8},{8,9},{9,10... | collective-permute-start | bytes 1671176 | tf_op jit(solution)/shard_map/ppermute | solution.py:76
  35.2 47.1 %copy-start.16 = (bf16[272,1024]{1,0:T(8,128)(2,1)}, bf16[272,1024]{1,0:T(8,128)(2,1)S(1)}, u32[]{:S(2)}) copy-start(bf16[272,1024]{1,0:T(8,128)(2,1)S(1)} %collective-permute-done.1.refs_1_) | copy-start | bytes 1671172
  35.2 17.4 %collective-permute-start.2 = (bf16[272,1024]{1,0:T(8,128)(2,1)S(1)}, bf16[272,1024]{1,0:T(8,128)(2,1)S(1)}, u32[]{:S(2)}, u32[]{:S(2)}) collective-permute-start(bf16[272,1024]{1,0:T(8,128)(2,1)S(1)} %collective-permute-done.1.refs_1_), channel_id=1, source_target_pairs={{0,1},{1,2},{2,3},{3,4},{4,5},{5,6},{6,7},{7,0},{8,15},{9,8},{10,9... | collective-permute-start | bytes 1671176 | tf_op jit(solution)/shard_map/ppermute | solution.py:75
  40.6 41.8 %copy-start.19 = (bf16[1024,256]{1,0:T(8,128)(2,1)}, bf16[1024,256]{1,0:T(8,128)(2,1)S(1)}, u32[]{:S(2)}) copy-start(bf16[1024,256]{1,0:T(8,128)(2,1)S(1)} %collective-permute-done.9.refs_8_) | copy-start | bytes 1572868
  40.6 17.4 %collective-permute-start.10 = (bf16[1024,256]{1,0:T(8,128)(2,1)S(1)}, bf16[1024,256]{1,0:T(8,128)(2,1)S(1)}, u32[]{:S(2)}, u32[]{:S(2)}) collective-permute-start(bf16[1024,256]{1,0:T(8,128)(2,1)S(1)} %collective-permute-done.9.refs_8_), channel_id=1, source_target_pairs={{0,64},{8,456},{16,80},{24,472},{32,96},{40,488},{48,112},{56,504}... | collective-permute-start | bytes 1572872 | tf_op jit(solution)/shard_map/ppermute | solution.py:75
  45.7 36.7 %copy-start.20 = (bf16[1024,256]{1,0:T(8,128)(2,1)}, bf16[1024,256]{1,0:T(8,128)(2,1)S(1)}, u32[]{:S(2)}) copy-start(bf16[1024,256]{1,0:T(8,128)(2,1)S(1)} %collective-permute-done.13.refs_11_) | copy-start | bytes 1572868
  45.7 17.4 %collective-permute-start.14 = (bf16[1024,256]{1,0:T(8,128)(2,1)S(1)}, bf16[1024,256]{1,0:T(8,128)(2,1)S(1)}, u32[]{:S(2)}, u32[]{:S(2)}) collective-permute-start(bf16[1024,256]{1,0:T(8,128)(2,1)S(1)} %collective-permute-done.13.refs_11_), channel_id=1, source_target_pairs={{64,0},{456,8},{80,16},{472,24},{96,32},{488,40},{112,48},{504,56}... | collective-permute-start | bytes 1572872 | tf_op jit(solution)/shard_map/ppermute | solution.py:76
  47.6 34.7 %copy-start.17 = (bf16[272,1024]{1,0:T(8,128)(2,1)}, bf16[272,1024]{1,0:T(8,128)(2,1)S(1)}, u32[]{:S(2)}) copy-start(bf16[272,1024]{1,0:T(8,128)(2,1)S(1)} %collective-permute-done.6.refs_5_) | copy-start | bytes 1671172
  47.6 17.4 %collective-permute-start.7 = (bf16[272,1024]{1,0:T(8,128)(2,1)S(1)}, bf16[272,1024]{1,0:T(8,128)(2,1)S(1)}, u32[]{:S(2)}, u32[]{:S(2)}) collective-permute-start(bf16[272,1024]{1,0:T(8,128)(2,1)S(1)} %collective-permute-done.6.refs_5_), channel_id=1, source_target_pairs={{1,0},{2,1},{3,2},{4,3},{5,4},{6,5},{7,6},{0,7},{15,8},{8,9},{9,10... | collective-permute-start | bytes 1671176 | tf_op jit(solution)/shard_map/ppermute | solution.py:76
  52.6 29.7 %copy-start.18 = (bf16[272,1024]{1,0:T(8,128)(2,1)}, bf16[272,1024]{1,0:T(8,128)(2,1)S(1)}, u32[]{:S(2)}) copy-start(bf16[272,1024]{1,0:T(8,128)(2,1)S(1)} %collective-permute-done.2.refs_2_) | copy-start | bytes 1671172
  52.6 17.2 %collective-permute-start.3 = (bf16[272,1024]{1,0:T(8,128)(2,1)S(1)}, bf16[272,1024]{1,0:T(8,128)(2,1)S(1)}, u32[]{:S(2)}, u32[]{:S(2)}) collective-permute-start(bf16[272,1024]{1,0:T(8,128)(2,1)S(1)} %collective-permute-done.2.refs_2_), channel_id=1, source_target_pairs={{0,1},{1,2},{2,3},{3,4},{4,5},{5,6},{6,7},{7,0},{8,15},{9,8},{10,9... | collective-permute-start | bytes 1671176 | tf_op jit(solution)/shard_map/ppermute | solution.py:75
  57.9 24.4 %copy-start.21 = (bf16[1024,256]{1,0:T(8,128)(2,1)}, bf16[1024,256]{1,0:T(8,128)(2,1)S(1)}, u32[]{:S(2)}) copy-start(bf16[1024,256]{1,0:T(8,128)(2,1)S(1)} %collective-permute-done.10.refs_9_) | copy-start | bytes 1572868
  58.0 17.2 %collective-permute-start.11 = (bf16[1024,256]{1,0:T(8,128)(2,1)S(1)}, bf16[1024,256]{1,0:T(8,128)(2,1)S(1)}, u32[]{:S(2)}, u32[]{:S(2)}) collective-permute-start(bf16[1024,256]{1,0:T(8,128)(2,1)S(1)} %collective-permute-done.10.refs_9_), channel_id=1, source_target_pairs={{0,64},{8,456},{16,80},{24,472},{32,96},{40,488},{48,112},{56,504}... | collective-permute-start | bytes 1572872 | tf_op jit(solution)/shard_map/ppermute | solution.py:75
  63.1 19.3 %copy-start.22 = (bf16[1024,256]{1,0:T(8,128)(2,1)}, bf16[1024,256]{1,0:T(8,128)(2,1)S(1)}, u32[]{:S(2)}) copy-start(bf16[1024,256]{1,0:T(8,128)(2,1)S(1)} %collective-permute-done.14.refs_12_) | copy-start | bytes 1572868
  63.1 17.2 %collective-permute-start.15 = (bf16[1024,256]{1,0:T(8,128)(2,1)S(1)}, bf16[1024,256]{1,0:T(8,128)(2,1)S(1)}, u32[]{:S(2)}, u32[]{:S(2)}) collective-permute-start(bf16[1024,256]{1,0:T(8,128)(2,1)S(1)} %collective-permute-done.14.refs_12_), channel_id=1, source_target_pairs={{64,0},{456,8},{80,16},{472,24},{96,32},{488,40},{112,48},{504,56}... | collective-permute-start | bytes 1572872 | tf_op jit(solution)/shard_map/ppermute | solution.py:76
  65.0 4.8 %copy-start.11 = (bf16[272,1024]{1,0:T(8,128)(2,1)}, bf16[272,1024]{1,0:T(8,128)(2,1)S(1)}, u32[]{:S(2)}) copy-start(bf16[272,1024]{1,0:T(8,128)(2,1)S(1)} %collective-permute-done.7.refs_6_) | copy-start | bytes 1671172
  65.1 24.0 %collective-permute-start.8 = (bf16[144,1024]{1,0:T(8,128)(2,1)S(1)}, bf16[144,1024]{1,0:T(8,128)(2,1)S(1)}, u32[]{:S(2)}, u32[]{:S(2)}) collective-permute-start(bf16[144,1024]{1,0:T(8,128)(2,1)S(1)} %slice.17), channel_id=1, source_target_pairs={{1,0},{2,1},{3,2},{4,3},{5,4},{6,5},{7,6},{0,7},{15,8},{8,9},{9,10... | collective-permute-start | bytes 884744 | tf_op jit(solution)/shard_map/ppermute | solution.py:79
  69.8 10.6 %copy-start.12 = (bf16[272,1024]{1,0:T(8,128)(2,1)}, bf16[272,1024]{1,0:T(8,128)(2,1)S(1)}, u32[]{:S(2)}) copy-start(bf16[272,1024]{1,0:T(8,128)(2,1)S(1)} %collective-permute-done.3.refs_3_) | copy-start | bytes 1671172
  69.8 19.2 %collective-permute-start.4 = (bf16[128,1024]{1,0:T(8,128)(2,1)S(1)}, bf16[128,1024]{1,0:T(8,128)(2,1)S(1)}, u32[]{:S(2)}, u32[]{:S(2)}) collective-permute-start(bf16[128,1024]{1,0:T(8,128)(2,1)S(1)} %slice.16), channel_id=1, source_target_pairs={{0,1},{1,2},{2,3},{3,4},{4,5},{5,6},{6,7},{7,0},{8,15},{9,8},{10,9... | collective-permute-start | bytes 786440 | tf_op jit(solution)/shard_map/ppermute | solution.py:78
  75.2 7.2 %copy-start.13 = (bf16[1024,256]{1,0:T(8,128)(2,1)}, bf16[1024,256]{1,0:T(8,128)(2,1)S(1)}, u32[]{:S(2)}) copy-start(bf16[1024,256]{1,0:T(8,128)(2,1)S(1)} %collective-permute-done.11.refs_10_) | copy-start | bytes 1572868
  75.2 13.8 %collective-permute-start.12 = (bf16[512,256]{1,0:T(8,128)(2,1)S(1)}, bf16[512,256]{1,0:T(8,128)(2,1)S(1)}, u32[]{:S(2)}, u32[]{:S(2)}) collective-permute-start(bf16[512,256]{1,0:T(8,128)(2,1)S(1)} %slice.18), channel_id=1, source_target_pairs={{0,64},{8,456},{16,80},{24,472},{32,96},{40,488},{48,112},{56,504}... | collective-permute-start | bytes 786440 | tf_op jit(solution)/shard_map/ppermute | solution.py:78
  80.3 2.1 %copy-start.14 = (bf16[1024,256]{1,0:T(8,128)(2,1)}, bf16[1024,256]{1,0:T(8,128)(2,1)S(1)}, u32[]{:S(2)}) copy-start(bf16[1024,256]{1,0:T(8,128)(2,1)S(1)} %collective-permute-done.15.refs_13_) | copy-start | bytes 1572868
  80.4 9.9 %collective-permute-start.16 = (bf16[512,256]{1,0:T(8,128)(2,1)S(1)}, bf16[512,256]{1,0:T(8,128)(2,1)S(1)}, u32[]{:S(2)}, u32[]{:S(2)}) collective-permute-start(bf16[512,256]{1,0:T(8,128)(2,1)S(1)} %slice.19), channel_id=1, source_target_pairs={{64,0},{456,8},{80,16},{472,24},{96,32},{488,40},{112,48},{504,56}... | collective-permute-start | bytes 786440 | tf_op jit(solution)/shard_map/ppermute | solution.py:79
  87.4 0.8 copy-start.4
  88.2 0.8 copy-start.5
  90.3 7.7 %copy-start.2 = (bf16[128,2048]{1,0:T(8,128)(2,1)S(1)}, bf16[128,2048]{1,0:T(8,128)(2,1)}, u32[]{:S(2)}) copy-start(bf16[128,2048]{1,0:T(8,128)(2,1)} %q_ref.1) | copy-start | bytes 1572868
  90.3 7.7 %copy-start.3 = (bf16[128,2048]{1,0:T(8,128)(2,1)S(1)}, bf16[128,2048]{1,0:T(8,128)(2,1)}, u32[]{:S(2)}) copy-start(bf16[128,2048]{1,0:T(8,128)(2,1)} %p_ref.1) | copy-start | bytes 1572868
  90.3 7.7 %copy-start.7 = (bf16[64,128]{1,0:T(8,128)(2,1)S(1)}, bf16[64,128]{1,0:T(8,128)(2,1)}, u32[]{:S(2)}) copy-start(bf16[64,128]{1,0:T(8,128)(2,1)} %upk_ref.1) | copy-start | bytes 49156
  90.3 7.7 %copy-start.8 = (bf16[64,128]{1,0:T(8,128)(2,1)S(1)}, bf16[64,128]{1,0:T(8,128)(2,1)}, u32[]{:S(2)}) copy-start(bf16[64,128]{1,0:T(8,128)(2,1)} %upv_ref.1) | copy-start | bytes 49156
  90.3 7.7 %copy-start.9 = (s32[1,8]{1,0:T(1,128)S(1)}, s32[1,8]{1,0:T(1,128)}, u32[]{:S(2)}) copy-start(s32[1,8]{1,0:T(1,128)} %lengths_ref.3) | copy-start | bytes 100
  92.8 5.2 %collective-permute-start.17 = (f32[128,256]{1,0:T(8,128)S(1)}, f32[128,256]{1,0:T(8,128)S(1)}, u32[]{:S(2)}, u32[]{:S(2)}) collective-permute-start(f32[128,256]{1,0:T(8,128)S(1)} %get-tuple-element.28), channel_id=1, source_target_pairs={{0,8},{8,0},{16,24},{24,16},{32,40},{40,32},{48,56},{56,48},{64,72... | collective-permute-start | bytes 393224 | tf_op jit(solution)/shard_map/ppermute | solution.py:380
  115.5 5.0 %collective-permute-start.18 = (bf16[64,1024]{1,0:T(8,128)(2,1)S(1)}, bf16[64,1024]{1,0:T(8,128)(2,1)S(1)}, u32[]{:S(2)}, u32[]{:S(2)}) collective-permute-start(bf16[64,1024]{1,0:T(8,128)(2,1)S(1)} %get-tuple-element.34), channel_id=1, source_target_pairs={{0,8},{8,0},{16,24},{24,16},{32,40},{40,32},{48,56},{56,48},{64,72... | collective-permute-start | bytes 393224 | tf_op jit(solution)/shard_map/ppermute | solution.py:402
  155.0 5.9 %collective-permute-start.19 = (bf16[32,24,128]{2,1,0:T(8,128)(2,1)S(1)}, bf16[32,24,128]{2,1,0:T(8,128)(2,1)S(1)}, u32[]{:S(2)}, u32[]{:S(2)}) collective-permute-start(bf16[32,24,128]{2,1,0:T(8,128)(2,1)S(1)} %all_to_all.22.mine_ref), channel_id=1, source_target_pairs={{0,8},{8,0},{16,24},{24,16},{32,40},{40,32},{48,56},{56,48},{64,72... | collective-permute-start | bytes 589832 | tf_op jit(solution)/shard_map/ppermute | solution.py:410

commit v12 on v9

--- a/solution.py
+++ b/solution.py
@@ -86,29 +86,34 @@
 
 def project_kernel(pos_ref, *refs):
     t_refs, w_refs, refs = refs[:7], refs[7:14], refs[14:]
-    total_ref, low_ref, t_left_ref, w_left_ref, t_scr, w_scr, sem = refs
-    n = t_scr.shape[0]
-    copies = []
-    for axis, (parts, scr) in enumerate(((t_refs, t_scr), (w_refs, w_scr))):
-        for j, part in enumerate(parts):
-            k = block_at(pos_ref, axis, STEPS[j], n)
-            copies.append(pltpu.make_async_copy(part, scr.at[k], sem.at[axis, j]))
+    total_ref, low_ref, t_left_ref, w_left_ref, w_scr, sem = refs
+    n = w_scr.shape[0]
+    copies = [
+        pltpu.make_async_copy(part, w_scr.at[block_at(pos_ref, 1, STEPS[j], n)], sem.at[j])
+        for j, part in enumerate(w_refs)
+    ]
     for c in copies:
         c.start()
     t_far, w_far = (block_at(pos_ref, axis, STEPS[7], n) for axis in range(2))
-    t_scr[t_far] = jnp.zeros(t_scr.shape[1:], BF)
     w_scr[w_far] = jnp.zeros(w_scr.shape[1:], BF)
+    t_left_ref[...] = jnp.zeros(t_left_ref.shape, BF)
+    rows = total_ref.shape[0]
+    low = jnp.zeros(low_ref.shape, F32)
+    for t_ref in t_refs:
+        low = low + t_ref[pl.ds(rows, low.shape[0])].astype(F32)
+    low_ref[...] = low
     for c in copies:
         c.wait()
-    rows = total_ref.shape[0]
     total = jnp.zeros(total_ref.shape, F32)
-    low = jnp.zeros(low_ref.shape, F32)
-    for k in range(n):
-        total = total + mm(t_scr[k, pl.ds(0, rows)], w_scr[k], NN)
-        low = low + t_scr[k, pl.ds(rows, low.shape[0])].astype(F32)
+    for j, t_ref in enumerate(t_refs):
+        k = block_at(pos_ref, 0, STEPS[j], n)
+        total = total + mm(t_ref[pl.ds(0, rows)], w_scr[k], NN)
+
+        @pl.when(k == w_far)
+        def _():
+            t_left_ref[...] = t_ref[pl.ds(0, rows)]
+
     total_ref[...] = total
-    low_ref[...] = low
-    t_left_ref[...] = t_scr[w_far, pl.ds(0, rows)]
     w_left_ref[...] = w_scr[t_far]
 
 
@@ -173,22 +178,26 @@
     s_at = lax.broadcasted_iota(jnp.int32, (rows, rows), 0)
     t_at = lax.broadcasted_iota(jnp.int32, (rows, rows), 1)
     allowed = (doc_s == doc_t) & (t_at >= s_at)
+    banned = jnp.where(allowed, 0.0, -1e30)
+    banned = jnp.concatenate([banned, banned], axis=1)
 
     def raised(scores):
-        scores = jnp.where(allowed, scores, -1e30)
+        scores = jnp.where(banned < 0.0, -1e30, scores)
         peak = jnp.max(scores, axis=0, keepdims=True)
         e = jnp.exp2((scores - peak) * (score_scale * LOG2E))
         return e, 1.0 / jnp.sum(e, axis=0, keepdims=True)
 
     gk = jnp.zeros((rows, HD), F32)
     gv = jnp.zeros((rows, HD), F32)
-    gap = jnp.zeros((1, rows), F32)
-    for h in range(heads):
+    gap = jnp.zeros((1, 2 * rows), F32)
+    for h in range(0, heads, 2):
         if h % batch == 0:
             for c in copies[2 * h // batch:2 * h // batch + 2]:
                 c.wait()
-        q = q_scr[:, pl.ds(h * HD, HD)]
-        probe = p_scr[:, pl.ds(h * HD, HD)]
+        q, probe = (
+            jnp.concatenate([scr[:, pl.ds((h + i) * HD, HD)] for i in range(2)], axis=0)
+            for scr in (q_scr, p_scr)
+        )
         scores = mm(keys, q, NT)
         grads = mm(values, probe, NT)
         pol, share = raised(scores[:rows])
@@ -201,6 +210,7 @@
         grad_scores = (pol * (grad_pol - mean_pol)).astype(BF)
         gk = gk + mm(grad_scores, q, NN)
         gv = gv + mm(pol.astype(BF), probe, NN)
+    gap = gap[:, :rows] + gap[:, rows:]
     gk = gk * (score_scale * probe_scale)
     gv = gv * probe_scale
     gap = gap * probe_scale
@@ -319,15 +329,14 @@
     total, low_sum, t_left, w_left = call(
         project_kernel,
         [((2 * rows, wide), F32), ((16, deep), F32), ((2 * rows, deep), BF), (w_own.shape, BF)],
-        [SMEM] + [HBM] * 14,
+        [SMEM] + [VMEM] * 7 + [HBM] * 7,
         [VMEM] * 4,
         pos, *t_parts[:7], *w_parts[:7],
         scratch=[
-            pltpu.VMEM((8,) + pair.shape, BF),
             pltpu.VMEM((8,) + w_own.shape, BF),
-            pltpu.SemaphoreType.DMA((2, 7)),
+            pltpu.SemaphoreType.DMA((7,)),
         ],
-        mib=52,
+        mib=40,
         cost=(2 * 16 * rows * deep * wide, 14 * (pair.size + w_own.size)),
     )
     own, other, low_half = call(
@@ -345,7 +354,7 @@
             pltpu.VMEM(w_left.shape, BF),
             pltpu.SemaphoreType.DMA((8,)),
         ],
-        mib=52,
+        mib=16,
     )
     got = lax.ppermute(other, "row", swap)
     pack, gk, gv = call(

time: 162 us -> 158 us (0.975)
  Pallas kernels: 15.5 us -> 11.5 us
  waiting for transfers between devices: 11.7 us -> 15.6 us
  starting transfers between devices: 72.7 us -> 70.4 us
  local copies, waits for them, and re-layouts: 3.63 us -> 1.98 us
    pallas_call x9, Pallas kernels: 15.5 us -> 11.5 us  [call(): pl.pallas_call(kernel, out_shape=[jax.ShapeDtypeStruct(s, d) for s, d in...]
    ppermute x2, waiting for transfers between devices: 1.22 us -> 4.61 us  [ring_of(): lax.ppermute(aft_going[3][cut:], axis, aft)]
    ppermute x1, starting transfers between devices: 4.23 us -> 1.92 us  [on_device(): got = lax.ppermute(other, 'row', swap)]
    unnamed x50 -> x20, local copies, waits for them, and re-layouts: 2.73 us -> 1.08 us
  transfers between devices with their start and end apart: 19 -> 19, of which waited for: 6 -> 6; matrix products, arithmetic and copies ran while one was open for 1% -> 1% of each run, Pallas kernels for 3% -> 2%
where the time goes in v12:
time: 158 us; the launch traced here: 157 us
  starting transfers between devices  70.4 us (45%)
  blocking collectives  56.6 us (36%)
  waiting for transfers between devices  15.6 us (10%)
  Pallas kernels  11.5 us (7%)
  local copies, waits for them, and re-layouts  1.98 us (1%)
    ppermute x6, starting transfers between devices, ring_of(): fore_going.append(lax.ppermute(fore_going[-1], axis, fore))  30.3 us
    all_to_all x1, blocking collectives, on_device(): lax.all_to_all(square, 'row', 0, 0, axis_index_groups=y_lines)  18.4 us
    all_to_all x1, blocking collectives, on_device(): term_parts = lax.all_to_all(terms, 'row', 0, 0, axis_index_groups=squares)  13.9 us
    all_to_all x1, blocking collectives, on_device(): packs = lax.all_to_all(pack, 'col', 0, 0)  12.2 us
    all_to_all x1, blocking collectives, on_device(): pieces = lax.all_to_all(summed, 'row', 0, 0, axis_index_groups=squares)  12.2 us
    ppermute x6, starting transfers between devices, ring_of(): aft_going.append(lax.ppermute(aft_going[-1], axis, aft))  11.5 us
    pallas_call x9, Pallas kernels, call(): pl.pallas_call(kernel, out_shape=[jax.ShapeDtypeStruct(s, d) for s, d in...  11.5 us
    ppermute x2, starting transfers between devices, ring_of(): lax.ppermute(fore_going[3][:cut], axis, fore)  10.4 us
  transfers between devices with their start and end apart: 19, of which 6 were waited for; matrix products, arithmetic and copies ran while one was open for 1% of the time, Pallas kernels for 2%

profile of v12, /device:TPU:1, one launch (start us, length us, event | category | flops | bytes accessed | tf_op | source)
XLA Modules:
  0.0 157.2 jit_solution(16562033230968416492)
XLA Ops:
  0.7 0.1 pad_add_fusion.pos_ref
  0.7 1.0 copy-done
  1.8 0.7 shard_map.112
  2.5 8.8 %collective-permute-start = (bf16[128,1024]{1,0:T(8,128)(2,1)S(1)}, bf16[128,1024]{1,0:T(8,128)(2,1)S(1)}, u32[]{:S(2)}, u32[]{:S(2)}) collective-permute-start(bf16[128,1024]{1,0:T(8,128)(2,1)S(1)} %get-tuple-element.19), channel_id=1, source_target_pairs={{0,8},{8,0},{16,24},{24,16},{32,40},{40,32},{48,56},{56,48},{64,72... | collective-permute-start | bytes 786440 | tf_op jit(solution)/shard_map/ppermute | solution.py:313
  11.3 0.8 broadcast_in_dim.3
  12.2 3.6 %all-to-all-start = ((bf16[4,256,256]{2,1,0:T(8,128)(2,1)}), bf16[4,256,256]{2,1,0:T(8,128)(2,1)S(1)}, u32[]{:S(2)}, u32[]{:S(2)}) async-start(bf16[4,256,256]{2,1,0:T(8,128)(2,1)} %broadcast_in_dim.3), calls=%async_computation | async-start | bytes 1048576 | tf_op jit(solution)/shard_map/all_to_all | solution.py:321
  15.8 0.4 shard_map.113
  16.2 0.0 collective-permute-done
  16.2 1.9 %collective-permute-start.5 = (bf16[272,1024]{1,0:T(8,128)(2,1)S(1)}, bf16[272,1024]{1,0:T(8,128)(2,1)S(1)}, u32[]{:S(2)}, u32[]{:S(2)}) collective-permute-start(bf16[272,1024]{1,0:T(8,128)(2,1)S(1)} %pad_maximum_fusion.refs_0_), channel_id=1, source_target_pairs={{1,0},{2,1},{3,2},{4,3},{5,4},{6,5},{7,6},{0,7},{15,8},{8,9},{9,10... | collective-permute-start | bytes 1671176 | tf_op jit(solution)/shard_map/ppermute | solution.py:76
  18.1 5.8 %collective-permute-start.1 = (bf16[272,1024]{1,0:T(8,128)(2,1)S(1)}, bf16[272,1024]{1,0:T(8,128)(2,1)S(1)}, u32[]{:S(2)}, u32[]{:S(2)}) collective-permute-start(bf16[272,1024]{1,0:T(8,128)(2,1)S(1)} %pad_maximum_fusion.refs_0_), channel_id=1, source_target_pairs={{0,1},{1,2},{2,3},{3,4},{4,5},{5,6},{6,7},{7,0},{8,15},{9,8},{10,9... | collective-permute-start | bytes 1671176 | tf_op jit(solution)/shard_map/ppermute | solution.py:75
  24.0 1.4 all-to-all-done
  25.4 3.7 %collective-permute-start.9 = (bf16[1024,256]{1,0:T(8,128)(2,1)S(1)}, bf16[1024,256]{1,0:T(8,128)(2,1)S(1)}, u32[]{:S(2)}, u32[]{:S(2)}) collective-permute-start(bf16[1024,256]{1,0:T(8,128)(2,1)S(1)} %bitcast.6), channel_id=1, source_target_pairs={{0,64},{8,456},{16,80},{24,472},{32,96},{40,488},{48,112},{56,504}... | collective-permute-start | bytes 1572872 | tf_op jit(solution)/shard_map/ppermute | solution.py:75
  29.1 1.9 %collective-permute-start.13 = (bf16[1024,256]{1,0:T(8,128)(2,1)S(1)}, bf16[1024,256]{1,0:T(8,128)(2,1)S(1)}, u32[]{:S(2)}, u32[]{:S(2)}) collective-permute-start(bf16[1024,256]{1,0:T(8,128)(2,1)S(1)} %bitcast.7), channel_id=1, source_target_pairs={{64,0},{456,8},{80,16},{472,24},{96,32},{488,40},{112,48},{504,56}... | collective-permute-start | bytes 1572872 | tf_op jit(solution)/shard_map/ppermute | solution.py:76
  31.0 1.9 %collective-permute-start.6 = (bf16[272,1024]{1,0:T(8,128)(2,1)S(1)}, bf16[272,1024]{1,0:T(8,128)(2,1)S(1)}, u32[]{:S(2)}, u32[]{:S(2)}) collective-permute-start(bf16[272,1024]{1,0:T(8,128)(2,1)S(1)} %collective-permute-done.5.refs_4_), channel_id=1, source_target_pairs={{1,0},{2,1},{3,2},{4,3},{5,4},{6,5},{7,6},{0,7},{15,8},{8,9},{9,10... | collective-permute-start | bytes 1671176 | tf_op jit(solution)/shard_map/ppermute | solution.py:76
  33.0 2.3 %collective-permute-done.1.refs_1_ = bf16[272,1024]{1,0:T(8,128)(2,1)S(1)} collective-permute-done((bf16[272,1024]{1,0:T(8,128)(2,1)S(1)}, bf16[272,1024]{1,0:T(8,128)(2,1)S(1)}, u32[]{:S(2)}, u32[]{:S(2)}) %collective-permute-start.1) | collective-permute-done | bytes 557088 | tf_op jit(solution)/shard_map/ppermute | solution.py:75
  35.2 5.3 %collective-permute-start.2 = (bf16[272,1024]{1,0:T(8,128)(2,1)S(1)}, bf16[272,1024]{1,0:T(8,128)(2,1)S(1)}, u32[]{:S(2)}, u32[]{:S(2)}) collective-permute-start(bf16[272,1024]{1,0:T(8,128)(2,1)S(1)} %collective-permute-done.1.refs_1_), channel_id=1, source_target_pairs={{0,1},{1,2},{2,3},{3,4},{4,5},{5,6},{6,7},{7,0},{8,15},{9,8},{10,9... | collective-permute-start | bytes 1671176 | tf_op jit(solution)/shard_map/ppermute | solution.py:75
  40.5 0.0 collective-permute-done.9.refs_8_
  40.5 5.1 %collective-permute-start.10 = (bf16[1024,256]{1,0:T(8,128)(2,1)S(1)}, bf16[1024,256]{1,0:T(8,128)(2,1)S(1)}, u32[]{:S(2)}, u32[]{:S(2)}) collective-permute-start(bf16[1024,256]{1,0:T(8,128)(2,1)S(1)} %collective-permute-done.9.refs_8_), channel_id=1, source_target_pairs={{0,64},{8,456},{16,80},{24,472},{32,96},{40,488},{48,112},{56,504}... | collective-permute-start | bytes 1572872 | tf_op jit(solution)/shard_map/ppermute | solution.py:75
  45.7 1.9 %collective-permute-start.14 = (bf16[1024,256]{1,0:T(8,128)(2,1)S(1)}, bf16[1024,256]{1,0:T(8,128)(2,1)S(1)}, u32[]{:S(2)}, u32[]{:S(2)}) collective-permute-start(bf16[1024,256]{1,0:T(8,128)(2,1)S(1)} %collective-permute-done.13.refs_11_), channel_id=1, source_target_pairs={{64,0},{456,8},{80,16},{472,24},{96,32},{488,40},{112,48},{504,56}... | collective-permute-start | bytes 1572872 | tf_op jit(solution)/shard_map/ppermute | solution.py:76
  47.6 0.0 collective-permute-done.6.refs_5_
  47.6 1.9 %collective-permute-start.7 = (bf16[272,1024]{1,0:T(8,128)(2,1)S(1)}, bf16[272,1024]{1,0:T(8,128)(2,1)S(1)}, u32[]{:S(2)}, u32[]{:S(2)}) collective-permute-start(bf16[272,1024]{1,0:T(8,128)(2,1)S(1)} %collective-permute-done.6.refs_5_), channel_id=1, source_target_pairs={{1,0},{2,1},{3,2},{4,3},{5,4},{6,5},{7,6},{0,7},{15,8},{8,9},{9,10... | collective-permute-start | bytes 1671176 | tf_op jit(solution)/shard_map/ppermute | solution.py:76
  49.5 3.1 %collective-permute-done.2.refs_2_ = bf16[272,1024]{1,0:T(8,128)(2,1)S(1)} collective-permute-done((bf16[272,1024]{1,0:T(8,128)(2,1)S(1)}, bf16[272,1024]{1,0:T(8,128)(2,1)S(1)}, u32[]{:S(2)}, u32[]{:S(2)}) %collective-permute-start.2) | collective-permute-done | bytes 557088 | tf_op jit(solution)/shard_map/ppermute | solution.py:75
  52.6 5.3 %collective-permute-start.3 = (bf16[272,1024]{1,0:T(8,128)(2,1)S(1)}, bf16[272,1024]{1,0:T(8,128)(2,1)S(1)}, u32[]{:S(2)}, u32[]{:S(2)}) collective-permute-start(bf16[272,1024]{1,0:T(8,128)(2,1)S(1)} %collective-permute-done.2.refs_2_), channel_id=1, source_target_pairs={{0,1},{1,2},{2,3},{3,4},{4,5},{5,6},{6,7},{7,0},{8,15},{9,8},{10,9... | collective-permute-start | bytes 1671176 | tf_op jit(solution)/shard_map/ppermute | solution.py:75
  57.9 5.1 %collective-permute-start.11 = (bf16[1024,256]{1,0:T(8,128)(2,1)S(1)}, bf16[1024,256]{1,0:T(8,128)(2,1)S(1)}, u32[]{:S(2)}, u32[]{:S(2)}) collective-permute-start(bf16[1024,256]{1,0:T(8,128)(2,1)S(1)} %collective-permute-done.10.refs_9_), channel_id=1, source_target_pairs={{0,64},{8,456},{16,80},{24,472},{32,96},{40,488},{48,112},{56,504}... | collective-permute-start | bytes 1572872 | tf_op jit(solution)/shard_map/ppermute | solution.py:75
  63.0 0.0 collective-permute-done.14.refs_12_
  63.1 1.9 %collective-permute-start.15 = (bf16[1024,256]{1,0:T(8,128)(2,1)S(1)}, bf16[1024,256]{1,0:T(8,128)(2,1)S(1)}, u32[]{:S(2)}, u32[]{:S(2)}) collective-permute-start(bf16[1024,256]{1,0:T(8,128)(2,1)S(1)} %collective-permute-done.14.refs_12_), channel_id=1, source_target_pairs={{64,0},{456,8},{80,16},{472,24},{96,32},{488,40},{112,48},{504,56}... | collective-permute-start | bytes 1572872 | tf_op jit(solution)/shard_map/ppermute | solution.py:76
  65.0 1.9 %collective-permute-start.8 = (bf16[144,1024]{1,0:T(8,128)(2,1)S(1)}, bf16[144,1024]{1,0:T(8,128)(2,1)S(1)}, u32[]{:S(2)}, u32[]{:S(2)}) collective-permute-start(bf16[144,1024]{1,0:T(8,128)(2,1)S(1)} %slice.17), channel_id=1, source_target_pairs={{1,0},{2,1},{3,2},{4,3},{5,4},{6,5},{7,6},{0,7},{15,8},{8,9},{9,10... | collective-permute-start | bytes 884744 | tf_op jit(solution)/shard_map/ppermute | solution.py:79
  66.9 2.8 %collective-permute-done.3.refs_3_ = bf16[272,1024]{1,0:T(8,128)(2,1)S(1)} collective-permute-done((bf16[272,1024]{1,0:T(8,128)(2,1)S(1)}, bf16[272,1024]{1,0:T(8,128)(2,1)S(1)}, u32[]{:S(2)}, u32[]{:S(2)}) %collective-permute-start.3) | collective-permute-done | bytes 557088 | tf_op jit(solution)/shard_map/ppermute | solution.py:75
  69.8 5.3 %collective-permute-start.4 = (bf16[128,1024]{1,0:T(8,128)(2,1)S(1)}, bf16[128,1024]{1,0:T(8,128)(2,1)S(1)}, u32[]{:S(2)}, u32[]{:S(2)}) collective-permute-start(bf16[128,1024]{1,0:T(8,128)(2,1)S(1)} %slice.16), channel_id=1, source_target_pairs={{0,1},{1,2},{2,3},{3,4},{4,5},{5,6},{6,7},{7,0},{8,15},{9,8},{10,9... | collective-permute-start | bytes 786440 | tf_op jit(solution)/shard_map/ppermute | solution.py:78
  75.1 0.0 collective-permute-done.11.refs_10_
  75.2 5.1 %collective-permute-start.12 = (bf16[512,256]{1,0:T(8,128)(2,1)S(1)}, bf16[512,256]{1,0:T(8,128)(2,1)S(1)}, u32[]{:S(2)}, u32[]{:S(2)}) collective-permute-start(bf16[512,256]{1,0:T(8,128)(2,1)S(1)} %slice.18), channel_id=1, source_target_pairs={{0,64},{8,456},{16,80},{24,472},{32,96},{40,488},{48,112},{56,504}... | collective-permute-start | bytes 786440 | tf_op jit(solution)/shard_map/ppermute | solution.py:78
  80.3 0.0 collective-permute-done.15.refs_13_
  80.3 1.9 %collective-permute-start.16 = (bf16[512,256]{1,0:T(8,128)(2,1)S(1)}, bf16[512,256]{1,0:T(8,128)(2,1)S(1)}, u32[]{:S(2)}, u32[]{:S(2)}) collective-permute-start(bf16[512,256]{1,0:T(8,128)(2,1)S(1)} %slice.19), channel_id=1, source_target_pairs={{64,0},{456,8},{80,16},{472,24},{96,32},{488,40},{112,48},{504,56}... | collective-permute-start | bytes 786440 | tf_op jit(solution)/shard_map/ppermute | solution.py:79
  82.2 3.3 %shard_map.114 = (f32[256,256]{1,0:T(8,128)S(1)}, f32[16,1024]{1,0:T(8,128)S(1)}, bf16[256,1024]{1,0:T(8,128)(2,1)S(1)}, bf16[1024,256]{1,0:T(8,128)(2,1)S(1)}) custom-call(s32[3]{0:T(128)S(1)} %pad_add_fusion.pos_ref, bf16[272,1024]{1,0:T(8,128)(2,1)S(1)} %pad_maximum_fusion.refs_0_, bf16[272,1024]{1,0:T(8,128)(2,1)S(1)} %collective-permute-done.1.refs_1_, ...), custom_call_target="tpu_custom_call" | custom-call | flops 1073741824 | bytes 7569408 | tf_op jit(solution)/shard_map/pallas_call | solution.py:273
  85.6 0.0 collective-permute-done.8.t2_ref
  85.6 0.0 collective-permute-done.12.w1_ref
  85.6 4.6 %collective-permute-done.16.w2_ref = bf16[512,256]{1,0:T(8,128)(2,1)S(1)} collective-permute-done((bf16[512,256]{1,0:T(8,128)(2,1)S(1)}, bf16[512,256]{1,0:T(8,128)(2,1)S(1)}, u32[]{:S(2)}, u32[]{:S(2)}) %collective-permute-start.16) | collective-permute-done | bytes 262176 | tf_op jit(solution)/shard_map/ppermute | solution.py:79
  90.2 0.0 copy-start.7
  90.2 1.4 shard_map.115
  91.6 1.9 %collective-permute-start.17 = (f32[128,256]{1,0:T(8,128)S(1)}, f32[128,256]{1,0:T(8,128)S(1)}, u32[]{:S(2)}, u32[]{:S(2)}) collective-permute-start(f32[128,256]{1,0:T(8,128)S(1)} %get-tuple-element.25), channel_id=1, source_target_pairs={{0,8},{8,0},{16,24},{24,16},{32,40},{40,32},{48,56},{56,48},{64,72... | collective-permute-start | bytes 393224 | tf_op jit(solution)/shard_map/ppermute | solution.py:359
  93.5 1.3 collective-permute-done.17.got_ref
  94.9 3.9 %shard_map.116 = (bf16[8,80,128]{2,1,0:T(8,128)(2,1)S(1)}, f32[128,128]{1,0:T(8,128)S(1)}, f32[128,128]{1,0:T(8,128)S(1)}) custom-call(s32[1,8]{1,0:T(1,128)S(1)} %copy-done.7, f32[128,256]{1,0:T(8,128)S(1)} %get-tuple-element.24.own_ref, f32[128,256]{1,0:T(8,128)S(1)} %collective-permute-done.17.got_ref, ...), custom_call_target="tpu_custom_call" | custom-call | tf_op jit(solution)/shard_map/pallas_call | solution.py:273
  98.8 12.2 %all_to_all.25.pack_ref = bf16[8,80,128]{2,1,0:T(8,128)(2,1)S(1)} all-to-all(bf16[8,80,128]{2,1,0:T(8,128)(2,1)S(1)} %get-tuple-element.27), channel_id=1, replica_groups=mesh['row'=64,'col'=8] {'col'}, dimensions={0} | all-to-all | bytes 327680 | tf_op jit(solution)/shard_map/all_to_all | solution.py:372
  110.9 0.9 shard_map.117
  111.9 13.9 %all_to_all.26.in_ref = bf16[8,72,256]{2,1,0:T(8,128)(2,1)S(1)} all-to-all(bf16[8,72,256]{2,1,0:T(8,128)(2,1)S(1)} %shard_map.117), channel_id=1, replica_groups={{0,8,16,24,32,40,48,56},{64,72,80,88,96,104,112,120},{128,136,144,152,1..., dimensions={0} | all-to-all | bytes 589824 | tf_op jit(solution)/shard_map/all_to_all | solution.py:378
  125.8 18.4 %all_to_all.27.in_ref = bf16[8,72,256]{2,1,0:T(8,128)(2,1)S(1)} all-to-all(bf16[8,72,256]{2,1,0:T(8,128)(2,1)S(1)} %shard_map.118), channel_id=1, replica_groups={{0,64,128,192,256,320,384,448},{8,72,136,200,264,328,392,456},{16,80,14..., dimensions={0} | all-to-all | bytes 589824 | tf_op jit(solution)/shard_map/all_to_all | solution.py:380
  144.3 12.2 %all_to_all.28.in_ref = bf16[8,72,256]{2,1,0:T(8,128)(2,1)S(1)} all-to-all(bf16[8,72,256]{2,1,0:T(8,128)(2,1)S(1)} %shard_map.119), channel_id=1, replica_groups={{0,8,16,24,32,40,48,56},{64,72,80,88,96,104,112,120},{128,136,144,152,1..., dimensions={0} | all-to-all | bytes 589824 | tf_op jit(solution)/shard_map/all_to_all | solution.py:382
  156.4 0.8 shard_map.120
  (31 shorter events, 0.3 us)
Async XLA Ops:
  0.7 1.0 copy-start
  1.8 9.5 %copy-start.8 = (bf16[256,128]{1,0:T(8,128)(2,1)S(1)}, bf16[256,128]{1,0:T(8,128)(2,1)}, u32[]{:S(2)}) copy-start(bf16[256,128]{1,0:T(8,128)(2,1)} %param.13) | copy-start | bytes 196612
  1.8 9.5 %copy-start.9 = (bf16[256,128]{1,0:T(8,128)(2,1)S(1)}, bf16[256,128]{1,0:T(8,128)(2,1)}, u32[]{:S(2)}) copy-start(bf16[256,128]{1,0:T(8,128)(2,1)} %param.12) | copy-start | bytes 196612
  2.5 13.7 %collective-permute-start = (bf16[128,1024]{1,0:T(8,128)(2,1)S(1)}, bf16[128,1024]{1,0:T(8,128)(2,1)S(1)}, u32[]{:S(2)}, u32[]{:S(2)}) collective-permute-start(bf16[128,1024]{1,0:T(8,128)(2,1)S(1)} %get-tuple-element.19), channel_id=1, source_target_pairs={{0,8},{8,0},{16,24},{24,16},{32,40},{40,32},{48,56},{56,48},{64,72... | collective-permute-start | bytes 786440 | tf_op jit(solution)/shard_map/ppermute | solution.py:313
  12.2 3.6 %copy-start.1 = (bf16[128,2048]{1,0:T(8,128)(2,1)S(1)}, bf16[128,2048]{1,0:T(8,128)(2,1)}, u32[]{:S(2)}) copy-start(bf16[128,2048]{1,0:T(8,128)(2,1)} %t_ref.5) | copy-start | bytes 1572868
  12.2 3.6 %copy-start.4 = (bf16[2048,64]{0,1:T(8,128)(2,1)S(1)}, bf16[2048,64]{0,1:T(8,128)(2,1)}, u32[]{:S(2)}) copy-start(bf16[2048,64]{0,1:T(8,128)(2,1)} %param.14) | copy-start | bytes 786436
  12.2 13.2 %all-to-all-start = ((bf16[4,256,256]{2,1,0:T(8,128)(2,1)}), bf16[4,256,256]{2,1,0:T(8,128)(2,1)S(1)}, u32[]{:S(2)}, u32[]{:S(2)}) async-start(bf16[4,256,256]{2,1,0:T(8,128)(2,1)} %broadcast_in_dim.3), calls=%async_computation | async-start | bytes 1048576 | tf_op jit(solution)/shard_map/all_to_all | solution.py:321
  16.2 14.8 %collective-permute-start.5 = (bf16[272,1024]{1,0:T(8,128)(2,1)S(1)}, bf16[272,1024]{1,0:T(8,128)(2,1)S(1)}, u32[]{:S(2)}, u32[]{:S(2)}) collective-permute-start(bf16[272,1024]{1,0:T(8,128)(2,1)S(1)} %pad_maximum_fusion.refs_0_), channel_id=1, source_target_pairs={{1,0},{2,1},{3,2},{4,3},{5,4},{6,5},{7,6},{0,7},{15,8},{8,9},{9,10... | collective-permute-start | bytes 1671176 | tf_op jit(solution)/shard_map/ppermute | solution.py:76
  18.1 17.1 %collective-permute-start.1 = (bf16[272,1024]{1,0:T(8,128)(2,1)S(1)}, bf16[272,1024]{1,0:T(8,128)(2,1)S(1)}, u32[]{:S(2)}, u32[]{:S(2)}) collective-permute-start(bf16[272,1024]{1,0:T(8,128)(2,1)S(1)} %pad_maximum_fusion.refs_0_), channel_id=1, source_target_pairs={{0,1},{1,2},{2,3},{3,4},{4,5},{5,6},{6,7},{7,0},{8,15},{9,8},{10,9... | collective-permute-start | bytes 1671176 | tf_op jit(solution)/shard_map/ppermute | solution.py:75
  25.4 15.1 %collective-permute-start.9 = (bf16[1024,256]{1,0:T(8,128)(2,1)S(1)}, bf16[1024,256]{1,0:T(8,128)(2,1)S(1)}, u32[]{:S(2)}, u32[]{:S(2)}) collective-permute-start(bf16[1024,256]{1,0:T(8,128)(2,1)S(1)} %bitcast.6), channel_id=1, source_target_pairs={{0,64},{8,456},{16,80},{24,472},{32,96},{40,488},{48,112},{56,504}... | collective-permute-start | bytes 1572872 | tf_op jit(solution)/shard_map/ppermute | solution.py:75
  29.1 16.6 %collective-permute-start.13 = (bf16[1024,256]{1,0:T(8,128)(2,1)S(1)}, bf16[1024,256]{1,0:T(8,128)(2,1)S(1)}, u32[]{:S(2)}, u32[]{:S(2)}) collective-permute-start(bf16[1024,256]{1,0:T(8,128)(2,1)S(1)} %bitcast.7), channel_id=1, source_target_pairs={{64,0},{456,8},{80,16},{472,24},{96,32},{488,40},{112,48},{504,56}... | collective-permute-start | bytes 1572872 | tf_op jit(solution)/shard_map/ppermute | solution.py:76
  31.0 16.6 %collective-permute-start.6 = (bf16[272,1024]{1,0:T(8,128)(2,1)S(1)}, bf16[272,1024]{1,0:T(8,128)(2,1)S(1)}, u32[]{:S(2)}, u32[]{:S(2)}) collective-permute-start(bf16[272,1024]{1,0:T(8,128)(2,1)S(1)} %collective-permute-done.5.refs_4_), channel_id=1, source_target_pairs={{1,0},{2,1},{3,2},{4,3},{5,4},{6,5},{7,6},{0,7},{15,8},{8,9},{9,10... | collective-permute-start | bytes 1671176 | tf_op jit(solution)/shard_map/ppermute | solution.py:76
  35.2 17.4 %collective-permute-start.2 = (bf16[272,1024]{1,0:T(8,128)(2,1)S(1)}, bf16[272,1024]{1,0:T(8,128)(2,1)S(1)}, u32[]{:S(2)}, u32[]{:S(2)}) collective-permute-start(bf16[272,1024]{1,0:T(8,128)(2,1)S(1)} %collective-permute-done.1.refs_1_), channel_id=1, source_target_pairs={{0,1},{1,2},{2,3},{3,4},{4,5},{5,6},{6,7},{7,0},{8,15},{9,8},{10,9... | collective-permute-start | bytes 1671176 | tf_op jit(solution)/shard_map/ppermute | solution.py:75
  40.5 17.4 %collective-permute-start.10 = (bf16[1024,256]{1,0:T(8,128)(2,1)S(1)}, bf16[1024,256]{1,0:T(8,128)(2,1)S(1)}, u32[]{:S(2)}, u32[]{:S(2)}) collective-permute-start(bf16[1024,256]{1,0:T(8,128)(2,1)S(1)} %collective-permute-done.9.refs_8_), channel_id=1, source_target_pairs={{0,64},{8,456},{16,80},{24,472},{32,96},{40,488},{48,112},{56,504}... | collective-permute-start | bytes 1572872 | tf_op jit(solution)/shard_map/ppermute | solution.py:75
  45.7 17.4 %collective-permute-start.14 = (bf16[1024,256]{1,0:T(8,128)(2,1)S(1)}, bf16[1024,256]{1,0:T(8,128)(2,1)S(1)}, u32[]{:S(2)}, u32[]{:S(2)}) collective-permute-start(bf16[1024,256]{1,0:T(8,128)(2,1)S(1)} %collective-permute-done.13.refs_11_), channel_id=1, source_target_pairs={{64,0},{456,8},{80,16},{472,24},{96,32},{488,40},{112,48},{504,56}... | collective-permute-start | bytes 1572872 | tf_op jit(solution)/shard_map/ppermute | solution.py:76
  47.6 17.4 %collective-permute-start.7 = (bf16[272,1024]{1,0:T(8,128)(2,1)S(1)}, bf16[272,1024]{1,0:T(8,128)(2,1)S(1)}, u32[]{:S(2)}, u32[]{:S(2)}) collective-permute-start(bf16[272,1024]{1,0:T(8,128)(2,1)S(1)} %collective-permute-done.6.refs_5_), channel_id=1, source_target_pairs={{1,0},{2,1},{3,2},{4,3},{5,4},{6,5},{7,6},{0,7},{15,8},{8,9},{9,10... | collective-permute-start | bytes 1671176 | tf_op jit(solution)/shard_map/ppermute | solution.py:76
  52.6 17.2 %collective-permute-start.3 = (bf16[272,1024]{1,0:T(8,128)(2,1)S(1)}, bf16[272,1024]{1,0:T(8,128)(2,1)S(1)}, u32[]{:S(2)}, u32[]{:S(2)}) collective-permute-start(bf16[272,1024]{1,0:T(8,128)(2,1)S(1)} %collective-permute-done.2.refs_2_), channel_id=1, source_target_pairs={{0,1},{1,2},{2,3},{3,4},{4,5},{5,6},{6,7},{7,0},{8,15},{9,8},{10,9... | collective-permute-start | bytes 1671176 | tf_op jit(solution)/shard_map/ppermute | solution.py:75
  57.9 17.2 %collective-permute-start.11 = (bf16[1024,256]{1,0:T(8,128)(2,1)S(1)}, bf16[1024,256]{1,0:T(8,128)(2,1)S(1)}, u32[]{:S(2)}, u32[]{:S(2)}) collective-permute-start(bf16[1024,256]{1,0:T(8,128)(2,1)S(1)} %collective-permute-done.10.refs_9_), channel_id=1, source_target_pairs={{0,64},{8,456},{16,80},{24,472},{32,96},{40,488},{48,112},{56,504}... | collective-permute-start | bytes 1572872 | tf_op jit(solution)/shard_map/ppermute | solution.py:75
  63.1 17.2 %collective-permute-start.15 = (bf16[1024,256]{1,0:T(8,128)(2,1)S(1)}, bf16[1024,256]{1,0:T(8,128)(2,1)S(1)}, u32[]{:S(2)}, u32[]{:S(2)}) collective-permute-start(bf16[1024,256]{1,0:T(8,128)(2,1)S(1)} %collective-permute-done.14.refs_12_), channel_id=1, source_target_pairs={{64,0},{456,8},{80,16},{472,24},{96,32},{488,40},{112,48},{504,56}... | collective-permute-start | bytes 1572872 | tf_op jit(solution)/shard_map/ppermute | solution.py:76
  65.0 20.6 %collective-permute-start.8 = (bf16[144,1024]{1,0:T(8,128)(2,1)S(1)}, bf16[144,1024]{1,0:T(8,128)(2,1)S(1)}, u32[]{:S(2)}, u32[]{:S(2)}) collective-permute-start(bf16[144,1024]{1,0:T(8,128)(2,1)S(1)} %slice.17), channel_id=1, source_target_pairs={{1,0},{2,1},{3,2},{4,3},{5,4},{6,5},{7,6},{0,7},{15,8},{8,9},{9,10... | collective-permute-start | bytes 884744 | tf_op jit(solution)/shard_map/ppermute | solution.py:79
  69.8 15.8 %collective-permute-start.4 = (bf16[128,1024]{1,0:T(8,128)(2,1)S(1)}, bf16[128,1024]{1,0:T(8,128)(2,1)S(1)}, u32[]{:S(2)}, u32[]{:S(2)}) collective-permute-start(bf16[128,1024]{1,0:T(8,128)(2,1)S(1)} %slice.16), channel_id=1, source_target_pairs={{0,1},{1,2},{2,3},{3,4},{4,5},{5,6},{6,7},{7,0},{8,15},{9,8},{10,9... | collective-permute-start | bytes 786440 | tf_op jit(solution)/shard_map/ppermute | solution.py:78
  75.2 10.4 %collective-permute-start.12 = (bf16[512,256]{1,0:T(8,128)(2,1)S(1)}, bf16[512,256]{1,0:T(8,128)(2,1)S(1)}, u32[]{:S(2)}, u32[]{:S(2)}) collective-permute-start(bf16[512,256]{1,0:T(8,128)(2,1)S(1)} %slice.18), channel_id=1, source_target_pairs={{0,64},{8,456},{16,80},{24,472},{32,96},{40,488},{48,112},{56,504}... | collective-permute-start | bytes 786440 | tf_op jit(solution)/shard_map/ppermute | solution.py:78
  80.3 9.9 %collective-permute-start.16 = (bf16[512,256]{1,0:T(8,128)(2,1)S(1)}, bf16[512,256]{1,0:T(8,128)(2,1)S(1)}, u32[]{:S(2)}, u32[]{:S(2)}) collective-permute-start(bf16[512,256]{1,0:T(8,128)(2,1)S(1)} %slice.19), channel_id=1, source_target_pairs={{64,0},{456,8},{80,16},{472,24},{96,32},{488,40},{112,48},{504,56}... | collective-permute-start | bytes 786440 | tf_op jit(solution)/shard_map/ppermute | solution.py:79
  90.2 4.6 %copy-start.2 = (bf16[128,2048]{1,0:T(8,128)(2,1)S(1)}, bf16[128,2048]{1,0:T(8,128)(2,1)}, u32[]{:S(2)}) copy-start(bf16[128,2048]{1,0:T(8,128)(2,1)} %q_ref.1) | copy-start | bytes 1572868
  90.2 4.6 %copy-start.3 = (bf16[128,2048]{1,0:T(8,128)(2,1)S(1)}, bf16[128,2048]{1,0:T(8,128)(2,1)}, u32[]{:S(2)}) copy-start(bf16[128,2048]{1,0:T(8,128)(2,1)} %p_ref.1) | copy-start | bytes 1572868
  90.2 4.6 %copy-start.5 = (bf16[64,128]{1,0:T(8,128)(2,1)S(1)}, bf16[64,128]{1,0:T(8,128)(2,1)}, u32[]{:S(2)}) copy-start(bf16[64,128]{1,0:T(8,128)(2,1)} %upk_ref.1) | copy-start | bytes 49156
  90.2 4.6 %copy-start.6 = (bf16[64,128]{1,0:T(8,128)(2,1)S(1)}, bf16[64,128]{1,0:T(8,128)(2,1)}, u32[]{:S(2)}) copy-start(bf16[64,128]{1,0:T(8,128)(2,1)} %upv_ref.1) | copy-start | bytes 49156
  90.2 4.7 %copy-start.7 = (s32[1,8]{1,0:T(1,128)S(1)}, s32[1,8]{1,0:T(1,128)}, u32[]{:S(2)}) copy-start(s32[1,8]{1,0:T(1,128)} %lengths_ref.3) | copy-start | bytes 100
  91.6 3.2 %collective-permute-start.17 = (f32[128,256]{1,0:T(8,128)S(1)}, f32[128,256]{1,0:T(8,128)S(1)}, u32[]{:S(2)}, u32[]{:S(2)}) collective-permute-start(f32[128,256]{1,0:T(8,128)S(1)} %get-tuple-element.25), channel_id=1, source_target_pairs={{0,8},{8,0},{16,24},{24,16},{32,40},{40,32},{48,56},{56,48},{64,72... | collective-permute-start | bytes 393224 | tf_op jit(solution)/shard_map/ppermute | solution.py:359

commit v13 on v12

--- a/solution.py
+++ b/solution.py
@@ -69,15 +69,21 @@
 STEPS = (0, 1, 2, 3, -1, -2, -3, 4)
 
 
-def ring_of(own, axis, fore, aft, cut):
-    fore_going, aft_going = [own], [own]
-    for _ in range(3):
-        fore_going.append(lax.ppermute(fore_going[-1], axis, fore))
-        aft_going.append(lax.ppermute(aft_going[-1], axis, aft))
-    return fore_going + aft_going[1:] + [
-        lax.ppermute(fore_going[3][:cut], axis, fore),
-        lax.ppermute(aft_going[3][cut:], axis, aft),
-    ]
+def rings_of(owns, axes, fores, afts, halves):
+    both = range(2)
+    going = [list(owns), list(owns)]
+    blocks = [[[own] for own in owns] for _ in going]
+    for step in range(4):
+        for side, ways in enumerate((fores, afts)):
+            now = going[side]
+            if step == 0 and side == 1:
+                now = lax.optimization_barrier(tuple(now))
+            if step == 3:
+                now = [halves[i](now[i])[side] for i in both]
+            going[side] = [lax.ppermute(now[i], axes[i], ways[i]) for i in both]
+            for i in both:
+                blocks[side][i].append(going[side][i])
+    return [blocks[0][i][:4] + blocks[1][i][1:4] + [blocks[0][i][4], blocks[1][i][4]] for i in both]
 
 
 def block_at(pos_ref, axis, step, n):
@@ -104,17 +110,18 @@
     low_ref[...] = low
     for c in copies:
         c.wait()
+    deep = w_left_ref.shape[0]
     total = jnp.zeros(total_ref.shape, F32)
     for j, t_ref in enumerate(t_refs):
         k = block_at(pos_ref, 0, STEPS[j], n)
-        total = total + mm(t_ref[pl.ds(0, rows)], w_scr[k], NN)
+        total = total + mm(t_ref[pl.ds(0, rows)], w_scr[k, pl.ds(0, deep)], NN)
 
         @pl.when(k == w_far)
         def _():
             t_left_ref[...] = t_ref[pl.ds(0, rows)]
 
     total_ref[...] = total
-    w_left_ref[...] = w_scr[t_far]
+    w_left_ref[...] = w_scr[t_far, pl.ds(0, deep)]
 
 
 def finish_kernel(
@@ -123,8 +130,8 @@
     t_scr, w_scr, total_scr, low_scr, t_left_scr, w_left_scr, sem,
 ):
     pairs = [
-        (t1_ref, t_scr.at[pl.ds(0, t1_ref.shape[0])]),
-        (t2_ref, t_scr.at[pl.ds(t1_ref.shape[0], t2_ref.shape[0])]),
+        (t1_ref, t_scr.at[:, pl.ds(0, t1_ref.shape[1])]),
+        (t2_ref, t_scr.at[:, pl.ds(t1_ref.shape[1], t2_ref.shape[1])]),
         (w1_ref, w_scr.at[pl.ds(0, w1_ref.shape[0])]),
         (w2_ref, w_scr.at[pl.ds(w1_ref.shape[0], w2_ref.shape[0])]),
         (total_ref, total_scr),
@@ -139,7 +146,7 @@
         c.wait()
     rows = own_ref.shape[0]
     same = pos_ref[1] == pos_ref[2]
-    w_late = w_scr[...]
+    w_late = w_scr[pl.ds(0, w_left_scr.shape[0])]
     w_match = jnp.where(same, w_late, w_left_scr[...])
     total = total_scr[...] + mm(t_scr[pl.ds(0, 2 * rows)], w_match, NN)
     total = total + mm(t_left_scr[...], w_late, NN)
@@ -322,13 +329,16 @@
         jnp.broadcast_to(w_both, (4,) + w_both.shape), "row", 0, 0, axis_index_groups=x_lines
     )
     w_own = w_line.reshape(feats // 2, wide)
-    t_parts = ring_of(pair, ("row", "col"), z_fore, z_aft, rows)
-    w_parts = ring_of(w_own, "row", y_fore, y_aft, feats // 4)
+    w_own = jnp.pad(w_own, ((0, pair.size // wide - w_own.shape[0]), (0, 0)))
+    t_parts, w_parts = rings_of(
+        (pair, w_own), (("row", "col"), "row"), (z_fore, y_fore), (z_aft, y_aft),
+        (lambda t: jnp.split(t, 2, axis=1), lambda w: jnp.split(w, 2, axis=0)),
+    )
 
     deep = feats // 2
     total, low_sum, t_left, w_left = call(
         project_kernel,
-        [((2 * rows, wide), F32), ((16, deep), F32), ((2 * rows, deep), BF), (w_own.shape, BF)],
+        [((2 * rows, wide), F32), ((16, deep), F32), ((2 * rows, deep), BF), ((deep, wide), BF)],
         [SMEM] + [VMEM] * 7 + [HBM] * 7,
         [VMEM] * 4,
         pos, *t_parts[:7], *w_parts[:7],

time: 158 us -> 154 us (0.975)
  starting transfers between devices: 70.4 us -> 80.8 us
  blocking collectives: 56.6 us -> 48.4 us
  waiting for transfers between devices: 15.6 us -> 9.15 us
    ppermute x1, starting transfers between devices: 1.92 us -> 12.1 us  [on_device(): got = lax.ppermute(other, 'row', swap)]
    ppermute x16, waiting for transfers between devices: 12.8 us -> 7.41 us  [rings_of(): going[side] = [lax.ppermute(now[i], axes[i], ways[i]) for i in both]]
    all_to_all x1, blocking collectives: 18.4 us -> 14.7 us  [on_device(): lax.all_to_all(square, 'row', 0, 0, axis_index_groups=y_lines)]
    all_to_all x1, blocking collectives: 13.9 us -> 11.5 us  [on_device(): term_parts = lax.all_to_all(terms, 'row', 0, 0, axis_index_groups=squares)]
  transfers between devices with their start and end apart: 19 -> 19, of which waited for: 6 -> 8; matrix products, arithmetic and copies ran while one was open for 1% -> 0% of each run, Pallas kernels for 2% -> 3%
where the time goes in v13:
time: 154 us; the launch traced here: 153 us
  starting transfers between devices  80.8 us (52%)
  blocking collectives  48.4 us (31%)
  Pallas kernels  11.8 us (8%)
  waiting for transfers between devices  9.15 us (6%)
    ppermute x16, starting transfers between devices, rings_of(): going[side] = [lax.ppermute(now[i], axes[i], ways[i]) for i in both]  56.3 us
    all_to_all x1, blocking collectives, on_device(): lax.all_to_all(square, 'row', 0, 0, axis_index_groups=y_lines)  14.7 us
    ppermute x1, starting transfers between devices, on_device(): got = lax.ppermute(other, 'row', swap)  12.1 us
    pallas_call x9, Pallas kernels, call(): pl.pallas_call(kernel, out_shape=[jax.ShapeDtypeStruct(s, d) for s, d in...  11.8 us
    all_to_all x1, blocking collectives, on_device(): term_parts = lax.all_to_all(terms, 'row', 0, 0, axis_index_groups=squares)  11.5 us
    all_to_all x1, blocking collectives, on_device(): packs = lax.all_to_all(pack, 'col', 0, 0)  11.3 us
    all_to_all x1, blocking collectives, on_device(): pieces = lax.all_to_all(summed, 'row', 0, 0, axis_index_groups=squares)  10.9 us
    ppermute x1, starting transfers between devices, on_device(): swapped = lax.ppermute(theirs, 'row', swap)  7.46 us
  transfers between devices with their start and end apart: 19, of which 8 were waited for; matrix products, arithmetic and copies ran while one was open for 0% of the time, Pallas kernels for 3%

profile of v13, /device:TPU:1, one launch (start us, length us, event | category | flops | bytes accessed | tf_op | source)
XLA Modules:
  0.0 153.1 jit_solution(3970433513697584974)
XLA Ops:
  0.6 0.9 pad_maximum_fusion.1
  1.5 0.8 broadcast_in_dim.3
  2.4 5.0 %all-to-all-start = ((bf16[4,256,256]{2,1,0:T(8,128)(2,1)}), bf16[4,256,256]{2,1,0:T(8,128)(2,1)S(1)}, u32[]{:S(2)}, u32[]{:S(2)}) async-start(bf16[4,256,256]{2,1,0:T(8,128)(2,1)} %broadcast_in_dim.3), calls=%async_computation | async-start | bytes 1048576 | tf_op jit(solution)/shard_map/all_to_all | solution.py:328
  7.3 0.1 pad_add_fusion.pos_ref
  7.4 0.7 shard_map.112
  8.1 7.5 %collective-permute-start = (bf16[128,1024]{1,0:T(8,128)(2,1)S(1)}, bf16[128,1024]{1,0:T(8,128)(2,1)S(1)}, u32[]{:S(2)}, u32[]{:S(2)}) collective-permute-start(bf16[128,1024]{1,0:T(8,128)(2,1)S(1)} %get-tuple-element.21), channel_id=1, source_target_pairs={{0,8},{8,0},{16,24},{24,16},{32,40},{40,32},{48,56},{56,48},{64,72... | collective-permute-start | bytes 786440 | tf_op jit(solution)/shard_map/ppermute | solution.py:320
  15.6 0.4 shard_map.113
  16.0 0.8 collective-permute-done
  16.8 6.1 %collective-permute-start.1 = (bf16[272,1024]{1,0:T(8,128)(2,1)S(1)}, bf16[272,1024]{1,0:T(8,128)(2,1)S(1)}, u32[]{:S(2)}, u32[]{:S(2)}) collective-permute-start(bf16[272,1024]{1,0:T(8,128)(2,1)S(1)} %pad_maximum_fusion.refs_0_), channel_id=1, source_target_pairs={{0,1},{1,2},{2,3},{3,4},{4,5},{5,6},{6,7},{7,0},{8,15},{9,8},{10,9... | collective-permute-start | bytes 1671176 | tf_op jit(solution)/shard_map/ppermute | solution.py:83
  22.9 3.2 %collective-permute-start.13 = (bf16[1088,256]{1,0:T(8,128)(2,1)S(1)}, bf16[1088,256]{1,0:T(8,128)(2,1)S(1)}, u32[]{:S(2)}, u32[]{:S(2)}) collective-permute-start(bf16[1088,256]{1,0:T(8,128)(2,1)S(1)} %pad.4.refs_7_), channel_id=1, source_target_pairs={{64,0},{456,8},{80,16},{472,24},{96,32},{488,40},{112,48},{504,56}... | collective-permute-start | bytes 1671176 | tf_op jit(solution)/shard_map/ppermute | solution.py:83
  26.1 1.9 %collective-permute-start.5 = (bf16[272,1024]{1,0:T(8,128)(2,1)S(1)}, bf16[272,1024]{1,0:T(8,128)(2,1)S(1)}, u32[]{:S(2)}, u32[]{:S(2)}) collective-permute-start(bf16[272,1024]{1,0:T(8,128)(2,1)S(1)} %pad_maximum_fusion.refs_0_), channel_id=1, source_target_pairs={{1,0},{2,1},{3,2},{4,3},{5,4},{6,5},{7,6},{0,7},{15,8},{8,9},{9,10... | collective-permute-start | bytes 1671176 | tf_op jit(solution)/shard_map/ppermute | solution.py:83
  28.1 3.8 %collective-permute-start.9 = (bf16[1088,256]{1,0:T(8,128)(2,1)S(1)}, bf16[1088,256]{1,0:T(8,128)(2,1)S(1)}, u32[]{:S(2)}, u32[]{:S(2)}) collective-permute-start(bf16[1088,256]{1,0:T(8,128)(2,1)S(1)} %pad.4.refs_7_), channel_id=1, source_target_pairs={{0,64},{8,456},{16,80},{24,472},{32,96},{40,488},{48,112},{56,504}... | collective-permute-start | bytes 1671176 | tf_op jit(solution)/shard_map/ppermute | solution.py:83
  31.9 0.0 collective-permute-done.1.refs_1_
  31.9 4.6 %collective-permute-start.2 = (bf16[272,1024]{1,0:T(8,128)(2,1)S(1)}, bf16[272,1024]{1,0:T(8,128)(2,1)S(1)}, u32[]{:S(2)}, u32[]{:S(2)}) collective-permute-start(bf16[272,1024]{1,0:T(8,128)(2,1)S(1)} %collective-permute-done.1.refs_1_), channel_id=1, source_target_pairs={{0,1},{1,2},{2,3},{3,4},{4,5},{5,6},{6,7},{7,0},{8,15},{9,8},{10,9... | collective-permute-start | bytes 1671176 | tf_op jit(solution)/shard_map/ppermute | solution.py:83
  36.5 1.9 %collective-permute-start.14 = (bf16[1088,256]{1,0:T(8,128)(2,1)S(1)}, bf16[1088,256]{1,0:T(8,128)(2,1)S(1)}, u32[]{:S(2)}, u32[]{:S(2)}) collective-permute-start(bf16[1088,256]{1,0:T(8,128)(2,1)S(1)} %collective-permute-done.13.refs_11_), channel_id=1, source_target_pairs={{64,0},{456,8},{80,16},{472,24},{96,32},{488,40},{112,48},{504,56}... | collective-permute-start | bytes 1671176 | tf_op jit(solution)/shard_map/ppermute | solution.py:83
  38.4 0.0 collective-permute-done.5.refs_4_
  38.4 1.9 %collective-permute-start.6 = (bf16[272,1024]{1,0:T(8,128)(2,1)S(1)}, bf16[272,1024]{1,0:T(8,128)(2,1)S(1)}, u32[]{:S(2)}, u32[]{:S(2)}) collective-permute-start(bf16[272,1024]{1,0:T(8,128)(2,1)S(1)} %collective-permute-done.5.refs_4_), channel_id=1, source_target_pairs={{1,0},{2,1},{3,2},{4,3},{5,4},{6,5},{7,6},{0,7},{15,8},{8,9},{9,10... | collective-permute-start | bytes 1671176 | tf_op jit(solution)/shard_map/ppermute | solution.py:83
  40.4 0.0 collective-permute-done.9.refs_8_
  40.4 4.6 %collective-permute-start.10 = (bf16[1088,256]{1,0:T(8,128)(2,1)S(1)}, bf16[1088,256]{1,0:T(8,128)(2,1)S(1)}, u32[]{:S(2)}, u32[]{:S(2)}) collective-permute-start(bf16[1088,256]{1,0:T(8,128)(2,1)S(1)} %collective-permute-done.9.refs_8_), channel_id=1, source_target_pairs={{0,64},{8,456},{16,80},{24,472},{32,96},{40,488},{48,112},{56,504}... | collective-permute-start | bytes 1671176 | tf_op jit(solution)/shard_map/ppermute | solution.py:83
  44.9 1.8 %collective-permute-done.2.refs_2_ = bf16[272,1024]{1,0:T(8,128)(2,1)S(1)} collective-permute-done((bf16[272,1024]{1,0:T(8,128)(2,1)S(1)}, bf16[272,1024]{1,0:T(8,128)(2,1)S(1)}, u32[]{:S(2)}, u32[]{:S(2)}) %collective-permute-start.2) | collective-permute-done | bytes 557088 | tf_op jit(solution)/shard_map/ppermute | solution.py:83
  46.7 5.3 %collective-permute-start.3 = (bf16[272,1024]{1,0:T(8,128)(2,1)S(1)}, bf16[272,1024]{1,0:T(8,128)(2,1)S(1)}, u32[]{:S(2)}, u32[]{:S(2)}) collective-permute-start(bf16[272,1024]{1,0:T(8,128)(2,1)S(1)} %collective-permute-done.2.refs_2_), channel_id=1, source_target_pairs={{0,1},{1,2},{2,3},{3,4},{4,5},{5,6},{6,7},{7,0},{8,15},{9,8},{10,9... | collective-permute-start | bytes 1671176 | tf_op jit(solution)/shard_map/ppermute | solution.py:83
  52.1 0.3 collective-permute-done.14.refs_12_
  52.3 1.9 %collective-permute-start.15 = (bf16[1088,256]{1,0:T(8,128)(2,1)S(1)}, bf16[1088,256]{1,0:T(8,128)(2,1)S(1)}, u32[]{:S(2)}, u32[]{:S(2)}) collective-permute-start(bf16[1088,256]{1,0:T(8,128)(2,1)S(1)} %collective-permute-done.14.refs_12_), channel_id=1, source_target_pairs={{64,0},{456,8},{80,16},{472,24},{96,32},{488,40},{112,48},{504,56}... | collective-permute-start | bytes 1671176 | tf_op jit(solution)/shard_map/ppermute | solution.py:83
  54.2 0.0 collective-permute-done.6.refs_5_
  54.3 1.9 %collective-permute-start.7 = (bf16[272,1024]{1,0:T(8,128)(2,1)S(1)}, bf16[272,1024]{1,0:T(8,128)(2,1)S(1)}, u32[]{:S(2)}, u32[]{:S(2)}) collective-permute-start(bf16[272,1024]{1,0:T(8,128)(2,1)S(1)} %collective-permute-done.6.refs_5_), channel_id=1, source_target_pairs={{1,0},{2,1},{3,2},{4,3},{5,4},{6,5},{7,6},{0,7},{15,8},{8,9},{9,10... | collective-permute-start | bytes 1671176 | tf_op jit(solution)/shard_map/ppermute | solution.py:83
  56.2 4.9 %collective-permute-start.11 = (bf16[1088,256]{1,0:T(8,128)(2,1)S(1)}, bf16[1088,256]{1,0:T(8,128)(2,1)S(1)}, u32[]{:S(2)}, u32[]{:S(2)}) collective-permute-start(bf16[1088,256]{1,0:T(8,128)(2,1)S(1)} %collective-permute-done.10.refs_9_), channel_id=1, source_target_pairs={{0,64},{8,456},{16,80},{24,472},{32,96},{40,488},{48,112},{56,504}... | collective-permute-start | bytes 1671176 | tf_op jit(solution)/shard_map/ppermute | solution.py:83
  61.1 2.0 %collective-permute-done.3.refs_3_ = bf16[272,1024]{1,0:T(8,128)(2,1)S(1)} collective-permute-done((bf16[272,1024]{1,0:T(8,128)(2,1)S(1)}, bf16[272,1024]{1,0:T(8,128)(2,1)S(1)}, u32[]{:S(2)}, u32[]{:S(2)}) %collective-permute-start.3) | collective-permute-done | bytes 557088 | tf_op jit(solution)/shard_map/ppermute | solution.py:83
  63.1 5.3 %collective-permute-start.4 = (bf16[272,512]{1,0:T(8,128)(2,1)S(1)}, bf16[272,512]{1,0:T(8,128)(2,1)S(1)}, u32[]{:S(2)}, u32[]{:S(2)}) collective-permute-start(bf16[272,512]{1,0:T(8,128)(2,1)S(1)} %split.16), channel_id=1, source_target_pairs={{0,1},{1,2},{2,3},{3,4},{4,5},{5,6},{6,7},{7,0},{8,15},{9,8},{10,9... | collective-permute-start | bytes 835592 | tf_op jit(solution)/shard_map/ppermute | solution.py:83
  68.5 0.5 collective-permute-done.15.refs_13_
  69.0 1.9 %collective-permute-start.16 = (bf16[544,256]{1,0:T(8,128)(2,1)S(1)}, bf16[544,256]{1,0:T(8,128)(2,1)S(1)}, u32[]{:S(2)}, u32[]{:S(2)}) collective-permute-start(bf16[544,256]{1,0:T(8,128)(2,1)S(1)} %split.19), channel_id=1, source_target_pairs={{64,0},{456,8},{80,16},{472,24},{96,32},{488,40},{112,48},{504,56}... | collective-permute-start | bytes 835592 | tf_op jit(solution)/shard_map/ppermute | solution.py:83
  71.0 1.9 %collective-permute-start.8 = (bf16[272,512]{1,0:T(8,128)(2,1)S(1)}, bf16[272,512]{1,0:T(8,128)(2,1)S(1)}, u32[]{:S(2)}, u32[]{:S(2)}) collective-permute-start(bf16[272,512]{1,0:T(8,128)(2,1)S(1)} %split.17), channel_id=1, source_target_pairs={{1,0},{2,1},{3,2},{4,3},{5,4},{6,5},{7,6},{0,7},{15,8},{8,9},{9,10... | collective-permute-start | bytes 835592 | tf_op jit(solution)/shard_map/ppermute | solution.py:83
  72.9 0.0 collective-permute-done.11.refs_10_
  72.9 5.1 %collective-permute-start.12 = (bf16[544,256]{1,0:T(8,128)(2,1)S(1)}, bf16[544,256]{1,0:T(8,128)(2,1)S(1)}, u32[]{:S(2)}, u32[]{:S(2)}) collective-permute-start(bf16[544,256]{1,0:T(8,128)(2,1)S(1)} %split.18), channel_id=1, source_target_pairs={{0,64},{8,456},{16,80},{24,472},{32,96},{40,488},{48,112},{56,504}... | collective-permute-start | bytes 835592 | tf_op jit(solution)/shard_map/ppermute | solution.py:83
  78.1 3.6 %shard_map.114 = (f32[256,256]{1,0:T(8,128)S(1)}, f32[16,1024]{1,0:T(8,128)S(1)}, bf16[256,1024]{1,0:T(8,128)(2,1)S(1)}, bf16[1024,256]{1,0:T(8,128)(2,1)S(1)}) custom-call(s32[3]{0:T(128)S(1)} %pad_add_fusion.pos_ref, bf16[272,1024]{1,0:T(8,128)(2,1)S(1)} %pad_maximum_fusion.refs_0_, bf16[272,1024]{1,0:T(8,128)(2,1)S(1)} %collective-permute-done.1.refs_1_, ...), custom_call_target="tpu_custom_call" | custom-call | flops 1073741824 | bytes 7798784 | tf_op jit(solution)/shard_map/pallas_call | solution.py:280
  81.7 0.0 collective-permute-done.4.t1_ref
  81.7 0.0 collective-permute-done.16.w2_ref
  81.7 0.8 collective-permute-done.8.t2_ref
  82.5 2.0 %collective-permute-done.12.w1_ref = bf16[544,256]{1,0:T(8,128)(2,1)S(1)} collective-permute-done((bf16[544,256]{1,0:T(8,128)(2,1)S(1)}, bf16[544,256]{1,0:T(8,128)(2,1)S(1)}, u32[]{:S(2)}, u32[]{:S(2)}) %collective-permute-start.12) | collective-permute-done | bytes 278560 | tf_op jit(solution)/shard_map/ppermute | solution.py:83
  84.5 1.4 shard_map.115
  85.9 12.1 %collective-permute-start.17 = (f32[128,256]{1,0:T(8,128)S(1)}, f32[128,256]{1,0:T(8,128)S(1)}, u32[]{:S(2)}, u32[]{:S(2)}) collective-permute-start(f32[128,256]{1,0:T(8,128)S(1)} %get-tuple-element.29), channel_id=1, source_target_pairs={{0,8},{8,0},{16,24},{24,16},{32,40},{40,32},{48,56},{56,48},{64,72... | collective-permute-start | bytes 393224 | tf_op jit(solution)/shard_map/ppermute | solution.py:369
  98.0 1.0 collective-permute-done.17.got_ref
  98.9 3.9 %shard_map.116 = (bf16[8,80,128]{2,1,0:T(8,128)(2,1)S(1)}, f32[128,128]{1,0:T(8,128)S(1)}, f32[128,128]{1,0:T(8,128)S(1)}) custom-call(s32[1,8]{1,0:T(1,128)S(1)} %copy-done.6, f32[128,256]{1,0:T(8,128)S(1)} %get-tuple-element.28.own_ref, f32[128,256]{1,0:T(8,128)S(1)} %collective-permute-done.17.got_ref, ...), custom_call_target="tpu_custom_call" | custom-call | tf_op jit(solution)/shard_map/pallas_call | solution.py:280
  102.8 11.3 %all_to_all.25.pack_ref = bf16[8,80,128]{2,1,0:T(8,128)(2,1)S(1)} all-to-all(bf16[8,80,128]{2,1,0:T(8,128)(2,1)S(1)} %get-tuple-element.31), channel_id=1, replica_groups=mesh['row'=64,'col'=8] {'col'}, dimensions={0} | all-to-all | bytes 327680 | tf_op jit(solution)/shard_map/all_to_all | solution.py:382
  114.1 0.9 shard_map.117
  115.0 11.5 %all_to_all.26.in_ref = bf16[8,72,256]{2,1,0:T(8,128)(2,1)S(1)} all-to-all(bf16[8,72,256]{2,1,0:T(8,128)(2,1)S(1)} %shard_map.117), channel_id=1, replica_groups={{0,8,16,24,32,40,48,56},{64,72,80,88,96,104,112,120},{128,136,144,152,1..., dimensions={0} | all-to-all | bytes 589824 | tf_op jit(solution)/shard_map/all_to_all | solution.py:388
  126.6 14.7 %all_to_all.27.in_ref = bf16[8,72,256]{2,1,0:T(8,128)(2,1)S(1)} all-to-all(bf16[8,72,256]{2,1,0:T(8,128)(2,1)S(1)} %shard_map.118), channel_id=1, replica_groups={{0,64,128,192,256,320,384,448},{8,72,136,200,264,328,392,456},{16,80,14..., dimensions={0} | all-to-all | bytes 589824 | tf_op jit(solution)/shard_map/all_to_all | solution.py:390
  141.4 10.9 %all_to_all.28.in_ref = bf16[8,72,256]{2,1,0:T(8,128)(2,1)S(1)} all-to-all(bf16[8,72,256]{2,1,0:T(8,128)(2,1)S(1)} %shard_map.119), channel_id=1, replica_groups={{0,8,16,24,32,40,48,56},{64,72,80,88,96,104,112,120},{128,136,144,152,1..., dimensions={0} | all-to-all | bytes 589824 | tf_op jit(solution)/shard_map/all_to_all | solution.py:392
  152.3 0.8 shard_map.120
  (26 shorter events, 0.3 us)
Async XLA Ops:
  2.3 5.1 %copy-start = (bf16[128,2048]{1,0:T(8,128)(2,1)S(1)}, bf16[128,2048]{1,0:T(8,128)(2,1)}, u32[]{:S(2)}) copy-start(bf16[128,2048]{1,0:T(8,128)(2,1)} %t_ref.5) | copy-start | bytes 1572868
  2.4 20.5 %all-to-all-start = ((bf16[4,256,256]{2,1,0:T(8,128)(2,1)}), bf16[4,256,256]{2,1,0:T(8,128)(2,1)S(1)}, u32[]{:S(2)}, u32[]{:S(2)}) async-start(bf16[4,256,256]{2,1,0:T(8,128)(2,1)} %broadcast_in_dim.3), calls=%async_computation | async-start | bytes 1048576 | tf_op jit(solution)/shard_map/all_to_all | solution.py:328
  7.3 8.3 %copy-start.3 = (bf16[2048,64]{0,1:T(8,128)(2,1)S(1)}, bf16[2048,64]{0,1:T(8,128)(2,1)}, u32[]{:S(2)}) copy-start(bf16[2048,64]{0,1:T(8,128)(2,1)} %param.14) | copy-start | bytes 786436
  8.1 8.6 %collective-permute-start = (bf16[128,1024]{1,0:T(8,128)(2,1)S(1)}, bf16[128,1024]{1,0:T(8,128)(2,1)S(1)}, u32[]{:S(2)}, u32[]{:S(2)}) collective-permute-start(bf16[128,1024]{1,0:T(8,128)(2,1)S(1)} %get-tuple-element.21), channel_id=1, source_target_pairs={{0,8},{8,0},{16,24},{24,16},{32,40},{40,32},{48,56},{56,48},{64,72... | collective-permute-start | bytes 786440 | tf_op jit(solution)/shard_map/ppermute | solution.py:320
  16.8 15.1 %collective-permute-start.1 = (bf16[272,1024]{1,0:T(8,128)(2,1)S(1)}, bf16[272,1024]{1,0:T(8,128)(2,1)S(1)}, u32[]{:S(2)}, u32[]{:S(2)}) collective-permute-start(bf16[272,1024]{1,0:T(8,128)(2,1)S(1)} %pad_maximum_fusion.refs_0_), channel_id=1, source_target_pairs={{0,1},{1,2},{2,3},{3,4},{4,5},{5,6},{6,7},{7,0},{8,15},{9,8},{10,9... | collective-permute-start | bytes 1671176 | tf_op jit(solution)/shard_map/ppermute | solution.py:83
  22.9 13.6 %collective-permute-start.13 = (bf16[1088,256]{1,0:T(8,128)(2,1)S(1)}, bf16[1088,256]{1,0:T(8,128)(2,1)S(1)}, u32[]{:S(2)}, u32[]{:S(2)}) collective-permute-start(bf16[1088,256]{1,0:T(8,128)(2,1)S(1)} %pad.4.refs_7_), channel_id=1, source_target_pairs={{64,0},{456,8},{80,16},{472,24},{96,32},{488,40},{112,48},{504,56}... | collective-permute-start | bytes 1671176 | tf_op jit(solution)/shard_map/ppermute | solution.py:83
  26.1 12.3 %collective-permute-start.5 = (bf16[272,1024]{1,0:T(8,128)(2,1)S(1)}, bf16[272,1024]{1,0:T(8,128)(2,1)S(1)}, u32[]{:S(2)}, u32[]{:S(2)}) collective-permute-start(bf16[272,1024]{1,0:T(8,128)(2,1)S(1)} %pad_maximum_fusion.refs_0_), channel_id=1, source_target_pairs={{1,0},{2,1},{3,2},{4,3},{5,4},{6,5},{7,6},{0,7},{15,8},{8,9},{9,10... | collective-permute-start | bytes 1671176 | tf_op jit(solution)/shard_map/ppermute | solution.py:83
  28.1 12.3 %collective-permute-start.9 = (bf16[1088,256]{1,0:T(8,128)(2,1)S(1)}, bf16[1088,256]{1,0:T(8,128)(2,1)S(1)}, u32[]{:S(2)}, u32[]{:S(2)}) collective-permute-start(bf16[1088,256]{1,0:T(8,128)(2,1)S(1)} %pad.4.refs_7_), channel_id=1, source_target_pairs={{0,64},{8,456},{16,80},{24,472},{32,96},{40,488},{48,112},{56,504}... | collective-permute-start | bytes 1671176 | tf_op jit(solution)/shard_map/ppermute | solution.py:83
  31.9 14.8 %collective-permute-start.2 = (bf16[272,1024]{1,0:T(8,128)(2,1)S(1)}, bf16[272,1024]{1,0:T(8,128)(2,1)S(1)}, u32[]{:S(2)}, u32[]{:S(2)}) collective-permute-start(bf16[272,1024]{1,0:T(8,128)(2,1)S(1)} %collective-permute-done.1.refs_1_), channel_id=1, source_target_pairs={{0,1},{1,2},{2,3},{3,4},{4,5},{5,6},{6,7},{7,0},{8,15},{9,8},{10,9... | collective-permute-start | bytes 1671176 | tf_op jit(solution)/shard_map/ppermute | solution.py:83
  36.5 15.8 %collective-permute-start.14 = (bf16[1088,256]{1,0:T(8,128)(2,1)S(1)}, bf16[1088,256]{1,0:T(8,128)(2,1)S(1)}, u32[]{:S(2)}, u32[]{:S(2)}) collective-permute-start(bf16[1088,256]{1,0:T(8,128)(2,1)S(1)} %collective-permute-done.13.refs_11_), channel_id=1, source_target_pairs={{64,0},{456,8},{80,16},{472,24},{96,32},{488,40},{112,48},{504,56}... | collective-permute-start | bytes 1671176 | tf_op jit(solution)/shard_map/ppermute | solution.py:83
  38.4 15.8 %collective-permute-start.6 = (bf16[272,1024]{1,0:T(8,128)(2,1)S(1)}, bf16[272,1024]{1,0:T(8,128)(2,1)S(1)}, u32[]{:S(2)}, u32[]{:S(2)}) collective-permute-start(bf16[272,1024]{1,0:T(8,128)(2,1)S(1)} %collective-permute-done.5.refs_4_), channel_id=1, source_target_pairs={{1,0},{2,1},{3,2},{4,3},{5,4},{6,5},{7,6},{0,7},{15,8},{8,9},{9,10... | collective-permute-start | bytes 1671176 | tf_op jit(solution)/shard_map/ppermute | solution.py:83
  40.4 15.8 %collective-permute-start.10 = (bf16[1088,256]{1,0:T(8,128)(2,1)S(1)}, bf16[1088,256]{1,0:T(8,128)(2,1)S(1)}, u32[]{:S(2)}, u32[]{:S(2)}) collective-permute-start(bf16[1088,256]{1,0:T(8,128)(2,1)S(1)} %collective-permute-done.9.refs_8_), channel_id=1, source_target_pairs={{0,64},{8,456},{16,80},{24,472},{32,96},{40,488},{48,112},{56,504}... | collective-permute-start | bytes 1671176 | tf_op jit(solution)/shard_map/ppermute | solution.py:83
  46.7 16.4 %collective-permute-start.3 = (bf16[272,1024]{1,0:T(8,128)(2,1)S(1)}, bf16[272,1024]{1,0:T(8,128)(2,1)S(1)}, u32[]{:S(2)}, u32[]{:S(2)}) collective-permute-start(bf16[272,1024]{1,0:T(8,128)(2,1)S(1)} %collective-permute-done.2.refs_2_), channel_id=1, source_target_pairs={{0,1},{1,2},{2,3},{3,4},{4,5},{5,6},{6,7},{7,0},{8,15},{9,8},{10,9... | collective-permute-start | bytes 1671176 | tf_op jit(solution)/shard_map/ppermute | solution.py:83
  52.3 16.7 %collective-permute-start.15 = (bf16[1088,256]{1,0:T(8,128)(2,1)S(1)}, bf16[1088,256]{1,0:T(8,128)(2,1)S(1)}, u32[]{:S(2)}, u32[]{:S(2)}) collective-permute-start(bf16[1088,256]{1,0:T(8,128)(2,1)S(1)} %collective-permute-done.14.refs_12_), channel_id=1, source_target_pairs={{64,0},{456,8},{80,16},{472,24},{96,32},{488,40},{112,48},{504,56}... | collective-permute-start | bytes 1671176 | tf_op jit(solution)/shard_map/ppermute | solution.py:83
  54.3 16.7 %collective-permute-start.7 = (bf16[272,1024]{1,0:T(8,128)(2,1)S(1)}, bf16[272,1024]{1,0:T(8,128)(2,1)S(1)}, u32[]{:S(2)}, u32[]{:S(2)}) collective-permute-start(bf16[272,1024]{1,0:T(8,128)(2,1)S(1)} %collective-permute-done.6.refs_5_), channel_id=1, source_target_pairs={{1,0},{2,1},{3,2},{4,3},{5,4},{6,5},{7,6},{0,7},{15,8},{8,9},{9,10... | collective-permute-start | bytes 1671176 | tf_op jit(solution)/shard_map/ppermute | solution.py:83
  56.2 16.7 %collective-permute-start.11 = (bf16[1088,256]{1,0:T(8,128)(2,1)S(1)}, bf16[1088,256]{1,0:T(8,128)(2,1)S(1)}, u32[]{:S(2)}, u32[]{:S(2)}) collective-permute-start(bf16[1088,256]{1,0:T(8,128)(2,1)S(1)} %collective-permute-done.10.refs_9_), channel_id=1, source_target_pairs={{0,64},{8,456},{16,80},{24,472},{32,96},{40,488},{48,112},{56,504}... | collective-permute-start | bytes 1671176 | tf_op jit(solution)/shard_map/ppermute | solution.py:83
  63.1 18.6 %collective-permute-start.4 = (bf16[272,512]{1,0:T(8,128)(2,1)S(1)}, bf16[272,512]{1,0:T(8,128)(2,1)S(1)}, u32[]{:S(2)}, u32[]{:S(2)}) collective-permute-start(bf16[272,512]{1,0:T(8,128)(2,1)S(1)} %split.16), channel_id=1, source_target_pairs={{0,1},{1,2},{2,3},{3,4},{4,5},{5,6},{6,7},{7,0},{8,15},{9,8},{10,9... | collective-permute-start | bytes 835592 | tf_op jit(solution)/shard_map/ppermute | solution.py:83
  69.0 12.7 %collective-permute-start.16 = (bf16[544,256]{1,0:T(8,128)(2,1)S(1)}, bf16[544,256]{1,0:T(8,128)(2,1)S(1)}, u32[]{:S(2)}, u32[]{:S(2)}) collective-permute-start(bf16[544,256]{1,0:T(8,128)(2,1)S(1)} %split.19), channel_id=1, source_target_pairs={{64,0},{456,8},{80,16},{472,24},{96,32},{488,40},{112,48},{504,56}... | collective-permute-start | bytes 835592 | tf_op jit(solution)/shard_map/ppermute | solution.py:83
  71.0 11.5 %collective-permute-start.8 = (bf16[272,512]{1,0:T(8,128)(2,1)S(1)}, bf16[272,512]{1,0:T(8,128)(2,1)S(1)}, u32[]{:S(2)}, u32[]{:S(2)}) collective-permute-start(bf16[272,512]{1,0:T(8,128)(2,1)S(1)} %split.17), channel_id=1, source_target_pairs={{1,0},{2,1},{3,2},{4,3},{5,4},{6,5},{7,6},{0,7},{15,8},{8,9},{9,10... | collective-permute-start | bytes 835592 | tf_op jit(solution)/shard_map/ppermute | solution.py:83
  72.9 11.5 %collective-permute-start.12 = (bf16[544,256]{1,0:T(8,128)(2,1)S(1)}, bf16[544,256]{1,0:T(8,128)(2,1)S(1)}, u32[]{:S(2)}, u32[]{:S(2)}) collective-permute-start(bf16[544,256]{1,0:T(8,128)(2,1)S(1)} %split.18), channel_id=1, source_target_pairs={{0,64},{8,456},{16,80},{24,472},{32,96},{40,488},{48,112},{56,504}... | collective-permute-start | bytes 835592 | tf_op jit(solution)/shard_map/ppermute | solution.py:83
  84.5 14.5 %copy-start.1 = (bf16[128,2048]{1,0:T(8,128)(2,1)S(1)}, bf16[128,2048]{1,0:T(8,128)(2,1)}, u32[]{:S(2)}) copy-start(bf16[128,2048]{1,0:T(8,128)(2,1)} %q_ref.1) | copy-start | bytes 1572868
  84.5 14.5 %copy-start.2 = (bf16[128,2048]{1,0:T(8,128)(2,1)S(1)}, bf16[128,2048]{1,0:T(8,128)(2,1)}, u32[]{:S(2)}) copy-start(bf16[128,2048]{1,0:T(8,128)(2,1)} %p_ref.1) | copy-start | bytes 1572868
  84.5 14.5 %copy-start.4 = (bf16[64,128]{1,0:T(8,128)(2,1)S(1)}, bf16[64,128]{1,0:T(8,128)(2,1)}, u32[]{:S(2)}) copy-start(bf16[64,128]{1,0:T(8,128)(2,1)} %upk_ref.1) | copy-start | bytes 49156
  84.5 14.5 %copy-start.5 = (bf16[64,128]{1,0:T(8,128)(2,1)S(1)}, bf16[64,128]{1,0:T(8,128)(2,1)}, u32[]{:S(2)}) copy-start(bf16[64,128]{1,0:T(8,128)(2,1)} %upv_ref.1) | copy-start | bytes 49156
  84.5 14.5 %copy-start.6 = (s32[1,8]{1,0:T(1,128)S(1)}, s32[1,8]{1,0:T(1,128)}, u32[]{:S(2)}) copy-start(s32[1,8]{1,0:T(1,128)} %lengths_ref.3) | copy-start | bytes 100
  85.9 13.1 %collective-permute-start.17 = (f32[128,256]{1,0:T(8,128)S(1)}, f32[128,256]{1,0:T(8,128)S(1)}, u32[]{:S(2)}, u32[]{:S(2)}) collective-permute-start(f32[128,256]{1,0:T(8,128)S(1)} %get-tuple-element.29), channel_id=1, source_target_pairs={{0,8},{8,0},{16,24},{24,16},{32,40},{40,32},{48,56},{56,48},{64,72... | collective-permute-start | bytes 393224 | tf_op jit(solution)/shard_map/ppermute | solution.py:369

commit v14 on v13

--- a/solution.py
+++ b/solution.py
@@ -69,21 +69,20 @@
 STEPS = (0, 1, 2, 3, -1, -2, -3, 4)
 
 
-def rings_of(owns, axes, fores, afts, halves):
+def rings_of(owns, axes, fores, afts):
     both = range(2)
     going = [list(owns), list(owns)]
     blocks = [[[own] for own in owns] for _ in going]
-    for step in range(4):
+    for step in range(3):
         for side, ways in enumerate((fores, afts)):
             now = going[side]
             if step == 0 and side == 1:
                 now = lax.optimization_barrier(tuple(now))
-            if step == 3:
-                now = [halves[i](now[i])[side] for i in both]
             going[side] = [lax.ppermute(now[i], axes[i], ways[i]) for i in both]
             for i in both:
                 blocks[side][i].append(going[side][i])
-    return [blocks[0][i][:4] + blocks[1][i][1:4] + [blocks[0][i][4], blocks[1][i][4]] for i in both]
+    far = [lax.ppermute(going[i][i], axes[i], (fores, afts)[i][i]) for i in both]
+    return [blocks[0][i] + blocks[1][i][1:] + [far[i]] for i in both]
 
 
 def block_at(pos_ref, axis, step, n):
@@ -125,15 +124,13 @@
 
 
 def finish_kernel(
-    pos_ref, t1_ref, t2_ref, w1_ref, w2_ref, total_ref, low_ref, t_left_ref, w_left_ref,
+    pos_ref, t_ref, w_ref, total_ref, low_ref, t_left_ref, w_left_ref,
     own_ref, other_ref, low_half_ref,
     t_scr, w_scr, total_scr, low_scr, t_left_scr, w_left_scr, sem,
 ):
     pairs = [
-        (t1_ref, t_scr.at[:, pl.ds(0, t1_ref.shape[1])]),
-        (t2_ref, t_scr.at[:, pl.ds(t1_ref.shape[1], t2_ref.shape[1])]),
-        (w1_ref, w_scr.at[pl.ds(0, w1_ref.shape[0])]),
-        (w2_ref, w_scr.at[pl.ds(w1_ref.shape[0], w2_ref.shape[0])]),
+        (t_ref, t_scr),
+        (w_ref, w_scr),
         (total_ref, total_scr),
         (low_ref, low_scr),
         (t_left_ref, t_left_scr),
@@ -332,7 +329,6 @@
     w_own = jnp.pad(w_own, ((0, pair.size // wide - w_own.shape[0]), (0, 0)))
     t_parts, w_parts = rings_of(
         (pair, w_own), (("row", "col"), "row"), (z_fore, y_fore), (z_aft, y_aft),
-        (lambda t: jnp.split(t, 2, axis=1), lambda w: jnp.split(w, 2, axis=0)),
     )
 
     deep = feats // 2
@@ -352,9 +348,9 @@
     own, other, low_half = call(
         finish_kernel,
         [((rows, wide), F32), ((rows, wide), F32), ((rows, 64), BF)],
-        [SMEM] + [HBM] * 8,
+        [SMEM] + [HBM] * 6,
         [VMEM] * 3,
-        pos, *t_parts[7:], *w_parts[7:], total, low_sum, t_left, w_left,
+        pos, t_parts[7], w_parts[7], total, low_sum, t_left, w_left,
         scratch=[
             pltpu.VMEM(pair.shape, BF),
             pltpu.VMEM(w_own.shape, BF),
@@ -362,7 +358,7 @@
             pltpu.VMEM(low_sum.shape, F32),
             pltpu.VMEM(t_left.shape, BF),
             pltpu.VMEM(w_left.shape, BF),
-            pltpu.SemaphoreType.DMA((8,)),
+            pltpu.SemaphoreType.DMA((6,)),
         ],
         mib=16,
     )

time: 154 us -> 151 us (0.981)
  starting transfers between devices: 80.8 us -> 67.6 us
  waiting for transfers between devices: 9.15 us -> 18.1 us
    ppermute x16 -> x12, starting transfers between devices: 56.3 us -> 42 us  [rings_of(): going[side] = [lax.ppermute(now[i], axes[i], ways[i]) for i in both]]
    ppermute x0 -> x2, waiting for transfers between devices: none -> 9.95 us  [rings_of(): lax.ppermute(going[i][i], axes[i], (fores, afts)[i][i])]
    ppermute x0 -> x2, starting transfers between devices: none -> 7.22 us  [rings_of(): lax.ppermute(going[i][i], axes[i], (fores, afts)[i][i])]
    ppermute x1, starting transfers between devices: 12.1 us -> 5.97 us  [on_device(): got = lax.ppermute(other, 'row', swap)]
    ppermute x16 -> x12, waiting for transfers between devices: 7.41 us -> 6.44 us  [rings_of(): going[side] = [lax.ppermute(now[i], axes[i], ways[i]) for i in both]]
  transfers between devices with their start and end apart: 19 -> 17, of which waited for: 8 -> 9; matrix products, arithmetic and copies ran while one was open for 0% -> 0% of each run, Pallas kernels for 3% -> 3%
where the time goes in v14:
time: 151 us; the launch traced here: 150 us
  starting transfers between devices  67.6 us (45%)
  blocking collectives  49.5 us (33%)
  waiting for transfers between devices  18.1 us (12%)
  Pallas kernels  11.8 us (8%)
    ppermute x12, starting transfers between devices, rings_of(): going[side] = [lax.ppermute(now[i], axes[i], ways[i]) for i in both]  42 us
    all_to_all x1, blocking collectives, on_device(): lax.all_to_all(square, 'row', 0, 0, axis_index_groups=y_lines)  14.4 us
    all_to_all x1, blocking collectives, on_device(): pieces = lax.all_to_all(summed, 'row', 0, 0, axis_index_groups=squares)  12.2 us
    pallas_call x9, Pallas kernels, call(): pl.pallas_call(kernel, out_shape=[jax.ShapeDtypeStruct(s, d) for s, d in...  11.8 us
    all_to_all x1, blocking collectives, on_device(): packs = lax.all_to_all(pack, 'col', 0, 0)  11.5 us
    all_to_all x1, blocking collectives, on_device(): term_parts = lax.all_to_all(terms, 'row', 0, 0, axis_index_groups=squares)  11.5 us
    ppermute x2, waiting for transfers between devices, rings_of(): lax.ppermute(going[i][i], axes[i], (fores, afts)[i][i])  9.95 us
    ppermute x1, starting transfers between devices, on_device(): swapped = lax.ppermute(theirs, 'row', swap)  7.46 us
  transfers between devices with their start and end apart: 17, of which 9 were waited for; matrix products, arithmetic and copies ran while one was open for 0% of the time, Pallas kernels for 3%

profile of v14, /device:TPU:1, one launch (start us, length us, event | category | flops | bytes accessed | tf_op | source)
XLA Modules:
  0.0 149.9 jit_solution(5164767989210848100)
XLA Ops:
  0.6 0.9 pad_maximum_fusion.1
  1.5 0.8 broadcast_in_dim.3
  2.4 5.0 %all-to-all-start = ((bf16[4,256,256]{2,1,0:T(8,128)(2,1)}), bf16[4,256,256]{2,1,0:T(8,128)(2,1)S(1)}, u32[]{:S(2)}, u32[]{:S(2)}) async-start(bf16[4,256,256]{2,1,0:T(8,128)(2,1)} %broadcast_in_dim.3), calls=%async_computation | async-start | bytes 1048576 | tf_op jit(solution)/shard_map/all_to_all | solution.py:325
  7.3 0.1 pad_add_fusion.pos_ref
  7.4 0.7 shard_map.112
  8.1 7.5 %collective-permute-start = (bf16[128,1024]{1,0:T(8,128)(2,1)S(1)}, bf16[128,1024]{1,0:T(8,128)(2,1)S(1)}, u32[]{:S(2)}, u32[]{:S(2)}) collective-permute-start(bf16[128,1024]{1,0:T(8,128)(2,1)S(1)} %get-tuple-element.21), channel_id=1, source_target_pairs={{0,8},{8,0},{16,24},{24,16},{32,40},{40,32},{48,56},{56,48},{64,72... | collective-permute-start | bytes 786440 | tf_op jit(solution)/shard_map/ppermute | solution.py:317
  15.6 0.4 shard_map.113
  16.0 0.8 collective-permute-done
  16.8 6.1 %collective-permute-start.1 = (bf16[272,1024]{1,0:T(8,128)(2,1)S(1)}, bf16[272,1024]{1,0:T(8,128)(2,1)S(1)}, u32[]{:S(2)}, u32[]{:S(2)}) collective-permute-start(bf16[272,1024]{1,0:T(8,128)(2,1)S(1)} %pad_maximum_fusion.refs_0_), channel_id=1, source_target_pairs={{0,1},{1,2},{2,3},{3,4},{4,5},{5,6},{6,7},{7,0},{8,15},{9,8},{10,9... | collective-permute-start | bytes 1671176 | tf_op jit(solution)/shard_map/ppermute | solution.py:81
  22.9 0.0 all-to-all-done
  22.9 3.2 %collective-permute-start.5 = (bf16[1088,256]{1,0:T(8,128)(2,1)S(1)}, bf16[1088,256]{1,0:T(8,128)(2,1)S(1)}, u32[]{:S(2)}, u32[]{:S(2)}) collective-permute-start(bf16[1088,256]{1,0:T(8,128)(2,1)S(1)} %pad.4.refs_7_), channel_id=1, source_target_pairs={{64,0},{456,8},{80,16},{472,24},{96,32},{488,40},{112,48},{504,56}... | collective-permute-start | bytes 1671176 | tf_op jit(solution)/shard_map/ppermute | solution.py:81
  26.1 1.9 %collective-permute-start.9 = (bf16[272,1024]{1,0:T(8,128)(2,1)S(1)}, bf16[272,1024]{1,0:T(8,128)(2,1)S(1)}, u32[]{:S(2)}, u32[]{:S(2)}) collective-permute-start(bf16[272,1024]{1,0:T(8,128)(2,1)S(1)} %pad_maximum_fusion.refs_0_), channel_id=1, source_target_pairs={{1,0},{2,1},{3,2},{4,3},{5,4},{6,5},{7,6},{0,7},{15,8},{8,9},{9,10... | collective-permute-start | bytes 1671176 | tf_op jit(solution)/shard_map/ppermute | solution.py:81
  28.1 3.8 %collective-permute-start.12 = (bf16[1088,256]{1,0:T(8,128)(2,1)S(1)}, bf16[1088,256]{1,0:T(8,128)(2,1)S(1)}, u32[]{:S(2)}, u32[]{:S(2)}) collective-permute-start(bf16[1088,256]{1,0:T(8,128)(2,1)S(1)} %pad.4.refs_7_), channel_id=1, source_target_pairs={{0,64},{8,456},{16,80},{24,472},{32,96},{40,488},{48,112},{56,504}... | collective-permute-start | bytes 1671176 | tf_op jit(solution)/shard_map/ppermute | solution.py:81
  31.9 0.0 collective-permute-done.1.refs_1_
  31.9 4.6 %collective-permute-start.2 = (bf16[272,1024]{1,0:T(8,128)(2,1)S(1)}, bf16[272,1024]{1,0:T(8,128)(2,1)S(1)}, u32[]{:S(2)}, u32[]{:S(2)}) collective-permute-start(bf16[272,1024]{1,0:T(8,128)(2,1)S(1)} %collective-permute-done.1.refs_1_), channel_id=1, source_target_pairs={{0,1},{1,2},{2,3},{3,4},{4,5},{5,6},{6,7},{7,0},{8,15},{9,8},{10,9... | collective-permute-start | bytes 1671176 | tf_op jit(solution)/shard_map/ppermute | solution.py:81
  36.5 0.0 collective-permute-done.5.refs_11_
  36.5 1.9 %collective-permute-start.6 = (bf16[1088,256]{1,0:T(8,128)(2,1)S(1)}, bf16[1088,256]{1,0:T(8,128)(2,1)S(1)}, u32[]{:S(2)}, u32[]{:S(2)}) collective-permute-start(bf16[1088,256]{1,0:T(8,128)(2,1)S(1)} %collective-permute-done.5.refs_11_), channel_id=1, source_target_pairs={{64,0},{456,8},{80,16},{472,24},{96,32},{488,40},{112,48},{504,56}... | collective-permute-start | bytes 1671176 | tf_op jit(solution)/shard_map/ppermute | solution.py:81
  38.4 0.0 collective-permute-done.9.refs_4_
  38.4 1.9 %collective-permute-start.10 = (bf16[272,1024]{1,0:T(8,128)(2,1)S(1)}, bf16[272,1024]{1,0:T(8,128)(2,1)S(1)}, u32[]{:S(2)}, u32[]{:S(2)}) collective-permute-start(bf16[272,1024]{1,0:T(8,128)(2,1)S(1)} %collective-permute-done.9.refs_4_), channel_id=1, source_target_pairs={{1,0},{2,1},{3,2},{4,3},{5,4},{6,5},{7,6},{0,7},{15,8},{8,9},{9,10... | collective-permute-start | bytes 1671176 | tf_op jit(solution)/shard_map/ppermute | solution.py:81
  40.4 0.0 collective-permute-done.12.refs_8_
  40.4 4.6 %collective-permute-start.13 = (bf16[1088,256]{1,0:T(8,128)(2,1)S(1)}, bf16[1088,256]{1,0:T(8,128)(2,1)S(1)}, u32[]{:S(2)}, u32[]{:S(2)}) collective-permute-start(bf16[1088,256]{1,0:T(8,128)(2,1)S(1)} %collective-permute-done.12.refs_8_), channel_id=1, source_target_pairs={{0,64},{8,456},{16,80},{24,472},{32,96},{40,488},{48,112},{56,504}... | collective-permute-start | bytes 1671176 | tf_op jit(solution)/shard_map/ppermute | solution.py:81
  44.9 1.8 %collective-permute-done.2.refs_2_ = bf16[272,1024]{1,0:T(8,128)(2,1)S(1)} collective-permute-done((bf16[272,1024]{1,0:T(8,128)(2,1)S(1)}, bf16[272,1024]{1,0:T(8,128)(2,1)S(1)}, u32[]{:S(2)}, u32[]{:S(2)}) %collective-permute-start.2) | collective-permute-done | bytes 557088 | tf_op jit(solution)/shard_map/ppermute | solution.py:81
  46.7 5.3 %collective-permute-start.3 = (bf16[272,1024]{1,0:T(8,128)(2,1)S(1)}, bf16[272,1024]{1,0:T(8,128)(2,1)S(1)}, u32[]{:S(2)}, u32[]{:S(2)}) collective-permute-start(bf16[272,1024]{1,0:T(8,128)(2,1)S(1)} %collective-permute-done.2.refs_2_), channel_id=1, source_target_pairs={{0,1},{1,2},{2,3},{3,4},{4,5},{5,6},{6,7},{7,0},{8,15},{9,8},{10,9... | collective-permute-start | bytes 1671176 | tf_op jit(solution)/shard_map/ppermute | solution.py:81
  52.1 0.3 collective-permute-done.6.refs_12_
  52.3 1.9 %collective-permute-start.7 = (bf16[1088,256]{1,0:T(8,128)(2,1)S(1)}, bf16[1088,256]{1,0:T(8,128)(2,1)S(1)}, u32[]{:S(2)}, u32[]{:S(2)}) collective-permute-start(bf16[1088,256]{1,0:T(8,128)(2,1)S(1)} %collective-permute-done.6.refs_12_), channel_id=1, source_target_pairs={{64,0},{456,8},{80,16},{472,24},{96,32},{488,40},{112,48},{504,56}... | collective-permute-start | bytes 1671176 | tf_op jit(solution)/shard_map/ppermute | solution.py:81
  54.3 1.9 %collective-permute-start.11 = (bf16[272,1024]{1,0:T(8,128)(2,1)S(1)}, bf16[272,1024]{1,0:T(8,128)(2,1)S(1)}, u32[]{:S(2)}, u32[]{:S(2)}) collective-permute-start(bf16[272,1024]{1,0:T(8,128)(2,1)S(1)} %collective-permute-done.10.refs_5_), channel_id=1, source_target_pairs={{1,0},{2,1},{3,2},{4,3},{5,4},{6,5},{7,6},{0,7},{15,8},{8,9},{9,10... | collective-permute-start | bytes 1671176 | tf_op jit(solution)/shard_map/ppermute | solution.py:81
  56.2 0.0 collective-permute-done.13.refs_9_
  56.2 4.9 %collective-permute-start.14 = (bf16[1088,256]{1,0:T(8,128)(2,1)S(1)}, bf16[1088,256]{1,0:T(8,128)(2,1)S(1)}, u32[]{:S(2)}, u32[]{:S(2)}) collective-permute-start(bf16[1088,256]{1,0:T(8,128)(2,1)S(1)} %collective-permute-done.13.refs_9_), channel_id=1, source_target_pairs={{0,64},{8,456},{16,80},{24,472},{32,96},{40,488},{48,112},{56,504}... | collective-permute-start | bytes 1671176 | tf_op jit(solution)/shard_map/ppermute | solution.py:81
  61.1 2.0 %collective-permute-done.3.refs_3_ = bf16[272,1024]{1,0:T(8,128)(2,1)S(1)} collective-permute-done((bf16[272,1024]{1,0:T(8,128)(2,1)S(1)}, bf16[272,1024]{1,0:T(8,128)(2,1)S(1)}, u32[]{:S(2)}, u32[]{:S(2)}) %collective-permute-start.3) | collective-permute-done | bytes 557088 | tf_op jit(solution)/shard_map/ppermute | solution.py:81
  63.1 5.3 %collective-permute-start.4 = (bf16[272,1024]{1,0:T(8,128)(2,1)S(1)}, bf16[272,1024]{1,0:T(8,128)(2,1)S(1)}, u32[]{:S(2)}, u32[]{:S(2)}) collective-permute-start(bf16[272,1024]{1,0:T(8,128)(2,1)S(1)} %collective-permute-done.3.refs_3_), channel_id=1, source_target_pairs={{0,1},{1,2},{2,3},{3,4},{4,5},{5,6},{6,7},{7,0},{8,15},{9,8},{10,9... | collective-permute-start | bytes 1671176 | tf_op jit(solution)/shard_map/ppermute | solution.py:84
  68.4 0.6 collective-permute-done.7.refs_13_
  69.0 1.9 %collective-permute-start.8 = (bf16[1088,256]{1,0:T(8,128)(2,1)S(1)}, bf16[1088,256]{1,0:T(8,128)(2,1)S(1)}, u32[]{:S(2)}, u32[]{:S(2)}) collective-permute-start(bf16[1088,256]{1,0:T(8,128)(2,1)S(1)} %collective-permute-done.7.refs_13_), channel_id=1, source_target_pairs={{64,0},{456,8},{80,16},{472,24},{96,32},{488,40},{112,48},{504,56}... | collective-permute-start | bytes 1671176 | tf_op jit(solution)/shard_map/ppermute | solution.py:84
  70.9 0.0 collective-permute-done.11.refs_6_
  70.9 1.8 %collective-permute-done.14.refs_10_ = bf16[1088,256]{1,0:T(8,128)(2,1)S(1)} collective-permute-done((bf16[1088,256]{1,0:T(8,128)(2,1)S(1)}, bf16[1088,256]{1,0:T(8,128)(2,1)S(1)}, u32[]{:S(2)}, u32[]{:S(2)}) %collective-permute-start.14) | collective-permute-done | bytes 557088 | tf_op jit(solution)/shard_map/ppermute | solution.py:81
  72.7 3.6 %shard_map.114 = (f32[256,256]{1,0:T(8,128)S(1)}, f32[16,1024]{1,0:T(8,128)S(1)}, bf16[256,1024]{1,0:T(8,128)(2,1)S(1)}, bf16[1024,256]{1,0:T(8,128)(2,1)S(1)}) custom-call(s32[3]{0:T(128)S(1)} %pad_add_fusion.pos_ref, bf16[272,1024]{1,0:T(8,128)(2,1)S(1)} %pad_maximum_fusion.refs_0_, bf16[272,1024]{1,0:T(8,128)(2,1)S(1)} %collective-permute-done.1.refs_1_, ...), custom_call_target="tpu_custom_call" | custom-call | flops 1073741824 | bytes 7798784 | tf_op jit(solution)/shard_map/pallas_call | solution.py:277
  76.3 4.0 %collective-permute-done.4.t_ref = bf16[272,1024]{1,0:T(8,128)(2,1)S(1)} collective-permute-done((bf16[272,1024]{1,0:T(8,128)(2,1)S(1)}, bf16[272,1024]{1,0:T(8,128)(2,1)S(1)}, u32[]{:S(2)}, u32[]{:S(2)}) %collective-permute-start.4) | collective-permute-done | bytes 557088 | tf_op jit(solution)/shard_map/ppermute | solution.py:84
  80.3 6.0 %collective-permute-done.8.w_ref = bf16[1088,256]{1,0:T(8,128)(2,1)S(1)} collective-permute-done((bf16[1088,256]{1,0:T(8,128)(2,1)S(1)}, bf16[1088,256]{1,0:T(8,128)(2,1)S(1)}, u32[]{:S(2)}, u32[]{:S(2)}) %collective-permute-start.8) | collective-permute-done | bytes 557088 | tf_op jit(solution)/shard_map/ppermute | solution.py:84
  86.2 0.0 copy-start.6
  86.3 1.4 shard_map.115
  87.7 6.0 %collective-permute-start.15 = (f32[128,256]{1,0:T(8,128)S(1)}, f32[128,256]{1,0:T(8,128)S(1)}, u32[]{:S(2)}, u32[]{:S(2)}) collective-permute-start(f32[128,256]{1,0:T(8,128)S(1)} %get-tuple-element.29), channel_id=1, source_target_pairs={{0,8},{8,0},{16,24},{24,16},{32,40},{40,32},{48,56},{56,48},{64,72... | collective-permute-start | bytes 393224 | tf_op jit(solution)/shard_map/ppermute | solution.py:365
  93.6 1.0 collective-permute-done.15.got_ref
  94.6 3.9 %shard_map.116 = (bf16[8,80,128]{2,1,0:T(8,128)(2,1)S(1)}, f32[128,128]{1,0:T(8,128)S(1)}, f32[128,128]{1,0:T(8,128)S(1)}) custom-call(s32[1,8]{1,0:T(1,128)S(1)} %copy-done.6, f32[128,256]{1,0:T(8,128)S(1)} %get-tuple-element.28.own_ref, f32[128,256]{1,0:T(8,128)S(1)} %collective-permute-done.15.got_ref, ...), custom_call_target="tpu_custom_call" | custom-call | tf_op jit(solution)/shard_map/pallas_call | solution.py:277
  98.5 11.5 %all_to_all.25.pack_ref = bf16[8,80,128]{2,1,0:T(8,128)(2,1)S(1)} all-to-all(bf16[8,80,128]{2,1,0:T(8,128)(2,1)S(1)} %get-tuple-element.31), channel_id=1, replica_groups=mesh['row'=64,'col'=8] {'col'}, dimensions={0} | all-to-all | bytes 327680 | tf_op jit(solution)/shard_map/all_to_all | solution.py:378
  110.0 0.9 shard_map.117
  111.0 11.5 %all_to_all.26.in_ref = bf16[8,72,256]{2,1,0:T(8,128)(2,1)S(1)} all-to-all(bf16[8,72,256]{2,1,0:T(8,128)(2,1)S(1)} %shard_map.117), channel_id=1, replica_groups={{0,8,16,24,32,40,48,56},{64,72,80,88,96,104,112,120},{128,136,144,152,1..., dimensions={0} | all-to-all | bytes 589824 | tf_op jit(solution)/shard_map/all_to_all | solution.py:384
  122.5 14.4 %all_to_all.27.in_ref = bf16[8,72,256]{2,1,0:T(8,128)(2,1)S(1)} all-to-all(bf16[8,72,256]{2,1,0:T(8,128)(2,1)S(1)} %shard_map.118), channel_id=1, replica_groups={{0,64,128,192,256,320,384,448},{8,72,136,200,264,328,392,456},{16,80,14..., dimensions={0} | all-to-all | bytes 589824 | tf_op jit(solution)/shard_map/all_to_all | solution.py:386
  136.9 12.2 %all_to_all.28.in_ref = bf16[8,72,256]{2,1,0:T(8,128)(2,1)S(1)} all-to-all(bf16[8,72,256]{2,1,0:T(8,128)(2,1)S(1)} %shard_map.119), channel_id=1, replica_groups={{0,8,16,24,32,40,48,56},{64,72,80,88,96,104,112,120},{128,136,144,152,1..., dimensions={0} | all-to-all | bytes 589824 | tf_op jit(solution)/shard_map/all_to_all | solution.py:388
  149.1 0.8 shard_map.120
  (18 shorter events, 0.2 us)
Async XLA Ops:
  2.3 5.1 %copy-start = (bf16[128,2048]{1,0:T(8,128)(2,1)S(1)}, bf16[128,2048]{1,0:T(8,128)(2,1)}, u32[]{:S(2)}) copy-start(bf16[128,2048]{1,0:T(8,128)(2,1)} %t_ref.5) | copy-start | bytes 1572868
  2.4 20.5 %all-to-all-start = ((bf16[4,256,256]{2,1,0:T(8,128)(2,1)}), bf16[4,256,256]{2,1,0:T(8,128)(2,1)S(1)}, u32[]{:S(2)}, u32[]{:S(2)}) async-start(bf16[4,256,256]{2,1,0:T(8,128)(2,1)} %broadcast_in_dim.3), calls=%async_computation | async-start | bytes 1048576 | tf_op jit(solution)/shard_map/all_to_all | solution.py:325
  7.3 8.3 %copy-start.3 = (bf16[2048,64]{0,1:T(8,128)(2,1)S(1)}, bf16[2048,64]{0,1:T(8,128)(2,1)}, u32[]{:S(2)}) copy-start(bf16[2048,64]{0,1:T(8,128)(2,1)} %param.14) | copy-start | bytes 786436
  8.1 8.6 %collective-permute-start = (bf16[128,1024]{1,0:T(8,128)(2,1)S(1)}, bf16[128,1024]{1,0:T(8,128)(2,1)S(1)}, u32[]{:S(2)}, u32[]{:S(2)}) collective-permute-start(bf16[128,1024]{1,0:T(8,128)(2,1)S(1)} %get-tuple-element.21), channel_id=1, source_target_pairs={{0,8},{8,0},{16,24},{24,16},{32,40},{40,32},{48,56},{56,48},{64,72... | collective-permute-start | bytes 786440 | tf_op jit(solution)/shard_map/ppermute | solution.py:317
  16.8 15.1 %collective-permute-start.1 = (bf16[272,1024]{1,0:T(8,128)(2,1)S(1)}, bf16[272,1024]{1,0:T(8,128)(2,1)S(1)}, u32[]{:S(2)}, u32[]{:S(2)}) collective-permute-start(bf16[272,1024]{1,0:T(8,128)(2,1)S(1)} %pad_maximum_fusion.refs_0_), channel_id=1, source_target_pairs={{0,1},{1,2},{2,3},{3,4},{4,5},{5,6},{6,7},{7,0},{8,15},{9,8},{10,9... | collective-permute-start | bytes 1671176 | tf_op jit(solution)/shard_map/ppermute | solution.py:81
  22.9 13.6 %collective-permute-start.5 = (bf16[1088,256]{1,0:T(8,128)(2,1)S(1)}, bf16[1088,256]{1,0:T(8,128)(2,1)S(1)}, u32[]{:S(2)}, u32[]{:S(2)}) collective-permute-start(bf16[1088,256]{1,0:T(8,128)(2,1)S(1)} %pad.4.refs_7_), channel_id=1, source_target_pairs={{64,0},{456,8},{80,16},{472,24},{96,32},{488,40},{112,48},{504,56}... | collective-permute-start | bytes 1671176 | tf_op jit(solution)/shard_map/ppermute | solution.py:81
  26.1 12.3 %collective-permute-start.9 = (bf16[272,1024]{1,0:T(8,128)(2,1)S(1)}, bf16[272,1024]{1,0:T(8,128)(2,1)S(1)}, u32[]{:S(2)}, u32[]{:S(2)}) collective-permute-start(bf16[272,1024]{1,0:T(8,128)(2,1)S(1)} %pad_maximum_fusion.refs_0_), channel_id=1, source_target_pairs={{1,0},{2,1},{3,2},{4,3},{5,4},{6,5},{7,6},{0,7},{15,8},{8,9},{9,10... | collective-permute-start | bytes 1671176 | tf_op jit(solution)/shard_map/ppermute | solution.py:81
  28.1 12.3 %collective-permute-start.12 = (bf16[1088,256]{1,0:T(8,128)(2,1)S(1)}, bf16[1088,256]{1,0:T(8,128)(2,1)S(1)}, u32[]{:S(2)}, u32[]{:S(2)}) collective-permute-start(bf16[1088,256]{1,0:T(8,128)(2,1)S(1)} %pad.4.refs_7_), channel_id=1, source_target_pairs={{0,64},{8,456},{16,80},{24,472},{32,96},{40,488},{48,112},{56,504}... | collective-permute-start | bytes 1671176 | tf_op jit(solution)/shard_map/ppermute | solution.py:81
  31.9 14.8 %collective-permute-start.2 = (bf16[272,1024]{1,0:T(8,128)(2,1)S(1)}, bf16[272,1024]{1,0:T(8,128)(2,1)S(1)}, u32[]{:S(2)}, u32[]{:S(2)}) collective-permute-start(bf16[272,1024]{1,0:T(8,128)(2,1)S(1)} %collective-permute-done.1.refs_1_), channel_id=1, source_target_pairs={{0,1},{1,2},{2,3},{3,4},{4,5},{5,6},{6,7},{7,0},{8,15},{9,8},{10,9... | collective-permute-start | bytes 1671176 | tf_op jit(solution)/shard_map/ppermute | solution.py:81
  36.5 15.8 %collective-permute-start.6 = (bf16[1088,256]{1,0:T(8,128)(2,1)S(1)}, bf16[1088,256]{1,0:T(8,128)(2,1)S(1)}, u32[]{:S(2)}, u32[]{:S(2)}) collective-permute-start(bf16[1088,256]{1,0:T(8,128)(2,1)S(1)} %collective-permute-done.5.refs_11_), channel_id=1, source_target_pairs={{64,0},{456,8},{80,16},{472,24},{96,32},{488,40},{112,48},{504,56}... | collective-permute-start | bytes 1671176 | tf_op jit(solution)/shard_map/ppermute | solution.py:81
  38.4 15.8 %collective-permute-start.10 = (bf16[272,1024]{1,0:T(8,128)(2,1)S(1)}, bf16[272,1024]{1,0:T(8,128)(2,1)S(1)}, u32[]{:S(2)}, u32[]{:S(2)}) collective-permute-start(bf16[272,1024]{1,0:T(8,128)(2,1)S(1)} %collective-permute-done.9.refs_4_), channel_id=1, source_target_pairs={{1,0},{2,1},{3,2},{4,3},{5,4},{6,5},{7,6},{0,7},{15,8},{8,9},{9,10... | collective-permute-start | bytes 1671176 | tf_op jit(solution)/shard_map/ppermute | solution.py:81
  40.4 15.8 %collective-permute-start.13 = (bf16[1088,256]{1,0:T(8,128)(2,1)S(1)}, bf16[1088,256]{1,0:T(8,128)(2,1)S(1)}, u32[]{:S(2)}, u32[]{:S(2)}) collective-permute-start(bf16[1088,256]{1,0:T(8,128)(2,1)S(1)} %collective-permute-done.12.refs_8_), channel_id=1, source_target_pairs={{0,64},{8,456},{16,80},{24,472},{32,96},{40,488},{48,112},{56,504}... | collective-permute-start | bytes 1671176 | tf_op jit(solution)/shard_map/ppermute | solution.py:81
  46.7 16.4 %collective-permute-start.3 = (bf16[272,1024]{1,0:T(8,128)(2,1)S(1)}, bf16[272,1024]{1,0:T(8,128)(2,1)S(1)}, u32[]{:S(2)}, u32[]{:S(2)}) collective-permute-start(bf16[272,1024]{1,0:T(8,128)(2,1)S(1)} %collective-permute-done.2.refs_2_), channel_id=1, source_target_pairs={{0,1},{1,2},{2,3},{3,4},{4,5},{5,6},{6,7},{7,0},{8,15},{9,8},{10,9... | collective-permute-start | bytes 1671176 | tf_op jit(solution)/shard_map/ppermute | solution.py:81
  52.3 16.7 %collective-permute-start.7 = (bf16[1088,256]{1,0:T(8,128)(2,1)S(1)}, bf16[1088,256]{1,0:T(8,128)(2,1)S(1)}, u32[]{:S(2)}, u32[]{:S(2)}) collective-permute-start(bf16[1088,256]{1,0:T(8,128)(2,1)S(1)} %collective-permute-done.6.refs_12_), channel_id=1, source_target_pairs={{64,0},{456,8},{80,16},{472,24},{96,32},{488,40},{112,48},{504,56}... | collective-permute-start | bytes 1671176 | tf_op jit(solution)/shard_map/ppermute | solution.py:81
  54.3 16.6 %collective-permute-start.11 = (bf16[272,1024]{1,0:T(8,128)(2,1)S(1)}, bf16[272,1024]{1,0:T(8,128)(2,1)S(1)}, u32[]{:S(2)}, u32[]{:S(2)}) collective-permute-start(bf16[272,1024]{1,0:T(8,128)(2,1)S(1)} %collective-permute-done.10.refs_5_), channel_id=1, source_target_pairs={{1,0},{2,1},{3,2},{4,3},{5,4},{6,5},{7,6},{0,7},{15,8},{8,9},{9,10... | collective-permute-start | bytes 1671176 | tf_op jit(solution)/shard_map/ppermute | solution.py:81
  56.2 16.5 %collective-permute-start.14 = (bf16[1088,256]{1,0:T(8,128)(2,1)S(1)}, bf16[1088,256]{1,0:T(8,128)(2,1)S(1)}, u32[]{:S(2)}, u32[]{:S(2)}) collective-permute-start(bf16[1088,256]{1,0:T(8,128)(2,1)S(1)} %collective-permute-done.13.refs_9_), channel_id=1, source_target_pairs={{0,64},{8,456},{16,80},{24,472},{32,96},{40,488},{48,112},{56,504}... | collective-permute-start | bytes 1671176 | tf_op jit(solution)/shard_map/ppermute | solution.py:81
  63.1 17.2 %collective-permute-start.4 = (bf16[272,1024]{1,0:T(8,128)(2,1)S(1)}, bf16[272,1024]{1,0:T(8,128)(2,1)S(1)}, u32[]{:S(2)}, u32[]{:S(2)}) collective-permute-start(bf16[272,1024]{1,0:T(8,128)(2,1)S(1)} %collective-permute-done.3.refs_3_), channel_id=1, source_target_pairs={{0,1},{1,2},{2,3},{3,4},{4,5},{5,6},{6,7},{7,0},{8,15},{9,8},{10,9... | collective-permute-start | bytes 1671176 | tf_op jit(solution)/shard_map/ppermute | solution.py:84
  69.0 17.2 %collective-permute-start.8 = (bf16[1088,256]{1,0:T(8,128)(2,1)S(1)}, bf16[1088,256]{1,0:T(8,128)(2,1)S(1)}, u32[]{:S(2)}, u32[]{:S(2)}) collective-permute-start(bf16[1088,256]{1,0:T(8,128)(2,1)S(1)} %collective-permute-done.7.refs_13_), channel_id=1, source_target_pairs={{64,0},{456,8},{80,16},{472,24},{96,32},{488,40},{112,48},{504,56}... | collective-permute-start | bytes 1671176 | tf_op jit(solution)/shard_map/ppermute | solution.py:84
  86.2 8.4 %copy-start.1 = (bf16[128,2048]{1,0:T(8,128)(2,1)S(1)}, bf16[128,2048]{1,0:T(8,128)(2,1)}, u32[]{:S(2)}) copy-start(bf16[128,2048]{1,0:T(8,128)(2,1)} %q_ref.1) | copy-start | bytes 1572868
  86.2 8.4 %copy-start.2 = (bf16[128,2048]{1,0:T(8,128)(2,1)S(1)}, bf16[128,2048]{1,0:T(8,128)(2,1)}, u32[]{:S(2)}) copy-start(bf16[128,2048]{1,0:T(8,128)(2,1)} %p_ref.1) | copy-start | bytes 1572868
  86.2 8.4 %copy-start.4 = (bf16[64,128]{1,0:T(8,128)(2,1)S(1)}, bf16[64,128]{1,0:T(8,128)(2,1)}, u32[]{:S(2)}) copy-start(bf16[64,128]{1,0:T(8,128)(2,1)} %upk_ref.1) | copy-start | bytes 49156
  86.2 8.4 %copy-start.5 = (bf16[64,128]{1,0:T(8,128)(2,1)S(1)}, bf16[64,128]{1,0:T(8,128)(2,1)}, u32[]{:S(2)}) copy-start(bf16[64,128]{1,0:T(8,128)(2,1)} %upv_ref.1) | copy-start | bytes 49156
  86.2 8.4 %copy-start.6 = (s32[1,8]{1,0:T(1,128)S(1)}, s32[1,8]{1,0:T(1,128)}, u32[]{:S(2)}) copy-start(s32[1,8]{1,0:T(1,128)} %lengths_ref.3) | copy-start | bytes 100
  87.7 6.9 %collective-permute-start.15 = (f32[128,256]{1,0:T(8,128)S(1)}, f32[128,256]{1,0:T(8,128)S(1)}, u32[]{:S(2)}, u32[]{:S(2)}) collective-permute-start(f32[128,256]{1,0:T(8,128)S(1)} %get-tuple-element.29), channel_id=1, source_target_pairs={{0,8},{8,0},{16,24},{24,16},{32,40},{40,32},{48,56},{56,48},{64,72... | collective-permute-start | bytes 393224 | tf_op jit(solution)/shard_map/ppermute | solution.py:365

commit v15 on v14

--- a/solution.py
+++ b/solution.py
@@ -67,6 +67,7 @@
 
 
 STEPS = (0, 1, 2, 3, -1, -2, -3, 4)
+W_LATE = (4, 3)
 
 
 def rings_of(owns, axes, fores, afts):
@@ -90,17 +91,19 @@
 
 
 def project_kernel(pos_ref, *refs):
-    t_refs, w_refs, refs = refs[:7], refs[7:14], refs[14:]
+    t_refs, w_refs, refs = refs[:7], refs[7:13], refs[13:]
     total_ref, low_ref, t_left_ref, w_left_ref, w_scr, sem = refs
     n = w_scr.shape[0]
     copies = [
-        pltpu.make_async_copy(part, w_scr.at[block_at(pos_ref, 1, STEPS[j], n)], sem.at[j])
-        for j, part in enumerate(w_refs)
+        pltpu.make_async_copy(part, w_scr.at[block_at(pos_ref, 1, step, n)], sem.at[j])
+        for j, (part, step) in enumerate(zip(w_refs, STEPS[:3] + STEPS[4:7]))
     ]
     for c in copies:
         c.start()
-    t_far, w_far = (block_at(pos_ref, axis, STEPS[7], n) for axis in range(2))
-    w_scr[w_far] = jnp.zeros(w_scr.shape[1:], BF)
+    t_far = block_at(pos_ref, 0, STEPS[7], n)
+    w_late = [block_at(pos_ref, 1, step, n) for step in W_LATE]
+    for k in w_late:
+        w_scr[k] = jnp.zeros(w_scr.shape[1:], BF)
     t_left_ref[...] = jnp.zeros(t_left_ref.shape, BF)
     rows = total_ref.shape[0]
     low = jnp.zeros(low_ref.shape, F32)
@@ -115,22 +118,25 @@
         k = block_at(pos_ref, 0, STEPS[j], n)
         total = total + mm(t_ref[pl.ds(0, rows)], w_scr[k, pl.ds(0, deep)], NN)
 
-        @pl.when(k == w_far)
-        def _():
-            t_left_ref[...] = t_ref[pl.ds(0, rows)]
+        for i in range(2):
+
+            @pl.when(k == w_late[i])
+            def _():
+                t_left_ref[i] = t_ref[pl.ds(0, rows)]
 
     total_ref[...] = total
     w_left_ref[...] = w_scr[t_far, pl.ds(0, deep)]
 
 
 def finish_kernel(
-    pos_ref, t_ref, w_ref, total_ref, low_ref, t_left_ref, w_left_ref,
+    pos_ref, t_ref, w_ref, w3_ref, total_ref, low_ref, t_left_ref, w_left_ref,
     own_ref, other_ref, low_half_ref,
-    t_scr, w_scr, total_scr, low_scr, t_left_scr, w_left_scr, sem,
+    t_scr, w_scr, w3_scr, total_scr, low_scr, t_left_scr, w_left_scr, sem,
 ):
     pairs = [
         (t_ref, t_scr),
         (w_ref, w_scr),
+        (w3_ref, w3_scr),
         (total_ref, total_scr),
         (low_ref, low_scr),
         (t_left_ref, t_left_scr),
@@ -142,11 +148,14 @@
     for c in copies:
         c.wait()
     rows = own_ref.shape[0]
-    same = pos_ref[1] == pos_ref[2]
-    w_late = w_scr[pl.ds(0, w_left_scr.shape[0])]
-    w_match = jnp.where(same, w_late, w_left_scr[...])
+    t_far = block_at(pos_ref, 0, STEPS[7], 8)
+    late = [scr[pl.ds(0, w_left_scr.shape[0])] for scr in (w_scr, w3_scr)]
+    w_match = w_left_scr[...]
+    for step, w in zip(W_LATE, late):
+        w_match = jnp.where(t_far == block_at(pos_ref, 1, step, 8), w, w_match)
     total = total_scr[...] + mm(t_scr[pl.ds(0, 2 * rows)], w_match, NN)
-    total = total + mm(t_left_scr[...], w_late, NN)
+    for i in range(2):
+        total = total + mm(t_left_scr[i], late[i], NN)
     own_ref[...] = total[:rows]
     other_ref[...] = total[rows:]
     low = low_scr[...] + t_scr[pl.ds(2 * rows, low_scr.shape[0])].astype(F32)
@@ -334,13 +343,13 @@
     deep = feats // 2
     total, low_sum, t_left, w_left = call(
         project_kernel,
-        [((2 * rows, wide), F32), ((16, deep), F32), ((2 * rows, deep), BF), ((deep, wide), BF)],
-        [SMEM] + [VMEM] * 7 + [HBM] * 7,
+        [((2 * rows, wide), F32), ((16, deep), F32), ((2, 2 * rows, deep), BF), ((deep, wide), BF)],
+        [SMEM] + [VMEM] * 7 + [HBM] * 6,
         [VMEM] * 4,
-        pos, *t_parts[:7], *w_parts[:7],
+        pos, *t_parts[:7], *w_parts[:3], *w_parts[4:7],
         scratch=[
             pltpu.VMEM((8,) + w_own.shape, BF),
-            pltpu.SemaphoreType.DMA((7,)),
+            pltpu.SemaphoreType.DMA((6,)),
         ],
         mib=40,
         cost=(2 * 16 * rows * deep * wide, 14 * (pair.size + w_own.size)),
@@ -348,17 +357,18 @@
     own, other, low_half = call(
         finish_kernel,
         [((rows, wide), F32), ((rows, wide), F32), ((rows, 64), BF)],
-        [SMEM] + [HBM] * 6,
+        [SMEM] + [HBM] * 7,
         [VMEM] * 3,
-        pos, t_parts[7], w_parts[7], total, low_sum, t_left, w_left,
+        pos, t_parts[7], w_parts[7], w_parts[3], total, low_sum, t_left, w_left,
         scratch=[
             pltpu.VMEM(pair.shape, BF),
+            pltpu.VMEM(w_own.shape, BF),
             pltpu.VMEM(w_own.shape, BF),
             pltpu.VMEM(total.shape, F32),
             pltpu.VMEM(low_sum.shape, F32),
             pltpu.VMEM(t_left.shape, BF),
             pltpu.VMEM(w_left.shape, BF),
-            pltpu.SemaphoreType.DMA((6,)),
+            pltpu.SemaphoreType.DMA((7,)),
         ],
         mib=16,
     )

time: 151 us -> 151 us (level)
  blocking collectives: 49.5 us -> 53.2 us
  starting transfers between devices: 67.6 us -> 63.9 us
    ppermute x1, starting transfers between devices: 5.97 us -> 2.34 us  [on_device(): got = lax.ppermute(other, 'row', swap)]
    all_to_all x1, blocking collectives: 11.5 us -> 13.6 us  [on_device(): packs = lax.all_to_all(pack, 'col', 0, 0)]
    ppermute x12, waiting for transfers between devices: 6.44 us -> 4.7 us  [rings_of(): going[side] = [lax.ppermute(now[i], axes[i], ways[i]) for i in both]]
    ppermute x2, waiting for transfers between devices: 9.95 us -> 11.7 us  [rings_of(): lax.ppermute(going[i][i], axes[i], (fores, afts)[i][i])]
  transfers between devices with their start and end apart: 17 -> 17, of which waited for: 9 -> 8; matrix products, arithmetic and copies ran while one was open for 0% -> 0% of each run, Pallas kernels for 3% -> 3%
where the time goes in v15:
time: 151 us; the launch traced here: 150 us
  starting transfers between devices  63.9 us (42%)
  blocking collectives  53.2 us (35%)
  waiting for transfers between devices  18.1 us (12%)
  Pallas kernels  12.1 us (8%)
    ppermute x12, starting transfers between devices, rings_of(): going[side] = [lax.ppermute(now[i], axes[i], ways[i]) for i in both]  42 us
    all_to_all x1, blocking collectives, on_device(): lax.all_to_all(square, 'row', 0, 0, axis_index_groups=y_lines)  15.6 us
    all_to_all x1, blocking collectives, on_device(): packs = lax.all_to_all(pack, 'col', 0, 0)  13.6 us
    all_to_all x1, blocking collectives, on_device(): pieces = lax.all_to_all(summed, 'row', 0, 0, axis_index_groups=squares)  12.2 us
    pallas_call x9, Pallas kernels, call(): pl.pallas_call(kernel, out_shape=[jax.ShapeDtypeStruct(s, d) for s, d in...  12.1 us
    all_to_all x1, blocking collectives, on_device(): term_parts = lax.all_to_all(terms, 'row', 0, 0, axis_index_groups=squares)  11.8 us
    ppermute x2, waiting for transfers between devices, rings_of(): lax.ppermute(going[i][i], axes[i], (fores, afts)[i][i])  11.7 us
    ppermute x1, starting transfers between devices, on_device(): swapped = lax.ppermute(theirs, 'row', swap)  7.45 us
  transfers between devices with their start and end apart: 17, of which 8 were waited for; matrix products, arithmetic and copies ran while one was open for 0% of the time, Pallas kernels for 3%

profile of v15, /device:TPU:1, one launch (start us, length us, event | category | flops | bytes accessed | tf_op | source)
XLA Modules:
  0.0 150.1 jit_solution(4041630359425669096)
XLA Ops:
  0.6 0.9 pad_maximum_fusion.1
  1.6 0.0 copy-start.3
  1.6 0.8 broadcast_in_dim.3
  2.4 4.8 %all-to-all-start = ((bf16[4,256,256]{2,1,0:T(8,128)(2,1)}), bf16[4,256,256]{2,1,0:T(8,128)(2,1)S(1)}, u32[]{:S(2)}, u32[]{:S(2)}) async-start(bf16[4,256,256]{2,1,0:T(8,128)(2,1)} %broadcast_in_dim.3), calls=%async_computation | async-start | bytes 1048576 | tf_op jit(solution)/shard_map/all_to_all | solution.py:334
  7.3 0.1 pad_add_fusion.pos_ref
  7.3 0.7 shard_map.112
  8.1 7.4 %collective-permute-start = (bf16[128,1024]{1,0:T(8,128)(2,1)S(1)}, bf16[128,1024]{1,0:T(8,128)(2,1)S(1)}, u32[]{:S(2)}, u32[]{:S(2)}) collective-permute-start(bf16[128,1024]{1,0:T(8,128)(2,1)S(1)} %get-tuple-element.21), channel_id=1, source_target_pairs={{0,8},{8,0},{16,24},{24,16},{32,40},{40,32},{48,56},{56,48},{64,72... | collective-permute-start | bytes 786440 | tf_op jit(solution)/shard_map/ppermute | solution.py:326
  15.5 0.4 shard_map.113
  15.9 0.8 collective-permute-done
  16.7 6.1 %collective-permute-start.1 = (bf16[272,1024]{1,0:T(8,128)(2,1)S(1)}, bf16[272,1024]{1,0:T(8,128)(2,1)S(1)}, u32[]{:S(2)}, u32[]{:S(2)}) collective-permute-start(bf16[272,1024]{1,0:T(8,128)(2,1)S(1)} %pad_maximum_fusion.refs_0_), channel_id=1, source_target_pairs={{0,1},{1,2},{2,3},{3,4},{4,5},{5,6},{6,7},{7,0},{8,15},{9,8},{10,9... | collective-permute-start | bytes 1671176 | tf_op jit(solution)/shard_map/ppermute | solution.py:82
  22.8 0.0 all-to-all-done
  22.9 3.2 %collective-permute-start.5 = (bf16[1088,256]{1,0:T(8,128)(2,1)S(1)}, bf16[1088,256]{1,0:T(8,128)(2,1)S(1)}, u32[]{:S(2)}, u32[]{:S(2)}) collective-permute-start(bf16[1088,256]{1,0:T(8,128)(2,1)S(1)} %pad.4.refs_7_), channel_id=1, source_target_pairs={{64,0},{456,8},{80,16},{472,24},{96,32},{488,40},{112,48},{504,56}... | collective-permute-start | bytes 1671176 | tf_op jit(solution)/shard_map/ppermute | solution.py:82
  26.1 1.9 %collective-permute-start.12 = (bf16[272,1024]{1,0:T(8,128)(2,1)S(1)}, bf16[272,1024]{1,0:T(8,128)(2,1)S(1)}, u32[]{:S(2)}, u32[]{:S(2)}) collective-permute-start(bf16[272,1024]{1,0:T(8,128)(2,1)S(1)} %pad_maximum_fusion.refs_0_), channel_id=1, source_target_pairs={{1,0},{2,1},{3,2},{4,3},{5,4},{6,5},{7,6},{0,7},{15,8},{8,9},{9,10... | collective-permute-start | bytes 1671176 | tf_op jit(solution)/shard_map/ppermute | solution.py:82
  28.0 3.8 %collective-permute-start.9 = (bf16[1088,256]{1,0:T(8,128)(2,1)S(1)}, bf16[1088,256]{1,0:T(8,128)(2,1)S(1)}, u32[]{:S(2)}, u32[]{:S(2)}) collective-permute-start(bf16[1088,256]{1,0:T(8,128)(2,1)S(1)} %pad.4.refs_7_), channel_id=1, source_target_pairs={{0,64},{8,456},{16,80},{24,472},{32,96},{40,488},{48,112},{56,504}... | collective-permute-start | bytes 1671176 | tf_op jit(solution)/shard_map/ppermute | solution.py:82
  31.8 0.0 collective-permute-done.1.refs_1_
  31.8 4.6 %collective-permute-start.2 = (bf16[272,1024]{1,0:T(8,128)(2,1)S(1)}, bf16[272,1024]{1,0:T(8,128)(2,1)S(1)}, u32[]{:S(2)}, u32[]{:S(2)}) collective-permute-start(bf16[272,1024]{1,0:T(8,128)(2,1)S(1)} %collective-permute-done.1.refs_1_), channel_id=1, source_target_pairs={{0,1},{1,2},{2,3},{3,4},{4,5},{5,6},{6,7},{7,0},{8,15},{9,8},{10,9... | collective-permute-start | bytes 1671176 | tf_op jit(solution)/shard_map/ppermute | solution.py:82
  36.4 0.0 collective-permute-done.5.refs_10_
  36.4 1.9 %collective-permute-start.6 = (bf16[1088,256]{1,0:T(8,128)(2,1)S(1)}, bf16[1088,256]{1,0:T(8,128)(2,1)S(1)}, u32[]{:S(2)}, u32[]{:S(2)}) collective-permute-start(bf16[1088,256]{1,0:T(8,128)(2,1)S(1)} %collective-permute-done.5.refs_10_), channel_id=1, source_target_pairs={{64,0},{456,8},{80,16},{472,24},{96,32},{488,40},{112,48},{504,56}... | collective-permute-start | bytes 1671176 | tf_op jit(solution)/shard_map/ppermute | solution.py:82
  38.4 0.0 collective-permute-done.12.refs_4_
  38.4 1.9 %collective-permute-start.13 = (bf16[272,1024]{1,0:T(8,128)(2,1)S(1)}, bf16[272,1024]{1,0:T(8,128)(2,1)S(1)}, u32[]{:S(2)}, u32[]{:S(2)}) collective-permute-start(bf16[272,1024]{1,0:T(8,128)(2,1)S(1)} %collective-permute-done.12.refs_4_), channel_id=1, source_target_pairs={{1,0},{2,1},{3,2},{4,3},{5,4},{6,5},{7,6},{0,7},{15,8},{8,9},{9,10... | collective-permute-start | bytes 1671176 | tf_op jit(solution)/shard_map/ppermute | solution.py:82
  40.3 0.0 collective-permute-done.9.refs_8_
  40.3 4.6 %collective-permute-start.10 = (bf16[1088,256]{1,0:T(8,128)(2,1)S(1)}, bf16[1088,256]{1,0:T(8,128)(2,1)S(1)}, u32[]{:S(2)}, u32[]{:S(2)}) collective-permute-start(bf16[1088,256]{1,0:T(8,128)(2,1)S(1)} %collective-permute-done.9.refs_8_), channel_id=1, source_target_pairs={{0,64},{8,456},{16,80},{24,472},{32,96},{40,488},{48,112},{56,504}... | collective-permute-start | bytes 1671176 | tf_op jit(solution)/shard_map/ppermute | solution.py:82
  44.9 1.8 %collective-permute-done.2.refs_2_ = bf16[272,1024]{1,0:T(8,128)(2,1)S(1)} collective-permute-done((bf16[272,1024]{1,0:T(8,128)(2,1)S(1)}, bf16[272,1024]{1,0:T(8,128)(2,1)S(1)}, u32[]{:S(2)}, u32[]{:S(2)}) %collective-permute-start.2) | collective-permute-done | bytes 557088 | tf_op jit(solution)/shard_map/ppermute | solution.py:82
  46.7 5.3 %collective-permute-start.3 = (bf16[272,1024]{1,0:T(8,128)(2,1)S(1)}, bf16[272,1024]{1,0:T(8,128)(2,1)S(1)}, u32[]{:S(2)}, u32[]{:S(2)}) collective-permute-start(bf16[272,1024]{1,0:T(8,128)(2,1)S(1)} %collective-permute-done.2.refs_2_), channel_id=1, source_target_pairs={{0,1},{1,2},{2,3},{3,4},{4,5},{5,6},{6,7},{7,0},{8,15},{9,8},{10,9... | collective-permute-start | bytes 1671176 | tf_op jit(solution)/shard_map/ppermute | solution.py:82
  52.0 0.3 collective-permute-done.6.refs_11_
  52.3 1.9 %collective-permute-start.7 = (bf16[1088,256]{1,0:T(8,128)(2,1)S(1)}, bf16[1088,256]{1,0:T(8,128)(2,1)S(1)}, u32[]{:S(2)}, u32[]{:S(2)}) collective-permute-start(bf16[1088,256]{1,0:T(8,128)(2,1)S(1)} %collective-permute-done.6.refs_11_), channel_id=1, source_target_pairs={{64,0},{456,8},{80,16},{472,24},{96,32},{488,40},{112,48},{504,56}... | collective-permute-start | bytes 1671176 | tf_op jit(solution)/shard_map/ppermute | solution.py:82
  54.2 0.0 collective-permute-done.13.refs_5_
  54.2 1.9 %collective-permute-start.14 = (bf16[272,1024]{1,0:T(8,128)(2,1)S(1)}, bf16[272,1024]{1,0:T(8,128)(2,1)S(1)}, u32[]{:S(2)}, u32[]{:S(2)}) collective-permute-start(bf16[272,1024]{1,0:T(8,128)(2,1)S(1)} %collective-permute-done.13.refs_5_), channel_id=1, source_target_pairs={{1,0},{2,1},{3,2},{4,3},{5,4},{6,5},{7,6},{0,7},{15,8},{8,9},{9,10... | collective-permute-start | bytes 1671176 | tf_op jit(solution)/shard_map/ppermute | solution.py:82
  56.1 0.0 collective-permute-done.10.refs_9_
  56.1 4.9 %collective-permute-start.11 = (bf16[1088,256]{1,0:T(8,128)(2,1)S(1)}, bf16[1088,256]{1,0:T(8,128)(2,1)S(1)}, u32[]{:S(2)}, u32[]{:S(2)}) collective-permute-start(bf16[1088,256]{1,0:T(8,128)(2,1)S(1)} %collective-permute-done.10.refs_9_), channel_id=1, source_target_pairs={{0,64},{8,456},{16,80},{24,472},{32,96},{40,488},{48,112},{56,504}... | collective-permute-start | bytes 1671176 | tf_op jit(solution)/shard_map/ppermute | solution.py:82
  61.0 2.0 %collective-permute-done.3.refs_3_ = bf16[272,1024]{1,0:T(8,128)(2,1)S(1)} collective-permute-done((bf16[272,1024]{1,0:T(8,128)(2,1)S(1)}, bf16[272,1024]{1,0:T(8,128)(2,1)S(1)}, u32[]{:S(2)}, u32[]{:S(2)}) %collective-permute-start.3) | collective-permute-done | bytes 557088 | tf_op jit(solution)/shard_map/ppermute | solution.py:82
  63.1 5.3 %collective-permute-start.4 = (bf16[272,1024]{1,0:T(8,128)(2,1)S(1)}, bf16[272,1024]{1,0:T(8,128)(2,1)S(1)}, u32[]{:S(2)}, u32[]{:S(2)}) collective-permute-start(bf16[272,1024]{1,0:T(8,128)(2,1)S(1)} %collective-permute-done.3.refs_3_), channel_id=1, source_target_pairs={{0,1},{1,2},{2,3},{3,4},{4,5},{5,6},{6,7},{7,0},{8,15},{9,8},{10,9... | collective-permute-start | bytes 1671176 | tf_op jit(solution)/shard_map/ppermute | solution.py:85
  68.4 0.6 collective-permute-done.7.refs_12_
  68.9 1.9 %collective-permute-start.8 = (bf16[1088,256]{1,0:T(8,128)(2,1)S(1)}, bf16[1088,256]{1,0:T(8,128)(2,1)S(1)}, u32[]{:S(2)}, u32[]{:S(2)}) collective-permute-start(bf16[1088,256]{1,0:T(8,128)(2,1)S(1)} %collective-permute-done.7.refs_12_), channel_id=1, source_target_pairs={{64,0},{456,8},{80,16},{472,24},{96,32},{488,40},{112,48},{504,56}... | collective-permute-start | bytes 1671176 | tf_op jit(solution)/shard_map/ppermute | solution.py:85
  70.9 3.6 %shard_map.114 = (f32[256,256]{1,0:T(8,128)S(1)}, f32[16,1024]{1,0:T(8,128)S(1)}, bf16[2,256,1024]{2,1,0:T(8,128)(2,1)S(1)}, bf16[1024,256]{1,0:T(8,128)(2,1)S(1)}) custom-call(s32[3]{0:T(128)S(1)} %pad_add_fusion.pos_ref, bf16[272,1024]{1,0:T(8,128)(2,1)S(1)} %pad_maximum_fusion.refs_0_, bf16[272,1024]{1,0:T(8,128)(2,1)S(1)} %collective-permute-done.1.refs_1_, ...), custom_call_target="tpu_custom_call" | custom-call | flops 1073741824 | bytes 7798784 | tf_op jit(solution)/shard_map/pallas_call | solution.py:286
  74.5 5.7 %collective-permute-done.4.t_ref = bf16[272,1024]{1,0:T(8,128)(2,1)S(1)} collective-permute-done((bf16[272,1024]{1,0:T(8,128)(2,1)S(1)}, bf16[272,1024]{1,0:T(8,128)(2,1)S(1)}, u32[]{:S(2)}, u32[]{:S(2)}) %collective-permute-start.4) | collective-permute-done | bytes 557088 | tf_op jit(solution)/shard_map/ppermute | solution.py:85
  80.2 6.0 %collective-permute-done.8.w_ref = bf16[1088,256]{1,0:T(8,128)(2,1)S(1)} collective-permute-done((bf16[1088,256]{1,0:T(8,128)(2,1)S(1)}, bf16[1088,256]{1,0:T(8,128)(2,1)S(1)}, u32[]{:S(2)}, u32[]{:S(2)}) %collective-permute-start.8) | collective-permute-done | bytes 557088 | tf_op jit(solution)/shard_map/ppermute | solution.py:85
  86.2 0.0 copy-start.6
  86.2 1.6 %shard_map.115 = (f32[128,256]{1,0:T(8,128)S(1)}, f32[128,256]{1,0:T(8,128)S(1)}, bf16[128,64]{1,0:T(8,128)(2,1)S(1)}) custom-call(s32[3]{0:T(128)S(1)} %pad_add_fusion.pos_ref, bf16[272,1024]{1,0:T(8,128)(2,1)S(1)} %collective-permute-done.4.t_ref, bf16[1088,256]{1,0:T(8,128)(2,1)S(1)} %collective-permute-done.8.w_ref, ...), custom_call_target="tpu_custom_call" | custom-call | tf_op jit(solution)/shard_map/pallas_call | solution.py:286
  87.9 2.3 %collective-permute-start.15 = (f32[128,256]{1,0:T(8,128)S(1)}, f32[128,256]{1,0:T(8,128)S(1)}, u32[]{:S(2)}, u32[]{:S(2)}) collective-permute-start(f32[128,256]{1,0:T(8,128)S(1)} %get-tuple-element.29), channel_id=1, source_target_pairs={{0,8},{8,0},{16,24},{24,16},{32,40},{40,32},{48,56},{56,48},{64,72... | collective-permute-start | bytes 393224 | tf_op jit(solution)/shard_map/ppermute | solution.py:375
  90.2 1.0 collective-permute-done.15.got_ref
  91.2 3.9 %shard_map.116 = (bf16[8,80,128]{2,1,0:T(8,128)(2,1)S(1)}, f32[128,128]{1,0:T(8,128)S(1)}, f32[128,128]{1,0:T(8,128)S(1)}) custom-call(s32[1,8]{1,0:T(1,128)S(1)} %copy-done.6, f32[128,256]{1,0:T(8,128)S(1)} %get-tuple-element.28.own_ref, f32[128,256]{1,0:T(8,128)S(1)} %collective-permute-done.15.got_ref, ...), custom_call_target="tpu_custom_call" | custom-call | tf_op jit(solution)/shard_map/pallas_call | solution.py:286
  95.1 13.6 %all_to_all.25.pack_ref = bf16[8,80,128]{2,1,0:T(8,128)(2,1)S(1)} all-to-all(bf16[8,80,128]{2,1,0:T(8,128)(2,1)S(1)} %get-tuple-element.31), channel_id=1, replica_groups=mesh['row'=64,'col'=8] {'col'}, dimensions={0} | all-to-all | bytes 327680 | tf_op jit(solution)/shard_map/all_to_all | solution.py:388
  108.7 0.9 shard_map.117
  109.7 11.8 %all_to_all.26.in_ref = bf16[8,72,256]{2,1,0:T(8,128)(2,1)S(1)} all-to-all(bf16[8,72,256]{2,1,0:T(8,128)(2,1)S(1)} %shard_map.117), channel_id=1, replica_groups={{0,8,16,24,32,40,48,56},{64,72,80,88,96,104,112,120},{128,136,144,152,1..., dimensions={0} | all-to-all | bytes 589824 | tf_op jit(solution)/shard_map/all_to_all | solution.py:394
  121.5 15.6 %all_to_all.27.in_ref = bf16[8,72,256]{2,1,0:T(8,128)(2,1)S(1)} all-to-all(bf16[8,72,256]{2,1,0:T(8,128)(2,1)S(1)} %shard_map.118), channel_id=1, replica_groups={{0,64,128,192,256,320,384,448},{8,72,136,200,264,328,392,456},{16,80,14..., dimensions={0} | all-to-all | bytes 589824 | tf_op jit(solution)/shard_map/all_to_all | solution.py:396
  137.1 12.2 %all_to_all.28.in_ref = bf16[8,72,256]{2,1,0:T(8,128)(2,1)S(1)} all-to-all(bf16[8,72,256]{2,1,0:T(8,128)(2,1)S(1)} %shard_map.119), channel_id=1, replica_groups={{0,8,16,24,32,40,48,56},{64,72,80,88,96,104,112,120},{128,136,144,152,1..., dimensions={0} | all-to-all | bytes 589824 | tf_op jit(solution)/shard_map/all_to_all | solution.py:398
  149.3 0.8 shard_map.120
  (18 shorter events, 0.2 us)
Async XLA Ops:
  0.6 6.7 %copy-start = (bf16[128,2048]{1,0:T(8,128)(2,1)S(1)}, bf16[128,2048]{1,0:T(8,128)(2,1)}, u32[]{:S(2)}) copy-start(bf16[128,2048]{1,0:T(8,128)(2,1)} %t_ref.5) | copy-start | bytes 1572868
  1.6 14.0 %copy-start.3 = (bf16[2048,64]{0,1:T(8,128)(2,1)S(1)}, bf16[2048,64]{0,1:T(8,128)(2,1)}, u32[]{:S(2)}) copy-start(bf16[2048,64]{0,1:T(8,128)(2,1)} %param.14) | copy-start | bytes 786436
  2.4 20.4 %all-to-all-start = ((bf16[4,256,256]{2,1,0:T(8,128)(2,1)}), bf16[4,256,256]{2,1,0:T(8,128)(2,1)S(1)}, u32[]{:S(2)}, u32[]{:S(2)}) async-start(bf16[4,256,256]{2,1,0:T(8,128)(2,1)} %broadcast_in_dim.3), calls=%async_computation | async-start | bytes 1048576 | tf_op jit(solution)/shard_map/all_to_all | solution.py:334
  8.1 8.6 %collective-permute-start = (bf16[128,1024]{1,0:T(8,128)(2,1)S(1)}, bf16[128,1024]{1,0:T(8,128)(2,1)S(1)}, u32[]{:S(2)}, u32[]{:S(2)}) collective-permute-start(bf16[128,1024]{1,0:T(8,128)(2,1)S(1)} %get-tuple-element.21), channel_id=1, source_target_pairs={{0,8},{8,0},{16,24},{24,16},{32,40},{40,32},{48,56},{56,48},{64,72... | collective-permute-start | bytes 786440 | tf_op jit(solution)/shard_map/ppermute | solution.py:326
  16.7 15.1 %collective-permute-start.1 = (bf16[272,1024]{1,0:T(8,128)(2,1)S(1)}, bf16[272,1024]{1,0:T(8,128)(2,1)S(1)}, u32[]{:S(2)}, u32[]{:S(2)}) collective-permute-start(bf16[272,1024]{1,0:T(8,128)(2,1)S(1)} %pad_maximum_fusion.refs_0_), channel_id=1, source_target_pairs={{0,1},{1,2},{2,3},{3,4},{4,5},{5,6},{6,7},{7,0},{8,15},{9,8},{10,9... | collective-permute-start | bytes 1671176 | tf_op jit(solution)/shard_map/ppermute | solution.py:82
  22.9 13.6 %collective-permute-start.5 = (bf16[1088,256]{1,0:T(8,128)(2,1)S(1)}, bf16[1088,256]{1,0:T(8,128)(2,1)S(1)}, u32[]{:S(2)}, u32[]{:S(2)}) collective-permute-start(bf16[1088,256]{1,0:T(8,128)(2,1)S(1)} %pad.4.refs_7_), channel_id=1, source_target_pairs={{64,0},{456,8},{80,16},{472,24},{96,32},{488,40},{112,48},{504,56}... | collective-permute-start | bytes 1671176 | tf_op jit(solution)/shard_map/ppermute | solution.py:82
  26.1 12.3 %collective-permute-start.12 = (bf16[272,1024]{1,0:T(8,128)(2,1)S(1)}, bf16[272,1024]{1,0:T(8,128)(2,1)S(1)}, u32[]{:S(2)}, u32[]{:S(2)}) collective-permute-start(bf16[272,1024]{1,0:T(8,128)(2,1)S(1)} %pad_maximum_fusion.refs_0_), channel_id=1, source_target_pairs={{1,0},{2,1},{3,2},{4,3},{5,4},{6,5},{7,6},{0,7},{15,8},{8,9},{9,10... | collective-permute-start | bytes 1671176 | tf_op jit(solution)/shard_map/ppermute | solution.py:82
  28.0 12.3 %collective-permute-start.9 = (bf16[1088,256]{1,0:T(8,128)(2,1)S(1)}, bf16[1088,256]{1,0:T(8,128)(2,1)S(1)}, u32[]{:S(2)}, u32[]{:S(2)}) collective-permute-start(bf16[1088,256]{1,0:T(8,128)(2,1)S(1)} %pad.4.refs_7_), channel_id=1, source_target_pairs={{0,64},{8,456},{16,80},{24,472},{32,96},{40,488},{48,112},{56,504}... | collective-permute-start | bytes 1671176 | tf_op jit(solution)/shard_map/ppermute | solution.py:82
  31.8 14.8 %collective-permute-start.2 = (bf16[272,1024]{1,0:T(8,128)(2,1)S(1)}, bf16[272,1024]{1,0:T(8,128)(2,1)S(1)}, u32[]{:S(2)}, u32[]{:S(2)}) collective-permute-start(bf16[272,1024]{1,0:T(8,128)(2,1)S(1)} %collective-permute-done.1.refs_1_), channel_id=1, source_target_pairs={{0,1},{1,2},{2,3},{3,4},{4,5},{5,6},{6,7},{7,0},{8,15},{9,8},{10,9... | collective-permute-start | bytes 1671176 | tf_op jit(solution)/shard_map/ppermute | solution.py:82
  36.4 15.9 %collective-permute-start.6 = (bf16[1088,256]{1,0:T(8,128)(2,1)S(1)}, bf16[1088,256]{1,0:T(8,128)(2,1)S(1)}, u32[]{:S(2)}, u32[]{:S(2)}) collective-permute-start(bf16[1088,256]{1,0:T(8,128)(2,1)S(1)} %collective-permute-done.5.refs_10_), channel_id=1, source_target_pairs={{64,0},{456,8},{80,16},{472,24},{96,32},{488,40},{112,48},{504,56}... | collective-permute-start | bytes 1671176 | tf_op jit(solution)/shard_map/ppermute | solution.py:82
  38.4 15.8 %collective-permute-start.13 = (bf16[272,1024]{1,0:T(8,128)(2,1)S(1)}, bf16[272,1024]{1,0:T(8,128)(2,1)S(1)}, u32[]{:S(2)}, u32[]{:S(2)}) collective-permute-start(bf16[272,1024]{1,0:T(8,128)(2,1)S(1)} %collective-permute-done.12.refs_4_), channel_id=1, source_target_pairs={{1,0},{2,1},{3,2},{4,3},{5,4},{6,5},{7,6},{0,7},{15,8},{8,9},{9,10... | collective-permute-start | bytes 1671176 | tf_op jit(solution)/shard_map/ppermute | solution.py:82
  40.3 15.8 %collective-permute-start.10 = (bf16[1088,256]{1,0:T(8,128)(2,1)S(1)}, bf16[1088,256]{1,0:T(8,128)(2,1)S(1)}, u32[]{:S(2)}, u32[]{:S(2)}) collective-permute-start(bf16[1088,256]{1,0:T(8,128)(2,1)S(1)} %collective-permute-done.9.refs_8_), channel_id=1, source_target_pairs={{0,64},{8,456},{16,80},{24,472},{32,96},{40,488},{48,112},{56,504}... | collective-permute-start | bytes 1671176 | tf_op jit(solution)/shard_map/ppermute | solution.py:82
  46.7 16.4 %collective-permute-start.3 = (bf16[272,1024]{1,0:T(8,128)(2,1)S(1)}, bf16[272,1024]{1,0:T(8,128)(2,1)S(1)}, u32[]{:S(2)}, u32[]{:S(2)}) collective-permute-start(bf16[272,1024]{1,0:T(8,128)(2,1)S(1)} %collective-permute-done.2.refs_2_), channel_id=1, source_target_pairs={{0,1},{1,2},{2,3},{3,4},{4,5},{5,6},{6,7},{7,0},{8,15},{9,8},{10,9... | collective-permute-start | bytes 1671176 | tf_op jit(solution)/shard_map/ppermute | solution.py:82
  52.3 16.7 %collective-permute-start.7 = (bf16[1088,256]{1,0:T(8,128)(2,1)S(1)}, bf16[1088,256]{1,0:T(8,128)(2,1)S(1)}, u32[]{:S(2)}, u32[]{:S(2)}) collective-permute-start(bf16[1088,256]{1,0:T(8,128)(2,1)S(1)} %collective-permute-done.6.refs_11_), channel_id=1, source_target_pairs={{64,0},{456,8},{80,16},{472,24},{96,32},{488,40},{112,48},{504,56}... | collective-permute-start | bytes 1671176 | tf_op jit(solution)/shard_map/ppermute | solution.py:82
  54.2 16.6 %collective-permute-start.14 = (bf16[272,1024]{1,0:T(8,128)(2,1)S(1)}, bf16[272,1024]{1,0:T(8,128)(2,1)S(1)}, u32[]{:S(2)}, u32[]{:S(2)}) collective-permute-start(bf16[272,1024]{1,0:T(8,128)(2,1)S(1)} %collective-permute-done.13.refs_5_), channel_id=1, source_target_pairs={{1,0},{2,1},{3,2},{4,3},{5,4},{6,5},{7,6},{0,7},{15,8},{8,9},{9,10... | collective-permute-start | bytes 1671176 | tf_op jit(solution)/shard_map/ppermute | solution.py:82
  56.1 18.4 %collective-permute-start.11 = (bf16[1088,256]{1,0:T(8,128)(2,1)S(1)}, bf16[1088,256]{1,0:T(8,128)(2,1)S(1)}, u32[]{:S(2)}, u32[]{:S(2)}) collective-permute-start(bf16[1088,256]{1,0:T(8,128)(2,1)S(1)} %collective-permute-done.10.refs_9_), channel_id=1, source_target_pairs={{0,64},{8,456},{16,80},{24,472},{32,96},{40,488},{48,112},{56,504}... | collective-permute-start | bytes 1671176 | tf_op jit(solution)/shard_map/ppermute | solution.py:82
  63.1 17.2 %collective-permute-start.4 = (bf16[272,1024]{1,0:T(8,128)(2,1)S(1)}, bf16[272,1024]{1,0:T(8,128)(2,1)S(1)}, u32[]{:S(2)}, u32[]{:S(2)}) collective-permute-start(bf16[272,1024]{1,0:T(8,128)(2,1)S(1)} %collective-permute-done.3.refs_3_), channel_id=1, source_target_pairs={{0,1},{1,2},{2,3},{3,4},{4,5},{5,6},{6,7},{7,0},{8,15},{9,8},{10,9... | collective-permute-start | bytes 1671176 | tf_op jit(solution)/shard_map/ppermute | solution.py:85
  68.9 17.2 %collective-permute-start.8 = (bf16[1088,256]{1,0:T(8,128)(2,1)S(1)}, bf16[1088,256]{1,0:T(8,128)(2,1)S(1)}, u32[]{:S(2)}, u32[]{:S(2)}) collective-permute-start(bf16[1088,256]{1,0:T(8,128)(2,1)S(1)} %collective-permute-done.7.refs_12_), channel_id=1, source_target_pairs={{64,0},{456,8},{80,16},{472,24},{96,32},{488,40},{112,48},{504,56}... | collective-permute-start | bytes 1671176 | tf_op jit(solution)/shard_map/ppermute | solution.py:85
  86.2 5.0 %copy-start.1 = (bf16[128,2048]{1,0:T(8,128)(2,1)S(1)}, bf16[128,2048]{1,0:T(8,128)(2,1)}, u32[]{:S(2)}) copy-start(bf16[128,2048]{1,0:T(8,128)(2,1)} %q_ref.1) | copy-start | bytes 1572868
  86.2 5.0 %copy-start.2 = (bf16[128,2048]{1,0:T(8,128)(2,1)S(1)}, bf16[128,2048]{1,0:T(8,128)(2,1)}, u32[]{:S(2)}) copy-start(bf16[128,2048]{1,0:T(8,128)(2,1)} %p_ref.1) | copy-start | bytes 1572868
  86.2 5.0 %copy-start.4 = (bf16[64,128]{1,0:T(8,128)(2,1)S(1)}, bf16[64,128]{1,0:T(8,128)(2,1)}, u32[]{:S(2)}) copy-start(bf16[64,128]{1,0:T(8,128)(2,1)} %upk_ref.1) | copy-start | bytes 49156
  86.2 5.0 %copy-start.5 = (bf16[64,128]{1,0:T(8,128)(2,1)S(1)}, bf16[64,128]{1,0:T(8,128)(2,1)}, u32[]{:S(2)}) copy-start(bf16[64,128]{1,0:T(8,128)(2,1)} %upv_ref.1) | copy-start | bytes 49156
  86.2 5.0 %copy-start.6 = (s32[1,8]{1,0:T(1,128)S(1)}, s32[1,8]{1,0:T(1,128)}, u32[]{:S(2)}) copy-start(s32[1,8]{1,0:T(1,128)} %lengths_ref.3) | copy-start | bytes 100
  87.9 3.3 %collective-permute-start.15 = (f32[128,256]{1,0:T(8,128)S(1)}, f32[128,256]{1,0:T(8,128)S(1)}, u32[]{:S(2)}, u32[]{:S(2)}) collective-permute-start(f32[128,256]{1,0:T(8,128)S(1)} %get-tuple-element.29), channel_id=1, source_target_pairs={{0,8},{8,0},{16,24},{24,16},{32,40},{40,32},{48,56},{56,48},{64,72... | collective-permute-start | bytes 393224 | tf_op jit(solution)/shard_map/ppermute | solution.py:375

commit v16 on v14

--- a/solution.py
+++ b/solution.py
@@ -225,12 +225,12 @@
     first = gap.astype(BF).astype(F32)
     second = (gap - first).astype(BF).astype(F32)
     third = gap - first - second
-    line = lax.broadcasted_iota(jnp.int32, (16, rows), 0)
+    line = lax.broadcasted_iota(jnp.int32, (8, rows), 0)
     tail = jnp.where(line == 0, first, jnp.where(line == 1, second, jnp.where(line == 2, third, 0.0)))
     tail = tail.astype(BF)
     for i in range(pack_ref.shape[0]):
         pack_ref[i, pl.ds(0, 64)] = back
-        pack_ref[i, pl.ds(64, 16)] = tail
+        pack_ref[i, pl.ds(64, 8)] = tail
 
 
 def weigh_kernel(lengths_ref, pack_ref, low_half_ref, gk_ref, gv_ref, t_ref, out_ref):
@@ -365,7 +365,7 @@
     got = lax.ppermute(other, "row", swap)
     pack, gk, gv = call(
         attend_kernel,
-        [((8, 80, 128), BF), ((rows, HD), F32), ((rows, HD), F32)],
+        [((8, 72, 128), BF), ((rows, HD), F32), ((rows, HD), F32)],
         [SMEM] + [VMEM] * 5 + [HBM] * 2,
         [VMEM] * 3,
         lengths, own, got, low_half, up_key, up_value, queries, probes,

time: 151 us -> 150 us (level)
  no operation moved by 1% of the time
where the time goes in v16:
time: 150 us
  starting transfers between devices  67.6 us (45%)
  blocking collectives  49.2 us (33%)
  waiting for transfers between devices  18.1 us (12%)
  Pallas kernels  11.8 us (8%)
    ppermute x12, starting transfers between devices, rings_of(): going[side] = [lax.ppermute(now[i], axes[i], ways[i]) for i in both]  42 us
    all_to_all x1, blocking collectives, on_device(): lax.all_to_all(square, 'row', 0, 0, axis_index_groups=y_lines)  14.4 us
    all_to_all x1, blocking collectives, on_device(): pieces = lax.all_to_all(summed, 'row', 0, 0, axis_index_groups=squares)  12.2 us
    pallas_call x9, Pallas kernels, call(): pl.pallas_call(kernel, out_shape=[jax.ShapeDtypeStruct(s, d) for s, d in...  11.8 us
    all_to_all x1, blocking collectives, on_device(): term_parts = lax.all_to_all(terms, 'row', 0, 0, axis_index_groups=squares)  11.5 us
    all_to_all x1, blocking collectives, on_device(): packs = lax.all_to_all(pack, 'col', 0, 0)  11.1 us
    ppermute x2, waiting for transfers between devices, rings_of(): lax.ppermute(going[i][i], axes[i], (fores, afts)[i][i])  9.95 us
    ppermute x1, starting transfers between devices, on_device(): swapped = lax.ppermute(theirs, 'row', swap)  7.46 us
  transfers between devices with their start and end apart: 17, of which 9 were waited for; matrix products, arithmetic and copies ran while one was open for 0% of the time, Pallas kernels for 3%

profile of v16, /device:TPU:1, one launch (start us, length us, event | category | flops | bytes accessed | tf_op | source)
XLA Modules:
  0.0 149.6 jit_solution(12485605532485532505)
XLA Ops:
  0.6 0.9 pad_maximum_fusion.1
  1.5 0.8 broadcast_in_dim.3
  2.4 5.0 %all-to-all-start = ((bf16[4,256,256]{2,1,0:T(8,128)(2,1)}), bf16[4,256,256]{2,1,0:T(8,128)(2,1)S(1)}, u32[]{:S(2)}, u32[]{:S(2)}) async-start(bf16[4,256,256]{2,1,0:T(8,128)(2,1)} %broadcast_in_dim.3), calls=%async_computation | async-start | bytes 1048576 | tf_op jit(solution)/shard_map/all_to_all | solution.py:325
  7.3 0.1 pad_add_fusion.pos_ref
  7.4 0.7 shard_map.112
  8.1 7.5 %collective-permute-start = (bf16[128,1024]{1,0:T(8,128)(2,1)S(1)}, bf16[128,1024]{1,0:T(8,128)(2,1)S(1)}, u32[]{:S(2)}, u32[]{:S(2)}) collective-permute-start(bf16[128,1024]{1,0:T(8,128)(2,1)S(1)} %get-tuple-element.21), channel_id=1, source_target_pairs={{0,8},{8,0},{16,24},{24,16},{32,40},{40,32},{48,56},{56,48},{64,72... | collective-permute-start | bytes 786440 | tf_op jit(solution)/shard_map/ppermute | solution.py:317
  15.6 0.4 shard_map.113
  16.0 0.8 collective-permute-done
  16.8 6.1 %collective-permute-start.1 = (bf16[272,1024]{1,0:T(8,128)(2,1)S(1)}, bf16[272,1024]{1,0:T(8,128)(2,1)S(1)}, u32[]{:S(2)}, u32[]{:S(2)}) collective-permute-start(bf16[272,1024]{1,0:T(8,128)(2,1)S(1)} %pad_maximum_fusion.refs_0_), channel_id=1, source_target_pairs={{0,1},{1,2},{2,3},{3,4},{4,5},{5,6},{6,7},{7,0},{8,15},{9,8},{10,9... | collective-permute-start | bytes 1671176 | tf_op jit(solution)/shard_map/ppermute | solution.py:81
  22.9 0.0 all-to-all-done
  22.9 3.2 %collective-permute-start.5 = (bf16[1088,256]{1,0:T(8,128)(2,1)S(1)}, bf16[1088,256]{1,0:T(8,128)(2,1)S(1)}, u32[]{:S(2)}, u32[]{:S(2)}) collective-permute-start(bf16[1088,256]{1,0:T(8,128)(2,1)S(1)} %pad.4.refs_7_), channel_id=1, source_target_pairs={{64,0},{456,8},{80,16},{472,24},{96,32},{488,40},{112,48},{504,56}... | collective-permute-start | bytes 1671176 | tf_op jit(solution)/shard_map/ppermute | solution.py:81
  26.1 1.9 %collective-permute-start.9 = (bf16[272,1024]{1,0:T(8,128)(2,1)S(1)}, bf16[272,1024]{1,0:T(8,128)(2,1)S(1)}, u32[]{:S(2)}, u32[]{:S(2)}) collective-permute-start(bf16[272,1024]{1,0:T(8,128)(2,1)S(1)} %pad_maximum_fusion.refs_0_), channel_id=1, source_target_pairs={{1,0},{2,1},{3,2},{4,3},{5,4},{6,5},{7,6},{0,7},{15,8},{8,9},{9,10... | collective-permute-start | bytes 1671176 | tf_op jit(solution)/shard_map/ppermute | solution.py:81
  28.1 3.8 %collective-permute-start.12 = (bf16[1088,256]{1,0:T(8,128)(2,1)S(1)}, bf16[1088,256]{1,0:T(8,128)(2,1)S(1)}, u32[]{:S(2)}, u32[]{:S(2)}) collective-permute-start(bf16[1088,256]{1,0:T(8,128)(2,1)S(1)} %pad.4.refs_7_), channel_id=1, source_target_pairs={{0,64},{8,456},{16,80},{24,472},{32,96},{40,488},{48,112},{56,504}... | collective-permute-start | bytes 1671176 | tf_op jit(solution)/shard_map/ppermute | solution.py:81
  31.9 0.0 collective-permute-done.1.refs_1_
  31.9 4.6 %collective-permute-start.2 = (bf16[272,1024]{1,0:T(8,128)(2,1)S(1)}, bf16[272,1024]{1,0:T(8,128)(2,1)S(1)}, u32[]{:S(2)}, u32[]{:S(2)}) collective-permute-start(bf16[272,1024]{1,0:T(8,128)(2,1)S(1)} %collective-permute-done.1.refs_1_), channel_id=1, source_target_pairs={{0,1},{1,2},{2,3},{3,4},{4,5},{5,6},{6,7},{7,0},{8,15},{9,8},{10,9... | collective-permute-start | bytes 1671176 | tf_op jit(solution)/shard_map/ppermute | solution.py:81
  36.5 0.0 collective-permute-done.5.refs_11_
  36.5 1.9 %collective-permute-start.6 = (bf16[1088,256]{1,0:T(8,128)(2,1)S(1)}, bf16[1088,256]{1,0:T(8,128)(2,1)S(1)}, u32[]{:S(2)}, u32[]{:S(2)}) collective-permute-start(bf16[1088,256]{1,0:T(8,128)(2,1)S(1)} %collective-permute-done.5.refs_11_), channel_id=1, source_target_pairs={{64,0},{456,8},{80,16},{472,24},{96,32},{488,40},{112,48},{504,56}... | collective-permute-start | bytes 1671176 | tf_op jit(solution)/shard_map/ppermute | solution.py:81
  38.4 0.0 collective-permute-done.9.refs_4_
  38.4 1.9 %collective-permute-start.10 = (bf16[272,1024]{1,0:T(8,128)(2,1)S(1)}, bf16[272,1024]{1,0:T(8,128)(2,1)S(1)}, u32[]{:S(2)}, u32[]{:S(2)}) collective-permute-start(bf16[272,1024]{1,0:T(8,128)(2,1)S(1)} %collective-permute-done.9.refs_4_), channel_id=1, source_target_pairs={{1,0},{2,1},{3,2},{4,3},{5,4},{6,5},{7,6},{0,7},{15,8},{8,9},{9,10... | collective-permute-start | bytes 1671176 | tf_op jit(solution)/shard_map/ppermute | solution.py:81
  40.4 0.0 collective-permute-done.12.refs_8_
  40.4 4.6 %collective-permute-start.13 = (bf16[1088,256]{1,0:T(8,128)(2,1)S(1)}, bf16[1088,256]{1,0:T(8,128)(2,1)S(1)}, u32[]{:S(2)}, u32[]{:S(2)}) collective-permute-start(bf16[1088,256]{1,0:T(8,128)(2,1)S(1)} %collective-permute-done.12.refs_8_), channel_id=1, source_target_pairs={{0,64},{8,456},{16,80},{24,472},{32,96},{40,488},{48,112},{56,504}... | collective-permute-start | bytes 1671176 | tf_op jit(solution)/shard_map/ppermute | solution.py:81
  44.9 1.8 %collective-permute-done.2.refs_2_ = bf16[272,1024]{1,0:T(8,128)(2,1)S(1)} collective-permute-done((bf16[272,1024]{1,0:T(8,128)(2,1)S(1)}, bf16[272,1024]{1,0:T(8,128)(2,1)S(1)}, u32[]{:S(2)}, u32[]{:S(2)}) %collective-permute-start.2) | collective-permute-done | bytes 557088 | tf_op jit(solution)/shard_map/ppermute | solution.py:81
  46.7 5.3 %collective-permute-start.3 = (bf16[272,1024]{1,0:T(8,128)(2,1)S(1)}, bf16[272,1024]{1,0:T(8,128)(2,1)S(1)}, u32[]{:S(2)}, u32[]{:S(2)}) collective-permute-start(bf16[272,1024]{1,0:T(8,128)(2,1)S(1)} %collective-permute-done.2.refs_2_), channel_id=1, source_target_pairs={{0,1},{1,2},{2,3},{3,4},{4,5},{5,6},{6,7},{7,0},{8,15},{9,8},{10,9... | collective-permute-start | bytes 1671176 | tf_op jit(solution)/shard_map/ppermute | solution.py:81
  52.1 0.3 collective-permute-done.6.refs_12_
  52.3 1.9 %collective-permute-start.7 = (bf16[1088,256]{1,0:T(8,128)(2,1)S(1)}, bf16[1088,256]{1,0:T(8,128)(2,1)S(1)}, u32[]{:S(2)}, u32[]{:S(2)}) collective-permute-start(bf16[1088,256]{1,0:T(8,128)(2,1)S(1)} %collective-permute-done.6.refs_12_), channel_id=1, source_target_pairs={{64,0},{456,8},{80,16},{472,24},{96,32},{488,40},{112,48},{504,56}... | collective-permute-start | bytes 1671176 | tf_op jit(solution)/shard_map/ppermute | solution.py:81
  54.3 1.9 %collective-permute-start.11 = (bf16[272,1024]{1,0:T(8,128)(2,1)S(1)}, bf16[272,1024]{1,0:T(8,128)(2,1)S(1)}, u32[]{:S(2)}, u32[]{:S(2)}) collective-permute-start(bf16[272,1024]{1,0:T(8,128)(2,1)S(1)} %collective-permute-done.10.refs_5_), channel_id=1, source_target_pairs={{1,0},{2,1},{3,2},{4,3},{5,4},{6,5},{7,6},{0,7},{15,8},{8,9},{9,10... | collective-permute-start | bytes 1671176 | tf_op jit(solution)/shard_map/ppermute | solution.py:81
  56.2 0.0 collective-permute-done.13.refs_9_
  56.2 4.9 %collective-permute-start.14 = (bf16[1088,256]{1,0:T(8,128)(2,1)S(1)}, bf16[1088,256]{1,0:T(8,128)(2,1)S(1)}, u32[]{:S(2)}, u32[]{:S(2)}) collective-permute-start(bf16[1088,256]{1,0:T(8,128)(2,1)S(1)} %collective-permute-done.13.refs_9_), channel_id=1, source_target_pairs={{0,64},{8,456},{16,80},{24,472},{32,96},{40,488},{48,112},{56,504}... | collective-permute-start | bytes 1671176 | tf_op jit(solution)/shard_map/ppermute | solution.py:81
  61.1 2.0 %collective-permute-done.3.refs_3_ = bf16[272,1024]{1,0:T(8,128)(2,1)S(1)} collective-permute-done((bf16[272,1024]{1,0:T(8,128)(2,1)S(1)}, bf16[272,1024]{1,0:T(8,128)(2,1)S(1)}, u32[]{:S(2)}, u32[]{:S(2)}) %collective-permute-start.3) | collective-permute-done | bytes 557088 | tf_op jit(solution)/shard_map/ppermute | solution.py:81
  63.1 5.3 %collective-permute-start.4 = (bf16[272,1024]{1,0:T(8,128)(2,1)S(1)}, bf16[272,1024]{1,0:T(8,128)(2,1)S(1)}, u32[]{:S(2)}, u32[]{:S(2)}) collective-permute-start(bf16[272,1024]{1,0:T(8,128)(2,1)S(1)} %collective-permute-done.3.refs_3_), channel_id=1, source_target_pairs={{0,1},{1,2},{2,3},{3,4},{4,5},{5,6},{6,7},{7,0},{8,15},{9,8},{10,9... | collective-permute-start | bytes 1671176 | tf_op jit(solution)/shard_map/ppermute | solution.py:84
  68.4 0.6 collective-permute-done.7.refs_13_
  69.0 1.9 %collective-permute-start.8 = (bf16[1088,256]{1,0:T(8,128)(2,1)S(1)}, bf16[1088,256]{1,0:T(8,128)(2,1)S(1)}, u32[]{:S(2)}, u32[]{:S(2)}) collective-permute-start(bf16[1088,256]{1,0:T(8,128)(2,1)S(1)} %collective-permute-done.7.refs_13_), channel_id=1, source_target_pairs={{64,0},{456,8},{80,16},{472,24},{96,32},{488,40},{112,48},{504,56}... | collective-permute-start | bytes 1671176 | tf_op jit(solution)/shard_map/ppermute | solution.py:84
  70.9 0.0 collective-permute-done.11.refs_6_
  70.9 1.8 %collective-permute-done.14.refs_10_ = bf16[1088,256]{1,0:T(8,128)(2,1)S(1)} collective-permute-done((bf16[1088,256]{1,0:T(8,128)(2,1)S(1)}, bf16[1088,256]{1,0:T(8,128)(2,1)S(1)}, u32[]{:S(2)}, u32[]{:S(2)}) %collective-permute-start.14) | collective-permute-done | bytes 557088 | tf_op jit(solution)/shard_map/ppermute | solution.py:81
  72.7 3.6 %shard_map.114 = (f32[256,256]{1,0:T(8,128)S(1)}, f32[16,1024]{1,0:T(8,128)S(1)}, bf16[256,1024]{1,0:T(8,128)(2,1)S(1)}, bf16[1024,256]{1,0:T(8,128)(2,1)S(1)}) custom-call(s32[3]{0:T(128)S(1)} %pad_add_fusion.pos_ref, bf16[272,1024]{1,0:T(8,128)(2,1)S(1)} %pad_maximum_fusion.refs_0_, bf16[272,1024]{1,0:T(8,128)(2,1)S(1)} %collective-permute-done.1.refs_1_, ...), custom_call_target="tpu_custom_call" | custom-call | flops 1073741824 | bytes 7798784 | tf_op jit(solution)/shard_map/pallas_call | solution.py:277
  76.3 4.0 %collective-permute-done.4.t_ref = bf16[272,1024]{1,0:T(8,128)(2,1)S(1)} collective-permute-done((bf16[272,1024]{1,0:T(8,128)(2,1)S(1)}, bf16[272,1024]{1,0:T(8,128)(2,1)S(1)}, u32[]{:S(2)}, u32[]{:S(2)}) %collective-permute-start.4) | collective-permute-done | bytes 557088 | tf_op jit(solution)/shard_map/ppermute | solution.py:84
  80.3 6.0 %collective-permute-done.8.w_ref = bf16[1088,256]{1,0:T(8,128)(2,1)S(1)} collective-permute-done((bf16[1088,256]{1,0:T(8,128)(2,1)S(1)}, bf16[1088,256]{1,0:T(8,128)(2,1)S(1)}, u32[]{:S(2)}, u32[]{:S(2)}) %collective-permute-start.8) | collective-permute-done | bytes 557088 | tf_op jit(solution)/shard_map/ppermute | solution.py:84
  86.2 0.0 copy-start.6
  86.3 1.4 shard_map.115
  87.7 6.0 %collective-permute-start.15 = (f32[128,256]{1,0:T(8,128)S(1)}, f32[128,256]{1,0:T(8,128)S(1)}, u32[]{:S(2)}, u32[]{:S(2)}) collective-permute-start(f32[128,256]{1,0:T(8,128)S(1)} %get-tuple-element.29), channel_id=1, source_target_pairs={{0,8},{8,0},{16,24},{24,16},{32,40},{40,32},{48,56},{56,48},{64,72... | collective-permute-start | bytes 393224 | tf_op jit(solution)/shard_map/ppermute | solution.py:365
  93.6 1.0 collective-permute-done.15.got_ref
  94.6 3.9 %shard_map.116 = (bf16[8,72,128]{2,1,0:T(8,128)(2,1)S(1)}, f32[128,128]{1,0:T(8,128)S(1)}, f32[128,128]{1,0:T(8,128)S(1)}) custom-call(s32[1,8]{1,0:T(1,128)S(1)} %copy-done.6, f32[128,256]{1,0:T(8,128)S(1)} %get-tuple-element.28.own_ref, f32[128,256]{1,0:T(8,128)S(1)} %collective-permute-done.15.got_ref, ...), custom_call_target="tpu_custom_call" | custom-call | tf_op jit(solution)/shard_map/pallas_call | solution.py:277
  98.5 11.1 %all_to_all.25.pack_ref = bf16[8,72,128]{2,1,0:T(8,128)(2,1)S(1)} all-to-all(bf16[8,72,128]{2,1,0:T(8,128)(2,1)S(1)} %get-tuple-element.31), channel_id=1, replica_groups=mesh['row'=64,'col'=8] {'col'}, dimensions={0} | all-to-all | bytes 294912 | tf_op jit(solution)/shard_map/all_to_all | solution.py:378
  109.6 0.9 shard_map.117
  110.6 11.5 %all_to_all.26.in_ref = bf16[8,72,256]{2,1,0:T(8,128)(2,1)S(1)} all-to-all(bf16[8,72,256]{2,1,0:T(8,128)(2,1)S(1)} %shard_map.117), channel_id=1, replica_groups={{0,8,16,24,32,40,48,56},{64,72,80,88,96,104,112,120},{128,136,144,152,1..., dimensions={0} | all-to-all | bytes 589824 | tf_op jit(solution)/shard_map/all_to_all | solution.py:384
  122.2 14.4 %all_to_all.27.in_ref = bf16[8,72,256]{2,1,0:T(8,128)(2,1)S(1)} all-to-all(bf16[8,72,256]{2,1,0:T(8,128)(2,1)S(1)} %shard_map.118), channel_id=1, replica_groups={{0,64,128,192,256,320,384,448},{8,72,136,200,264,328,392,456},{16,80,14..., dimensions={0} | all-to-all | bytes 589824 | tf_op jit(solution)/shard_map/all_to_all | solution.py:386
  136.6 12.2 %all_to_all.28.in_ref = bf16[8,72,256]{2,1,0:T(8,128)(2,1)S(1)} all-to-all(bf16[8,72,256]{2,1,0:T(8,128)(2,1)S(1)} %shard_map.119), channel_id=1, replica_groups={{0,8,16,24,32,40,48,56},{64,72,80,88,96,104,112,120},{128,136,144,152,1..., dimensions={0} | all-to-all | bytes 589824 | tf_op jit(solution)/shard_map/all_to_all | solution.py:388
  148.7 0.8 shard_map.120
  (18 shorter events, 0.2 us)
Async XLA Ops:
  2.3 5.1 %copy-start = (bf16[128,2048]{1,0:T(8,128)(2,1)S(1)}, bf16[128,2048]{1,0:T(8,128)(2,1)}, u32[]{:S(2)}) copy-start(bf16[128,2048]{1,0:T(8,128)(2,1)} %t_ref.5) | copy-start | bytes 1572868
  2.4 20.5 %all-to-all-start = ((bf16[4,256,256]{2,1,0:T(8,128)(2,1)}), bf16[4,256,256]{2,1,0:T(8,128)(2,1)S(1)}, u32[]{:S(2)}, u32[]{:S(2)}) async-start(bf16[4,256,256]{2,1,0:T(8,128)(2,1)} %broadcast_in_dim.3), calls=%async_computation | async-start | bytes 1048576 | tf_op jit(solution)/shard_map/all_to_all | solution.py:325
  7.3 8.3 %copy-start.3 = (bf16[2048,64]{0,1:T(8,128)(2,1)S(1)}, bf16[2048,64]{0,1:T(8,128)(2,1)}, u32[]{:S(2)}) copy-start(bf16[2048,64]{0,1:T(8,128)(2,1)} %param.14) | copy-start | bytes 786436
  8.1 8.6 %collective-permute-start = (bf16[128,1024]{1,0:T(8,128)(2,1)S(1)}, bf16[128,1024]{1,0:T(8,128)(2,1)S(1)}, u32[]{:S(2)}, u32[]{:S(2)}) collective-permute-start(bf16[128,1024]{1,0:T(8,128)(2,1)S(1)} %get-tuple-element.21), channel_id=1, source_target_pairs={{0,8},{8,0},{16,24},{24,16},{32,40},{40,32},{48,56},{56,48},{64,72... | collective-permute-start | bytes 786440 | tf_op jit(solution)/shard_map/ppermute | solution.py:317
  16.8 15.1 %collective-permute-start.1 = (bf16[272,1024]{1,0:T(8,128)(2,1)S(1)}, bf16[272,1024]{1,0:T(8,128)(2,1)S(1)}, u32[]{:S(2)}, u32[]{:S(2)}) collective-permute-start(bf16[272,1024]{1,0:T(8,128)(2,1)S(1)} %pad_maximum_fusion.refs_0_), channel_id=1, source_target_pairs={{0,1},{1,2},{2,3},{3,4},{4,5},{5,6},{6,7},{7,0},{8,15},{9,8},{10,9... | collective-permute-start | bytes 1671176 | tf_op jit(solution)/shard_map/ppermute | solution.py:81
  22.9 13.6 %collective-permute-start.5 = (bf16[1088,256]{1,0:T(8,128)(2,1)S(1)}, bf16[1088,256]{1,0:T(8,128)(2,1)S(1)}, u32[]{:S(2)}, u32[]{:S(2)}) collective-permute-start(bf16[1088,256]{1,0:T(8,128)(2,1)S(1)} %pad.4.refs_7_), channel_id=1, source_target_pairs={{64,0},{456,8},{80,16},{472,24},{96,32},{488,40},{112,48},{504,56}... | collective-permute-start | bytes 1671176 | tf_op jit(solution)/shard_map/ppermute | solution.py:81
  26.1 12.3 %collective-permute-start.9 = (bf16[272,1024]{1,0:T(8,128)(2,1)S(1)}, bf16[272,1024]{1,0:T(8,128)(2,1)S(1)}, u32[]{:S(2)}, u32[]{:S(2)}) collective-permute-start(bf16[272,1024]{1,0:T(8,128)(2,1)S(1)} %pad_maximum_fusion.refs_0_), channel_id=1, source_target_pairs={{1,0},{2,1},{3,2},{4,3},{5,4},{6,5},{7,6},{0,7},{15,8},{8,9},{9,10... | collective-permute-start | bytes 1671176 | tf_op jit(solution)/shard_map/ppermute | solution.py:81
  28.1 12.3 %collective-permute-start.12 = (bf16[1088,256]{1,0:T(8,128)(2,1)S(1)}, bf16[1088,256]{1,0:T(8,128)(2,1)S(1)}, u32[]{:S(2)}, u32[]{:S(2)}) collective-permute-start(bf16[1088,256]{1,0:T(8,128)(2,1)S(1)} %pad.4.refs_7_), channel_id=1, source_target_pairs={{0,64},{8,456},{16,80},{24,472},{32,96},{40,488},{48,112},{56,504}... | collective-permute-start | bytes 1671176 | tf_op jit(solution)/shard_map/ppermute | solution.py:81
  31.9 14.8 %collective-permute-start.2 = (bf16[272,1024]{1,0:T(8,128)(2,1)S(1)}, bf16[272,1024]{1,0:T(8,128)(2,1)S(1)}, u32[]{:S(2)}, u32[]{:S(2)}) collective-permute-start(bf16[272,1024]{1,0:T(8,128)(2,1)S(1)} %collective-permute-done.1.refs_1_), channel_id=1, source_target_pairs={{0,1},{1,2},{2,3},{3,4},{4,5},{5,6},{6,7},{7,0},{8,15},{9,8},{10,9... | collective-permute-start | bytes 1671176 | tf_op jit(solution)/shard_map/ppermute | solution.py:81
  36.5 15.8 %collective-permute-start.6 = (bf16[1088,256]{1,0:T(8,128)(2,1)S(1)}, bf16[1088,256]{1,0:T(8,128)(2,1)S(1)}, u32[]{:S(2)}, u32[]{:S(2)}) collective-permute-start(bf16[1088,256]{1,0:T(8,128)(2,1)S(1)} %collective-permute-done.5.refs_11_), channel_id=1, source_target_pairs={{64,0},{456,8},{80,16},{472,24},{96,32},{488,40},{112,48},{504,56}... | collective-permute-start | bytes 1671176 | tf_op jit(solution)/shard_map/ppermute | solution.py:81
  38.4 15.8 %collective-permute-start.10 = (bf16[272,1024]{1,0:T(8,128)(2,1)S(1)}, bf16[272,1024]{1,0:T(8,128)(2,1)S(1)}, u32[]{:S(2)}, u32[]{:S(2)}) collective-permute-start(bf16[272,1024]{1,0:T(8,128)(2,1)S(1)} %collective-permute-done.9.refs_4_), channel_id=1, source_target_pairs={{1,0},{2,1},{3,2},{4,3},{5,4},{6,5},{7,6},{0,7},{15,8},{8,9},{9,10... | collective-permute-start | bytes 1671176 | tf_op jit(solution)/shard_map/ppermute | solution.py:81
  40.4 15.8 %collective-permute-start.13 = (bf16[1088,256]{1,0:T(8,128)(2,1)S(1)}, bf16[1088,256]{1,0:T(8,128)(2,1)S(1)}, u32[]{:S(2)}, u32[]{:S(2)}) collective-permute-start(bf16[1088,256]{1,0:T(8,128)(2,1)S(1)} %collective-permute-done.12.refs_8_), channel_id=1, source_target_pairs={{0,64},{8,456},{16,80},{24,472},{32,96},{40,488},{48,112},{56,504}... | collective-permute-start | bytes 1671176 | tf_op jit(solution)/shard_map/ppermute | solution.py:81
  46.7 16.4 %collective-permute-start.3 = (bf16[272,1024]{1,0:T(8,128)(2,1)S(1)}, bf16[272,1024]{1,0:T(8,128)(2,1)S(1)}, u32[]{:S(2)}, u32[]{:S(2)}) collective-permute-start(bf16[272,1024]{1,0:T(8,128)(2,1)S(1)} %collective-permute-done.2.refs_2_), channel_id=1, source_target_pairs={{0,1},{1,2},{2,3},{3,4},{4,5},{5,6},{6,7},{7,0},{8,15},{9,8},{10,9... | collective-permute-start | bytes 1671176 | tf_op jit(solution)/shard_map/ppermute | solution.py:81
  52.3 16.7 %collective-permute-start.7 = (bf16[1088,256]{1,0:T(8,128)(2,1)S(1)}, bf16[1088,256]{1,0:T(8,128)(2,1)S(1)}, u32[]{:S(2)}, u32[]{:S(2)}) collective-permute-start(bf16[1088,256]{1,0:T(8,128)(2,1)S(1)} %collective-permute-done.6.refs_12_), channel_id=1, source_target_pairs={{64,0},{456,8},{80,16},{472,24},{96,32},{488,40},{112,48},{504,56}... | collective-permute-start | bytes 1671176 | tf_op jit(solution)/shard_map/ppermute | solution.py:81
  54.3 16.6 %collective-permute-start.11 = (bf16[272,1024]{1,0:T(8,128)(2,1)S(1)}, bf16[272,1024]{1,0:T(8,128)(2,1)S(1)}, u32[]{:S(2)}, u32[]{:S(2)}) collective-permute-start(bf16[272,1024]{1,0:T(8,128)(2,1)S(1)} %collective-permute-done.10.refs_5_), channel_id=1, source_target_pairs={{1,0},{2,1},{3,2},{4,3},{5,4},{6,5},{7,6},{0,7},{15,8},{8,9},{9,10... | collective-permute-start | bytes 1671176 | tf_op jit(solution)/shard_map/ppermute | solution.py:81
  56.2 16.5 %collective-permute-start.14 = (bf16[1088,256]{1,0:T(8,128)(2,1)S(1)}, bf16[1088,256]{1,0:T(8,128)(2,1)S(1)}, u32[]{:S(2)}, u32[]{:S(2)}) collective-permute-start(bf16[1088,256]{1,0:T(8,128)(2,1)S(1)} %collective-permute-done.13.refs_9_), channel_id=1, source_target_pairs={{0,64},{8,456},{16,80},{24,472},{32,96},{40,488},{48,112},{56,504}... | collective-permute-start | bytes 1671176 | tf_op jit(solution)/shard_map/ppermute | solution.py:81
  63.1 17.2 %collective-permute-start.4 = (bf16[272,1024]{1,0:T(8,128)(2,1)S(1)}, bf16[272,1024]{1,0:T(8,128)(2,1)S(1)}, u32[]{:S(2)}, u32[]{:S(2)}) collective-permute-start(bf16[272,1024]{1,0:T(8,128)(2,1)S(1)} %collective-permute-done.3.refs_3_), channel_id=1, source_target_pairs={{0,1},{1,2},{2,3},{3,4},{4,5},{5,6},{6,7},{7,0},{8,15},{9,8},{10,9... | collective-permute-start | bytes 1671176 | tf_op jit(solution)/shard_map/ppermute | solution.py:84
  69.0 17.2 %collective-permute-start.8 = (bf16[1088,256]{1,0:T(8,128)(2,1)S(1)}, bf16[1088,256]{1,0:T(8,128)(2,1)S(1)}, u32[]{:S(2)}, u32[]{:S(2)}) collective-permute-start(bf16[1088,256]{1,0:T(8,128)(2,1)S(1)} %collective-permute-done.7.refs_13_), channel_id=1, source_target_pairs={{64,0},{456,8},{80,16},{472,24},{96,32},{488,40},{112,48},{504,56}... | collective-permute-start | bytes 1671176 | tf_op jit(solution)/shard_map/ppermute | solution.py:84
  86.2 8.4 %copy-start.1 = (bf16[128,2048]{1,0:T(8,128)(2,1)S(1)}, bf16[128,2048]{1,0:T(8,128)(2,1)}, u32[]{:S(2)}) copy-start(bf16[128,2048]{1,0:T(8,128)(2,1)} %q_ref.1) | copy-start | bytes 1572868
  86.2 8.4 %copy-start.2 = (bf16[128,2048]{1,0:T(8,128)(2,1)S(1)}, bf16[128,2048]{1,0:T(8,128)(2,1)}, u32[]{:S(2)}) copy-start(bf16[128,2048]{1,0:T(8,128)(2,1)} %p_ref.1) | copy-start | bytes 1572868
  86.2 8.4 %copy-start.4 = (bf16[64,128]{1,0:T(8,128)(2,1)S(1)}, bf16[64,128]{1,0:T(8,128)(2,1)}, u32[]{:S(2)}) copy-start(bf16[64,128]{1,0:T(8,128)(2,1)} %upk_ref.1) | copy-start | bytes 49156
  86.2 8.4 %copy-start.5 = (bf16[64,128]{1,0:T(8,128)(2,1)S(1)}, bf16[64,128]{1,0:T(8,128)(2,1)}, u32[]{:S(2)}) copy-start(bf16[64,128]{1,0:T(8,128)(2,1)} %upv_ref.1) | copy-start | bytes 49156
  86.2 8.4 %copy-start.6 = (s32[1,8]{1,0:T(1,128)S(1)}, s32[1,8]{1,0:T(1,128)}, u32[]{:S(2)}) copy-start(s32[1,8]{1,0:T(1,128)} %lengths_ref.3) | copy-start | bytes 100
  87.7 6.9 %collective-permute-start.15 = (f32[128,256]{1,0:T(8,128)S(1)}, f32[128,256]{1,0:T(8,128)S(1)}, u32[]{:S(2)}, u32[]{:S(2)}) collective-permute-start(f32[128,256]{1,0:T(8,128)S(1)} %get-tuple-element.29), channel_id=1, source_target_pairs={{0,8},{8,0},{16,24},{24,16},{32,40},{40,32},{48,56},{56,48},{64,72... | collective-permute-start | bytes 393224 | tf_op jit(solution)/shard_map/ppermute | solution.py:365
